TPU v7x, 32 devices: a whole 2x2x4 slice. The times are simulated.
32 devices in a mesh: prompt: 4 (over y, x), resp: 8 (over z, core).
Axes of the slice: x: 2, y: 2, z: 4, core: 2. Of those that a mesh axis runs over, the one named last changes fastest.
Arguments:
- prompt_rows: bfloat16 [2048, 5120], P(('prompt', 'resp')), may hold values from -6 to 6
- key_weight: bfloat16 [5120, 512], replicated, may hold values from -0.078125 to 0.078125
- value_weight: bfloat16 [5120, 512], replicated, may hold values from -0.078125 to 0.078125
- queries: bfloat16 [4096, 2560], P(('prompt', 'resp')), may hold values from -180 to 180
- own_keys: bfloat16 [4096, 512], P(('prompt', 'resp')), may hold values from -6 to 6
- own_values: bfloat16 [4096, 512], P(('prompt', 'resp')), may hold values from -6 to 6
- out_grad: bfloat16 [4096, 2560], P(('prompt', 'resp')), may hold values from -24 to 24
- first_length: int32 [32], P(('prompt', 'resp')), may hold values from 16 to 112
- resp_prompt: int32 [32, 2], P(('prompt', 'resp')), may hold values from 0 to 3
Outputs:
- query_grad: bfloat16 [4096, 2560], P(('prompt', 'resp'))
- key_grad: bfloat16 [4096, 512], P(('prompt', 'resp'))
- value_grad: bfloat16 [4096, 512], P(('prompt', 'resp'))
- prompt_grad: bfloat16 [2048, 5120], P(('prompt', 'resp'))
All inputs are finite; a program needn't handle non-finite values.
Results may differ from a plain program's by a relative error of at most 0.038.
Values may be sent and summed in bfloat16 or wider, within the bound.
No kernel may reach another device: no remote copies, remote signals or barrier semaphores. Data moves between devices by JAX's collectives and lax.ppermute only.
A program may use at most 192 MiB of HBM per device.

v0:
```python
import functools
import math

import jax
import jax.numpy as jnp
from jax import lax
from jax.experimental import pallas as pl
from jax.experimental.pallas import tpu as pltpu
from jax.sharding import PartitionSpec as P

E = 128
PLEN = 512
SCALE = E ** (-0.5)
EXP2_SCALE = SCALE * math.log2(math.e)
HIDDEN = -1e30
BF16 = jnp.bfloat16
F32 = jnp.float32
VMEM_LIMIT = 40 * 1024 * 1024

ANY = pl.BlockSpec(memory_space=pl.ANY)
SMEM = pl.BlockSpec(memory_space=pltpu.SMEM)
VMEM = pl.BlockSpec(memory_space=pltpu.VMEM)


def params(**kwargs):
    return pltpu.CompilerParams(vmem_limit_bytes=VMEM_LIMIT, **kwargs)


def cost(flops, bytes_accessed, transcendentals=0):
    return pl.CostEstimate(
        flops=int(flops), bytes_accessed=int(bytes_accessed), transcendentals=int(transcendentals)
    )


def lanes(index, width):
    return pl.ds(pl.multiple_of(index * width, 128), width)


def dot(a, b, a_dim, b_dim):
    return lax.dot_general(a, b, (((a_dim,), (b_dim,)), ((), ())), preferred_element_type=F32)


def pack_kernel(n, place_ref, q_ref, g_ref, k_ref, v_ref, *rest):
    outs, sems = rest[:n], rest[n]
    copies = []
    for j in range(n):
        head = place_ref[0] ^ j
        start = 0
        for source in (q_ref, g_ref, k_ref, v_ref):
            width = source.shape[1] // n
            copies.append(
                pltpu.make_async_copy(
                    source.at[:, lanes(head, width)],
                    outs[j].at[:, start : start + width],
                    sems.at[len(copies)],
                )
            )
            start += width
    for copy in copies:
        copy.start()
    for copy in copies:
        copy.wait()


def pack(place, queries, out_grad, own_keys, own_values, n):
    rows = queries.shape[0]
    width = (2 * queries.shape[1] + 2 * own_keys.shape[1]) // n
    return pl.pallas_call(
        functools.partial(pack_kernel, n),
        out_shape=[jax.ShapeDtypeStruct((rows, width), BF16)] * n,
        in_specs=[SMEM, ANY, ANY, ANY, ANY],
        out_specs=[ANY] * n,
        scratch_shapes=[pltpu.SemaphoreType.DMA((4 * n,))],
        compiler_params=params(),
        cost_estimate=cost(0, 4 * n * rows * width),
        name="pack_rows",
    )(place, queries, out_grad, own_keys, own_values)


def unpack_kernel(n, place_ref, *rest):
    packets, (q_ref, k_ref, v_ref), sems = rest[:n], rest[n : n + 3], rest[n + 3]
    copies = []
    for j in range(n):
        head = place_ref[0] ^ j
        start = 0
        for target in (q_ref, k_ref, v_ref):
            width = target.shape[1] // n
            copies.append(
                pltpu.make_async_copy(
                    packets[j].at[:, start : start + width],
                    target.at[:, lanes(head, width)],
                    sems.at[len(copies)],
                )
            )
            start += width
    for copy in copies:
        copy.start()
    for copy in copies:
        copy.wait()


def unpack(place, packets, q_width, kv_width):
    n = len(packets)
    rows = packets[0].shape[0]
    return pl.pallas_call(
        functools.partial(unpack_kernel, n),
        out_shape=[
            jax.ShapeDtypeStruct((rows, width), BF16) for width in (q_width, kv_width, kv_width)
        ],
        in_specs=[SMEM] + [ANY] * n,
        out_specs=[ANY] * 3,
        scratch_shapes=[pltpu.SemaphoreType.DMA((3 * n,))],
        compiler_params=params(),
        cost_estimate=cost(0, 4 * rows * (q_width + 2 * kv_width)),
        name="unpack_rows",
    )(place, *packets)


def project_kernel(n, place_ref, x_ref, kw_ref, vw_ref, *rest):
    outs, key_sum, value_sum = rest[:n], rest[n], rest[n + 1]
    step = pl.program_id(0)
    keys = dot(x_ref[...], kw_ref[...], 1, 0)
    values = dot(x_ref[...], vw_ref[...], 1, 0)

    @pl.when(step == 0)
    def _():
        key_sum[...] = keys
        value_sum[...] = values

    @pl.when(step > 0)
    def _():
        key_sum[...] += keys
        value_sum[...] += values

    @pl.when(step == pl.num_programs(0) - 1)
    def _():
        width = key_sum.shape[1] // n
        for j in range(n):
            head = lanes(place_ref[0] ^ j, width)
            outs[j][:, :width] = key_sum[:, head].astype(BF16)
            outs[j][:, width:] = value_sum[:, head].astype(BF16)


def project(place, prompt_rows, key_weight, value_weight, n, chunk=1024):
    rows, depth = prompt_rows.shape
    width = key_weight.shape[1]
    weight_spec = pl.BlockSpec((chunk, width), lambda i: (i, 0))
    return pl.pallas_call(
        functools.partial(project_kernel, n),
        grid=(depth // chunk,),
        out_shape=[jax.ShapeDtypeStruct((rows, 2 * width // n), BF16)] * n,
        in_specs=[SMEM, pl.BlockSpec((rows, chunk), lambda i: (0, i)), weight_spec, weight_spec],
        out_specs=[pl.BlockSpec((rows, 2 * width // n), lambda i: (0, 0))] * n,
        scratch_shapes=[pltpu.VMEM((rows, width), F32)] * 2,
        compiler_params=params(),
        cost_estimate=cost(4 * rows * depth * width, 4 * depth * width + 2 * rows * depth),
        name="project_prefix",
    )(place, prompt_rows, key_weight, value_weight)


def attend_kernel(n, pieces, group, rows, place_ref, *rest):
    rest = list(rest)

    def take(count):
        taken = rest[:count]
        del rest[:count]
        return taken

    meta = take(n)
    packets = take(n)
    kv_in = take(pieces)
    grads_out = take(n)
    send_out = take(pieces // 2)
    keep_out = take(pieces // 2)
    packed, keys, values, key_acc, value_acc, grads, sems, out_sems = rest
    part = PLEN // pieces

    copies = []
    for m in range(pieces):
        for index, buffer in enumerate((keys, values)):
            copies.append(
                pltpu.make_async_copy(
                    kv_in[m].at[:, :, index * E : (index + 1) * E],
                    buffer.at[:, m * part : (m + 1) * part, :],
                    sems.at[len(copies)],
                )
            )
    for j in range(n):
        copies.append(
            pltpu.make_async_copy(packets[j], packed.at[j], sems.at[len(copies)])
        )
    for copy in copies:
        copy.start()
    key_acc[...] = jnp.zeros_like(key_acc)
    value_acc[...] = jnp.zeros_like(value_acc)
    for copy in copies:
        copy.wait()

    place = place_ref[0]
    total_rows = group * rows
    row_in_column = lax.broadcasted_iota(jnp.int32, (total_rows, E), 0) & (rows - 1)
    row_in_lane = lax.broadcasted_iota(jnp.int32, (rows, total_rows), 1) & (rows - 1)
    own_key = lax.broadcasted_iota(jnp.int32, (rows, total_rows), 0)
    lane_row = lax.broadcasted_iota(jnp.int32, (E, total_rows), 1) & (rows - 1)

    def pick(j, index):
        value = meta[0][index]
        for other in range(1, n):
            value = jnp.where(j == other, meta[other][index], value)
        return value

    def member(j, carry):
        boundary = pick(j, 0)
        first_at = pick(j, 1) ^ place
        second_at = pick(j, 2) ^ place
        heads = [packed[j, :, h * E : (h + 1) * E] for h in range(2 * group + 2)]
        query = jnp.concatenate(heads[:group], axis=0)
        grad = jnp.concatenate(heads[group : 2 * group], axis=0)
        own_k, own_v = heads[2 * group], heads[2 * group + 1]
        in_first = row_in_column < boundary

        def split(x):
            x = x.astype(F32)
            return jnp.concatenate(
                [jnp.where(in_first, x, 0.0), jnp.where(in_first, 0.0, x)], axis=1
            ).astype(BF16)

        query_pair = split(query)
        grad_pair = split(grad)
        key_pair = jnp.concatenate([keys[first_at], keys[second_at]], axis=1)
        value_pair = jnp.concatenate([values[first_at], values[second_at]], axis=1)

        scores = dot(key_pair, query_pair, 1, 1)
        visible = (own_key <= row_in_lane) & ((own_key >= boundary) == (row_in_lane >= boundary))
        own_scores = jnp.where(visible, dot(own_k, query, 1, 1), HIDDEN)
        top = jnp.maximum(
            jnp.max(scores, axis=0, keepdims=True), jnp.max(own_scores, axis=0, keepdims=True)
        )
        weight = jnp.exp2((scores - top) * EXP2_SCALE)
        own_weight = jnp.exp2((own_scores - top) * EXP2_SCALE)
        inverse = 1.0 / (
            jnp.sum(weight, axis=0, keepdims=True) + jnp.sum(own_weight, axis=0, keepdims=True)
        )
        probs = weight * inverse
        own_probs = own_weight * inverse
        probs_low = probs.astype(BF16)
        own_probs_low = own_probs.astype(BF16)
        dprobs = dot(value_pair, grad_pair, 1, 1)
        own_dprobs = dot(own_v, grad, 1, 1)
        delta = jnp.sum(probs_low.astype(F32) * dprobs, axis=0, keepdims=True) + jnp.sum(
            own_probs_low.astype(F32) * own_dprobs, axis=0, keepdims=True
        )
        dscores = (probs * (dprobs - delta)).astype(BF16)
        own_dscores = (own_probs * (own_dprobs - delta)).astype(BF16)

        key_part = dot(dscores, query_pair, 1, 0)
        value_part = dot(probs_low, grad_pair, 1, 0)
        key_acc[first_at] += key_part[:, :E]
        key_acc[second_at] += key_part[:, E:]
        value_acc[first_at] += value_part[:, :E]
        value_acc[second_at] += value_part[:, E:]

        query_both = dot(key_pair, dscores, 0, 0)
        query_part = jnp.where(lane_row < boundary, query_both[:E], query_both[E:])
        query_part = (query_part + dot(own_k, own_dscores, 0, 0)) * SCALE
        for h in range(group):
            grads[j, :, h * E : (h + 1) * E] = query_part[:, h * rows : (h + 1) * rows].T.astype(
                BF16
            )
        grads[j, :, group * E : (group + 1) * E] = (dot(own_dscores, query, 1, 0) * SCALE).astype(
            BF16
        )
        grads[j, :, (group + 1) * E :] = dot(own_probs_low, grad, 1, 0).astype(BF16)
        return carry

    lax.fori_loop(0, n, member, 0)

    out_copies = [
        pltpu.make_async_copy(grads.at[j], grads_out[j], out_sems.at[j]) for j in range(n)
    ]
    for copy in out_copies:
        copy.start()
    for m in range(pieces):
        target = keep_out[m // 2] if m % 2 == 0 else send_out[m // 2]
        span = slice(m * part, (m + 1) * part)
        target[:, :, :E] = (key_acc[:, span, :] * SCALE).astype(target.dtype)
        target[:, :, E:] = value_acc[:, span, :].astype(target.dtype)
    for copy in out_copies:
        copy.wait()


def attend(place, meta, packets, kv_in):
    n = len(packets)
    pieces = len(kv_in)
    rows, packet_width = packets[0].shape
    group = (packet_width // E - 2) // 2
    part = PLEN // pieces
    out_width = (group + 2) * E
    keys = PLEN + rows
    return pl.pallas_call(
        functools.partial(attend_kernel, n, pieces, group, rows),
        out_shape=[jax.ShapeDtypeStruct((rows, out_width), BF16)] * n
        + [jax.ShapeDtypeStruct((n, part, 2 * E), BF16)] * (pieces // 2)
        + [jax.ShapeDtypeStruct((n, part, 2 * E), F32)] * (pieces // 2),
        in_specs=[SMEM] * (1 + n) + [ANY] * (n + pieces),
        out_specs=[ANY] * n + [VMEM] * pieces,
        scratch_shapes=[
            pltpu.VMEM((n, rows, packet_width), BF16),
            pltpu.VMEM((n, PLEN, E), BF16),
            pltpu.VMEM((n, PLEN, E), BF16),
            pltpu.VMEM((n, PLEN, E), F32),
            pltpu.VMEM((n, PLEN, E), F32),
            pltpu.VMEM((n, rows, out_width), BF16),
            pltpu.SemaphoreType.DMA((2 * pieces + n,)),
            pltpu.SemaphoreType.DMA((n,)),
        ],
        compiler_params=params(),
        cost_estimate=cost(
            20 * n * group * rows * keys * E, 8 * 1024 * 1024, n * group * rows * keys
        ),
        name="attend_heads",
    )(place, *meta, *packets, *kv_in)


def total_kernel(n, keep_ref, *rest):
    parts, outs = rest[:-n], rest[-n:]
    for j in range(n):
        total = keep_ref[j]
        for part in parts:
            total = total + part[j].astype(F32)
        outs[j][...] = total.astype(BF16)


def total(keep, parts):
    n, rows, width = keep.shape
    return pl.pallas_call(
        functools.partial(total_kernel, n),
        out_shape=[jax.ShapeDtypeStruct((rows, width), BF16)] * n,
        in_specs=[VMEM] * (1 + len(parts)),
        out_specs=[VMEM] * n,
        compiler_params=params(),
        cost_estimate=cost(len(parts) * keep.size, (6 + 2 * len(parts)) * keep.size),
        name="total_prefix_grads",
    )(keep, *parts)


def prompt_kernel(n, place_ref, *rest):
    shares, (kw_ref, vw_ref, out_ref, key_grad, value_grad) = rest[:n], rest[n:]

    @pl.when(pl.program_id(0) == 0)
    def _():
        width = key_grad.shape[1] // n
        for j in range(n):
            head = lanes(place_ref[0] ^ j, width)
            key_grad[:, head] = shares[j][:, :width]
            value_grad[:, head] = shares[j][:, width:]

    out_ref[...] = (
        dot(key_grad[...], kw_ref[...], 1, 1) + dot(value_grad[...], vw_ref[...], 1, 1)
    ).astype(BF16)


def prompt_gradient(place, shares, key_weight, value_weight, chunk=1024):
    n = len(shares)
    rows = shares[0].shape[0]
    depth, width = key_weight.shape
    weight_spec = pl.BlockSpec((chunk, width), lambda i: (i, 0))
    return pl.pallas_call(
        functools.partial(prompt_kernel, n),
        grid=(depth // chunk,),
        out_shape=jax.ShapeDtypeStruct((rows, depth), BF16),
        in_specs=[SMEM]
        + [pl.BlockSpec(shares[0].shape, lambda i: (0, 0))] * n
        + [weight_spec, weight_spec],
        out_specs=pl.BlockSpec((rows, chunk), lambda i: (0, i)),
        scratch_shapes=[pltpu.VMEM((rows, width), BF16)] * 2,
        compiler_params=params(),
        cost_estimate=cost(4 * rows * depth * width, 4 * depth * width + 2 * rows * depth),
        name="prompt_gradient",
    )(place, *shares, key_weight, value_weight)


def per_device(
    n_prompt,
    n_resp,
    prompt_rows,
    key_weight,
    value_weight,
    queries,
    own_keys,
    own_values,
    out_grad,
    first_length,
    resp_prompt,
):
    def swap(x, axis, size, offset):
        return lax.ppermute(x, axis, [(i, i ^ offset) for i in range(size)])

    def swap_plane(items):
        return [items[0]] + [swap(items[j], "prompt", n_prompt, j) for j in range(1, n_prompt)]

    place = lax.axis_index("prompt").astype(jnp.int32).reshape(1)
    mine = jnp.concatenate([first_length, resp_prompt.reshape(-1)])
    meta = swap_plane([mine] * n_prompt)
    packets = swap_plane(pack(place, queries, out_grad, own_keys, own_values, n_prompt))

    plane_kv = swap_plane(project(place, prompt_rows, key_weight, value_weight, n_prompt))
    kv = jnp.stack(plane_kv)
    line_kv = [kv] + [swap(kv, "resp", n_resp, m) for m in range(2, n_resp, 2)]
    kv_in = []
    for piece in line_kv:
        kv_in += [piece, swap(piece, "resp", n_resp, 1)]

    outs = attend(place, meta, packets, kv_in)
    half = n_resp // 2
    grads, send, keep = outs[:n_prompt], outs[n_prompt : n_prompt + half], outs[n_prompt + half :]
    sent = [swap(piece, "resp", n_resp, 1) for piece in send]
    arrived = [sent[0]]
    for index in range(1, half):
        chip_sum = (keep[index] + sent[index].astype(F32)).astype(BF16)
        arrived.append(swap(chip_sum, "resp", n_resp, 2 * index))
    shares = swap_plane(total(keep[0], arrived))

    query_grad, key_grad, value_grad = unpack(
        place, swap_plane(grads), queries.shape[1], own_keys.shape[1]
    )
    prompt_grad = prompt_gradient(place, shares, key_weight, value_weight)
    return (query_grad, key_grad, value_grad, prompt_grad)


def solution(mesh):
    both = P(("prompt", "resp"), None)
    return jax.shard_map(
        functools.partial(per_device, mesh.shape["prompt"], mesh.shape["resp"]),
        mesh=mesh,
        in_specs=(both, P(), P(), both, both, both, both, P(("prompt", "resp")), both),
        out_specs=(both, both, both, both),
        check_vma=False,
    )
```

profile of v0, /device:TPU:0, one launch (start us, length us, event | category | flops | bytes accessed | tf_op | source)
XLA Modules:
  0.0 86.1 jit_solution(12170901126186904061)
XLA Ops:
  0.6 2.5 %copy-done = bf16[5120,512]{1,0:T(8,128)(2,1)S(1)} copy-done((bf16[5120,512]{1,0:T(8,128)(2,1)S(1)}, bf16[5120,512]{1,0:T(8,128)(2,1)}, u32[]{:S(2)}) %copy-start) | copy-done | bytes 5242904
  3.1 2.5 %copy-done.1 = bf16[5120,512]{1,0:T(8,128)(2,1)S(1)} copy-done((bf16[5120,512]{1,0:T(8,128)(2,1)S(1)}, bf16[5120,512]{1,0:T(8,128)(2,1)}, u32[]{:S(2)}) %copy-start.1) | copy-done | bytes 5242904
  6.7 2.7 %project_prefix.1 = (bf16[64,256]{1,0:T(8,128)(2,1)S(1)}, bf16[64,256]{1,0:T(8,128)(2,1)S(1)}, bf16[64,256]{1,0:T(8,128)(2,1)S(1)}, bf16[64,256]{1,0:T(8,128)(2,1)S(1)}) custom-call(s32[1]{0:T(128)} %bitcast.place_ref, bf16[64,5120]{1,0:T(8,128)(2,1)S(1)} %copy-done.2, bf16[5120,512]{1,0:T(8,128)(2,1)S(1)} %copy-done, bf16[5120,512]{1,0:T(8,128)(2,1)S(1)} %copy-done.1), custom_call_target="tpu_custom_call" | custom-call | flops 671088640 | bytes 11141120 | tf_op jit(solution)/shard_map/project_prefix/pallas_call | solution.py:148
  9.4 3.0 %collective-permute-start.6 = (bf16[64,256]{1,0:T(8,128)(2,1)S(1)}, bf16[64,256]{1,0:T(8,128)(2,1)S(1)}, u32[]{:S(2)}, u32[]{:S(2)}) collective-permute-start(bf16[64,256]{1,0:T(8,128)(2,1)S(1)} %get-tuple-element.36), channel_id=1, source_target_pairs={{0,8},{8,0},{16,24},{24,16},{1,9},{9,1},{17,25},{25,17},{2,10},{10... | collective-permute-start | bytes 98312 | tf_op jit(solution)/shard_map/ppermute | solution.py:397
  12.4 1.5 %collective-permute-start.7 = (bf16[64,256]{1,0:T(8,128)(2,1)S(1)}, bf16[64,256]{1,0:T(8,128)(2,1)S(1)}, u32[]{:S(2)}, u32[]{:S(2)}) collective-permute-start(bf16[64,256]{1,0:T(8,128)(2,1)S(1)} %get-tuple-element.37), channel_id=1, source_target_pairs={{0,16},{8,24},{16,0},{24,8},{1,17},{9,25},{17,1},{25,9},{2,18},{10... | collective-permute-start | bytes 98312 | tf_op jit(solution)/shard_map/ppermute | solution.py:397
  14.3 2.0 %collective-permute-done.7 = bf16[64,256]{1,0:T(8,128)(2,1)S(1)} collective-permute-done((bf16[64,256]{1,0:T(8,128)(2,1)S(1)}, bf16[64,256]{1,0:T(8,128)(2,1)S(1)}, u32[]{:S(2)}, u32[]{:S(2)}) %collective-permute-start.7) | collective-permute-done | bytes 32800 | tf_op jit(solution)/shard_map/ppermute | solution.py:397
  16.4 2.4 %collective-permute-done.8 = bf16[64,256]{1,0:T(8,128)(2,1)S(1)} collective-permute-done((bf16[64,256]{1,0:T(8,128)(2,1)S(1)}, bf16[64,256]{1,0:T(8,128)(2,1)S(1)}, u32[]{:S(2)}, u32[]{:S(2)}) %collective-permute-start.8) | collective-permute-done | bytes 32800 | tf_op jit(solution)/shard_map/ppermute | solution.py:397
  18.8 3.7 %collective-permute-start.14 = (bf16[4,64,256]{2,1,0:T(8,128)(2,1)S(1)}, bf16[4,64,256]{2,1,0:T(8,128)(2,1)S(1)}, u32[]{:S(2)}, u32[]{:S(2)}) collective-permute-start(bf16[4,64,256]{2,1,0:T(8,128)(2,1)S(1)} %pad_maximum_fusion.rest_8_), channel_id=1, source_target_pairs={{0,6},{1,7},{2,4},{3,5},{4,2},{5,3},{6,0},{7,1},{8,14},{9,15},{10,... | collective-permute-start | bytes 393224 | tf_op jit(solution)/shard_map/ppermute | solution.py:397
  23.7 1.5 %collective-permute-start.1 = (s32[3]{0:T(128)S(1)}, s32[3]{0:T(128)S(1)}, u32[]{:S(2)}, u32[]{:S(2)}) collective-permute-start(s32[3]{0:T(128)S(1)} %pad_add_fusion.rest_0_), channel_id=1, source_target_pairs={{0,16},{8,24},{16,0},{24,8},{1,17},{9,25},{17,1},{25,9},{2,18},{10... | collective-permute-start | bytes 44 | tf_op jit(solution)/shard_map/ppermute | solution.py:397
  25.2 1.5 %collective-permute-start = (s32[3]{0:T(128)S(1)}, s32[3]{0:T(128)S(1)}, u32[]{:S(2)}, u32[]{:S(2)}) collective-permute-start(s32[3]{0:T(128)S(1)} %pad_add_fusion.rest_0_), channel_id=1, source_target_pairs={{0,8},{8,0},{16,24},{24,16},{1,9},{9,1},{17,25},{25,17},{2,10},{10... | collective-permute-start | bytes 44 | tf_op jit(solution)/shard_map/ppermute | solution.py:397
  29.3 2.4 %collective-permute-start.5 = (bf16[128,1536]{1,0:T(8,128)(2,1)S(1)}, bf16[128,1536]{1,0:T(8,128)(2,1)S(1)}, u32[]{:S(2)}, u32[]{:S(2)}) collective-permute-start(bf16[128,1536]{1,0:T(8,128)(2,1)S(1)} %get-tuple-element.34), channel_id=1, source_target_pairs={{0,24},{8,16},{16,8},{24,0},{1,25},{9,17},{17,9},{25,1},{2,26},{10... | collective-permute-start | bytes 1179656 | tf_op jit(solution)/shard_map/ppermute | solution.py:397
  31.8 2.3 %collective-permute-done.12.rest_12_ = bf16[4,64,256]{2,1,0:T(8,128)(2,1)S(1)} collective-permute-done((bf16[4,64,256]{2,1,0:T(8,128)(2,1)S(1)}, bf16[4,64,256]{2,1,0:T(8,128)(2,1)S(1)}, u32[]{:S(2)}, u32[]{:S(2)}) %collective-permute-start.12) | collective-permute-done | bytes 131104 | tf_op jit(solution)/shard_map/ppermute | solution.py:397
  37.0 2.3 %collective-permute-done.3.rest_5_ = bf16[128,1536]{1,0:T(8,128)(2,1)S(1)} collective-permute-done((bf16[128,1536]{1,0:T(8,128)(2,1)S(1)}, bf16[128,1536]{1,0:T(8,128)(2,1)S(1)}, u32[]{:S(2)}, u32[]{:S(2)}) %collective-permute-start.3) | collective-permute-done | bytes 393248 | tf_op jit(solution)/shard_map/ppermute | solution.py:397
  39.2 5.5 %collective-permute-done.4.rest_6_ = bf16[128,1536]{1,0:T(8,128)(2,1)S(1)} collective-permute-done((bf16[128,1536]{1,0:T(8,128)(2,1)S(1)}, bf16[128,1536]{1,0:T(8,128)(2,1)S(1)}, u32[]{:S(2)}, u32[]{:S(2)}) %collective-permute-start.4) | collective-permute-done | bytes 393248 | tf_op jit(solution)/shard_map/ppermute | solution.py:397
  44.7 11.8 %attend_heads.1 = (bf16[128,896]{1,0:T(8,128)(2,1)S(1)}, bf16[128,896]{1,0:T(8,128)(2,1)S(1)}, bf16[128,896]{1,0:T(8,128)(2,1)S(1)}, bf16[128,896]{1,0:T(8,128)(...) custom-call(s32[1]{0:T(128)} %bitcast.place_ref, ...), custom_call_target="tpu_custom_call" | custom-call | flops 4194304000 | bytes 8388608 | tf_op jit(solution)/shard_map/attend_heads/pallas_call | solution.py:300
  59.4 1.8 %collective-permute-start.18 = (bf16[128,896]{1,0:T(8,128)(2,1)S(1)}, bf16[128,896]{1,0:T(8,128)(2,1)S(1)}, u32[]{:S(2)}, u32[]{:S(2)}) collective-permute-start(bf16[128,896]{1,0:T(8,128)(2,1)S(1)} %get-tuple-element.42), channel_id=1, source_target_pairs={{0,24},{8,16},{16,8},{24,0},{1,25},{9,17},{17,9},{25,1},{2,26},{10... | collective-permute-start | bytes 688136 | tf_op jit(solution)/shard_map/ppermute | solution.py:397
  62.5 2.7 %collective-permute-start.23 = (bf16[4,64,256]{2,1,0:T(8,128)(2,1)S(1)}, bf16[4,64,256]{2,1,0:T(8,128)(2,1)S(1)}, u32[]{:S(2)}, u32[]{:S(2)}) collective-permute-start(bf16[4,64,256]{2,1,0:T(8,128)(2,1)S(1)} %add_convert_fusion.1), channel_id=1, source_target_pairs={{0,4},{1,5},{2,6},{3,7},{4,0},{5,1},{6,2},{7,3},{8,12},{9,13},{10,... | collective-permute-start | bytes 393224 | tf_op jit(solution)/shard_map/ppermute | solution.py:397
  65.2 2.8 %collective-permute-done.21.rest_1_ = bf16[4,64,256]{2,1,0:T(8,128)(2,1)S(1)} collective-permute-done((bf16[4,64,256]{2,1,0:T(8,128)(2,1)S(1)}, bf16[4,64,256]{2,1,0:T(8,128)(2,1)S(1)}, u32[]{:S(2)}, u32[]{:S(2)}) %collective-permute-start.21) | collective-permute-done | bytes 131104 | tf_op jit(solution)/shard_map/ppermute | solution.py:397
  68.0 2.8 %collective-permute-start.25 = (bf16[4,64,256]{2,1,0:T(8,128)(2,1)S(1)}, bf16[4,64,256]{2,1,0:T(8,128)(2,1)S(1)}, u32[]{:S(2)}, u32[]{:S(2)}) collective-permute-start(bf16[4,64,256]{2,1,0:T(8,128)(2,1)S(1)} %add_convert_fusion), channel_id=1, source_target_pairs={{0,6},{1,7},{2,4},{3,5},{4,2},{5,3},{6,0},{7,1},{8,14},{9,15},{10,... | collective-permute-start | bytes 393224 | tf_op jit(solution)/shard_map/ppermute | solution.py:397
  70.8 2.3 %collective-permute-done.23.rest_2_ = bf16[4,64,256]{2,1,0:T(8,128)(2,1)S(1)} collective-permute-done((bf16[4,64,256]{2,1,0:T(8,128)(2,1)S(1)}, bf16[4,64,256]{2,1,0:T(8,128)(2,1)S(1)}, u32[]{:S(2)}, u32[]{:S(2)}) %collective-permute-start.23) | collective-permute-done | bytes 131104 | tf_op jit(solution)/shard_map/ppermute | solution.py:397
  73.1 1.8 %collective-permute-done.25.rest_3_ = bf16[4,64,256]{2,1,0:T(8,128)(2,1)S(1)} collective-permute-done((bf16[4,64,256]{2,1,0:T(8,128)(2,1)S(1)}, bf16[4,64,256]{2,1,0:T(8,128)(2,1)S(1)}, u32[]{:S(2)}, u32[]{:S(2)}) %collective-permute-start.25) | collective-permute-done | bytes 131104 | tf_op jit(solution)/shard_map/ppermute | solution.py:397
  76.8 1.8 %collective-permute-start.28 = (bf16[64,256]{1,0:T(8,128)(2,1)S(1)}, bf16[64,256]{1,0:T(8,128)(2,1)S(1)}, u32[]{:S(2)}, u32[]{:S(2)}) collective-permute-start(bf16[64,256]{1,0:T(8,128)(2,1)S(1)} %get-tuple-element.57), channel_id=1, source_target_pairs={{0,24},{8,16},{16,8},{24,0},{1,25},{9,17},{17,9},{25,1},{2,26},{10... | collective-permute-start | bytes 98312 | tf_op jit(solution)/shard_map/ppermute | solution.py:397
  80.0 1.6 %collective-permute-done.28.rest_3_ = bf16[64,256]{1,0:T(8,128)(2,1)S(1)} collective-permute-done((bf16[64,256]{1,0:T(8,128)(2,1)S(1)}, bf16[64,256]{1,0:T(8,128)(2,1)S(1)}, u32[]{:S(2)}, u32[]{:S(2)}) %collective-permute-start.28) | collective-permute-done | bytes 32800 | tf_op jit(solution)/shard_map/ppermute | solution.py:397
  81.6 4.5 %prompt_gradient.1 = bf16[64,5120]{1,0:T(8,128)(2,1)} custom-call(s32[1]{0:T(128)} %bitcast.place_ref, bf16[64,256]{1,0:T(8,128)(2,1)S(1)} %get-tuple-element.54.rest_0_, bf16[64,256]{1,0:T(8,128)(2,1)S(1)} %collective-permute-done.26.rest_1_, bf16[64,256]{1,0:T(8,128)(2,1)S(1)} %collective-permute-done.27.rest_2_, ...), custom_call_target="tpu_custom_call" | custom-call | flops 671088640 | bytes 11141120 | tf_op jit(solution)/shard_map/prompt_gradient/pallas_call | solution.py:368
  (71 shorter events, 15.0 us)
Async XLA Ops:
  9.4 4.9 %collective-permute-start.6 = (bf16[64,256]{1,0:T(8,128)(2,1)S(1)}, bf16[64,256]{1,0:T(8,128)(2,1)S(1)}, u32[]{:S(2)}, u32[]{:S(2)}) collective-permute-start(bf16[64,256]{1,0:T(8,128)(2,1)S(1)} %get-tuple-element.36), channel_id=1, source_target_pairs={{0,8},{8,0},{16,24},{24,16},{1,9},{9,1},{17,25},{25,17},{2,10},{10... | collective-permute-start | bytes 98312 | tf_op jit(solution)/shard_map/ppermute | solution.py:397
  12.4 3.9 %collective-permute-start.7 = (bf16[64,256]{1,0:T(8,128)(2,1)S(1)}, bf16[64,256]{1,0:T(8,128)(2,1)S(1)}, u32[]{:S(2)}, u32[]{:S(2)}) collective-permute-start(bf16[64,256]{1,0:T(8,128)(2,1)S(1)} %get-tuple-element.37), channel_id=1, source_target_pairs={{0,16},{8,24},{16,0},{24,8},{1,17},{9,25},{17,1},{25,9},{2,18},{10... | collective-permute-start | bytes 98312 | tf_op jit(solution)/shard_map/ppermute | solution.py:397
  14.0 4.8 %collective-permute-start.8 = (bf16[64,256]{1,0:T(8,128)(2,1)S(1)}, bf16[64,256]{1,0:T(8,128)(2,1)S(1)}, u32[]{:S(2)}, u32[]{:S(2)}) collective-permute-start(bf16[64,256]{1,0:T(8,128)(2,1)S(1)} %get-tuple-element.38), channel_id=1, source_target_pairs={{0,24},{8,16},{16,8},{24,0},{1,25},{9,17},{17,9},{25,1},{2,26},{10... | collective-permute-start | bytes 98312 | tf_op jit(solution)/shard_map/ppermute | solution.py:397
  18.8 10.5 %collective-permute-start.14 = (bf16[4,64,256]{2,1,0:T(8,128)(2,1)S(1)}, bf16[4,64,256]{2,1,0:T(8,128)(2,1)S(1)}, u32[]{:S(2)}, u32[]{:S(2)}) collective-permute-start(bf16[4,64,256]{2,1,0:T(8,128)(2,1)S(1)} %pad_maximum_fusion.rest_8_), channel_id=1, source_target_pairs={{0,6},{1,7},{2,4},{3,5},{4,2},{5,3},{6,0},{7,1},{8,14},{9,15},{10,... | collective-permute-start | bytes 393224 | tf_op jit(solution)/shard_map/ppermute | solution.py:397
  23.2 4.5 %collective-permute-start.2 = (s32[3]{0:T(128)S(1)}, s32[3]{0:T(128)S(1)}, u32[]{:S(2)}, u32[]{:S(2)}) collective-permute-start(s32[3]{0:T(128)S(1)} %pad_add_fusion.rest_0_), channel_id=1, source_target_pairs={{0,24},{8,16},{16,8},{24,0},{1,25},{9,17},{17,9},{25,1},{2,26},{10... | collective-permute-start | bytes 44 | tf_op jit(solution)/shard_map/ppermute | solution.py:397
  23.7 4.0 %collective-permute-start.1 = (s32[3]{0:T(128)S(1)}, s32[3]{0:T(128)S(1)}, u32[]{:S(2)}, u32[]{:S(2)}) collective-permute-start(s32[3]{0:T(128)S(1)} %pad_add_fusion.rest_0_), channel_id=1, source_target_pairs={{0,16},{8,24},{16,0},{24,8},{1,17},{9,25},{17,1},{25,9},{2,18},{10... | collective-permute-start | bytes 44 | tf_op jit(solution)/shard_map/ppermute | solution.py:397
  25.2 3.6 %collective-permute-start = (s32[3]{0:T(128)S(1)}, s32[3]{0:T(128)S(1)}, u32[]{:S(2)}, u32[]{:S(2)}) collective-permute-start(s32[3]{0:T(128)S(1)} %pad_add_fusion.rest_0_), channel_id=1, source_target_pairs={{0,8},{8,0},{16,24},{24,16},{1,9},{9,1},{17,25},{25,17},{2,10},{10... | collective-permute-start | bytes 44 | tf_op jit(solution)/shard_map/ppermute | solution.py:397
  27.1 12.1 %collective-permute-start.3 = (bf16[128,1536]{1,0:T(8,128)(2,1)S(1)}, bf16[128,1536]{1,0:T(8,128)(2,1)S(1)}, u32[]{:S(2)}, u32[]{:S(2)}) collective-permute-start(bf16[128,1536]{1,0:T(8,128)(2,1)S(1)} %get-tuple-element.32), channel_id=1, source_target_pairs={{0,8},{8,0},{16,24},{24,16},{1,9},{9,1},{17,25},{25,17},{2,10},{10... | collective-permute-start | bytes 1179656 | tf_op jit(solution)/shard_map/ppermute | solution.py:397
  27.7 6.4 %collective-permute-start.12 = (bf16[4,64,256]{2,1,0:T(8,128)(2,1)S(1)}, bf16[4,64,256]{2,1,0:T(8,128)(2,1)S(1)}, u32[]{:S(2)}, u32[]{:S(2)}) collective-permute-start(bf16[4,64,256]{2,1,0:T(8,128)(2,1)S(1)} %pad_maximum_fusion.rest_8_), channel_id=1, source_target_pairs={{0,4},{1,5},{2,6},{3,7},{4,0},{5,1},{6,2},{7,3},{8,12},{9,13},{10,... | collective-permute-start | bytes 393224 | tf_op jit(solution)/shard_map/ppermute | solution.py:397
  27.7 6.4 %collective-permute-start.10 = (bf16[4,64,256]{2,1,0:T(8,128)(2,1)S(1)}, bf16[4,64,256]{2,1,0:T(8,128)(2,1)S(1)}, u32[]{:S(2)}, u32[]{:S(2)}) collective-permute-start(bf16[4,64,256]{2,1,0:T(8,128)(2,1)S(1)} %pad_maximum_fusion.rest_8_), channel_id=1, source_target_pairs={{0,2},{1,3},{2,0},{3,1},{4,6},{5,7},{6,4},{7,5},{8,10},{9,11},{10,... | collective-permute-start | bytes 393224 | tf_op jit(solution)/shard_map/ppermute | solution.py:397
  28.8 15.9 %collective-permute-start.4 = (bf16[128,1536]{1,0:T(8,128)(2,1)S(1)}, bf16[128,1536]{1,0:T(8,128)(2,1)S(1)}, u32[]{:S(2)}, u32[]{:S(2)}) collective-permute-start(bf16[128,1536]{1,0:T(8,128)(2,1)S(1)} %get-tuple-element.33), channel_id=1, source_target_pairs={{0,16},{8,24},{16,0},{24,8},{1,17},{9,25},{17,1},{25,9},{2,18},{10... | collective-permute-start | bytes 1179656 | tf_op jit(solution)/shard_map/ppermute | solution.py:397
  29.3 15.4 %collective-permute-start.5 = (bf16[128,1536]{1,0:T(8,128)(2,1)S(1)}, bf16[128,1536]{1,0:T(8,128)(2,1)S(1)}, u32[]{:S(2)}, u32[]{:S(2)}) collective-permute-start(bf16[128,1536]{1,0:T(8,128)(2,1)S(1)} %get-tuple-element.34), channel_id=1, source_target_pairs={{0,24},{8,16},{16,8},{24,0},{1,25},{9,17},{17,9},{25,1},{2,26},{10... | collective-permute-start | bytes 1179656 | tf_op jit(solution)/shard_map/ppermute | solution.py:397
  56.6 5.9 %collective-permute-start.19 = (bf16[4,64,256]{2,1,0:T(8,128)(2,1)S(1)}, bf16[4,64,256]{2,1,0:T(8,128)(2,1)S(1)}, u32[]{:S(2)}, u32[]{:S(2)}) collective-permute-start(bf16[4,64,256]{2,1,0:T(8,128)(2,1)S(1)} %get-tuple-element.47), channel_id=1, source_target_pairs={{0,1},{1,0},{2,3},{3,2},{4,5},{5,4},{6,7},{7,6},{8,9},{9,8},{10,11... | collective-permute-start | bytes 393224 | tf_op jit(solution)/shard_map/ppermute | solution.py:397
  57.1 2.3 %collective-permute-start.22 = (bf16[4,64,256]{2,1,0:T(8,128)(2,1)S(1)}, bf16[4,64,256]{2,1,0:T(8,128)(2,1)S(1)}, u32[]{:S(2)}, u32[]{:S(2)}) collective-permute-start(bf16[4,64,256]{2,1,0:T(8,128)(2,1)S(1)} %get-tuple-element.51), channel_id=1, source_target_pairs={{0,1},{1,0},{2,3},{3,2},{4,5},{5,4},{6,7},{7,6},{8,9},{9,8},{10,11... | collective-permute-start | bytes 393224 | tf_op jit(solution)/shard_map/ppermute | solution.py:397
  57.1 4.1 %collective-permute-start.24 = (bf16[4,64,256]{2,1,0:T(8,128)(2,1)S(1)}, bf16[4,64,256]{2,1,0:T(8,128)(2,1)S(1)}, u32[]{:S(2)}, u32[]{:S(2)}) collective-permute-start(bf16[4,64,256]{2,1,0:T(8,128)(2,1)S(1)} %get-tuple-element.53), channel_id=1, source_target_pairs={{0,1},{1,0},{2,3},{3,2},{4,5},{5,4},{6,7},{7,6},{8,9},{9,8},{10,11... | collective-permute-start | bytes 393224 | tf_op jit(solution)/shard_map/ppermute | solution.py:397
  57.6 19.2 %collective-permute-start.16 = (bf16[128,896]{1,0:T(8,128)(2,1)S(1)}, bf16[128,896]{1,0:T(8,128)(2,1)S(1)}, u32[]{:S(2)}, u32[]{:S(2)}) collective-permute-start(bf16[128,896]{1,0:T(8,128)(2,1)S(1)} %get-tuple-element.40), channel_id=1, source_target_pairs={{0,8},{8,0},{16,24},{24,16},{1,9},{9,1},{17,25},{25,17},{2,10},{10... | collective-permute-start | bytes 688136 | tf_op jit(solution)/shard_map/ppermute | solution.py:397
  58.7 19.8 %collective-permute-start.17 = (bf16[128,896]{1,0:T(8,128)(2,1)S(1)}, bf16[128,896]{1,0:T(8,128)(2,1)S(1)}, u32[]{:S(2)}, u32[]{:S(2)}) collective-permute-start(bf16[128,896]{1,0:T(8,128)(2,1)S(1)} %get-tuple-element.41), channel_id=1, source_target_pairs={{0,16},{8,24},{16,0},{24,8},{1,17},{9,25},{17,1},{25,9},{2,18},{10... | collective-permute-start | bytes 688136 | tf_op jit(solution)/shard_map/ppermute | solution.py:397
  59.4 19.2 %collective-permute-start.18 = (bf16[128,896]{1,0:T(8,128)(2,1)S(1)}, bf16[128,896]{1,0:T(8,128)(2,1)S(1)}, u32[]{:S(2)}, u32[]{:S(2)}) collective-permute-start(bf16[128,896]{1,0:T(8,128)(2,1)S(1)} %get-tuple-element.42), channel_id=1, source_target_pairs={{0,24},{8,16},{16,8},{24,0},{1,25},{9,17},{17,9},{25,1},{2,26},{10... | collective-permute-start | bytes 688136 | tf_op jit(solution)/shard_map/ppermute | solution.py:397
  61.2 6.8 %collective-permute-start.21 = (bf16[4,64,256]{2,1,0:T(8,128)(2,1)S(1)}, bf16[4,64,256]{2,1,0:T(8,128)(2,1)S(1)}, u32[]{:S(2)}, u32[]{:S(2)}) collective-permute-start(bf16[4,64,256]{2,1,0:T(8,128)(2,1)S(1)} %add_convert_fusion.2), channel_id=1, source_target_pairs={{0,2},{1,3},{2,0},{3,1},{4,6},{5,7},{6,4},{7,5},{8,10},{9,11},{10,... | collective-permute-start | bytes 393224 | tf_op jit(solution)/shard_map/ppermute | solution.py:397
  62.5 10.6 %collective-permute-start.23 = (bf16[4,64,256]{2,1,0:T(8,128)(2,1)S(1)}, bf16[4,64,256]{2,1,0:T(8,128)(2,1)S(1)}, u32[]{:S(2)}, u32[]{:S(2)}) collective-permute-start(bf16[4,64,256]{2,1,0:T(8,128)(2,1)S(1)} %add_convert_fusion.1), channel_id=1, source_target_pairs={{0,4},{1,5},{2,6},{3,7},{4,0},{5,1},{6,2},{7,3},{8,12},{9,13},{10,... | collective-permute-start | bytes 393224 | tf_op jit(solution)/shard_map/ppermute | solution.py:397
  68.0 6.9 %collective-permute-start.25 = (bf16[4,64,256]{2,1,0:T(8,128)(2,1)S(1)}, bf16[4,64,256]{2,1,0:T(8,128)(2,1)S(1)}, u32[]{:S(2)}, u32[]{:S(2)}) collective-permute-start(bf16[4,64,256]{2,1,0:T(8,128)(2,1)S(1)} %add_convert_fusion), channel_id=1, source_target_pairs={{0,6},{1,7},{2,4},{3,5},{4,2},{5,3},{6,0},{7,1},{8,14},{9,15},{10,... | collective-permute-start | bytes 393224 | tf_op jit(solution)/shard_map/ppermute | solution.py:397
  75.0 4.6 %collective-permute-start.26 = (bf16[64,256]{1,0:T(8,128)(2,1)S(1)}, bf16[64,256]{1,0:T(8,128)(2,1)S(1)}, u32[]{:S(2)}, u32[]{:S(2)}) collective-permute-start(bf16[64,256]{1,0:T(8,128)(2,1)S(1)} %get-tuple-element.55), channel_id=1, source_target_pairs={{0,8},{8,0},{16,24},{24,16},{1,9},{9,1},{17,25},{25,17},{2,10},{10... | collective-permute-start | bytes 98312 | tf_op jit(solution)/shard_map/ppermute | solution.py:397
  76.0 3.9 %collective-permute-start.27 = (bf16[64,256]{1,0:T(8,128)(2,1)S(1)}, bf16[64,256]{1,0:T(8,128)(2,1)S(1)}, u32[]{:S(2)}, u32[]{:S(2)}) collective-permute-start(bf16[64,256]{1,0:T(8,128)(2,1)S(1)} %get-tuple-element.56), channel_id=1, source_target_pairs={{0,16},{8,24},{16,0},{24,8},{1,17},{9,25},{17,1},{25,9},{2,18},{10... | collective-permute-start | bytes 98312 | tf_op jit(solution)/shard_map/ppermute | solution.py:397
  76.8 4.8 %collective-permute-start.28 = (bf16[64,256]{1,0:T(8,128)(2,1)S(1)}, bf16[64,256]{1,0:T(8,128)(2,1)S(1)}, u32[]{:S(2)}, u32[]{:S(2)}) collective-permute-start(bf16[64,256]{1,0:T(8,128)(2,1)S(1)} %get-tuple-element.57), channel_id=1, source_target_pairs={{0,24},{8,16},{16,8},{24,0},{1,25},{9,17},{17,9},{25,1},{2,26},{10... | collective-permute-start | bytes 98312 | tf_op jit(solution)/shard_map/ppermute | solution.py:397
  (17 other events, 257.8 us)
where the time goes:
time: 86.4 us; the launch traced here: 86.1 us
  starting transfers between devices  31.9 us (37%)
  waiting for transfers between devices  26.1 us (30%)
  Pallas kernels  20.5 us (24%)
  local copies, waits for them, and re-layouts  6.09 us (7%)
  between operations  1.48 us (2%)
    ppermute x29, starting transfers between devices, swap(): return lax.ppermute(x, axis, [(i, i ^ offset) for i in range(size)])  31.9 us
    ppermute x29, waiting for transfers between devices, swap(): return lax.ppermute(x, axis, [(i, i ^ offset) for i in range(size)])  26.1 us
    pallas_call x1, Pallas kernels, attend(): pl.pallas_call(functools.partial(attend_kernel, n, pieces, group, rows),...  11.8 us
    unnamed x24, local copies, waits for them, and re-layouts  6.09 us
    pallas_call x1, Pallas kernels, prompt_gradient(): pl.pallas_call(functools.partial(prompt_kernel, n), grid=(depth // chunk,...  4.52 us
    pallas_call x1, Pallas kernels, project(): pl.pallas_call(functools.partial(project_kernel, n), grid=(depth // chunk...  2.7 us
  transfers between devices with their start and end apart: 29, of which 16 were waited for; matrix products, arithmetic and copies ran while one was open for 0% of the time, Pallas kernels for 2%

commit v1 on v0

v1 whole, which is shorter than its diff:
```python
import functools
import math

import jax
import jax.numpy as jnp
from jax import lax
from jax.experimental import pallas as pl
from jax.experimental.pallas import tpu as pltpu
from jax.sharding import PartitionSpec as P

E = 128
PLEN = 512
SCALE = E ** (-0.5)
EXP2_SCALE = SCALE * math.log2(math.e)
HIDDEN = -1e30
BF16 = jnp.bfloat16
F32 = jnp.float32
NOTE_ROWS = 16

ANY = pl.BlockSpec(memory_space=pl.ANY)
SMEM = pl.BlockSpec(memory_space=pltpu.SMEM)
VMEM = pl.BlockSpec(memory_space=pltpu.VMEM)


def params(mebibytes=40):
    return pltpu.CompilerParams(vmem_limit_bytes=mebibytes * 1024 * 1024)


def cost(flops, bytes_accessed, transcendentals=0):
    return pl.CostEstimate(
        flops=int(flops), bytes_accessed=int(bytes_accessed), transcendentals=int(transcendentals)
    )


def dot(a, b, a_dim, b_dim):
    return lax.dot_general(a, b, (((a_dim,), (b_dim,)), ((), ())), preferred_element_type=F32)


def pack_kernel(n, length_ref, prompts_ref, q_ref, g_ref, k_ref, v_ref, out_ref, notes, sems):
    rows = q_ref.shape[0]
    lane = lax.broadcasted_iota(jnp.int32, notes.shape, 1)
    note = jnp.where(
        lane < E, length_ref[0], jnp.where(lane < 2 * E, prompts_ref[0, 0], prompts_ref[0, 1])
    )
    notes[...] = note.astype(F32).astype(BF16)
    copies = []
    for member in range(n):
        start = 0
        for source in (q_ref, g_ref, k_ref, v_ref):
            width = source.shape[1] // n
            copies.append(
                pltpu.make_async_copy(
                    source.at[:, member * width : (member + 1) * width],
                    out_ref.at[member, 0:rows, start : start + width],
                    sems.at[len(copies)],
                )
            )
            start += width
        copies.append(
            pltpu.make_async_copy(
                notes, out_ref.at[member, rows : rows + NOTE_ROWS, :], sems.at[len(copies)]
            )
        )
    for copy in copies:
        copy.start()
    for copy in copies:
        copy.wait()


def pack(first_length, resp_prompt, queries, out_grad, own_keys, own_values, n):
    rows = queries.shape[0]
    width = (2 * queries.shape[1] + 2 * own_keys.shape[1]) // n
    return pl.pallas_call(
        functools.partial(pack_kernel, n),
        out_shape=jax.ShapeDtypeStruct((n, rows + NOTE_ROWS, width), BF16),
        in_specs=[SMEM, SMEM, ANY, ANY, ANY, ANY],
        out_specs=ANY,
        scratch_shapes=[
            pltpu.VMEM((NOTE_ROWS, width), BF16),
            pltpu.SemaphoreType.DMA((5 * n,)),
        ],
        compiler_params=params(),
        cost_estimate=cost(0, 4 * n * rows * width),
        name="pack_rows",
    )(first_length, resp_prompt, queries, out_grad, own_keys, own_values)


def unpack_kernel(n, packets, q_ref, k_ref, v_ref, sems):
    copies = []
    for member in range(n):
        start = 0
        for target in (q_ref, k_ref, v_ref):
            width = target.shape[1] // n
            copies.append(
                pltpu.make_async_copy(
                    packets.at[member, :, start : start + width],
                    target.at[:, member * width : (member + 1) * width],
                    sems.at[len(copies)],
                )
            )
            start += width
    for copy in copies:
        copy.start()
    for copy in copies:
        copy.wait()


def unpack(packets, q_width, kv_width):
    n, rows, _ = packets.shape
    return pl.pallas_call(
        functools.partial(unpack_kernel, n),
        out_shape=[
            jax.ShapeDtypeStruct((rows, width), BF16) for width in (q_width, kv_width, kv_width)
        ],
        in_specs=[ANY],
        out_specs=[ANY] * 3,
        scratch_shapes=[pltpu.SemaphoreType.DMA((3 * n,))],
        compiler_params=params(),
        cost_estimate=cost(0, 4 * rows * (q_width + 2 * kv_width)),
        name="unpack_rows",
    )(packets)


def project_kernel(n, x_ref, kw_ref, vw_ref, out_ref, key_sum, value_sum):
    step = pl.program_id(0)
    keys = dot(x_ref[...], kw_ref[...], 1, 0)
    values = dot(x_ref[...], vw_ref[...], 1, 0)

    @pl.when(step == 0)
    def _():
        key_sum[...] = keys
        value_sum[...] = values

    @pl.when(step > 0)
    def _():
        key_sum[...] += keys
        value_sum[...] += values

    @pl.when(step == pl.num_programs(0) - 1)
    def _():
        width = key_sum.shape[1] // n
        for member in range(n):
            head = slice(member * width, (member + 1) * width)
            out_ref[member, :, :width] = key_sum[:, head].astype(BF16)
            out_ref[member, :, width:] = value_sum[:, head].astype(BF16)


def project(prompt_rows, key_weight, value_weight, n, chunk=1024):
    rows, depth = prompt_rows.shape
    width = key_weight.shape[1]
    weight_spec = pl.BlockSpec((chunk, width), lambda i: (i, 0))
    out_shape = (n, rows, 2 * width // n)
    return pl.pallas_call(
        functools.partial(project_kernel, n),
        grid=(depth // chunk,),
        out_shape=jax.ShapeDtypeStruct(out_shape, BF16),
        in_specs=[pl.BlockSpec((rows, chunk), lambda i: (0, i)), weight_spec, weight_spec],
        out_specs=pl.BlockSpec(out_shape, lambda i: (0, 0, 0)),
        scratch_shapes=[pltpu.VMEM((rows, width), F32)] * 2,
        compiler_params=params(60),
        cost_estimate=cost(4 * rows * depth * width, 4 * depth * width + 2 * rows * depth),
        name="project_prefix",
    )(prompt_rows, key_weight, value_weight)


def attend_kernel(n, pieces, group, rows, packets, *rest):
    rest = list(rest)

    def take(count):
        taken = rest[:count]
        del rest[:count]
        return taken

    kv_in = take(pieces)
    (grads_out,) = take(1)
    send_out = take(pieces // 2)
    keep_out = take(pieces // 2)
    packed, keys, values, key_acc, value_acc, grads, sems, out_sem = rest
    part = PLEN // pieces

    copies = []
    for m in range(pieces):
        for index, buffer in enumerate((keys, values)):
            copies.append(
                pltpu.make_async_copy(
                    kv_in[m].at[:, :, index * E : (index + 1) * E],
                    buffer.at[:, m * part : (m + 1) * part, :],
                    sems.at[len(copies)],
                )
            )
    copies.append(pltpu.make_async_copy(packets, packed, sems.at[len(copies)]))
    for copy in copies:
        copy.start()
    key_acc[...] = jnp.zeros_like(key_acc)
    value_acc[...] = jnp.zeros_like(value_acc)
    for copy in copies:
        copy.wait()

    total_rows = group * rows
    row_in_column = lax.broadcasted_iota(jnp.int32, (total_rows, E), 0) & (rows - 1)
    row_in_lane = lax.broadcasted_iota(jnp.int32, (rows, total_rows), 1) & (rows - 1)
    own_key = lax.broadcasted_iota(jnp.int32, (rows, total_rows), 0)
    lane_row = lax.broadcasted_iota(jnp.int32, (E, total_rows), 1) & (rows - 1)

    def note(j, index):
        block = packed[j, rows : rows + NOTE_ROWS, index * E : (index + 1) * E]
        return jnp.max(block.astype(F32)).astype(jnp.int32)

    def member(j, carry):
        boundary, first_at, second_at = note(j, 0), note(j, 1), note(j, 2)
        heads = [packed[j, :rows, h * E : (h + 1) * E] for h in range(2 * group + 2)]
        query = jnp.concatenate(heads[:group], axis=0)
        grad = jnp.concatenate(heads[group : 2 * group], axis=0)
        own_k, own_v = heads[2 * group], heads[2 * group + 1]
        in_first = row_in_column < boundary

        def split(x):
            x = x.astype(F32)
            return jnp.concatenate(
                [jnp.where(in_first, x, 0.0), jnp.where(in_first, 0.0, x)], axis=1
            ).astype(BF16)

        query_pair = split(query)
        grad_pair = split(grad)
        key_pair = jnp.concatenate([keys[first_at], keys[second_at]], axis=1)
        value_pair = jnp.concatenate([values[first_at], values[second_at]], axis=1)

        scores = dot(key_pair, query_pair, 1, 1)
        visible = (own_key <= row_in_lane) & ((own_key >= boundary) == (row_in_lane >= boundary))
        own_scores = jnp.where(visible, dot(own_k, query, 1, 1), HIDDEN)
        top = jnp.maximum(
            jnp.max(scores, axis=0, keepdims=True), jnp.max(own_scores, axis=0, keepdims=True)
        )
        weight = jnp.exp2((scores - top) * EXP2_SCALE)
        own_weight = jnp.exp2((own_scores - top) * EXP2_SCALE)
        inverse = 1.0 / (
            jnp.sum(weight, axis=0, keepdims=True) + jnp.sum(own_weight, axis=0, keepdims=True)
        )
        probs = weight * inverse
        own_probs = own_weight * inverse
        probs_low = probs.astype(BF16)
        own_probs_low = own_probs.astype(BF16)
        dprobs = dot(value_pair, grad_pair, 1, 1)
        own_dprobs = dot(own_v, grad, 1, 1)
        delta = jnp.sum(probs_low.astype(F32) * dprobs, axis=0, keepdims=True) + jnp.sum(
            own_probs_low.astype(F32) * own_dprobs, axis=0, keepdims=True
        )
        dscores = (probs * (dprobs - delta)).astype(BF16)
        own_dscores = (own_probs * (own_dprobs - delta)).astype(BF16)

        key_part = dot(dscores, query_pair, 1, 0)
        value_part = dot(probs_low, grad_pair, 1, 0)
        key_acc[first_at] += key_part[:, :E]
        key_acc[second_at] += key_part[:, E:]
        value_acc[first_at] += value_part[:, :E]
        value_acc[second_at] += value_part[:, E:]

        query_both = dot(key_pair, dscores, 0, 0)
        query_part = jnp.where(lane_row < boundary, query_both[:E], query_both[E:])
        query_part = (query_part + dot(own_k, own_dscores, 0, 0)) * SCALE
        for h in range(group):
            grads[j, :, h * E : (h + 1) * E] = query_part[:, h * rows : (h + 1) * rows].T.astype(
                BF16
            )
        grads[j, :, group * E : (group + 1) * E] = (dot(own_dscores, query, 1, 0) * SCALE).astype(
            BF16
        )
        grads[j, :, (group + 1) * E :] = dot(own_probs_low, grad, 1, 0).astype(BF16)
        return carry

    lax.fori_loop(0, n, member, 0)

    out_copy = pltpu.make_async_copy(grads, grads_out, out_sem)
    out_copy.start()
    for m in range(pieces):
        target = keep_out[m // 2] if m % 2 == 0 else send_out[m // 2]
        span = slice(m * part, (m + 1) * part)
        target[:, :, :E] = (key_acc[:, span, :] * SCALE).astype(target.dtype)
        target[:, :, E:] = value_acc[:, span, :].astype(target.dtype)
    out_copy.wait()


def attend(packets, kv_in):
    n, noted_rows, packet_width = packets.shape
    rows = noted_rows - NOTE_ROWS
    pieces = len(kv_in)
    group = (packet_width // E - 2) // 2
    part = PLEN // pieces
    grads_shape = (n, rows, (group + 2) * E)
    keys = PLEN + rows
    return pl.pallas_call(
        functools.partial(attend_kernel, n, pieces, group, rows),
        out_shape=[jax.ShapeDtypeStruct(grads_shape, BF16)]
        + [jax.ShapeDtypeStruct((n, part, 2 * E), BF16)] * (pieces // 2)
        + [jax.ShapeDtypeStruct((n, part, 2 * E), F32)] * (pieces // 2),
        in_specs=[ANY] * (1 + pieces),
        out_specs=[ANY] + [VMEM] * pieces,
        scratch_shapes=[
            pltpu.VMEM(packets.shape, BF16),
            pltpu.VMEM((n, PLEN, E), BF16),
            pltpu.VMEM((n, PLEN, E), BF16),
            pltpu.VMEM((n, PLEN, E), F32),
            pltpu.VMEM((n, PLEN, E), F32),
            pltpu.VMEM(grads_shape, BF16),
            pltpu.SemaphoreType.DMA((2 * pieces + 1,)),
            pltpu.SemaphoreType.DMA,
        ],
        compiler_params=params(),
        cost_estimate=cost(
            20 * n * group * rows * keys * E, 8 * 1024 * 1024, n * group * rows * keys
        ),
        name="attend_heads",
    )(packets, *kv_in)


def total_kernel(keep_ref, *rest):
    parts, out_ref = rest[:-1], rest[-1]
    result = keep_ref[...]
    for part in parts:
        result = result + part[...].astype(F32)
    out_ref[...] = result.astype(BF16)


def total(keep, parts):
    return pl.pallas_call(
        total_kernel,
        out_shape=jax.ShapeDtypeStruct(keep.shape, BF16),
        in_specs=[VMEM] * (1 + len(parts)),
        out_specs=VMEM,
        compiler_params=params(),
        cost_estimate=cost(len(parts) * keep.size, (6 + 2 * len(parts)) * keep.size),
        name="total_prefix_grads",
    )(keep, *parts)


def prompt_kernel(n, shares, kw_ref, vw_ref, out_ref, key_grad, value_grad):
    @pl.when(pl.program_id(0) == 0)
    def _():
        width = key_grad.shape[1] // n
        for member in range(n):
            head = slice(member * width, (member + 1) * width)
            key_grad[:, head] = shares[member, :, :width]
            value_grad[:, head] = shares[member, :, width:]

    out_ref[...] = (
        dot(key_grad[...], kw_ref[...], 1, 1) + dot(value_grad[...], vw_ref[...], 1, 1)
    ).astype(BF16)


def prompt_gradient(shares, key_weight, value_weight, chunk=1024):
    n, rows, _ = shares.shape
    depth, width = key_weight.shape
    weight_spec = pl.BlockSpec((chunk, width), lambda i: (i, 0))
    return pl.pallas_call(
        functools.partial(prompt_kernel, n),
        grid=(depth // chunk,),
        out_shape=jax.ShapeDtypeStruct((rows, depth), BF16),
        in_specs=[pl.BlockSpec(shares.shape, lambda i: (0, 0, 0)), weight_spec, weight_spec],
        out_specs=pl.BlockSpec((rows, chunk), lambda i: (0, i)),
        scratch_shapes=[pltpu.VMEM((rows, width), BF16)] * 2,
        compiler_params=params(),
        cost_estimate=cost(4 * rows * depth * width, 4 * depth * width + 2 * rows * depth),
        name="prompt_gradient",
    )(shares, key_weight, value_weight)


def per_device(
    n_prompt,
    n_resp,
    prompt_rows,
    key_weight,
    value_weight,
    queries,
    own_keys,
    own_values,
    out_grad,
    first_length,
    resp_prompt,
):
    def swap(x, offset):
        return lax.ppermute(x, "resp", [(i, i ^ offset) for i in range(n_resp)])

    def transpose_plane(x):
        return lax.all_to_all(x, "prompt", 0, 0, tiled=True)

    packets = pack(first_length, resp_prompt, queries, out_grad, own_keys, own_values, n_prompt)
    packets, prompt_rows = lax.optimization_barrier((packets, prompt_rows))
    packets = transpose_plane(packets)

    kv = transpose_plane(project(prompt_rows, key_weight, value_weight, n_prompt))
    kv_in = []
    for m in range(0, n_resp, 2):
        piece = swap(kv, m) if m else kv
        kv_in += [piece, swap(piece, 1)]

    grads, *pieces = attend(packets, kv_in)
    half = n_resp // 2
    send, keep = pieces[:half], pieces[half:]
    sent = [swap(piece, 1) for piece in send]
    arrived = [sent[0]]
    for index in range(1, half):
        chip_sum = (keep[index] + sent[index].astype(F32)).astype(BF16)
        arrived.append(swap(chip_sum, 2 * index))
    shares = transpose_plane(total(keep[0], arrived))

    query_grad, key_grad, value_grad = unpack(
        transpose_plane(grads), queries.shape[1], own_keys.shape[1]
    )
    prompt_grad = prompt_gradient(shares, key_weight, value_weight)
    return (query_grad, key_grad, value_grad, prompt_grad)


def solution(mesh):
    both = P(("prompt", "resp"), None)
    return jax.shard_map(
        functools.partial(per_device, mesh.shape["prompt"], mesh.shape["resp"]),
        mesh=mesh,
        in_specs=(both, P(), P(), both, both, both, both, P(("prompt", "resp")), both),
        out_specs=(both, both, both, both),
        check_vma=False,
    )
```

time: 86.4 us -> 98.5 us (1.14); the launches traced: 86.1 us -> 97.1 us
  blocking collectives: 0 us -> 17.7 us
  starting transfers between devices: 31.9 us -> 17.7 us
  Pallas kernels: 20.5 us -> 25.1 us
  local copies, waits for them, and re-layouts: 6.09 us -> 9.6 us
    ppermute x29 -> x14, starting transfers between devices: 31.9 us -> 10.6 us  [swap(): return lax.ppermute(x, 'resp', [(i, i ^ offset) for i in range(n_resp)])]
    all_to_all x0 -> x2, blocking collectives: none -> 17.7 us  [transpose_plane(): return lax.all_to_all(x, 'prompt', 0, 0, tiled=True)]
    all_to_all x0 -> x2, starting transfers between devices: none -> 7.08 us  [transpose_plane(): return lax.all_to_all(x, 'prompt', 0, 0, tiled=True)]
    ppermute x29 -> x14, waiting for transfers between devices: 26.1 us -> 20.2 us  [swap(): return lax.ppermute(x, 'resp', [(i, i ^ offset) for i in range(n_resp)])]
    all_to_all x0 -> x2, waiting for transfers between devices: none -> 5.33 us  [transpose_plane(): return lax.all_to_all(x, 'prompt', 0, 0, tiled=True)]
    pallas_call x1, Pallas kernels: 2.7 us -> 7.04 us  [project(): pl.pallas_call(functools.partial(project_kernel, n), grid=(depth // chunk...]
    unnamed x24 -> x14, local copies, waits for them, and re-layouts: 6.09 us -> 9.6 us
    pallas_call x2, Pallas kernels: 0.45 us -> 2.07 us  [the longest x1 1.99 us: pack(): pl.pallas_call(functools.partial(pack_kernel, n), out_shape=jax.ShapeDtyp...]
  transfers between devices with their start and end apart: 29 -> 16, of which waited for: 16 -> 8; matrix products, arithmetic and copies ran while one was open for 0% -> 0% of each run, Pallas kernels for 2% -> 5%
where the time goes in v1:
time: 98.5 us; the launch traced here: 97.1 us
  waiting for transfers between devices  25.5 us (26%)
  Pallas kernels  25.1 us (25%)
  blocking collectives  17.7 us (18%)
  starting transfers between devices  17.7 us (18%)
  local copies, waits for them, and re-layouts  9.6 us (10%)
  between operations  1.37 us (1%)
    ppermute x14, waiting for transfers between devices, swap(): return lax.ppermute(x, 'resp', [(i, i ^ offset) for i in range(n_resp)])  20.2 us
    all_to_all x2, blocking collectives, transpose_plane(): return lax.all_to_all(x, 'prompt', 0, 0, tiled=True)  17.7 us
    ppermute x14, starting transfers between devices, swap(): return lax.ppermute(x, 'resp', [(i, i ^ offset) for i in range(n_resp)])  10.6 us
    pallas_call x1, Pallas kernels, attend(): pl.pallas_call(functools.partial(attend_kernel, n, pieces, group, rows),...  10.5 us
    unnamed x14, local copies, waits for them, and re-layouts  9.6 us
    all_to_all x2, starting transfers between devices, transpose_plane(): return lax.all_to_all(x, 'prompt', 0, 0, tiled=True)  7.08 us
    pallas_call x1, Pallas kernels, project(): pl.pallas_call(functools.partial(project_kernel, n), grid=(depth // chunk...  7.04 us
    all_to_all x2, waiting for transfers between devices, transpose_plane(): return lax.all_to_all(x, 'prompt', 0, 0, tiled=True)  5.33 us
  transfers between devices with their start and end apart: 16, of which 8 were waited for; matrix products, arithmetic and copies ran while one was open for 0% of the time, Pallas kernels for 5%

profile of v1, /device:TPU:0, one launch (start us, length us, event | category | flops | bytes accessed | tf_op | source)
XLA Modules:
  0.0 97.1 jit_solution(15538063666559379528)
XLA Ops:
  1.3 1.1 %copy-done.2 = bf16[128,2560]{1,0:T(8,128)(2,1)S(1)} copy-done((bf16[128,2560]{1,0:T(8,128)(2,1)S(1)}, bf16[128,2560]{1,0:T(8,128)(2,1)}, u32[]{:S(2)}) %copy-start.2) | copy-done | bytes 655384
  2.4 1.1 %copy-done.3 = bf16[128,2560]{1,0:T(8,128)(2,1)S(1)} copy-done((bf16[128,2560]{1,0:T(8,128)(2,1)S(1)}, bf16[128,2560]{1,0:T(8,128)(2,1)}, u32[]{:S(2)}) %copy-start.3) | copy-done | bytes 655384
  3.5 0.9 copy-done.4
  4.4 0.9 copy-done.5
  5.9 2.0 %pack_rows.1 = bf16[4,144,1536]{2,1,0:T(8,128)(2,1)} custom-call(s32[1]{0:T(128)S(6)} %copy.13.length_ref, s32[1,2]{1,0:T(1,128)S(1)} %copy-done.6, bf16[128,2560]{1,0:T(8,128)(2,1)S(1)} %copy-done.2, bf16[128,2560]{1,0:T(8,128)(2,1)S(1)} %copy-done.3, bf16[128,512]{1,0:T(8,128)(2,1)S(1)} %copy-done.4, bf16[128,512]{1,0:T(8,128)(2,1)S(1)} %copy-done.5), custom_call_target="tpu_custom_call" | custom-call | bytes 3145728 | tf_op jit(solution)/shard_map/pack_rows/pallas_call | solution.py:73
  7.9 7.0 %project_prefix.1 = bf16[4,64,256]{2,1,0:T(8,128)(2,1)} custom-call(bf16[64,5120]{1,0:T(8,128)(2,1)} %x_ref, bf16[5120,512]{1,0:T(8,128)(2,1)} %kw_ref.3, bf16[5120,512]{1,0:T(8,128)(2,1)} %vw_ref.3), custom_call_target="tpu_custom_call" | custom-call | flops 671088640 | bytes 11141120 | tf_op jit(solution)/shard_map/project_prefix/pallas_call | solution.py:153
  15.0 10.2 %all_to_all.20.rest_0_ = bf16[4,64,256]{2,1,0:T(8,128)(2,1)S(1)} all-to-all(bf16[4,64,256]{2,1,0:T(8,128)(2,1)} %project_prefix.1), channel_id=1, replica_groups=mesh['prompt'=4,'resp'=8] {'prompt'}, dimensions={0} | all-to-all | bytes 262144 | tf_op jit(solution)/shard_map/all_to_all | solution.py:384
  25.1 3.6 %all-to-all-start = ((bf16[4,144,1536]{2,1,0:T(8,128)(2,1)}), bf16[4,144,1536]{2,1,0:T(8,128)(2,1)S(1)}, u32[]{:S(2)}, u32[]{:S(2)}) async-start(bf16[4,144,1536]{2,1,0:T(8,128)(2,1)} %pack_rows.1), calls=%async_computation | async-start | bytes 3538944 | tf_op jit(solution)/shard_map/all_to_all | solution.py:384
  28.7 3.7 %collective-permute-start.5 = (bf16[4,64,256]{2,1,0:T(8,128)(2,1)S(1)}, bf16[4,64,256]{2,1,0:T(8,128)(2,1)S(1)}, u32[]{:S(2)}, u32[]{:S(2)}) collective-permute-start(bf16[4,64,256]{2,1,0:T(8,128)(2,1)S(1)} %all_to_all.20.rest_0_), channel_id=1, source_target_pairs={{0,6},{1,7},{2,4},{3,5},{4,2},{5,3},{6,0},{7,1},{8,14},{9,15},{10,... | collective-permute-start | bytes 393224 | tf_op jit(solution)/shard_map/ppermute | solution.py:381
  33.2 3.4 %collective-permute-done.5.rest_6_ = bf16[4,64,256]{2,1,0:T(8,128)(2,1)S(1)} collective-permute-done((bf16[4,64,256]{2,1,0:T(8,128)(2,1)S(1)}, bf16[4,64,256]{2,1,0:T(8,128)(2,1)S(1)}, u32[]{:S(2)}, u32[]{:S(2)}) %collective-permute-start.5) | collective-permute-done | bytes 131104 | tf_op jit(solution)/shard_map/ppermute | solution.py:381
  36.6 5.4 %collective-permute-done.3.rest_4_ = bf16[4,64,256]{2,1,0:T(8,128)(2,1)S(1)} collective-permute-done((bf16[4,64,256]{2,1,0:T(8,128)(2,1)S(1)}, bf16[4,64,256]{2,1,0:T(8,128)(2,1)S(1)}, u32[]{:S(2)}, u32[]{:S(2)}) %collective-permute-start.3) | collective-permute-done | bytes 131104 | tf_op jit(solution)/shard_map/ppermute | solution.py:381
  42.6 0.8 collective-permute-done.4.rest_5_
  43.6 5.3 %all-to-all-done.packets = bf16[4,144,1536]{2,1,0:T(8,128)(2,1)S(1)} async-done(((bf16[4,144,1536]{2,1,0:T(8,128)(2,1)}), bf16[4,144,1536]{2,1,0:T(8,128)(2,1)S(1)}, u32[]{:S(2)}, u32[]{:S(2)}) %all-to-all-start) | async-done | bytes 1769504 | tf_op jit(solution)/shard_map/all_to_all | solution.py:384
  48.9 10.5 %attend_heads.1 = (bf16[4,128,896]{2,1,0:T(8,128)(2,1)}, bf16[4,64,256]{2,1,0:T(8,128)(2,1)S(1)}, bf16[4,64,256]{2,1,0:T(8,128)(2,1)S(1)}, bf16[4,64,256]{2,1,0:...) custom-call(bf16[4,144,1536]{2,1,0:T(8,128)(2,1)S(1)} %all-to-all-do, ...), custom_call_target="tpu_custom_call" | custom-call | flops 4194304000 | bytes 8388608 | tf_op jit(solution)/shard_map/attend_heads/pallas_call | solution.py:291
  60.8 1.6 %collective-permute-start.9 = (bf16[4,64,256]{2,1,0:T(8,128)(2,1)S(1)}, bf16[4,64,256]{2,1,0:T(8,128)(2,1)S(1)}, u32[]{:S(2)}, u32[]{:S(2)}) collective-permute-start(bf16[4,64,256]{2,1,0:T(8,128)(2,1)S(1)} %add_convert_fusion.2), channel_id=1, source_target_pairs={{0,2},{1,3},{2,0},{3,1},{4,6},{5,7},{6,4},{7,5},{8,10},{9,11},{10,... | collective-permute-start | bytes 393224 | tf_op jit(solution)/shard_map/ppermute | solution.py:381
  62.5 2.7 %collective-permute-start.11 = (bf16[4,64,256]{2,1,0:T(8,128)(2,1)S(1)}, bf16[4,64,256]{2,1,0:T(8,128)(2,1)S(1)}, u32[]{:S(2)}, u32[]{:S(2)}) collective-permute-start(bf16[4,64,256]{2,1,0:T(8,128)(2,1)S(1)} %add_convert_fusion.1), channel_id=1, source_target_pairs={{0,4},{1,5},{2,6},{3,7},{4,0},{5,1},{6,2},{7,3},{8,12},{9,13},{10,... | collective-permute-start | bytes 393224 | tf_op jit(solution)/shard_map/ppermute | solution.py:381
  65.5 2.8 %collective-permute-done.9.rest_1_ = bf16[4,64,256]{2,1,0:T(8,128)(2,1)S(1)} collective-permute-done((bf16[4,64,256]{2,1,0:T(8,128)(2,1)S(1)}, bf16[4,64,256]{2,1,0:T(8,128)(2,1)S(1)}, u32[]{:S(2)}, u32[]{:S(2)}) %collective-permute-start.9) | collective-permute-done | bytes 131104 | tf_op jit(solution)/shard_map/ppermute | solution.py:381
  68.3 7.1 %collective-permute-done.11.rest_2_ = bf16[4,64,256]{2,1,0:T(8,128)(2,1)S(1)} collective-permute-done((bf16[4,64,256]{2,1,0:T(8,128)(2,1)S(1)}, bf16[4,64,256]{2,1,0:T(8,128)(2,1)S(1)}, u32[]{:S(2)}, u32[]{:S(2)}) %collective-permute-start.11) | collective-permute-done | bytes 131104 | tf_op jit(solution)/shard_map/ppermute | solution.py:381
  75.6 7.6 %all_to_all.21.shares = bf16[4,64,256]{2,1,0:T(8,128)(2,1)S(1)} all-to-all(bf16[4,64,256]{2,1,0:T(8,128)(2,1)S(1)} %total_prefix_grads.1), channel_id=1, replica_groups=mesh['prompt'=4,'resp'=8] {'prompt'}, dimensions={0} | all-to-all | bytes 262144 | tf_op jit(solution)/shard_map/all_to_all | solution.py:384
  83.1 3.5 %all-to-all-start.2 = ((bf16[4,128,896]{2,1,0:T(8,128)(2,1)}), bf16[4,128,896]{2,1,0:T(8,128)(2,1)S(1)}, u32[]{:S(2)}, u32[]{:S(2)}) async-start(bf16[4,128,896]{2,1,0:T(8,128)(2,1)} %get-tuple-element.20), calls=%async_computation.2 | async-start | bytes 1835008 | tf_op jit(solution)/shard_map/all_to_all | solution.py:384
  86.6 2.5 %copy-done = bf16[5120,512]{1,0:T(8,128)(2,1)S(1)} copy-done((bf16[5120,512]{1,0:T(8,128)(2,1)S(1)}, bf16[5120,512]{1,0:T(8,128)(2,1)}, u32[]{:S(2)}) %copy-start) | copy-done | bytes 5242904
  89.1 2.5 %copy-done.1 = bf16[5120,512]{1,0:T(8,128)(2,1)S(1)} copy-done((bf16[5120,512]{1,0:T(8,128)(2,1)S(1)}, bf16[5120,512]{1,0:T(8,128)(2,1)}, u32[]{:S(2)}) %copy-start.1) | copy-done | bytes 5242904
  91.6 4.5 %prompt_gradient.1 = bf16[64,5120]{1,0:T(8,128)(2,1)} custom-call(bf16[4,64,256]{2,1,0:T(8,128)(2,1)S(1)} %all_to_all.21.shares, bf16[5120,512]{1,0:T(8,128)(2,1)S(1)} %copy-done, bf16[5120,512]{1,0:T(8,128)(2,1)S(1)} %copy-done.1), custom_call_target="tpu_custom_call" | custom-call | flops 671088640 | bytes 11141120 | tf_op jit(solution)/shard_map/prompt_gradient/pallas_call | solution.py:354
  96.1 1.0 %unpack_rows.1 = (bf16[128,2560]{1,0:T(8,128)(2,1)}, bf16[128,512]{1,0:T(8,128)(2,1)}, bf16[128,512]{1,0:T(8,128)(2,1)}) custom-call(bf16[4,128,896]{2,1,0:T(8,128)(2,1)S(1)} %all-to-all-done.2.packets), custom_call_target="tpu_custom_call" | custom-call | bytes 1835008 | tf_op jit(solution)/shard_map/unpack_rows/pallas_call | solution.py:110
  (33 shorter events, 4.1 us)
Async XLA Ops:
  1.3 1.1 %copy-start.2 = (bf16[128,2560]{1,0:T(8,128)(2,1)S(1)}, bf16[128,2560]{1,0:T(8,128)(2,1)}, u32[]{:S(2)}) copy-start(bf16[128,2560]{1,0:T(8,128)(2,1)} %q_ref.1) | copy-start | bytes 1966084
  2.4 1.1 %copy-start.3 = (bf16[128,2560]{1,0:T(8,128)(2,1)S(1)}, bf16[128,2560]{1,0:T(8,128)(2,1)}, u32[]{:S(2)}) copy-start(bf16[128,2560]{1,0:T(8,128)(2,1)} %g_ref.1) | copy-start | bytes 1966084
  3.5 0.9 copy-start.4
  4.4 0.9 copy-start.5
  5.3 0.7 copy-start.6
  25.1 23.8 %all-to-all-start = ((bf16[4,144,1536]{2,1,0:T(8,128)(2,1)}), bf16[4,144,1536]{2,1,0:T(8,128)(2,1)S(1)}, u32[]{:S(2)}, u32[]{:S(2)}) async-start(bf16[4,144,1536]{2,1,0:T(8,128)(2,1)} %pack_rows.1), calls=%async_computation | async-start | bytes 3538944 | tf_op jit(solution)/shard_map/all_to_all | solution.py:384
  28.7 7.9 %collective-permute-start.5 = (bf16[4,64,256]{2,1,0:T(8,128)(2,1)S(1)}, bf16[4,64,256]{2,1,0:T(8,128)(2,1)S(1)}, u32[]{:S(2)}, u32[]{:S(2)}) collective-permute-start(bf16[4,64,256]{2,1,0:T(8,128)(2,1)S(1)} %all_to_all.20.rest_0_), channel_id=1, source_target_pairs={{0,6},{1,7},{2,4},{3,5},{4,2},{5,3},{6,0},{7,1},{8,14},{9,15},{10,... | collective-permute-start | bytes 393224 | tf_op jit(solution)/shard_map/ppermute | solution.py:381
  32.4 9.6 %collective-permute-start.3 = (bf16[4,64,256]{2,1,0:T(8,128)(2,1)S(1)}, bf16[4,64,256]{2,1,0:T(8,128)(2,1)S(1)}, u32[]{:S(2)}, u32[]{:S(2)}) collective-permute-start(bf16[4,64,256]{2,1,0:T(8,128)(2,1)S(1)} %all_to_all.20.rest_0_), channel_id=1, source_target_pairs={{0,4},{1,5},{2,6},{3,7},{4,0},{5,1},{6,2},{7,3},{8,12},{9,13},{10,... | collective-permute-start | bytes 393224 | tf_op jit(solution)/shard_map/ppermute | solution.py:381
  32.4 9.6 %collective-permute-start.1 = (bf16[4,64,256]{2,1,0:T(8,128)(2,1)S(1)}, bf16[4,64,256]{2,1,0:T(8,128)(2,1)S(1)}, u32[]{:S(2)}, u32[]{:S(2)}) collective-permute-start(bf16[4,64,256]{2,1,0:T(8,128)(2,1)S(1)} %all_to_all.20.rest_0_), channel_id=1, source_target_pairs={{0,2},{1,3},{2,0},{3,1},{4,6},{5,7},{6,4},{7,5},{8,10},{9,11},{10,... | collective-permute-start | bytes 393224 | tf_op jit(solution)/shard_map/ppermute | solution.py:381
  33.2 9.4 %collective-permute-start = (bf16[4,64,256]{2,1,0:T(8,128)(2,1)S(1)}, bf16[4,64,256]{2,1,0:T(8,128)(2,1)S(1)}, u32[]{:S(2)}, u32[]{:S(2)}) collective-permute-start(bf16[4,64,256]{2,1,0:T(8,128)(2,1)S(1)} %all_to_all.20.rest_0_), channel_id=1, source_target_pairs={{0,1},{1,0},{2,3},{3,2},{4,5},{5,4},{6,7},{7,6},{8,9},{9,8},{10,11... | collective-permute-start | bytes 393224 | tf_op jit(solution)/shard_map/ppermute | solution.py:381
  36.6 5.9 %collective-permute-start.6 = (bf16[4,64,256]{2,1,0:T(8,128)(2,1)S(1)}, bf16[4,64,256]{2,1,0:T(8,128)(2,1)S(1)}, u32[]{:S(2)}, u32[]{:S(2)}) collective-permute-start(bf16[4,64,256]{2,1,0:T(8,128)(2,1)S(1)} %collective-permute-done.5.rest_6_), channel_id=1, source_target_pairs={{0,1},{1,0},{2,3},{3,2},{4,5},{5,4},{6,7},{7,6},{8,9},{9,8},{10,11... | collective-permute-start | bytes 393224 | tf_op jit(solution)/shard_map/ppermute | solution.py:381
  42.0 1.3 %collective-permute-start.4 = (bf16[4,64,256]{2,1,0:T(8,128)(2,1)S(1)}, bf16[4,64,256]{2,1,0:T(8,128)(2,1)S(1)}, u32[]{:S(2)}, u32[]{:S(2)}) collective-permute-start(bf16[4,64,256]{2,1,0:T(8,128)(2,1)S(1)} %collective-permute-done.3.rest_4_), channel_id=1, source_target_pairs={{0,1},{1,0},{2,3},{3,2},{4,5},{5,4},{6,7},{7,6},{8,9},{9,8},{10,11... | collective-permute-start | bytes 393224 | tf_op jit(solution)/shard_map/ppermute | solution.py:381
  42.1 1.5 %collective-permute-start.2 = (bf16[4,64,256]{2,1,0:T(8,128)(2,1)S(1)}, bf16[4,64,256]{2,1,0:T(8,128)(2,1)S(1)}, u32[]{:S(2)}, u32[]{:S(2)}) collective-permute-start(bf16[4,64,256]{2,1,0:T(8,128)(2,1)S(1)} %collective-permute-done.1.rest_2_), channel_id=1, source_target_pairs={{0,1},{1,0},{2,3},{3,2},{4,5},{5,4},{6,7},{7,6},{8,9},{9,8},{10,11... | collective-permute-start | bytes 393224 | tf_op jit(solution)/shard_map/ppermute | solution.py:381
  59.4 1.4 %collective-permute-start.8 = (bf16[4,64,256]{2,1,0:T(8,128)(2,1)S(1)}, bf16[4,64,256]{2,1,0:T(8,128)(2,1)S(1)}, u32[]{:S(2)}, u32[]{:S(2)}) collective-permute-start(bf16[4,64,256]{2,1,0:T(8,128)(2,1)S(1)} %get-tuple-element.27), channel_id=1, source_target_pairs={{0,1},{1,0},{2,3},{3,2},{4,5},{5,4},{6,7},{7,6},{8,9},{9,8},{10,11... | collective-permute-start | bytes 393224 | tf_op jit(solution)/shard_map/ppermute | solution.py:381
  59.5 6.0 %collective-permute-start.7 = (bf16[4,64,256]{2,1,0:T(8,128)(2,1)S(1)}, bf16[4,64,256]{2,1,0:T(8,128)(2,1)S(1)}, u32[]{:S(2)}, u32[]{:S(2)}) collective-permute-start(bf16[4,64,256]{2,1,0:T(8,128)(2,1)S(1)} %get-tuple-element.25), channel_id=1, source_target_pairs={{0,1},{1,0},{2,3},{3,2},{4,5},{5,4},{6,7},{7,6},{8,9},{9,8},{10,11... | collective-permute-start | bytes 393224 | tf_op jit(solution)/shard_map/ppermute | solution.py:381
  60.0 2.5 %collective-permute-start.10 = (bf16[4,64,256]{2,1,0:T(8,128)(2,1)S(1)}, bf16[4,64,256]{2,1,0:T(8,128)(2,1)S(1)}, u32[]{:S(2)}, u32[]{:S(2)}) collective-permute-start(bf16[4,64,256]{2,1,0:T(8,128)(2,1)S(1)} %get-tuple-element.29), channel_id=1, source_target_pairs={{0,1},{1,0},{2,3},{3,2},{4,5},{5,4},{6,7},{7,6},{8,9},{9,8},{10,11... | collective-permute-start | bytes 393224 | tf_op jit(solution)/shard_map/ppermute | solution.py:381
  60.0 5.1 %collective-permute-start.12 = (bf16[4,64,256]{2,1,0:T(8,128)(2,1)S(1)}, bf16[4,64,256]{2,1,0:T(8,128)(2,1)S(1)}, u32[]{:S(2)}, u32[]{:S(2)}) collective-permute-start(bf16[4,64,256]{2,1,0:T(8,128)(2,1)S(1)} %get-tuple-element.31), channel_id=1, source_target_pairs={{0,1},{1,0},{2,3},{3,2},{4,5},{5,4},{6,7},{7,6},{8,9},{9,8},{10,11... | collective-permute-start | bytes 393224 | tf_op jit(solution)/shard_map/ppermute | solution.py:381
  60.8 7.5 %collective-permute-start.9 = (bf16[4,64,256]{2,1,0:T(8,128)(2,1)S(1)}, bf16[4,64,256]{2,1,0:T(8,128)(2,1)S(1)}, u32[]{:S(2)}, u32[]{:S(2)}) collective-permute-start(bf16[4,64,256]{2,1,0:T(8,128)(2,1)S(1)} %add_convert_fusion.2), channel_id=1, source_target_pairs={{0,2},{1,3},{2,0},{3,1},{4,6},{5,7},{6,4},{7,5},{8,10},{9,11},{10,... | collective-permute-start | bytes 393224 | tf_op jit(solution)/shard_map/ppermute | solution.py:381
  62.5 13.0 %collective-permute-start.11 = (bf16[4,64,256]{2,1,0:T(8,128)(2,1)S(1)}, bf16[4,64,256]{2,1,0:T(8,128)(2,1)S(1)}, u32[]{:S(2)}, u32[]{:S(2)}) collective-permute-start(bf16[4,64,256]{2,1,0:T(8,128)(2,1)S(1)} %add_convert_fusion.1), channel_id=1, source_target_pairs={{0,4},{1,5},{2,6},{3,7},{4,0},{5,1},{6,2},{7,3},{8,12},{9,13},{10,... | collective-permute-start | bytes 393224 | tf_op jit(solution)/shard_map/ppermute | solution.py:381
  65.2 10.3 %collective-permute-start.13 = (bf16[4,64,256]{2,1,0:T(8,128)(2,1)S(1)}, bf16[4,64,256]{2,1,0:T(8,128)(2,1)S(1)}, u32[]{:S(2)}, u32[]{:S(2)}) collective-permute-start(bf16[4,64,256]{2,1,0:T(8,128)(2,1)S(1)} %add_convert_fusion), channel_id=1, source_target_pairs={{0,6},{1,7},{2,4},{3,5},{4,2},{5,3},{6,0},{7,1},{8,14},{9,15},{10,... | collective-permute-start | bytes 393224 | tf_op jit(solution)/shard_map/ppermute | solution.py:381
  83.1 13.0 %all-to-all-start.2 = ((bf16[4,128,896]{2,1,0:T(8,128)(2,1)}), bf16[4,128,896]{2,1,0:T(8,128)(2,1)S(1)}, u32[]{:S(2)}, u32[]{:S(2)}) async-start(bf16[4,128,896]{2,1,0:T(8,128)(2,1)} %get-tuple-element.20), calls=%async_computation.2 | async-start | bytes 1835008 | tf_op jit(solution)/shard_map/all_to_all | solution.py:384
  86.6 2.5 %copy-start = (bf16[5120,512]{1,0:T(8,128)(2,1)S(1)}, bf16[5120,512]{1,0:T(8,128)(2,1)}, u32[]{:S(2)}) copy-start(bf16[5120,512]{1,0:T(8,128)(2,1)} %kw_ref.3) | copy-start | bytes 15728644
  89.1 2.5 %copy-start.1 = (bf16[5120,512]{1,0:T(8,128)(2,1)S(1)}, bf16[5120,512]{1,0:T(8,128)(2,1)}, u32[]{:S(2)}) copy-start(bf16[5120,512]{1,0:T(8,128)(2,1)} %vw_ref.3) | copy-start | bytes 15728644

commit v2 on v0

v2 whole, which is shorter than its diff:
```python
import functools
import math

import jax
import jax.numpy as jnp
from jax import lax
from jax.experimental import pallas as pl
from jax.experimental.pallas import tpu as pltpu
from jax.sharding import PartitionSpec as P

E = 128
PLEN = 512
SCALE = E ** (-0.5)
EXP2_SCALE = SCALE * math.log2(math.e)
HIDDEN = -1e30
BF16 = jnp.bfloat16
F32 = jnp.float32
NOTE_ROWS = 16
HEAD_BITS = (3, 1)
GATHER_BITS = (2, 4, 0)

ANY = pl.BlockSpec(memory_space=pl.ANY)
SMEM = pl.BlockSpec(memory_space=pltpu.SMEM)
VMEM = pl.BlockSpec(memory_space=pltpu.VMEM)


def params(mebibytes=40):
    return pltpu.CompilerParams(vmem_limit_bytes=mebibytes * 1024 * 1024)


def cost(flops, bytes_accessed, transcendentals=0):
    return pl.CostEstimate(
        flops=int(flops), bytes_accessed=int(bytes_accessed), transcendentals=int(transcendentals)
    )


def lanes(index, width):
    return pl.ds(pl.multiple_of(index * width, 128), width)


def dot(a, b, a_dim, b_dim):
    return lax.dot_general(a, b, (((a_dim,), (b_dim,)), ((), ())), preferred_element_type=F32)


def pack_kernel(n, place_ref, length_ref, prompts_ref, q_ref, g_ref, k_ref, v_ref, *rest):
    outs, notes, sems = rest[:n], rest[n], rest[n + 1]
    rows = q_ref.shape[0]
    copies = []
    for j in reversed(range(n)):
        start = 0
        for source in (q_ref, g_ref, k_ref, v_ref):
            width = source.shape[1] // n
            copies.append(
                pltpu.make_async_copy(
                    source.at[:, lanes(place_ref[0] ^ j, width)],
                    outs[j].at[0:rows, start : start + width],
                    sems.at[len(copies)],
                )
            )
            start += width
    for copy in copies:
        copy.start()
    lane = lax.broadcasted_iota(jnp.int32, notes.shape, 1)
    note = jnp.where(
        lane < E, length_ref[0], jnp.where(lane < 2 * E, prompts_ref[0, 0], prompts_ref[0, 1])
    )
    notes[...] = note.astype(F32).astype(BF16)
    for j in range(n):
        copy = pltpu.make_async_copy(
            notes, outs[j].at[rows : rows + NOTE_ROWS, :], sems.at[len(copies)]
        )
        copy.start()
        copies.append(copy)
    for copy in copies:
        copy.wait()


def pack(place, first_length, resp_prompt, queries, out_grad, own_keys, own_values, n):
    rows = queries.shape[0]
    width = (2 * queries.shape[1] + 2 * own_keys.shape[1]) // n
    return pl.pallas_call(
        functools.partial(pack_kernel, n),
        out_shape=[jax.ShapeDtypeStruct((rows + NOTE_ROWS, width), BF16)] * n,
        in_specs=[SMEM, SMEM, SMEM, ANY, ANY, ANY, ANY],
        out_specs=[ANY] * n,
        scratch_shapes=[
            pltpu.VMEM((NOTE_ROWS, width), BF16),
            pltpu.SemaphoreType.DMA((5 * n,)),
        ],
        compiler_params=params(60),
        cost_estimate=cost(0, 1024),
        name="pack_rows",
    )(place, first_length, resp_prompt, queries, out_grad, own_keys, own_values)


def unpack_kernel(n, place_ref, *rest):
    packets, targets, sems = rest[:n], rest[n : n + 3], rest[n + 3]
    copies = []
    for j in range(n):
        start = 0
        for target in targets:
            width = target.shape[1] // n
            copies.append(
                pltpu.make_async_copy(
                    packets[j].at[:, start : start + width],
                    target.at[:, lanes(place_ref[0] ^ j, width)],
                    sems.at[len(copies)],
                )
            )
            start += width
    for copy in copies:
        copy.start()
    for copy in copies:
        copy.wait()


def unpack(place, packets, q_width, kv_width):
    n = len(packets)
    rows = packets[0].shape[0]
    return pl.pallas_call(
        functools.partial(unpack_kernel, n),
        out_shape=[
            jax.ShapeDtypeStruct((rows, width), BF16) for width in (q_width, kv_width, kv_width)
        ],
        in_specs=[SMEM] + [ANY] * n,
        out_specs=[ANY] * 3,
        scratch_shapes=[pltpu.SemaphoreType.DMA((3 * n,))],
        compiler_params=params(),
        cost_estimate=cost(0, 4 * rows * (q_width + 2 * kv_width)),
        name="unpack_rows",
    )(place, *packets)


def project_kernel(n, steps, place_ref, x_ref, kw_ref, vw_ref, *rest):
    outs, (kw, vw, key_sum, value_sum, sems) = rest[:n], rest[n:]
    chunk = kw.shape[0] // steps
    copies = []
    for step in range(steps):
        span = slice(step * chunk, (step + 1) * chunk)
        for source, target in ((kw_ref, kw), (vw_ref, vw)):
            copies.append(
                pltpu.make_async_copy(
                    source.at[span, :], target.at[span, :], sems.at[len(copies)]
                )
            )
    for copy in copies:
        copy.start()
    keys = values = None
    for step in range(steps):
        span = slice(step * chunk, (step + 1) * chunk)
        copies[2 * step].wait()
        part = dot(x_ref[:, span], kw[span, :], 1, 0)
        keys = part if step == 0 else keys + part
        copies[2 * step + 1].wait()
        part = dot(x_ref[:, span], vw[span, :], 1, 0)
        values = part if step == 0 else values + part
    key_sum[...] = keys.astype(BF16)
    value_sum[...] = values.astype(BF16)
    width = key_sum.shape[1] // n
    for j in range(n):
        head = lanes(place_ref[0] ^ j, width)
        outs[j][:, :width] = key_sum[:, head]
        outs[j][:, width:] = value_sum[:, head]


def project(place, prompt_rows, key_weight, value_weight, n, steps=5):
    rows = prompt_rows.shape[0]
    width = key_weight.shape[1]
    return pl.pallas_call(
        functools.partial(project_kernel, n, steps),
        out_shape=[jax.ShapeDtypeStruct((rows, 2 * width // n), BF16)] * n,
        in_specs=[SMEM, VMEM, ANY, ANY],
        out_specs=[VMEM] * n,
        scratch_shapes=[pltpu.VMEM(key_weight.shape, BF16)] * 2
        + [pltpu.VMEM((rows, width), BF16)] * 2
        + [pltpu.SemaphoreType.DMA((2 * steps,))],
        compiler_params=params(60),
        cost_estimate=cost(0, 1024),
        name="project_prefix",
    )(place, prompt_rows, key_weight, value_weight)


def attend_kernel(slots, n, group, rows, place_ref, *rest):
    rest = list(rest)

    def take(count):
        taken = rest[:count]
        del rest[:count]
        return taken

    pieces = len(slots)
    packets = take(n)
    kv_in = take(pieces)
    grads_out = take(n)
    prefix_out = take(pieces)
    keys, values, key_acc, value_acc = rest
    part = kv_in[0].shape[1]

    for index in range(pieces):
        for j in range(n):
            prompt, slot = slots[index][j]
            span = slice(slot * part, (slot + 1) * part)
            keys[prompt, span, :] = kv_in[index][j, :, :E]
            values[prompt, span, :] = kv_in[index][j, :, E:]
    key_acc[...] = jnp.zeros_like(key_acc)
    value_acc[...] = jnp.zeros_like(value_acc)

    total_rows = group * rows
    row_in_column = lax.broadcasted_iota(jnp.int32, (total_rows, E), 0) & (rows - 1)
    row_in_lane = lax.broadcasted_iota(jnp.int32, (rows, total_rows), 1) & (rows - 1)
    own_key = lax.broadcasted_iota(jnp.int32, (rows, total_rows), 0)
    lane_row = lax.broadcasted_iota(jnp.int32, (E, total_rows), 1) & (rows - 1)

    for packet, grads in zip(packets, grads_out):

        def note(index):
            block = packet[rows : rows + NOTE_ROWS, index * E : (index + 1) * E]
            return jnp.max(block.astype(F32)).astype(jnp.int32)

        boundary, first_at, second_at = note(0), note(1) ^ place_ref[1], note(2) ^ place_ref[1]
        heads = [packet[:rows, h * E : (h + 1) * E] for h in range(2 * group + 2)]
        query = jnp.concatenate(heads[:group], axis=0)
        grad = jnp.concatenate(heads[group : 2 * group], axis=0)
        own_k, own_v = heads[2 * group], heads[2 * group + 1]
        in_first = row_in_column < boundary

        def split(x):
            x = x.astype(F32)
            return jnp.concatenate(
                [jnp.where(in_first, x, 0.0), jnp.where(in_first, 0.0, x)], axis=1
            ).astype(BF16)

        query_pair = split(query)
        grad_pair = split(grad)
        key_pair = jnp.concatenate([keys[first_at], keys[second_at]], axis=1)
        value_pair = jnp.concatenate([values[first_at], values[second_at]], axis=1)

        scores = dot(key_pair, query_pair, 1, 1)
        visible = (own_key <= row_in_lane) & ((own_key >= boundary) == (row_in_lane >= boundary))
        own_scores = jnp.where(visible, dot(own_k, query, 1, 1), HIDDEN)
        top = jnp.maximum(
            jnp.max(scores, axis=0, keepdims=True), jnp.max(own_scores, axis=0, keepdims=True)
        )
        weight = jnp.exp2((scores - top) * EXP2_SCALE)
        own_weight = jnp.exp2((own_scores - top) * EXP2_SCALE)
        inverse = 1.0 / (
            jnp.sum(weight, axis=0, keepdims=True) + jnp.sum(own_weight, axis=0, keepdims=True)
        )
        probs = weight * inverse
        own_probs = own_weight * inverse
        probs_low = probs.astype(BF16)
        own_probs_low = own_probs.astype(BF16)
        dprobs = dot(value_pair, grad_pair, 1, 1)
        own_dprobs = dot(own_v, grad, 1, 1)
        delta = jnp.sum(probs_low.astype(F32) * dprobs, axis=0, keepdims=True) + jnp.sum(
            own_probs_low.astype(F32) * own_dprobs, axis=0, keepdims=True
        )
        dscores = (probs * (dprobs - delta)).astype(BF16)
        own_dscores = (own_probs * (own_dprobs - delta)).astype(BF16)

        key_part = dot(dscores, query_pair, 1, 0)
        value_part = dot(probs_low, grad_pair, 1, 0)
        key_acc[first_at] += key_part[:, :E]
        key_acc[second_at] += key_part[:, E:]
        value_acc[first_at] += value_part[:, :E]
        value_acc[second_at] += value_part[:, E:]

        query_both = dot(key_pair, dscores, 0, 0)
        query_part = jnp.where(lane_row < boundary, query_both[:E], query_both[E:])
        query_part = (query_part + dot(own_k, own_dscores, 0, 0)) * SCALE
        for h in range(group):
            grads[:, h * E : (h + 1) * E] = query_part[:, h * rows : (h + 1) * rows].T.astype(BF16)
        grads[:, group * E : (group + 1) * E] = (dot(own_dscores, query, 1, 0) * SCALE).astype(BF16)
        grads[:, (group + 1) * E :] = dot(own_probs_low, grad, 1, 0).astype(BF16)

    for index in range(pieces):
        for j in range(n):
            prompt, slot = slots[index][j]
            span = slice(slot * part, (slot + 1) * part)
            target = prefix_out[index]
            target[j, :, :E] = (key_acc[prompt, span, :] * SCALE).astype(target.dtype)
            target[j, :, E:] = value_acc[prompt, span, :].astype(target.dtype)


def attend(place, packets, kv_in, slots, out_types, prompts):
    n = len(packets)
    noted_rows, packet_width = packets[0].shape
    rows = noted_rows - NOTE_ROWS
    group = (packet_width // E - 2) // 2
    keys = PLEN + rows
    return pl.pallas_call(
        functools.partial(attend_kernel, slots, n, group, rows),
        out_shape=[jax.ShapeDtypeStruct((rows, (group + 2) * E), BF16)] * n
        + [jax.ShapeDtypeStruct(kv_in[0].shape, kind) for kind in out_types],
        in_specs=[SMEM] + [VMEM] * (n + len(kv_in)),
        out_specs=[VMEM] * (n + len(kv_in)),
        scratch_shapes=[
            pltpu.VMEM((prompts, PLEN, E), BF16),
            pltpu.VMEM((prompts, PLEN, E), BF16),
            pltpu.VMEM((prompts, PLEN, E), F32),
            pltpu.VMEM((prompts, PLEN, E), F32),
        ],
        compiler_params=params(),
        cost_estimate=cost(
            20 * n * group * rows * keys * E, 8 * 1024 * 1024, n * group * rows * keys
        ),
        name="attend_head",
    )(place, *packets, *kv_in)


def total_kernel(n, keep_ref, *rest):
    parts, outs = rest[:-n], rest[-n:]
    for j in range(n):
        result = keep_ref[j]
        for part in parts:
            result = result + part[j].astype(F32)
        outs[j][...] = result.astype(BF16)


def total(keep, parts):
    n = keep.shape[0]
    return pl.pallas_call(
        functools.partial(total_kernel, n),
        out_shape=[jax.ShapeDtypeStruct(keep.shape[1:], BF16)] * n,
        in_specs=[VMEM] * (1 + len(parts)),
        out_specs=[VMEM] * n,
        compiler_params=params(),
        cost_estimate=cost(len(parts) * keep.size, (6 + 2 * len(parts)) * keep.size),
        name="total_prefix_grads",
    )(keep, *parts)


def prompt_kernel(n, place_ref, *rest):
    shares, (kw_ref, vw_ref, out_ref, key_grad, value_grad) = rest[:n], rest[n:]

    @pl.when(pl.program_id(0) == 0)
    def _():
        width = key_grad.shape[1] // n
        for j in range(n):
            head = lanes(place_ref[0] ^ j, width)
            key_grad[:, head] = shares[j][:, :width]
            value_grad[:, head] = shares[j][:, width:]

    out_ref[...] = (
        dot(key_grad[...], kw_ref[...], 1, 1) + dot(value_grad[...], vw_ref[...], 1, 1)
    ).astype(BF16)


def prompt_gradient(place, shares, key_weight, value_weight, chunk=1024):
    n = len(shares)
    rows = shares[0].shape[0]
    depth, width = key_weight.shape
    weight_spec = pl.BlockSpec((chunk, width), lambda i: (i, 0))
    return pl.pallas_call(
        functools.partial(prompt_kernel, n),
        grid=(depth // chunk,),
        out_shape=jax.ShapeDtypeStruct((rows, depth), BF16),
        in_specs=[SMEM]
        + [pl.BlockSpec(shares[0].shape, lambda i: (0, 0))] * n
        + [weight_spec, weight_spec],
        out_specs=pl.BlockSpec((rows, chunk), lambda i: (0, i)),
        scratch_shapes=[pltpu.VMEM((rows, width), BF16)] * 2,
        compiler_params=params(),
        cost_estimate=cost(4 * rows * depth * width, 4 * depth * width + 2 * rows * depth),
        name="prompt_gradient",
    )(place, *shares, key_weight, value_weight)


def spread(number, bits):
    return sum(((number >> i) & 1) << bit for i, bit in enumerate(bits))


def per_device(
    n_prompt,
    n_resp,
    prompt_rows,
    key_weight,
    value_weight,
    queries,
    own_keys,
    own_values,
    out_grad,
    first_length,
    resp_prompt,
):
    devices = n_prompt * n_resp
    heads = own_keys.shape[1] // E
    every_bit = range(devices.bit_length() - 1)
    rest_bits = [bit for bit in GATHER_BITS if bit in every_bit]
    rest_bits += [bit for bit in every_bit if bit not in rest_bits and bit not in HEAD_BITS]
    member = [spread(j, HEAD_BITS) for j in range(heads)]

    def swap(x, offset):
        return lax.ppermute(x, ("prompt", "resp"), [(i, i ^ offset) for i in range(devices)])

    def swap_group(items):
        return [items[0]] + [swap(items[j], member[j]) for j in range(1, heads)]

    prompt = lax.axis_index("prompt").astype(jnp.int32)
    device = prompt * n_resp + lax.axis_index("resp").astype(jnp.int32)
    head = sum(((device >> bit) & 1) << i for i, bit in enumerate(HEAD_BITS))
    place = jnp.stack([head, prompt])

    packed = pack(
        place, first_length, resp_prompt, queries, out_grad, own_keys, own_values, heads
    )
    packed, prompt_rows = lax.optimization_barrier((packed, prompt_rows))
    packets = swap_group(packed)

    projected = project(place, prompt_rows, key_weight, value_weight, heads)
    pieces = {0: jnp.stack(swap_group(projected))}
    for bit in rest_bits:
        for offset in list(pieces):
            pieces[offset | 1 << bit] = swap(pieces[offset], 1 << bit)
    offsets = list(pieces)

    filled = [0] * n_prompt
    slots = []
    for offset in offsets:
        places = []
        for j in range(heads):
            at = (offset ^ member[j]) // n_resp
            places.append((at, filled[at]))
            filled[at] += 1
        slots.append(tuple(places))

    first_out = 1 << rest_bits[-1]
    out_types = [BF16 if offset & first_out else F32 for offset in offsets]
    outs = attend(place, packets, [pieces[o] for o in offsets], tuple(slots), out_types, n_prompt)
    grads = outs[:heads]
    sums = dict(zip(offsets, outs[heads:]))
    arrived = {offset: [] for offset in offsets}
    for bit in reversed(rest_bits):
        for offset in reversed(offsets):
            if offset & 1 << bit:
                piece = sums.pop(offset)
                for part in arrived.pop(offset):
                    piece = piece + part.astype(F32)
                arrived[offset ^ 1 << bit].append(swap(piece.astype(BF16), 1 << bit))
        offsets = list(sums)
    shares = swap_group(total(sums[0], arrived[0]))

    query_grad, key_grad, value_grad = unpack(
        place, swap_group(grads), queries.shape[1], own_keys.shape[1]
    )
    prompt_grad = prompt_gradient(place, shares, key_weight, value_weight)
    return (query_grad, key_grad, value_grad, prompt_grad)


def solution(mesh):
    both = P(("prompt", "resp"), None)
    return jax.shard_map(
        functools.partial(per_device, mesh.shape["prompt"], mesh.shape["resp"]),
        mesh=mesh,
        in_specs=(both, P(), P(), both, both, both, both, P(("prompt", "resp")), both),
        out_specs=(both, both, both, both),
        check_vma=False,
    )
```

time: 86.4 us -> 139 us (1.61)
  Pallas kernels: 20.5 us -> 71.2 us
  waiting for transfers between devices: 26.1 us -> 36.7 us
  local copies, waits for them, and re-layouts: 6.09 us -> 0.05 us
  starting transfers between devices: 31.9 us -> 28.1 us
  other arithmetic: 0.18 us -> 1.64 us
    pallas_call x1, Pallas kernels: 0.38 us -> 49.6 us  [pack(): pl.pallas_call(functools.partial(pack_kernel, n), out_shape=[jax.ShapeDty...]
    ppermute x29 -> x26, waiting for transfers between devices: 26.1 us -> 36.7 us  [swap(): lax.ppermute(x, ('prompt', 'resp'), [(i, i ^ offset) for i in range(devic...]
    unnamed x24 -> x18, local copies, waits for them, and re-layouts: 6.09 us -> 0.05 us
    ppermute x29 -> x26, starting transfers between devices: 31.9 us -> 28.1 us  [swap(): lax.ppermute(x, ('prompt', 'resp'), [(i, i ^ offset) for i in range(devic...]
    another operation x1 -> x2, other arithmetic: 0.02 us -> 1.53 us  [the longest x1 0.93 us: per_device(): pieces = {0: jnp.stack(swap_group(projected))}]
  transfers between devices with their start and end apart: 29 -> 26, of which waited for: 16 -> 11; matrix products, arithmetic and copies ran while one was open for 0% -> 0% of each run, Pallas kernels for 2% -> 1%
where the time goes in v2:
time: 139 us
  Pallas kernels  71.2 us (51%)
  waiting for transfers between devices  36.7 us (26%)
  starting transfers between devices  28.1 us (20%)
  other arithmetic  1.64 us (1%)
  between operations  1.52 us (1%)
    pallas_call x1, Pallas kernels, pack(): pl.pallas_call(functools.partial(pack_kernel, n), out_shape=[jax.ShapeDty...  49.6 us
    ppermute x26, waiting for transfers between devices, swap(): lax.ppermute(x, ('prompt', 'resp'), [(i, i ^ offset) for i in range(devic...  36.7 us
    ppermute x26, starting transfers between devices, swap(): lax.ppermute(x, ('prompt', 'resp'), [(i, i ^ offset) for i in range(devic...  28.1 us
    pallas_call x1, Pallas kernels, attend(): pl.pallas_call(functools.partial(attend_kernel, slots, n, group, rows), o...  8.64 us
    pallas_call x1, Pallas kernels, project(): pl.pallas_call(functools.partial(project_kernel, n, steps), out_shape=[ja...  6.25 us
    pallas_call x1, Pallas kernels, prompt_gradient(): pl.pallas_call(functools.partial(prompt_kernel, n), grid=(depth // chunk,...  5.1 us
  transfers between devices with their start and end apart: 26, of which 11 were waited for; matrix products, arithmetic and copies ran while one was open for 0% of the time, Pallas kernels for 1%

profile of v2, /device:TPU:0, one launch (start us, length us, event | category | flops | bytes accessed | tf_op | source)
XLA Modules:
  0.0 139.3 jit_solution(17295409960248980314)
XLA Ops:
  1.9 49.6 %pack_rows.1 = (bf16[144,1536]{1,0:T(8,128)(2,1)}, bf16[144,1536]{1,0:T(8,128)(2,1)}, bf16[144,1536]{1,0:T(8,128)(2,1)}, bf16[144,1536]{1,0:T(8,128)(2,1)}) custom-call(s32[2]{0:T(128)} %pad_add_fusion.place_ref, s32[1]{0:T(128)S(6)} %copy.13.length_ref, s32[1,2]{1,0:T(1,128)} %prompts_ref.1, bf16[128,2560]{1,0:T(8,128)(2,1)} %q_ref.1, ...), custom_call_target="tpu_custom_call" | custom-call | bytes 1024 | tf_op jit(solution)/shard_map/pack_rows/pallas_call | solution.py:81
  51.6 6.2 %project_prefix.1 = (bf16[64,256]{1,0:T(8,128)(2,1)}, bf16[64,256]{1,0:T(8,128)(2,1)}, bf16[64,256]{1,0:T(8,128)(2,1)}, bf16[64,256]{1,0:T(8,128)(2,1)}) custom-call(s32[2]{0:T(128)} %pad_add_fusion.place_ref, bf16[64,5120]{1,0:T(8,128)(2,1)} %x_ref, bf16[5120,512]{1,0:T(8,128)(2,1)} %rest_4_.1, bf16[5120,512]{1,0:T(8,128)(2,1)} %rest_5_.1), custom_call_target="tpu_custom_call" | custom-call | bytes 1024 | tf_op jit(solution)/shard_map/project_prefix/pallas_call | solution.py:169
  57.8 3.0 %collective-permute-start.3 = (bf16[64,256]{1,0:T(8,128)(2,1)}, bf16[64,256]{1,0:T(8,128)(2,1)S(1)}, u32[]{:S(2)}, u32[]{:S(2)}) collective-permute-start(bf16[64,256]{1,0:T(8,128)(2,1)} %get-tuple-element.46), channel_id=1, source_target_pairs={{0,8},{1,9},{2,10},{3,11},{4,12},{5,13},{6,14},{7,15},{8,0},{9,1},... | collective-permute-start | bytes 98312 | tf_op jit(solution)/shard_map/ppermute | solution.py:394
  60.8 1.6 %collective-permute-start.4 = (bf16[64,256]{1,0:T(8,128)(2,1)}, bf16[64,256]{1,0:T(8,128)(2,1)S(1)}, u32[]{:S(2)}, u32[]{:S(2)}) collective-permute-start(bf16[64,256]{1,0:T(8,128)(2,1)} %get-tuple-element.47), channel_id=1, source_target_pairs={{0,2},{1,3},{2,0},{3,1},{4,6},{5,7},{6,4},{7,5},{8,10},{9,11},{10,... | collective-permute-start | bytes 98312 | tf_op jit(solution)/shard_map/ppermute | solution.py:394
  62.9 2.2 %collective-permute-done.4 = bf16[64,256]{1,0:T(8,128)(2,1)S(1)} collective-permute-done((bf16[64,256]{1,0:T(8,128)(2,1)}, bf16[64,256]{1,0:T(8,128)(2,1)S(1)}, u32[]{:S(2)}, u32[]{:S(2)}) %collective-permute-start.4) | collective-permute-done | bytes 32800 | tf_op jit(solution)/shard_map/ppermute | solution.py:394
  65.1 2.3 %collective-permute-done.5 = bf16[64,256]{1,0:T(8,128)(2,1)S(1)} collective-permute-done((bf16[64,256]{1,0:T(8,128)(2,1)}, bf16[64,256]{1,0:T(8,128)(2,1)S(1)}, u32[]{:S(2)}, u32[]{:S(2)}) %collective-permute-start.5) | collective-permute-done | bytes 32800 | tf_op jit(solution)/shard_map/ppermute | solution.py:394
  69.5 2.6 %collective-permute-start.2 = (bf16[144,1536]{1,0:T(8,128)(2,1)S(1)}, bf16[144,1536]{1,0:T(8,128)(2,1)S(1)}, u32[]{:S(2)}, u32[]{:S(2)}) collective-permute-start(bf16[144,1536]{1,0:T(8,128)(2,1)S(1)} %copy-done.2), channel_id=1, source_target_pairs={{0,10},{1,11},{2,8},{3,9},{4,14},{5,15},{6,12},{7,13},{8,2},{9,3},... | collective-permute-start | bytes 1327112 | tf_op jit(solution)/shard_map/ppermute | solution.py:394
  72.0 1.5 %collective-permute-start.7 = (bf16[4,64,256]{2,1,0:T(8,128)(2,1)S(1)}, bf16[4,64,256]{2,1,0:T(8,128)(2,1)S(1)}, u32[]{:S(2)}, u32[]{:S(2)}) collective-permute-start(bf16[4,64,256]{2,1,0:T(8,128)(2,1)S(1)} %pad_maximum_fusion.rest_4_), channel_id=1, source_target_pairs={{0,16},{1,17},{2,18},{3,19},{4,20},{5,21},{6,22},{7,23},{8,24},{9,... | collective-permute-start | bytes 393224 | tf_op jit(solution)/shard_map/ppermute | solution.py:394
  73.5 2.6 %collective-permute-start.6 = (bf16[4,64,256]{2,1,0:T(8,128)(2,1)S(1)}, bf16[4,64,256]{2,1,0:T(8,128)(2,1)S(1)}, u32[]{:S(2)}, u32[]{:S(2)}) collective-permute-start(bf16[4,64,256]{2,1,0:T(8,128)(2,1)S(1)} %pad_maximum_fusion.rest_4_), channel_id=1, source_target_pairs={{0,4},{1,5},{2,6},{3,7},{4,0},{5,1},{6,2},{7,3},{8,12},{9,13},{10,... | collective-permute-start | bytes 393224 | tf_op jit(solution)/shard_map/ppermute | solution.py:394
  77.0 14.5 %collective-permute-done.6.rest_5_ = bf16[4,64,256]{2,1,0:T(8,128)(2,1)S(1)} collective-permute-done((bf16[4,64,256]{2,1,0:T(8,128)(2,1)S(1)}, bf16[4,64,256]{2,1,0:T(8,128)(2,1)S(1)}, u32[]{:S(2)}, u32[]{:S(2)}) %collective-permute-start.6) | collective-permute-done | bytes 131104 | tf_op jit(solution)/shard_map/ppermute | solution.py:394
  91.5 1.6 %collective-permute-start.8 = (bf16[4,64,256]{2,1,0:T(8,128)(2,1)S(1)}, bf16[4,64,256]{2,1,0:T(8,128)(2,1)S(1)}, u32[]{:S(2)}, u32[]{:S(2)}) collective-permute-start(bf16[4,64,256]{2,1,0:T(8,128)(2,1)S(1)} %collective-permute-done.6.rest_5_), channel_id=1, source_target_pairs={{0,16},{1,17},{2,18},{3,19},{4,20},{5,21},{6,22},{7,23},{8,24},{9,... | collective-permute-start | bytes 393224 | tf_op jit(solution)/shard_map/ppermute | solution.py:394
  93.1 3.4 %collective-permute-done.8.rest_7_ = bf16[4,64,256]{2,1,0:T(8,128)(2,1)S(1)} collective-permute-done((bf16[4,64,256]{2,1,0:T(8,128)(2,1)S(1)}, bf16[4,64,256]{2,1,0:T(8,128)(2,1)S(1)}, u32[]{:S(2)}, u32[]{:S(2)}) %collective-permute-start.8) | collective-permute-done | bytes 131104 | tf_op jit(solution)/shard_map/ppermute | solution.py:394
  96.5 1.3 collective-permute-done.12.rest_11_
  97.8 8.6 %attend_head.1 = (bf16[128,896]{1,0:T(8,128)(2,1)S(1)}, bf16[128,896]{1,0:T(8,128)(2,1)S(1)}, bf16[128,896]{1,0:T(8,128)(2,1)S(1)}, bf16[128,896]{1,0:T(8,128)(2...) custom-call(s32[2]{0:T(128)S(1)} %copy-done, ...), custom_call_target="tpu_custom_call" | custom-call | flops 4194304000 | bytes 8388608 | tf_op jit(solution)/shard_map/attend_head/pallas_call | solution.py:291
  107.6 1.6 %collective-permute-start.13 = (bf16[128,896]{1,0:T(8,128)(2,1)S(1)}, bf16[128,896]{1,0:T(8,128)(2,1)S(1)}, u32[]{:S(2)}, u32[]{:S(2)}) collective-permute-start(bf16[128,896]{1,0:T(8,128)(2,1)S(1)} %get-tuple-element.50), channel_id=1, source_target_pairs={{0,8},{1,9},{2,10},{3,11},{4,12},{5,13},{6,14},{7,15},{8,0},{9,1},... | collective-permute-start | bytes 688136 | tf_op jit(solution)/shard_map/ppermute | solution.py:394
  109.1 4.6 %collective-permute-start.14 = (bf16[128,896]{1,0:T(8,128)(2,1)S(1)}, bf16[128,896]{1,0:T(8,128)(2,1)S(1)}, u32[]{:S(2)}, u32[]{:S(2)}) collective-permute-start(bf16[128,896]{1,0:T(8,128)(2,1)S(1)} %get-tuple-element.51), channel_id=1, source_target_pairs={{0,2},{1,3},{2,0},{3,1},{4,6},{5,7},{6,4},{7,5},{8,10},{9,11},{10,... | collective-permute-start | bytes 688136 | tf_op jit(solution)/shard_map/ppermute | solution.py:394
  113.8 1.6 %collective-permute-start.21 = (bf16[4,64,256]{2,1,0:T(8,128)(2,1)S(1)}, bf16[4,64,256]{2,1,0:T(8,128)(2,1)S(1)}, u32[]{:S(2)}, u32[]{:S(2)}) collective-permute-start(bf16[4,64,256]{2,1,0:T(8,128)(2,1)S(1)} %add_convert_fusion.1), channel_id=1, source_target_pairs={{0,16},{1,17},{2,18},{3,19},{4,20},{5,21},{6,22},{7,23},{8,24},{9,... | collective-permute-start | bytes 393224 | tf_op jit(solution)/shard_map/ppermute | solution.py:394
  115.7 3.2 %collective-permute-done.21 = bf16[4,64,256]{2,1,0:T(8,128)(2,1)S(1)} collective-permute-done((bf16[4,64,256]{2,1,0:T(8,128)(2,1)S(1)}, bf16[4,64,256]{2,1,0:T(8,128)(2,1)S(1)}, u32[]{:S(2)}, u32[]{:S(2)}) %collective-permute-start.21) | collective-permute-done | bytes 131104 | tf_op jit(solution)/shard_map/ppermute | solution.py:394
  118.9 1.5 %collective-permute-start.18 = (bf16[4,64,256]{2,1,0:T(8,128)(2,1)S(1)}, bf16[4,64,256]{2,1,0:T(8,128)(2,1)S(1)}, u32[]{:S(2)}, u32[]{:S(2)}) collective-permute-start(bf16[4,64,256]{2,1,0:T(8,128)(2,1)S(1)} %add_convert_fusion.2), channel_id=1, source_target_pairs={{0,16},{1,17},{2,18},{3,19},{4,20},{5,21},{6,22},{7,23},{8,24},{9,... | collective-permute-start | bytes 393224 | tf_op jit(solution)/shard_map/ppermute | solution.py:394
  120.5 3.3 %collective-permute-done.18.rest_1_ = bf16[4,64,256]{2,1,0:T(8,128)(2,1)S(1)} collective-permute-done((bf16[4,64,256]{2,1,0:T(8,128)(2,1)S(1)}, bf16[4,64,256]{2,1,0:T(8,128)(2,1)S(1)}, u32[]{:S(2)}, u32[]{:S(2)}) %collective-permute-start.18) | collective-permute-done | bytes 131104 | tf_op jit(solution)/shard_map/ppermute | solution.py:394
  123.8 4.4 %collective-permute-done.22.rest_2_ = bf16[4,64,256]{2,1,0:T(8,128)(2,1)S(1)} collective-permute-done((bf16[4,64,256]{2,1,0:T(8,128)(2,1)S(1)}, bf16[4,64,256]{2,1,0:T(8,128)(2,1)S(1)}, u32[]{:S(2)}, u32[]{:S(2)}) %collective-permute-start.22) | collective-permute-done | bytes 131104 | tf_op jit(solution)/shard_map/ppermute | solution.py:394
  129.1 2.8 %collective-permute-start.25 = (bf16[64,256]{1,0:T(8,128)(2,1)S(1)}, bf16[64,256]{1,0:T(8,128)(2,1)S(1)}, u32[]{:S(2)}, u32[]{:S(2)}) collective-permute-start(bf16[64,256]{1,0:T(8,128)(2,1)S(1)} %get-tuple-element.67), channel_id=1, source_target_pairs={{0,10},{1,11},{2,8},{3,9},{4,14},{5,15},{6,12},{7,13},{8,2},{9,3},... | collective-permute-start | bytes 98312 | tf_op jit(solution)/shard_map/ppermute | solution.py:394
  131.9 1.6 %unpack_rows.1 = (bf16[128,2560]{1,0:T(8,128)(2,1)}, bf16[128,512]{1,0:T(8,128)(2,1)}, bf16[128,512]{1,0:T(8,128)(2,1)}) custom-call(s32[2]{0:T(128)S(1)} %copy-done, bf16[128,896]{1,0:T(8,128)(2,1)S(1)} %get-tuple-element.49.rest_0_, bf16[128,896]{1,0:T(8,128)(2,1)S(1)} %collective-permute-done.13.rest_1_, ...), custom_call_target="tpu_custom_call" | custom-call | bytes 1835008 | tf_op jit(solution)/shard_map/unpack_rows/pallas_call | solution.py:120
  134.2 5.1 %prompt_gradient.1 = bf16[64,5120]{1,0:T(8,128)(2,1)} custom-call(s32[2]{0:T(128)S(1)} %copy-done, bf16[64,256]{1,0:T(8,128)(2,1)S(1)} %get-tuple-element.64.rest_0_, bf16[64,256]{1,0:T(8,128)(2,1)S(1)} %collective-permute-done.23.rest_1_, bf16[64,256]{1,0:T(8,128)(2,1)S(1)} %collective-permute-done.24.rest_2_, ...), custom_call_target="tpu_custom_call" | custom-call | flops 671088640 | bytes 11141120 | tf_op jit(solution)/shard_map/prompt_gradient/pallas_call | solution.py:354
  (59 shorter events, 7.0 us)
Async XLA Ops:
  57.8 5.1 %collective-permute-start.3 = (bf16[64,256]{1,0:T(8,128)(2,1)}, bf16[64,256]{1,0:T(8,128)(2,1)S(1)}, u32[]{:S(2)}, u32[]{:S(2)}) collective-permute-start(bf16[64,256]{1,0:T(8,128)(2,1)} %get-tuple-element.46), channel_id=1, source_target_pairs={{0,8},{1,9},{2,10},{3,11},{4,12},{5,13},{6,14},{7,15},{8,0},{9,1},... | collective-permute-start | bytes 98312 | tf_op jit(solution)/shard_map/ppermute | solution.py:394
  60.8 4.3 %collective-permute-start.4 = (bf16[64,256]{1,0:T(8,128)(2,1)}, bf16[64,256]{1,0:T(8,128)(2,1)S(1)}, u32[]{:S(2)}, u32[]{:S(2)}) collective-permute-start(bf16[64,256]{1,0:T(8,128)(2,1)} %get-tuple-element.47), channel_id=1, source_target_pairs={{0,2},{1,3},{2,0},{3,1},{4,6},{5,7},{6,4},{7,5},{8,10},{9,11},{10,... | collective-permute-start | bytes 98312 | tf_op jit(solution)/shard_map/ppermute | solution.py:394
  62.4 5.0 %collective-permute-start.5 = (bf16[64,256]{1,0:T(8,128)(2,1)}, bf16[64,256]{1,0:T(8,128)(2,1)S(1)}, u32[]{:S(2)}, u32[]{:S(2)}) collective-permute-start(bf16[64,256]{1,0:T(8,128)(2,1)} %get-tuple-element.48), channel_id=1, source_target_pairs={{0,10},{1,11},{2,8},{3,9},{4,14},{5,15},{6,12},{7,13},{8,2},{9,3},... | collective-permute-start | bytes 98312 | tf_op jit(solution)/shard_map/ppermute | solution.py:394
  68.4 5.2 %collective-permute-start.9 = (bf16[4,64,256]{2,1,0:T(8,128)(2,1)S(1)}, bf16[4,64,256]{2,1,0:T(8,128)(2,1)S(1)}, u32[]{:S(2)}, u32[]{:S(2)}) collective-permute-start(bf16[4,64,256]{2,1,0:T(8,128)(2,1)S(1)} %pad_maximum_fusion.rest_4_), channel_id=1, source_target_pairs={{0,1},{1,0},{2,3},{3,2},{4,5},{5,4},{6,7},{7,6},{8,9},{9,8},{10,11... | collective-permute-start | bytes 393224 | tf_op jit(solution)/shard_map/ppermute | solution.py:394
  68.5 29.3 %collective-permute-start = (bf16[144,1536]{1,0:T(8,128)(2,1)S(1)}, bf16[144,1536]{1,0:T(8,128)(2,1)S(1)}, u32[]{:S(2)}, u32[]{:S(2)}) collective-permute-start(bf16[144,1536]{1,0:T(8,128)(2,1)S(1)} %copy-done.4), channel_id=1, source_target_pairs={{0,8},{1,9},{2,10},{3,11},{4,12},{5,13},{6,14},{7,15},{8,0},{9,1},... | collective-permute-start | bytes 1327112 | tf_op jit(solution)/shard_map/ppermute | solution.py:394
  69.1 28.7 %collective-permute-start.1 = (bf16[144,1536]{1,0:T(8,128)(2,1)S(1)}, bf16[144,1536]{1,0:T(8,128)(2,1)S(1)}, u32[]{:S(2)}, u32[]{:S(2)}) collective-permute-start(bf16[144,1536]{1,0:T(8,128)(2,1)S(1)} %copy-done.3), channel_id=1, source_target_pairs={{0,2},{1,3},{2,0},{3,1},{4,6},{5,7},{6,4},{7,5},{8,10},{9,11},{10,... | collective-permute-start | bytes 1327112 | tf_op jit(solution)/shard_map/ppermute | solution.py:394
  69.5 28.4 %collective-permute-start.2 = (bf16[144,1536]{1,0:T(8,128)(2,1)S(1)}, bf16[144,1536]{1,0:T(8,128)(2,1)S(1)}, u32[]{:S(2)}, u32[]{:S(2)}) collective-permute-start(bf16[144,1536]{1,0:T(8,128)(2,1)S(1)} %copy-done.2), channel_id=1, source_target_pairs={{0,10},{1,11},{2,8},{3,9},{4,14},{5,15},{6,12},{7,13},{8,2},{9,3},... | collective-permute-start | bytes 1327112 | tf_op jit(solution)/shard_map/ppermute | solution.py:394
  72.0 5.0 %collective-permute-start.7 = (bf16[4,64,256]{2,1,0:T(8,128)(2,1)S(1)}, bf16[4,64,256]{2,1,0:T(8,128)(2,1)S(1)}, u32[]{:S(2)}, u32[]{:S(2)}) collective-permute-start(bf16[4,64,256]{2,1,0:T(8,128)(2,1)S(1)} %pad_maximum_fusion.rest_4_), channel_id=1, source_target_pairs={{0,16},{1,17},{2,18},{3,19},{4,20},{5,21},{6,22},{7,23},{8,24},{9,... | collective-permute-start | bytes 393224 | tf_op jit(solution)/shard_map/ppermute | solution.py:394
  73.5 17.9 %collective-permute-start.6 = (bf16[4,64,256]{2,1,0:T(8,128)(2,1)S(1)}, bf16[4,64,256]{2,1,0:T(8,128)(2,1)S(1)}, u32[]{:S(2)}, u32[]{:S(2)}) collective-permute-start(bf16[4,64,256]{2,1,0:T(8,128)(2,1)S(1)} %pad_maximum_fusion.rest_4_), channel_id=1, source_target_pairs={{0,4},{1,5},{2,6},{3,7},{4,0},{5,1},{6,2},{7,3},{8,12},{9,13},{10,... | collective-permute-start | bytes 393224 | tf_op jit(solution)/shard_map/ppermute | solution.py:394
  77.0 16.1 %collective-permute-start.11 = (bf16[4,64,256]{2,1,0:T(8,128)(2,1)S(1)}, bf16[4,64,256]{2,1,0:T(8,128)(2,1)S(1)}, u32[]{:S(2)}, u32[]{:S(2)}) collective-permute-start(bf16[4,64,256]{2,1,0:T(8,128)(2,1)S(1)} %collective-permute-done.7.rest_6_), channel_id=1, source_target_pairs={{0,1},{1,0},{2,3},{3,2},{4,5},{5,4},{6,7},{7,6},{8,9},{9,8},{10,11... | collective-permute-start | bytes 393224 | tf_op jit(solution)/shard_map/ppermute | solution.py:394
  91.5 5.0 %collective-permute-start.8 = (bf16[4,64,256]{2,1,0:T(8,128)(2,1)S(1)}, bf16[4,64,256]{2,1,0:T(8,128)(2,1)S(1)}, u32[]{:S(2)}, u32[]{:S(2)}) collective-permute-start(bf16[4,64,256]{2,1,0:T(8,128)(2,1)S(1)} %collective-permute-done.6.rest_5_), channel_id=1, source_target_pairs={{0,16},{1,17},{2,18},{3,19},{4,20},{5,21},{6,22},{7,23},{8,24},{9,... | collective-permute-start | bytes 393224 | tf_op jit(solution)/shard_map/ppermute | solution.py:394
  93.1 3.4 %collective-permute-start.10 = (bf16[4,64,256]{2,1,0:T(8,128)(2,1)S(1)}, bf16[4,64,256]{2,1,0:T(8,128)(2,1)S(1)}, u32[]{:S(2)}, u32[]{:S(2)}) collective-permute-start(bf16[4,64,256]{2,1,0:T(8,128)(2,1)S(1)} %collective-permute-done.6.rest_5_), channel_id=1, source_target_pairs={{0,1},{1,0},{2,3},{3,2},{4,5},{5,4},{6,7},{7,6},{8,9},{9,8},{10,11... | collective-permute-start | bytes 393224 | tf_op jit(solution)/shard_map/ppermute | solution.py:394
  106.7 13.7 %collective-permute-start.16 = (bf16[4,64,256]{2,1,0:T(8,128)(2,1)S(1)}, bf16[4,64,256]{2,1,0:T(8,128)(2,1)S(1)}, u32[]{:S(2)}, u32[]{:S(2)}) collective-permute-start(bf16[4,64,256]{2,1,0:T(8,128)(2,1)S(1)} %get-tuple-element.57), channel_id=1, source_target_pairs={{0,1},{1,0},{2,3},{3,2},{4,5},{5,4},{6,7},{7,6},{8,9},{9,8},{10,11... | collective-permute-start | bytes 393224 | tf_op jit(solution)/shard_map/ppermute | solution.py:394
  107.1 6.7 %collective-permute-start.17 = (bf16[4,64,256]{2,1,0:T(8,128)(2,1)S(1)}, bf16[4,64,256]{2,1,0:T(8,128)(2,1)S(1)}, u32[]{:S(2)}, u32[]{:S(2)}) collective-permute-start(bf16[4,64,256]{2,1,0:T(8,128)(2,1)S(1)} %get-tuple-element.59), channel_id=1, source_target_pairs={{0,1},{1,0},{2,3},{3,2},{4,5},{5,4},{6,7},{7,6},{8,9},{9,8},{10,11... | collective-permute-start | bytes 393224 | tf_op jit(solution)/shard_map/ppermute | solution.py:394
  107.2 8.2 %collective-permute-start.19 = (bf16[4,64,256]{2,1,0:T(8,128)(2,1)S(1)}, bf16[4,64,256]{2,1,0:T(8,128)(2,1)S(1)}, u32[]{:S(2)}, u32[]{:S(2)}) collective-permute-start(bf16[4,64,256]{2,1,0:T(8,128)(2,1)S(1)} %get-tuple-element.61), channel_id=1, source_target_pairs={{0,1},{1,0},{2,3},{3,2},{4,5},{5,4},{6,7},{7,6},{8,9},{9,8},{10,11... | collective-permute-start | bytes 393224 | tf_op jit(solution)/shard_map/ppermute | solution.py:394
  107.6 21.5 %collective-permute-start.13 = (bf16[128,896]{1,0:T(8,128)(2,1)S(1)}, bf16[128,896]{1,0:T(8,128)(2,1)S(1)}, u32[]{:S(2)}, u32[]{:S(2)}) collective-permute-start(bf16[128,896]{1,0:T(8,128)(2,1)S(1)} %get-tuple-element.50), channel_id=1, source_target_pairs={{0,8},{1,9},{2,10},{3,11},{4,12},{5,13},{6,14},{7,15},{8,0},{9,1},... | collective-permute-start | bytes 688136 | tf_op jit(solution)/shard_map/ppermute | solution.py:394
  109.1 22.8 %collective-permute-start.14 = (bf16[128,896]{1,0:T(8,128)(2,1)S(1)}, bf16[128,896]{1,0:T(8,128)(2,1)S(1)}, u32[]{:S(2)}, u32[]{:S(2)}) collective-permute-start(bf16[128,896]{1,0:T(8,128)(2,1)S(1)} %get-tuple-element.51), channel_id=1, source_target_pairs={{0,2},{1,3},{2,0},{3,1},{4,6},{5,7},{6,4},{7,5},{8,10},{9,11},{10,... | collective-permute-start | bytes 688136 | tf_op jit(solution)/shard_map/ppermute | solution.py:394
  113.8 5.1 %collective-permute-start.21 = (bf16[4,64,256]{2,1,0:T(8,128)(2,1)S(1)}, bf16[4,64,256]{2,1,0:T(8,128)(2,1)S(1)}, u32[]{:S(2)}, u32[]{:S(2)}) collective-permute-start(bf16[4,64,256]{2,1,0:T(8,128)(2,1)S(1)} %add_convert_fusion.1), channel_id=1, source_target_pairs={{0,16},{1,17},{2,18},{3,19},{4,20},{5,21},{6,22},{7,23},{8,24},{9,... | collective-permute-start | bytes 393224 | tf_op jit(solution)/shard_map/ppermute | solution.py:394
  115.4 16.5 %collective-permute-start.15 = (bf16[128,896]{1,0:T(8,128)(2,1)S(1)}, bf16[128,896]{1,0:T(8,128)(2,1)S(1)}, u32[]{:S(2)}, u32[]{:S(2)}) collective-permute-start(bf16[128,896]{1,0:T(8,128)(2,1)S(1)} %get-tuple-element.52), channel_id=1, source_target_pairs={{0,10},{1,11},{2,8},{3,9},{4,14},{5,15},{6,12},{7,13},{8,2},{9,3},... | collective-permute-start | bytes 688136 | tf_op jit(solution)/shard_map/ppermute | solution.py:394
  118.9 5.0 %collective-permute-start.18 = (bf16[4,64,256]{2,1,0:T(8,128)(2,1)S(1)}, bf16[4,64,256]{2,1,0:T(8,128)(2,1)S(1)}, u32[]{:S(2)}, u32[]{:S(2)}) collective-permute-start(bf16[4,64,256]{2,1,0:T(8,128)(2,1)S(1)} %add_convert_fusion.2), channel_id=1, source_target_pairs={{0,16},{1,17},{2,18},{3,19},{4,20},{5,21},{6,22},{7,23},{8,24},{9,... | collective-permute-start | bytes 393224 | tf_op jit(solution)/shard_map/ppermute | solution.py:394
  120.4 7.8 %collective-permute-start.22 = (bf16[4,64,256]{2,1,0:T(8,128)(2,1)S(1)}, bf16[4,64,256]{2,1,0:T(8,128)(2,1)S(1)}, u32[]{:S(2)}, u32[]{:S(2)}) collective-permute-start(bf16[4,64,256]{2,1,0:T(8,128)(2,1)S(1)} %add_convert_fusion), channel_id=1, source_target_pairs={{0,4},{1,5},{2,6},{3,7},{4,0},{5,1},{6,2},{7,3},{8,12},{9,13},{10,... | collective-permute-start | bytes 393224 | tf_op jit(solution)/shard_map/ppermute | solution.py:394
  128.3 5.1 %collective-permute-start.23 = (bf16[64,256]{1,0:T(8,128)(2,1)S(1)}, bf16[64,256]{1,0:T(8,128)(2,1)S(1)}, u32[]{:S(2)}, u32[]{:S(2)}) collective-permute-start(bf16[64,256]{1,0:T(8,128)(2,1)S(1)} %get-tuple-element.65), channel_id=1, source_target_pairs={{0,8},{1,9},{2,10},{3,11},{4,12},{5,13},{6,14},{7,15},{8,0},{9,1},... | collective-permute-start | bytes 98312 | tf_op jit(solution)/shard_map/ppermute | solution.py:394
  129.1 4.4 %collective-permute-start.24 = (bf16[64,256]{1,0:T(8,128)(2,1)S(1)}, bf16[64,256]{1,0:T(8,128)(2,1)S(1)}, u32[]{:S(2)}, u32[]{:S(2)}) collective-permute-start(bf16[64,256]{1,0:T(8,128)(2,1)S(1)} %get-tuple-element.66), channel_id=1, source_target_pairs={{0,2},{1,3},{2,0},{3,1},{4,6},{5,7},{6,4},{7,5},{8,10},{9,11},{10,... | collective-permute-start | bytes 98312 | tf_op jit(solution)/shard_map/ppermute | solution.py:394
  129.1 5.0 %collective-permute-start.25 = (bf16[64,256]{1,0:T(8,128)(2,1)S(1)}, bf16[64,256]{1,0:T(8,128)(2,1)S(1)}, u32[]{:S(2)}, u32[]{:S(2)}) collective-permute-start(bf16[64,256]{1,0:T(8,128)(2,1)S(1)} %get-tuple-element.67), channel_id=1, source_target_pairs={{0,10},{1,11},{2,8},{3,9},{4,14},{5,15},{6,12},{7,13},{8,2},{9,3},... | collective-permute-start | bytes 98312 | tf_op jit(solution)/shard_map/ppermute | solution.py:394
  (11 other events, 414.0 us)

commit v3 on v2

--- a/solution.py
+++ b/solution.py
@@ -16,8 +16,8 @@
 BF16 = jnp.bfloat16
 F32 = jnp.float32
 NOTE_ROWS = 16
-HEAD_BITS = (3, 1)
-GATHER_BITS = (2, 4, 0)
+HEAD_BITS = (3, 4)
+GATHER_BITS = (2, 1, 0)
 
 ANY = pl.BlockSpec(memory_space=pl.ANY)
 SMEM = pl.BlockSpec(memory_space=pltpu.SMEM)
@@ -42,97 +42,9 @@
     return lax.dot_general(a, b, (((a_dim,), (b_dim,)), ((), ())), preferred_element_type=F32)
 
 
-def pack_kernel(n, place_ref, length_ref, prompts_ref, q_ref, g_ref, k_ref, v_ref, *rest):
-    outs, notes, sems = rest[:n], rest[n], rest[n + 1]
-    rows = q_ref.shape[0]
-    copies = []
-    for j in reversed(range(n)):
-        start = 0
-        for source in (q_ref, g_ref, k_ref, v_ref):
-            width = source.shape[1] // n
-            copies.append(
-                pltpu.make_async_copy(
-                    source.at[:, lanes(place_ref[0] ^ j, width)],
-                    outs[j].at[0:rows, start : start + width],
-                    sems.at[len(copies)],
-                )
-            )
-            start += width
-    for copy in copies:
-        copy.start()
-    lane = lax.broadcasted_iota(jnp.int32, notes.shape, 1)
-    note = jnp.where(
-        lane < E, length_ref[0], jnp.where(lane < 2 * E, prompts_ref[0, 0], prompts_ref[0, 1])
-    )
-    notes[...] = note.astype(F32).astype(BF16)
-    for j in range(n):
-        copy = pltpu.make_async_copy(
-            notes, outs[j].at[rows : rows + NOTE_ROWS, :], sems.at[len(copies)]
-        )
-        copy.start()
-        copies.append(copy)
-    for copy in copies:
-        copy.wait()
-
-
-def pack(place, first_length, resp_prompt, queries, out_grad, own_keys, own_values, n):
-    rows = queries.shape[0]
-    width = (2 * queries.shape[1] + 2 * own_keys.shape[1]) // n
-    return pl.pallas_call(
-        functools.partial(pack_kernel, n),
-        out_shape=[jax.ShapeDtypeStruct((rows + NOTE_ROWS, width), BF16)] * n,
-        in_specs=[SMEM, SMEM, SMEM, ANY, ANY, ANY, ANY],
-        out_specs=[ANY] * n,
-        scratch_shapes=[
-            pltpu.VMEM((NOTE_ROWS, width), BF16),
-            pltpu.SemaphoreType.DMA((5 * n,)),
-        ],
-        compiler_params=params(60),
-        cost_estimate=cost(0, 1024),
-        name="pack_rows",
-    )(place, first_length, resp_prompt, queries, out_grad, own_keys, own_values)
-
-
-def unpack_kernel(n, place_ref, *rest):
-    packets, targets, sems = rest[:n], rest[n : n + 3], rest[n + 3]
-    copies = []
-    for j in range(n):
-        start = 0
-        for target in targets:
-            width = target.shape[1] // n
-            copies.append(
-                pltpu.make_async_copy(
-                    packets[j].at[:, start : start + width],
-                    target.at[:, lanes(place_ref[0] ^ j, width)],
-                    sems.at[len(copies)],
-                )
-            )
-            start += width
-    for copy in copies:
-        copy.start()
-    for copy in copies:
-        copy.wait()
-
-
-def unpack(place, packets, q_width, kv_width):
-    n = len(packets)
-    rows = packets[0].shape[0]
-    return pl.pallas_call(
-        functools.partial(unpack_kernel, n),
-        out_shape=[
-            jax.ShapeDtypeStruct((rows, width), BF16) for width in (q_width, kv_width, kv_width)
-        ],
-        in_specs=[SMEM] + [ANY] * n,
-        out_specs=[ANY] * 3,
-        scratch_shapes=[pltpu.SemaphoreType.DMA((3 * n,))],
-        compiler_params=params(),
-        cost_estimate=cost(0, 4 * rows * (q_width + 2 * kv_width)),
-        name="unpack_rows",
-    )(place, *packets)
-
-
-def project_kernel(n, steps, place_ref, x_ref, kw_ref, vw_ref, *rest):
-    outs, (kw, vw, key_sum, value_sum, sems) = rest[:n], rest[n:]
+def open_kernel(n, steps, place_ref, length_ref, prompts_ref, x_ref, *rest):
+    sources, (kw_ref, vw_ref), packets, heads = rest[:4], rest[4:6], rest[6 : 6 + n], rest[6 + n :]
+    heads, (kw, vw, key_sum, value_sum, sems, row_sems) = heads[:n], heads[n:]
     chunk = kw.shape[0] // steps
     copies = []
     for step in range(steps):
@@ -143,8 +55,29 @@
                     source.at[span, :], target.at[span, :], sems.at[len(copies)]
                 )
             )
-    for copy in copies:
+    rows = sources[0].shape[0]
+    row_copies = []
+    for j in range(n):
+        start = 0
+        for source in sources:
+            width = source.shape[1] // n
+            row_copies.append(
+                pltpu.make_async_copy(
+                    source.at[:, lanes(place_ref[0] ^ j, width)],
+                    packets[j].at[0:rows, start : start + width],
+                    row_sems.at[len(row_copies)],
+                )
+            )
+            start += width
+    for copy in copies[:4] + row_copies + copies[4:]:
         copy.start()
+    lane = lax.broadcasted_iota(jnp.int32, (NOTE_ROWS, packets[0].shape[1]), 1)
+    note = jnp.where(
+        lane < E, length_ref[0], jnp.where(lane < 2 * E, prompts_ref[0, 0], prompts_ref[0, 1])
+    )
+    note = note.astype(F32).astype(BF16)
+    for j in range(n):
+        packets[j][rows : rows + NOTE_ROWS, :] = note
     keys = values = None
     for step in range(steps):
         span = slice(step * chunk, (step + 1) * chunk)
@@ -159,25 +92,57 @@
     width = key_sum.shape[1] // n
     for j in range(n):
         head = lanes(place_ref[0] ^ j, width)
-        outs[j][:, :width] = key_sum[:, head]
-        outs[j][:, width:] = value_sum[:, head]
-
-
-def project(place, prompt_rows, key_weight, value_weight, n, steps=5):
-    rows = prompt_rows.shape[0]
-    width = key_weight.shape[1]
+        heads[j][:, :width] = key_sum[:, head]
+        heads[j][:, width:] = value_sum[:, head]
+    for copy in row_copies:
+        copy.wait()
+
+
+def opening(place, first_length, resp_prompt, prompt_rows, rows_in, weights, n, steps=10):
+    rows = rows_in[0].shape[0]
+    packet = (rows + NOTE_ROWS, sum(x.shape[1] for x in rows_in) // n)
+    prompt_count = prompt_rows.shape[0]
+    width = weights[0].shape[1]
+    outs = pl.pallas_call(
+        functools.partial(open_kernel, n, steps),
+        out_shape=[jax.ShapeDtypeStruct(packet, BF16)] * n
+        + [jax.ShapeDtypeStruct((prompt_count, 2 * width // n), BF16)] * n,
+        in_specs=[SMEM, SMEM, SMEM, VMEM] + [ANY] * 6,
+        out_specs=[VMEM] * (2 * n),
+        scratch_shapes=[pltpu.VMEM(weights[0].shape, BF16)] * 2
+        + [pltpu.VMEM((prompt_count, width), BF16)] * 2
+        + [pltpu.SemaphoreType.DMA((2 * steps,)), pltpu.SemaphoreType.DMA((4 * n,))],
+        compiler_params=params(62),
+        cost_estimate=cost(0, 1024),
+        name="open",
+    )(place, first_length, resp_prompt, prompt_rows, *rows_in, *weights)
+    return outs[:n], outs[n:]
+
+
+def unpack_kernel(n, place_ref, *rest):
+    packets, targets = rest[:n], rest[n:]
+    for j in range(n):
+        start = 0
+        for target in targets:
+            width = target.shape[1] // n
+            target[:, lanes(place_ref[0] ^ j, width)] = packets[j][:, start : start + width]
+            start += width
+
+
+def unpack(place, packets, q_width, kv_width):
+    n = len(packets)
+    rows = packets[0].shape[0]
     return pl.pallas_call(
-        functools.partial(project_kernel, n, steps),
-        out_shape=[jax.ShapeDtypeStruct((rows, 2 * width // n), BF16)] * n,
-        in_specs=[SMEM, VMEM, ANY, ANY],
-        out_specs=[VMEM] * n,
-        scratch_shapes=[pltpu.VMEM(key_weight.shape, BF16)] * 2
-        + [pltpu.VMEM((rows, width), BF16)] * 2
-        + [pltpu.SemaphoreType.DMA((2 * steps,))],
-        compiler_params=params(60),
-        cost_estimate=cost(0, 1024),
-        name="project_prefix",
-    )(place, prompt_rows, key_weight, value_weight)
+        functools.partial(unpack_kernel, n),
+        out_shape=[
+            jax.ShapeDtypeStruct((rows, width), BF16) for width in (q_width, kv_width, kv_width)
+        ],
+        in_specs=[SMEM] + [VMEM] * n,
+        out_specs=[VMEM] * 3,
+        compiler_params=params(16),
+        cost_estimate=cost(0, 4 * rows * (q_width + 2 * kv_width)),
+        name="unpack_rows",
+    )(place, *packets)
 
 
 def attend_kernel(slots, n, group, rows, place_ref, *rest):
@@ -211,8 +176,7 @@
     own_key = lax.broadcasted_iota(jnp.int32, (rows, total_rows), 0)
     lane_row = lax.broadcasted_iota(jnp.int32, (E, total_rows), 1) & (rows - 1)
 
-    for packet, grads in zip(packets, grads_out):
-
+    def products(packet):
         def note(index):
             block = packet[rows : rows + NOTE_ROWS, index * E : (index + 1) * E]
             return jnp.max(block.astype(F32)).astype(jnp.int32)
@@ -235,9 +199,24 @@
         key_pair = jnp.concatenate([keys[first_at], keys[second_at]], axis=1)
         value_pair = jnp.concatenate([values[first_at], values[second_at]], axis=1)
 
-        scores = dot(key_pair, query_pair, 1, 1)
         visible = (own_key <= row_in_lane) & ((own_key >= boundary) == (row_in_lane >= boundary))
-        own_scores = jnp.where(visible, dot(own_k, query, 1, 1), HIDDEN)
+        return dict(
+            boundary=boundary,
+            first_at=first_at,
+            second_at=second_at,
+            query=query,
+            grad=grad,
+            own_k=own_k,
+            query_pair=query_pair,
+            grad_pair=grad_pair,
+            key_pair=key_pair,
+            scores=dot(key_pair, query_pair, 1, 1),
+            own_scores=jnp.where(visible, dot(own_k, query, 1, 1), HIDDEN),
+            dprobs=dot(value_pair, grad_pair, 1, 1),
+            own_dprobs=dot(own_v, grad, 1, 1),
+        )
+
+    def soften(scores, own_scores, dprobs, own_dprobs, **_):
         top = jnp.maximum(
             jnp.max(scores, axis=0, keepdims=True), jnp.max(own_scores, axis=0, keepdims=True)
         )
@@ -250,14 +229,20 @@
         own_probs = own_weight * inverse
         probs_low = probs.astype(BF16)
         own_probs_low = own_probs.astype(BF16)
-        dprobs = dot(value_pair, grad_pair, 1, 1)
-        own_dprobs = dot(own_v, grad, 1, 1)
         delta = jnp.sum(probs_low.astype(F32) * dprobs, axis=0, keepdims=True) + jnp.sum(
             own_probs_low.astype(F32) * own_dprobs, axis=0, keepdims=True
         )
-        dscores = (probs * (dprobs - delta)).astype(BF16)
-        own_dscores = (own_probs * (own_dprobs - delta)).astype(BF16)
-
+        return dict(
+            probs_low=probs_low,
+            own_probs_low=own_probs_low,
+            dscores=(probs * (dprobs - delta)).astype(BF16),
+            own_dscores=(own_probs * (own_dprobs - delta)).astype(BF16),
+        )
+
+    def gradients(
+        grads, boundary, first_at, second_at, query, grad, own_k, query_pair, grad_pair, key_pair,
+        probs_low, own_probs_low, dscores, own_dscores, **_
+    ):
         key_part = dot(dscores, query_pair, 1, 0)
         value_part = dot(probs_low, grad_pair, 1, 0)
         key_acc[first_at] += key_part[:, :E]
@@ -272,6 +257,13 @@
             grads[:, h * E : (h + 1) * E] = query_part[:, h * rows : (h + 1) * rows].T.astype(BF16)
         grads[:, group * E : (group + 1) * E] = (dot(own_dscores, query, 1, 0) * SCALE).astype(BF16)
         grads[:, (group + 1) * E :] = dot(own_probs_low, grad, 1, 0).astype(BF16)
+
+    ahead = products(packets[0])
+    for j in range(n):
+        now = ahead
+        if j + 1 < n:
+            ahead = products(packets[j + 1])
+        gradients(grads_out[j], **now, **soften(**now))
 
     for index in range(pieces):
         for j in range(n):
@@ -401,17 +393,23 @@
     head = sum(((device >> bit) & 1) << i for i, bit in enumerate(HEAD_BITS))
     place = jnp.stack([head, prompt])
 
-    packed = pack(
-        place, first_length, resp_prompt, queries, out_grad, own_keys, own_values, heads
+    packed, projected = opening(
+        place,
+        first_length,
+        resp_prompt,
+        prompt_rows,
+        (queries, out_grad, own_keys, own_values),
+        (key_weight, value_weight),
+        heads,
     )
-    packed, prompt_rows = lax.optimization_barrier((packed, prompt_rows))
     packets = swap_group(packed)
-
-    projected = project(place, prompt_rows, key_weight, value_weight, heads)
     pieces = {0: jnp.stack(swap_group(projected))}
     for bit in rest_bits:
         for offset in list(pieces):
-            pieces[offset | 1 << bit] = swap(pieces[offset], 1 << bit)
+            piece = pieces[offset]
+            if bit == rest_bits[-1] and offset == max(pieces):
+                piece, packets = lax.optimization_barrier((piece, packets))
+            pieces[offset | 1 << bit] = swap(piece, 1 << bit)
     offsets = list(pieces)
 
     filled = [0] * n_prompt
@@ -436,6 +434,8 @@
                 piece = sums.pop(offset)
                 for part in arrived.pop(offset):
                     piece = piece + part.astype(F32)
+                if arrived[0] and bit == rest_bits[-2] and offset == max(offsets):
+                    piece, grads = lax.optimization_barrier((piece, grads))
                 arrived[offset ^ 1 << bit].append(swap(piece.astype(BF16), 1 << bit))
         offsets = list(sums)
     shares = swap_group(total(sums[0], arrived[0]))

time: 139 us -> 90.9 us (0.65)
  Pallas kernels: 71.2 us -> 22.6 us
  starting transfers between devices: 28.1 us -> 26.1 us
  local copies, waits for them, and re-layouts: 0.05 us -> 1.7 us
    pallas_call x2 -> x1, Pallas kernels: 55.9 us -> 7.38 us  [opening(): pl.pallas_call(functools.partial(open_kernel, n, steps), out_shape=[jax.S...]
    ppermute x26, starting transfers between devices: 28.1 us -> 26.1 us  [swap(): lax.ppermute(x, ('prompt', 'resp'), [(i, i ^ offset) for i in range(devic...]
    unnamed x18 -> x12, local copies, waits for them, and re-layouts: 0.05 us -> 1.7 us
  transfers between devices with their start and end apart: 26 -> 26, of which waited for: 11 -> 10; matrix products, arithmetic and copies ran while one was open for 0% -> 1% of each run, Pallas kernels for 1% -> 2%
where the time goes in v3:
time: 90.9 us; the launch traced here: 90.7 us
  waiting for transfers between devices  37.4 us (41%)
  starting transfers between devices  26.1 us (29%)
  Pallas kernels  22.6 us (25%)
  local copies, waits for them, and re-layouts  1.7 us (2%)
  other arithmetic  1.49 us (2%)
  between operations  1.41 us (2%)
    ppermute x26, waiting for transfers between devices, swap(): lax.ppermute(x, ('prompt', 'resp'), [(i, i ^ offset) for i in range(devic...  37.4 us
    ppermute x26, starting transfers between devices, swap(): lax.ppermute(x, ('prompt', 'resp'), [(i, i ^ offset) for i in range(devic...  26.1 us
    pallas_call x1, Pallas kernels, attend(): pl.pallas_call(functools.partial(attend_kernel, slots, n, group, rows), o...  8.48 us
    pallas_call x1, Pallas kernels, opening(): pl.pallas_call(functools.partial(open_kernel, n, steps), out_shape=[jax.S...  7.38 us
    pallas_call x1, Pallas kernels, prompt_gradient(): pl.pallas_call(functools.partial(prompt_kernel, n), grid=(depth // chunk,...  5.1 us
  transfers between devices with their start and end apart: 26, of which 10 were waited for; matrix products, arithmetic and copies ran while one was open for 1% of the time, Pallas kernels for 2%

profile of v3, /device:TPU:0, one launch (start us, length us, event | category | flops | bytes accessed | tf_op | source)
XLA Modules:
  0.0 90.7 jit_solution(12525571402786523904)
XLA Ops:
  1.9 7.4 %open.1 = (bf16[144,1536]{1,0:T(8,128)(2,1)}, bf16[144,1536]{1,0:T(8,128)(2,1)}, bf16[144,1536]{1,0:T(8,128)(2,1)}, bf16[144,1536]{1,0:T(8,128)(2,1)}, bf16[64,2...) custom-call(s32[2]{0:T(128)} %pad_add_fusion.place_ref, ...), custom_call_target="tpu_custom_call" | custom-call | bytes 1024 | tf_op jit(solution)/shard_map/open/pallas_call | solution.py:106
  9.3 3.0 %collective-permute-start = (bf16[64,256]{1,0:T(8,128)(2,1)}, bf16[64,256]{1,0:T(8,128)(2,1)S(1)}, u32[]{:S(2)}, u32[]{:S(2)}) collective-permute-start(bf16[64,256]{1,0:T(8,128)(2,1)} %get-tuple-element.42), channel_id=1, source_target_pairs={{0,8},{1,9},{2,10},{3,11},{4,12},{5,13},{6,14},{7,15},{8,0},{9,1},... | collective-permute-start | bytes 98312 | tf_op jit(solution)/shard_map/ppermute | solution.py:386
  12.4 2.0 %collective-permute-start.6 = (bf16[144,1536]{1,0:T(8,128)(2,1)}, bf16[144,1536]{1,0:T(8,128)(2,1)S(1)}, u32[]{:S(2)}, u32[]{:S(2)}) collective-permute-start(bf16[144,1536]{1,0:T(8,128)(2,1)} %get-tuple-element.47), channel_id=1, source_target_pairs={{0,16},{1,17},{2,18},{3,19},{4,20},{5,21},{6,22},{7,23},{8,24},{9,... | collective-permute-start | bytes 1327112 | tf_op jit(solution)/shard_map/ppermute | solution.py:386
  14.3 1.4 %collective-permute-start.7 = (bf16[144,1536]{1,0:T(8,128)(2,1)}, bf16[144,1536]{1,0:T(8,128)(2,1)S(1)}, u32[]{:S(2)}, u32[]{:S(2)}) collective-permute-start(bf16[144,1536]{1,0:T(8,128)(2,1)} %get-tuple-element.48), channel_id=1, source_target_pairs={{0,24},{1,25},{2,26},{3,27},{4,28},{5,29},{6,30},{7,31},{8,16},{9,... | collective-permute-start | bytes 1327112 | tf_op jit(solution)/shard_map/ppermute | solution.py:386
  15.8 1.5 %collective-permute-start.1 = (bf16[64,256]{1,0:T(8,128)(2,1)}, bf16[64,256]{1,0:T(8,128)(2,1)S(1)}, u32[]{:S(2)}, u32[]{:S(2)}) collective-permute-start(bf16[64,256]{1,0:T(8,128)(2,1)} %get-tuple-element.43), channel_id=1, source_target_pairs={{0,16},{1,17},{2,18},{3,19},{4,20},{5,21},{6,22},{7,23},{8,24},{9,... | collective-permute-start | bytes 98312 | tf_op jit(solution)/shard_map/ppermute | solution.py:386
  17.7 16.7 %collective-permute-done.1 = bf16[64,256]{1,0:T(8,128)(2,1)S(1)} collective-permute-done((bf16[64,256]{1,0:T(8,128)(2,1)}, bf16[64,256]{1,0:T(8,128)(2,1)S(1)}, u32[]{:S(2)}, u32[]{:S(2)}) %collective-permute-start.1) | collective-permute-done | bytes 32800 | tf_op jit(solution)/shard_map/ppermute | solution.py:386
  34.4 1.1 %collective-permute-done.2 = bf16[64,256]{1,0:T(8,128)(2,1)S(1)} collective-permute-done((bf16[64,256]{1,0:T(8,128)(2,1)}, bf16[64,256]{1,0:T(8,128)(2,1)S(1)}, u32[]{:S(2)}, u32[]{:S(2)}) %collective-permute-start.2) | collective-permute-done | bytes 32800 | tf_op jit(solution)/shard_map/ppermute | solution.py:386
  36.3 2.7 %collective-permute-start.3 = (bf16[4,64,256]{2,1,0:T(8,128)(2,1)S(1)}, bf16[4,64,256]{2,1,0:T(8,128)(2,1)S(1)}, u32[]{:S(2)}, u32[]{:S(2)}) collective-permute-start(bf16[4,64,256]{2,1,0:T(8,128)(2,1)S(1)} %pad_maximum_fusion.rest_4_), channel_id=1, source_target_pairs={{0,4},{1,5},{2,6},{3,7},{4,0},{5,1},{6,2},{7,3},{8,12},{9,13},{10,... | collective-permute-start | bytes 393224 | tf_op jit(solution)/shard_map/ppermute | solution.py:386
  39.0 1.6 %collective-permute-start.8 = (bf16[4,64,256]{2,1,0:T(8,128)(2,1)S(1)}, bf16[4,64,256]{2,1,0:T(8,128)(2,1)S(1)}, u32[]{:S(2)}, u32[]{:S(2)}) collective-permute-start(bf16[4,64,256]{2,1,0:T(8,128)(2,1)S(1)} %pad_maximum_fusion.rest_4_), channel_id=1, source_target_pairs={{0,2},{1,3},{2,0},{3,1},{4,6},{5,7},{6,4},{7,5},{8,10},{9,11},{10,... | collective-permute-start | bytes 393224 | tf_op jit(solution)/shard_map/ppermute | solution.py:386
  40.6 4.0 %collective-permute-done.3.rest_5_ = bf16[4,64,256]{2,1,0:T(8,128)(2,1)S(1)} collective-permute-done((bf16[4,64,256]{2,1,0:T(8,128)(2,1)S(1)}, bf16[4,64,256]{2,1,0:T(8,128)(2,1)S(1)}, u32[]{:S(2)}, u32[]{:S(2)}) %collective-permute-start.3) | collective-permute-done | bytes 131104 | tf_op jit(solution)/shard_map/ppermute | solution.py:386
  45.1 4.4 %collective-permute-done.4.rest_7_ = bf16[4,64,256]{2,1,0:T(8,128)(2,1)S(1)} collective-permute-done((bf16[4,64,256]{2,1,0:T(8,128)(2,1)S(1)}, bf16[4,64,256]{2,1,0:T(8,128)(2,1)S(1)}, u32[]{:S(2)}, u32[]{:S(2)}) %collective-permute-start.4) | collective-permute-done | bytes 131104 | tf_op jit(solution)/shard_map/ppermute | solution.py:386
  51.5 1.7 %copy-done.1 = bf16[144,1536]{1,0:T(8,128)(2,1)S(1)} copy-done((bf16[144,1536]{1,0:T(8,128)(2,1)S(1)}, bf16[144,1536]{1,0:T(8,128)(2,1)}, u32[]{:S(2)}) %copy-start.1) | copy-done | bytes 442392
  53.1 8.5 %attend_head.1 = (bf16[128,896]{1,0:T(8,128)(2,1)S(1)}, bf16[128,896]{1,0:T(8,128)(2,1)S(1)}, bf16[128,896]{1,0:T(8,128)(2,1)S(1)}, bf16[128,896]{1,0:T(8,128)(2...) custom-call(s32[2]{0:T(128)S(1)} %copy-done, ...), custom_call_target="tpu_custom_call" | custom-call | flops 4194304000 | bytes 8388608 | tf_op jit(solution)/shard_map/attend_head/pallas_call | solution.py:283
  63.7 1.5 %collective-permute-start.19 = (bf16[4,64,256]{2,1,0:T(8,128)(2,1)S(1)}, bf16[4,64,256]{2,1,0:T(8,128)(2,1)S(1)}, u32[]{:S(2)}, u32[]{:S(2)}) collective-permute-start(bf16[4,64,256]{2,1,0:T(8,128)(2,1)S(1)} %add_convert_fusion.1), channel_id=1, source_target_pairs={{0,2},{1,3},{2,0},{3,1},{4,6},{5,7},{6,4},{7,5},{8,10},{9,11},{10,... | collective-permute-start | bytes 393224 | tf_op jit(solution)/shard_map/ppermute | solution.py:386
  66.1 1.1 %collective-permute-start.15 = (bf16[128,896]{1,0:T(8,128)(2,1)S(1)}, bf16[128,896]{1,0:T(8,128)(2,1)S(1)}, u32[]{:S(2)}, u32[]{:S(2)}) collective-permute-start(bf16[128,896]{1,0:T(8,128)(2,1)S(1)} %get-tuple-element.62), channel_id=1, source_target_pairs={{0,16},{1,17},{2,18},{3,19},{4,20},{5,21},{6,22},{7,23},{8,24},{9,... | collective-permute-start | bytes 688136 | tf_op jit(solution)/shard_map/ppermute | solution.py:386
  67.3 2.2 %collective-permute-done.21 = bf16[4,64,256]{2,1,0:T(8,128)(2,1)S(1)} collective-permute-done((bf16[4,64,256]{2,1,0:T(8,128)(2,1)S(1)}, bf16[4,64,256]{2,1,0:T(8,128)(2,1)S(1)}, u32[]{:S(2)}, u32[]{:S(2)}) %collective-permute-start.21) | collective-permute-done | bytes 131104 | tf_op jit(solution)/shard_map/ppermute | solution.py:386
  69.5 1.4 %collective-permute-start.16 = (bf16[128,896]{1,0:T(8,128)(2,1)S(1)}, bf16[128,896]{1,0:T(8,128)(2,1)S(1)}, u32[]{:S(2)}, u32[]{:S(2)}) collective-permute-start(bf16[128,896]{1,0:T(8,128)(2,1)S(1)} %get-tuple-element.63), channel_id=1, source_target_pairs={{0,24},{1,25},{2,26},{3,27},{4,28},{5,29},{6,30},{7,31},{8,16},{9,... | collective-permute-start | bytes 688136 | tf_op jit(solution)/shard_map/ppermute | solution.py:386
  71.0 2.1 %collective-permute-start.22 = (bf16[4,64,256]{2,1,0:T(8,128)(2,1)S(1)}, bf16[4,64,256]{2,1,0:T(8,128)(2,1)S(1)}, u32[]{:S(2)}, u32[]{:S(2)}) collective-permute-start(bf16[4,64,256]{2,1,0:T(8,128)(2,1)S(1)} %add_convert_fusion), channel_id=1, source_target_pairs={{0,4},{1,5},{2,6},{3,7},{4,0},{5,1},{6,2},{7,3},{8,12},{9,13},{10,... | collective-permute-start | bytes 393224 | tf_op jit(solution)/shard_map/ppermute | solution.py:386
  73.0 5.5 %collective-permute-done.22.rest_2_ = bf16[4,64,256]{2,1,0:T(8,128)(2,1)S(1)} collective-permute-done((bf16[4,64,256]{2,1,0:T(8,128)(2,1)S(1)}, bf16[4,64,256]{2,1,0:T(8,128)(2,1)S(1)}, u32[]{:S(2)}, u32[]{:S(2)}) %collective-permute-start.22) | collective-permute-done | bytes 131104 | tf_op jit(solution)/shard_map/ppermute | solution.py:386
  79.2 1.5 %collective-permute-start.24 = (bf16[64,256]{1,0:T(8,128)(2,1)S(1)}, bf16[64,256]{1,0:T(8,128)(2,1)S(1)}, u32[]{:S(2)}, u32[]{:S(2)}) collective-permute-start(bf16[64,256]{1,0:T(8,128)(2,1)S(1)} %get-tuple-element.76), channel_id=1, source_target_pairs={{0,16},{1,17},{2,18},{3,19},{4,20},{5,21},{6,22},{7,23},{8,24},{9,... | collective-permute-start | bytes 98312 | tf_op jit(solution)/shard_map/ppermute | solution.py:386
  80.7 1.4 %collective-permute-start.25 = (bf16[64,256]{1,0:T(8,128)(2,1)S(1)}, bf16[64,256]{1,0:T(8,128)(2,1)S(1)}, u32[]{:S(2)}, u32[]{:S(2)}) collective-permute-start(bf16[64,256]{1,0:T(8,128)(2,1)S(1)} %get-tuple-element.77), channel_id=1, source_target_pairs={{0,24},{1,25},{2,26},{3,27},{4,28},{5,29},{6,30},{7,31},{8,16},{9,... | collective-permute-start | bytes 98312 | tf_op jit(solution)/shard_map/ppermute | solution.py:386
  82.1 1.6 %unpack_rows.1 = (bf16[128,2560]{1,0:T(8,128)(2,1)}, bf16[128,512]{1,0:T(8,128)(2,1)}, bf16[128,512]{1,0:T(8,128)(2,1)}) custom-call(s32[2]{0:T(128)S(1)} %copy-done, bf16[128,896]{1,0:T(8,128)(2,1)S(1)} %get-tuple-element.60.rest_0_, bf16[128,896]{1,0:T(8,128)(2,1)S(1)} %collective-permute-done.14.rest_1_, ...), custom_call_target="tpu_custom_call" | custom-call | bytes 1835008 | tf_op jit(solution)/shard_map/unpack_rows/pallas_call | solution.py:135
  83.7 1.8 %collective-permute-done.25.rest_3_ = bf16[64,256]{1,0:T(8,128)(2,1)S(1)} collective-permute-done((bf16[64,256]{1,0:T(8,128)(2,1)S(1)}, bf16[64,256]{1,0:T(8,128)(2,1)S(1)}, u32[]{:S(2)}, u32[]{:S(2)}) %collective-permute-start.25) | collective-permute-done | bytes 32800 | tf_op jit(solution)/shard_map/ppermute | solution.py:386
  85.6 5.1 %prompt_gradient.1 = bf16[64,5120]{1,0:T(8,128)(2,1)} custom-call(s32[2]{0:T(128)S(1)} %copy-done, bf16[64,256]{1,0:T(8,128)(2,1)S(1)} %get-tuple-element.74.rest_0_, bf16[64,256]{1,0:T(8,128)(2,1)S(1)} %collective-permute-done.23.rest_1_, bf16[64,256]{1,0:T(8,128)(2,1)S(1)} %collective-permute-done.24.rest_2_, ...), custom_call_target="tpu_custom_call" | custom-call | flops 671088640 | bytes 11141120 | tf_op jit(solution)/shard_map/prompt_gradient/pallas_call | solution.py:346
  (52 shorter events, 8.2 us)
Async XLA Ops:
  9.3 8.0 %collective-permute-start = (bf16[64,256]{1,0:T(8,128)(2,1)}, bf16[64,256]{1,0:T(8,128)(2,1)S(1)}, u32[]{:S(2)}, u32[]{:S(2)}) collective-permute-start(bf16[64,256]{1,0:T(8,128)(2,1)} %get-tuple-element.42), channel_id=1, source_target_pairs={{0,8},{1,9},{2,10},{3,11},{4,12},{5,13},{6,14},{7,15},{8,0},{9,1},... | collective-permute-start | bytes 98312 | tf_op jit(solution)/shard_map/ppermute | solution.py:386
  12.3 37.2 %collective-permute-start.5 = (bf16[144,1536]{1,0:T(8,128)(2,1)}, bf16[144,1536]{1,0:T(8,128)(2,1)S(1)}, u32[]{:S(2)}, u32[]{:S(2)}) collective-permute-start(bf16[144,1536]{1,0:T(8,128)(2,1)} %get-tuple-element.46), channel_id=1, source_target_pairs={{0,8},{1,9},{2,10},{3,11},{4,12},{5,13},{6,14},{7,15},{8,0},{9,1},... | collective-permute-start | bytes 1327112 | tf_op jit(solution)/shard_map/ppermute | solution.py:386
  12.4 37.6 %collective-permute-start.6 = (bf16[144,1536]{1,0:T(8,128)(2,1)}, bf16[144,1536]{1,0:T(8,128)(2,1)S(1)}, u32[]{:S(2)}, u32[]{:S(2)}) collective-permute-start(bf16[144,1536]{1,0:T(8,128)(2,1)} %get-tuple-element.47), channel_id=1, source_target_pairs={{0,16},{1,17},{2,18},{3,19},{4,20},{5,21},{6,22},{7,23},{8,24},{9,... | collective-permute-start | bytes 1327112 | tf_op jit(solution)/shard_map/ppermute | solution.py:386
  14.3 35.7 %collective-permute-start.7 = (bf16[144,1536]{1,0:T(8,128)(2,1)}, bf16[144,1536]{1,0:T(8,128)(2,1)S(1)}, u32[]{:S(2)}, u32[]{:S(2)}) collective-permute-start(bf16[144,1536]{1,0:T(8,128)(2,1)} %get-tuple-element.48), channel_id=1, source_target_pairs={{0,24},{1,25},{2,26},{3,27},{4,28},{5,29},{6,30},{7,31},{8,16},{9,... | collective-permute-start | bytes 1327112 | tf_op jit(solution)/shard_map/ppermute | solution.py:386
  15.8 18.6 %collective-permute-start.1 = (bf16[64,256]{1,0:T(8,128)(2,1)}, bf16[64,256]{1,0:T(8,128)(2,1)S(1)}, u32[]{:S(2)}, u32[]{:S(2)}) collective-permute-start(bf16[64,256]{1,0:T(8,128)(2,1)} %get-tuple-element.43), channel_id=1, source_target_pairs={{0,16},{1,17},{2,18},{3,19},{4,20},{5,21},{6,22},{7,23},{8,24},{9,... | collective-permute-start | bytes 98312 | tf_op jit(solution)/shard_map/ppermute | solution.py:386
  17.3 18.2 %collective-permute-start.2 = (bf16[64,256]{1,0:T(8,128)(2,1)}, bf16[64,256]{1,0:T(8,128)(2,1)S(1)}, u32[]{:S(2)}, u32[]{:S(2)}) collective-permute-start(bf16[64,256]{1,0:T(8,128)(2,1)} %get-tuple-element.44), channel_id=1, source_target_pairs={{0,24},{1,25},{2,26},{3,27},{4,28},{5,29},{6,30},{7,31},{8,16},{9,... | collective-permute-start | bytes 98312 | tf_op jit(solution)/shard_map/ppermute | solution.py:386
  36.3 8.2 %collective-permute-start.3 = (bf16[4,64,256]{2,1,0:T(8,128)(2,1)S(1)}, bf16[4,64,256]{2,1,0:T(8,128)(2,1)S(1)}, u32[]{:S(2)}, u32[]{:S(2)}) collective-permute-start(bf16[4,64,256]{2,1,0:T(8,128)(2,1)S(1)} %pad_maximum_fusion.rest_4_), channel_id=1, source_target_pairs={{0,4},{1,5},{2,6},{3,7},{4,0},{5,1},{6,2},{7,3},{8,12},{9,13},{10,... | collective-permute-start | bytes 393224 | tf_op jit(solution)/shard_map/ppermute | solution.py:386
  39.0 6.1 %collective-permute-start.8 = (bf16[4,64,256]{2,1,0:T(8,128)(2,1)S(1)}, bf16[4,64,256]{2,1,0:T(8,128)(2,1)S(1)}, u32[]{:S(2)}, u32[]{:S(2)}) collective-permute-start(bf16[4,64,256]{2,1,0:T(8,128)(2,1)S(1)} %pad_maximum_fusion.rest_4_), channel_id=1, source_target_pairs={{0,2},{1,3},{2,0},{3,1},{4,6},{5,7},{6,4},{7,5},{8,10},{9,11},{10,... | collective-permute-start | bytes 393224 | tf_op jit(solution)/shard_map/ppermute | solution.py:386
  44.5 5.0 %collective-permute-start.4 = (bf16[4,64,256]{2,1,0:T(8,128)(2,1)S(1)}, bf16[4,64,256]{2,1,0:T(8,128)(2,1)S(1)}, u32[]{:S(2)}, u32[]{:S(2)}) collective-permute-start(bf16[4,64,256]{2,1,0:T(8,128)(2,1)S(1)} %collective-permute-done.3.rest_5_), channel_id=1, source_target_pairs={{0,2},{1,3},{2,0},{3,1},{4,6},{5,7},{6,4},{7,5},{8,10},{9,11},{10,... | collective-permute-start | bytes 393224 | tf_op jit(solution)/shard_map/ppermute | solution.py:386
  45.1 5.0 %collective-permute-start.9 = (bf16[4,64,256]{2,1,0:T(8,128)(2,1)S(1)}, bf16[4,64,256]{2,1,0:T(8,128)(2,1)S(1)}, u32[]{:S(2)}, u32[]{:S(2)}) collective-permute-start(bf16[4,64,256]{2,1,0:T(8,128)(2,1)S(1)} %pad_maximum_fusion.rest_4_), channel_id=1, source_target_pairs={{0,1},{1,0},{2,3},{3,2},{4,5},{5,4},{6,7},{7,6},{8,9},{9,8},{10,11... | collective-permute-start | bytes 393224 | tf_op jit(solution)/shard_map/ppermute | solution.py:386
  49.5 1.5 %collective-permute-start.10 = (bf16[4,64,256]{2,1,0:T(8,128)(2,1)S(1)}, bf16[4,64,256]{2,1,0:T(8,128)(2,1)S(1)}, u32[]{:S(2)}, u32[]{:S(2)}) collective-permute-start(bf16[4,64,256]{2,1,0:T(8,128)(2,1)S(1)} %collective-permute-done.3.rest_5_), channel_id=1, source_target_pairs={{0,1},{1,0},{2,3},{3,2},{4,5},{5,4},{6,7},{7,6},{8,9},{9,8},{10,11... | collective-permute-start | bytes 393224 | tf_op jit(solution)/shard_map/ppermute | solution.py:386
  49.5 1.5 %collective-permute-start.11 = (bf16[4,64,256]{2,1,0:T(8,128)(2,1)S(1)}, bf16[4,64,256]{2,1,0:T(8,128)(2,1)S(1)}, u32[]{:S(2)}, u32[]{:S(2)}) collective-permute-start(bf16[4,64,256]{2,1,0:T(8,128)(2,1)S(1)} %collective-permute-done.8.rest_6_), channel_id=1, source_target_pairs={{0,1},{1,0},{2,3},{3,2},{4,5},{5,4},{6,7},{7,6},{8,9},{9,8},{10,11... | collective-permute-start | bytes 393224 | tf_op jit(solution)/shard_map/ppermute | solution.py:386
  61.9 9.1 %collective-permute-start.17 = (bf16[4,64,256]{2,1,0:T(8,128)(2,1)S(1)}, bf16[4,64,256]{2,1,0:T(8,128)(2,1)S(1)}, u32[]{:S(2)}, u32[]{:S(2)}) collective-permute-start(bf16[4,64,256]{2,1,0:T(8,128)(2,1)S(1)} %get-tuple-element.68), channel_id=1, source_target_pairs={{0,1},{1,0},{2,3},{3,2},{4,5},{5,4},{6,7},{7,6},{8,9},{9,8},{10,11... | collective-permute-start | bytes 393224 | tf_op jit(solution)/shard_map/ppermute | solution.py:386
  62.2 1.5 %collective-permute-start.18 = (bf16[4,64,256]{2,1,0:T(8,128)(2,1)S(1)}, bf16[4,64,256]{2,1,0:T(8,128)(2,1)S(1)}, u32[]{:S(2)}, u32[]{:S(2)}) collective-permute-start(bf16[4,64,256]{2,1,0:T(8,128)(2,1)S(1)} %get-tuple-element.70), channel_id=1, source_target_pairs={{0,1},{1,0},{2,3},{3,2},{4,5},{5,4},{6,7},{7,6},{8,9},{9,8},{10,11... | collective-permute-start | bytes 393224 | tf_op jit(solution)/shard_map/ppermute | solution.py:386
  62.4 3.7 %collective-permute-start.20 = (bf16[4,64,256]{2,1,0:T(8,128)(2,1)S(1)}, bf16[4,64,256]{2,1,0:T(8,128)(2,1)S(1)}, u32[]{:S(2)}, u32[]{:S(2)}) collective-permute-start(bf16[4,64,256]{2,1,0:T(8,128)(2,1)S(1)} %get-tuple-element.72), channel_id=1, source_target_pairs={{0,1},{1,0},{2,3},{3,2},{4,5},{5,4},{6,7},{7,6},{8,9},{9,8},{10,11... | collective-permute-start | bytes 393224 | tf_op jit(solution)/shard_map/ppermute | solution.py:386
  63.1 6.4 %collective-permute-start.21 = (bf16[4,64,256]{2,1,0:T(8,128)(2,1)S(1)}, bf16[4,64,256]{2,1,0:T(8,128)(2,1)S(1)}, u32[]{:S(2)}, u32[]{:S(2)}) collective-permute-start(bf16[4,64,256]{2,1,0:T(8,128)(2,1)S(1)} %convert_add_fusion), channel_id=1, source_target_pairs={{0,2},{1,3},{2,0},{3,1},{4,6},{5,7},{6,4},{7,5},{8,10},{9,11},{10,... | collective-permute-start | bytes 393224 | tf_op jit(solution)/shard_map/ppermute | solution.py:386
  63.7 9.3 %collective-permute-start.19 = (bf16[4,64,256]{2,1,0:T(8,128)(2,1)S(1)}, bf16[4,64,256]{2,1,0:T(8,128)(2,1)S(1)}, u32[]{:S(2)}, u32[]{:S(2)}) collective-permute-start(bf16[4,64,256]{2,1,0:T(8,128)(2,1)S(1)} %add_convert_fusion.1), channel_id=1, source_target_pairs={{0,2},{1,3},{2,0},{3,1},{4,6},{5,7},{6,4},{7,5},{8,10},{9,11},{10,... | collective-permute-start | bytes 393224 | tf_op jit(solution)/shard_map/ppermute | solution.py:386
  65.3 15.4 %collective-permute-start.14 = (bf16[128,896]{1,0:T(8,128)(2,1)S(1)}, bf16[128,896]{1,0:T(8,128)(2,1)S(1)}, u32[]{:S(2)}, u32[]{:S(2)}) collective-permute-start(bf16[128,896]{1,0:T(8,128)(2,1)S(1)} %get-tuple-element.61), channel_id=1, source_target_pairs={{0,8},{1,9},{2,10},{3,11},{4,12},{5,13},{6,14},{7,15},{8,0},{9,1},... | collective-permute-start | bytes 688136 | tf_op jit(solution)/shard_map/ppermute | solution.py:386
  66.1 16.0 %collective-permute-start.15 = (bf16[128,896]{1,0:T(8,128)(2,1)S(1)}, bf16[128,896]{1,0:T(8,128)(2,1)S(1)}, u32[]{:S(2)}, u32[]{:S(2)}) collective-permute-start(bf16[128,896]{1,0:T(8,128)(2,1)S(1)} %get-tuple-element.62), channel_id=1, source_target_pairs={{0,16},{1,17},{2,18},{3,19},{4,20},{5,21},{6,22},{7,23},{8,24},{9,... | collective-permute-start | bytes 688136 | tf_op jit(solution)/shard_map/ppermute | solution.py:386
  69.5 12.7 %collective-permute-start.16 = (bf16[128,896]{1,0:T(8,128)(2,1)S(1)}, bf16[128,896]{1,0:T(8,128)(2,1)S(1)}, u32[]{:S(2)}, u32[]{:S(2)}) collective-permute-start(bf16[128,896]{1,0:T(8,128)(2,1)S(1)} %get-tuple-element.63), channel_id=1, source_target_pairs={{0,24},{1,25},{2,26},{3,27},{4,28},{5,29},{6,30},{7,31},{8,16},{9,... | collective-permute-start | bytes 688136 | tf_op jit(solution)/shard_map/ppermute | solution.py:386
  71.0 7.5 %collective-permute-start.22 = (bf16[4,64,256]{2,1,0:T(8,128)(2,1)S(1)}, bf16[4,64,256]{2,1,0:T(8,128)(2,1)S(1)}, u32[]{:S(2)}, u32[]{:S(2)}) collective-permute-start(bf16[4,64,256]{2,1,0:T(8,128)(2,1)S(1)} %add_convert_fusion), channel_id=1, source_target_pairs={{0,4},{1,5},{2,6},{3,7},{4,0},{5,1},{6,2},{7,3},{8,12},{9,13},{10,... | collective-permute-start | bytes 393224 | tf_op jit(solution)/shard_map/ppermute | solution.py:386
  78.6 5.1 %collective-permute-start.23 = (bf16[64,256]{1,0:T(8,128)(2,1)S(1)}, bf16[64,256]{1,0:T(8,128)(2,1)S(1)}, u32[]{:S(2)}, u32[]{:S(2)}) collective-permute-start(bf16[64,256]{1,0:T(8,128)(2,1)S(1)} %get-tuple-element.75), channel_id=1, source_target_pairs={{0,8},{1,9},{2,10},{3,11},{4,12},{5,13},{6,14},{7,15},{8,0},{9,1},... | collective-permute-start | bytes 98312 | tf_op jit(solution)/shard_map/ppermute | solution.py:386
  79.2 4.5 %collective-permute-start.24 = (bf16[64,256]{1,0:T(8,128)(2,1)S(1)}, bf16[64,256]{1,0:T(8,128)(2,1)S(1)}, u32[]{:S(2)}, u32[]{:S(2)}) collective-permute-start(bf16[64,256]{1,0:T(8,128)(2,1)S(1)} %get-tuple-element.76), channel_id=1, source_target_pairs={{0,16},{1,17},{2,18},{3,19},{4,20},{5,21},{6,22},{7,23},{8,24},{9,... | collective-permute-start | bytes 98312 | tf_op jit(solution)/shard_map/ppermute | solution.py:386
  80.7 4.8 %collective-permute-start.25 = (bf16[64,256]{1,0:T(8,128)(2,1)S(1)}, bf16[64,256]{1,0:T(8,128)(2,1)S(1)}, u32[]{:S(2)}, u32[]{:S(2)}) collective-permute-start(bf16[64,256]{1,0:T(8,128)(2,1)S(1)} %get-tuple-element.77), channel_id=1, source_target_pairs={{0,24},{1,25},{2,26},{3,27},{4,28},{5,29},{6,30},{7,31},{8,16},{9,... | collective-permute-start | bytes 98312 | tf_op jit(solution)/shard_map/ppermute | solution.py:386
  (8 other events, 196.1 us)

commit v4 on v3

v4 whole, which is shorter than its diff:
```python
import functools
import math

import jax
import jax.numpy as jnp
from jax import lax
from jax.experimental import pallas as pl
from jax.experimental.pallas import tpu as pltpu
from jax.sharding import PartitionSpec as P

E = 128
PLEN = 512
SCALE = E ** (-0.5)
EXP2_SCALE = SCALE * math.log2(math.e)
HIDDEN = -1e30
BF16 = jnp.bfloat16
F32 = jnp.float32
NOTE_ROWS = 16
HEAD_BITS = (3, 4)
GATHER_BITS = (2, 1, 0)

ANY = pl.BlockSpec(memory_space=pl.ANY)
VMEM = pl.BlockSpec(memory_space=pltpu.VMEM)


def params(mebibytes=40):
    return pltpu.CompilerParams(vmem_limit_bytes=mebibytes * 1024 * 1024)


def cost(flops, bytes_accessed, transcendentals=0):
    return pl.CostEstimate(
        flops=int(flops), bytes_accessed=int(bytes_accessed), transcendentals=int(transcendentals)
    )


def lanes(index, width):
    return pl.ds(pl.multiple_of(index * width, 128), width)


def dot(a, b, a_dim, b_dim):
    return lax.dot_general(a, b, (((a_dim,), (b_dim,)), ((), ())), preferred_element_type=F32)


def place():
    prompt = lax.axis_index("prompt")
    device = prompt * lax.axis_size("resp") + lax.axis_index("resp")
    return sum(((device >> bit) & 1) << i for i, bit in enumerate(HEAD_BITS)), prompt


def project_kernel(n, steps, length_ref, prompts_ref, x_ref, kw_ref, vw_ref, *rest):
    outs, (kw, vw, key_sum, value_sum, length, prompts, sems, note_sems) = rest[:n], rest[n:]
    chunk = kw.shape[0] // steps
    copies = []
    for step in range(steps):
        span = slice(step * chunk, (step + 1) * chunk)
        for source, target in ((kw_ref, kw), (vw_ref, vw)):
            copies.append(
                pltpu.make_async_copy(
                    source.at[span, :], target.at[span, :], sems.at[len(copies)]
                )
            )
    note_copies = [
        pltpu.make_async_copy(length_ref, length, note_sems.at[0]),
        pltpu.make_async_copy(prompts_ref, prompts, note_sems.at[1]),
    ]
    for copy in copies + note_copies:
        copy.start()
    keys = values = None
    for step in range(steps):
        span = slice(step * chunk, (step + 1) * chunk)
        copies[2 * step].wait()
        part = dot(x_ref[:, span], kw[span, :], 1, 0)
        keys = part if step == 0 else keys + part
        copies[2 * step + 1].wait()
        part = dot(x_ref[:, span], vw[span, :], 1, 0)
        values = part if step == 0 else values + part
    key_sum[...] = keys.astype(BF16)
    value_sum[...] = values.astype(BF16)
    for copy in note_copies:
        copy.wait()
    lane = lax.broadcasted_iota(jnp.int32, (NOTE_ROWS, 2 * E), 1)
    row = lax.broadcasted_iota(jnp.int32, (NOTE_ROWS, 2 * E), 0)
    note = jnp.where(
        lane < E, length[0, 0], jnp.where(row < NOTE_ROWS // 2, prompts[0, 0], prompts[0, 1])
    )
    note = note.astype(F32).astype(BF16)
    head, _ = place()
    rows = x_ref.shape[0]
    for j in range(n):
        outs[j][:rows, :E] = key_sum[:, lanes(head ^ j, E)]
        outs[j][:rows, E:] = value_sum[:, lanes(head ^ j, E)]
        outs[j][rows:, :] = note


def project(first_length, resp_prompt, prompt_rows, key_weight, value_weight, n, steps=10):
    rows = prompt_rows.shape[0]
    depth, width = key_weight.shape
    return pl.pallas_call(
        functools.partial(project_kernel, n, steps),
        out_shape=[jax.ShapeDtypeStruct((rows + NOTE_ROWS, 2 * E), BF16)] * n,
        in_specs=[ANY, ANY, VMEM, ANY, ANY],
        out_specs=[VMEM] * n,
        scratch_shapes=[pltpu.VMEM(key_weight.shape, BF16)] * 2
        + [pltpu.VMEM((rows, width), BF16)] * 2
        + [pltpu.SMEM(first_length.shape, jnp.int32), pltpu.SMEM(resp_prompt.shape, jnp.int32)]
        + [pltpu.SemaphoreType.DMA((2 * steps,)), pltpu.SemaphoreType.DMA((2,))],
        compiler_params=params(60),
        cost_estimate=cost(4 * rows * depth * width, 4 * depth * width + 2 * rows * depth),
        name="project_prefix",
    )(first_length, resp_prompt, prompt_rows, key_weight, value_weight)


def pack_kernel(n, q_ref, g_ref, k_ref, v_ref, *outs):
    head, _ = place()
    for j in range(n):
        start = 0
        for source in (q_ref, g_ref, k_ref, v_ref):
            width = source.shape[1] // n
            outs[j][:, start : start + width] = source[:, lanes(head ^ j, width)]
            start += width


def pack(queries, out_grad, own_keys, own_values, n):
    rows = queries.shape[0]
    width = (2 * queries.shape[1] + 2 * own_keys.shape[1]) // n
    return pl.pallas_call(
        functools.partial(pack_kernel, n),
        out_shape=[jax.ShapeDtypeStruct((rows, width), BF16)] * n,
        in_specs=[VMEM] * 4,
        out_specs=[VMEM] * n,
        compiler_params=params(16),
        cost_estimate=cost(0, 4 * n * rows * width),
        name="pack_rows",
    )(queries, out_grad, own_keys, own_values)


def unpack_kernel(n, *rest):
    packets, targets = rest[:n], rest[n:]
    head, _ = place()
    for j in range(n):
        start = 0
        for target in targets:
            width = target.shape[1] // n
            target[:, lanes(head ^ j, width)] = packets[j][:, start : start + width]
            start += width


def unpack(packets, q_width, kv_width):
    n = len(packets)
    rows = packets[0].shape[0]
    return pl.pallas_call(
        functools.partial(unpack_kernel, n),
        out_shape=[
            jax.ShapeDtypeStruct((rows, width), BF16) for width in (q_width, kv_width, kv_width)
        ],
        in_specs=[VMEM] * n,
        out_specs=[VMEM] * 3,
        compiler_params=params(16),
        cost_estimate=cost(0, 4 * rows * (q_width + 2 * kv_width)),
        name="unpack_rows",
    )(*packets)


def attend_kernel(slots, n, group, rows, first, last, *rest):
    rest = list(rest)

    def take(count):
        taken = rest[:count]
        del rest[:count]
        return taken

    pieces = len(slots)
    packets = take(n)
    notes = take(n)
    kv_in = take(pieces)
    sums_in = take(0 if first else 2)
    grads_out = take(n)
    prefix_out = take(pieces if last else 0)
    if not last:
        key_acc, value_acc = take(2)
    keys, values = take(2)
    if last:
        key_acc, value_acc = take(2)
    part = kv_in[0].shape[1]
    blocks = kv_in[0].shape[0]
    _, prompt_place = place()

    for index in range(pieces):
        for j in range(blocks):
            prompt, slot = slots[index][j]
            span = slice(slot * part, (slot + 1) * part)
            keys[prompt, span, :] = kv_in[index][j, :, :E]
            values[prompt, span, :] = kv_in[index][j, :, E:]
    key_acc[...] = jnp.zeros_like(key_acc) if first else sums_in[0][...]
    value_acc[...] = jnp.zeros_like(value_acc) if first else sums_in[1][...]

    total_rows = group * rows
    row_in_column = lax.broadcasted_iota(jnp.int32, (total_rows, E), 0) & (rows - 1)
    row_in_lane = lax.broadcasted_iota(jnp.int32, (rows, total_rows), 1) & (rows - 1)
    own_key = lax.broadcasted_iota(jnp.int32, (rows, total_rows), 0)
    lane_row = lax.broadcasted_iota(jnp.int32, (E, total_rows), 1) & (rows - 1)

    def products(packet, note):
        note = note[part:, :].astype(F32)
        half = NOTE_ROWS // 2
        boundary, first_at, second_at = (
            jnp.max(block).astype(jnp.int32)
            for block in (note[:half, :E], note[:half, E:], note[half:, E:])
        )
        first_at, second_at = first_at ^ prompt_place, second_at ^ prompt_place
        heads = [packet[:, h * E : (h + 1) * E] for h in range(2 * group + 2)]
        query = jnp.concatenate(heads[:group], axis=0)
        grad = jnp.concatenate(heads[group : 2 * group], axis=0)
        own_k, own_v = heads[2 * group], heads[2 * group + 1]
        in_first = row_in_column < boundary

        def split(x):
            x = x.astype(F32)
            return jnp.concatenate(
                [jnp.where(in_first, x, 0.0), jnp.where(in_first, 0.0, x)], axis=1
            ).astype(BF16)

        query_pair = split(query)
        grad_pair = split(grad)
        key_pair = jnp.concatenate([keys[first_at], keys[second_at]], axis=1)
        value_pair = jnp.concatenate([values[first_at], values[second_at]], axis=1)

        visible = (own_key <= row_in_lane) & ((own_key >= boundary) == (row_in_lane >= boundary))
        return dict(
            boundary=boundary,
            first_at=first_at,
            second_at=second_at,
            query=query,
            grad=grad,
            own_k=own_k,
            query_pair=query_pair,
            grad_pair=grad_pair,
            key_pair=key_pair,
            scores=dot(key_pair, query_pair, 1, 1),
            own_scores=jnp.where(visible, dot(own_k, query, 1, 1), HIDDEN),
            dprobs=dot(value_pair, grad_pair, 1, 1),
            own_dprobs=dot(own_v, grad, 1, 1),
        )

    def soften(scores, own_scores, dprobs, own_dprobs, **_):
        top = jnp.maximum(
            jnp.max(scores, axis=0, keepdims=True), jnp.max(own_scores, axis=0, keepdims=True)
        )
        weight = jnp.exp2((scores - top) * EXP2_SCALE)
        own_weight = jnp.exp2((own_scores - top) * EXP2_SCALE)
        inverse = 1.0 / (
            jnp.sum(weight, axis=0, keepdims=True) + jnp.sum(own_weight, axis=0, keepdims=True)
        )
        probs = weight * inverse
        own_probs = own_weight * inverse
        probs_low = probs.astype(BF16)
        own_probs_low = own_probs.astype(BF16)
        delta = jnp.sum(probs_low.astype(F32) * dprobs, axis=0, keepdims=True) + jnp.sum(
            own_probs_low.astype(F32) * own_dprobs, axis=0, keepdims=True
        )
        return dict(
            probs_low=probs_low,
            own_probs_low=own_probs_low,
            dscores=(probs * (dprobs - delta)).astype(BF16),
            own_dscores=(own_probs * (own_dprobs - delta)).astype(BF16),
        )

    def gradients(
        grads, boundary, first_at, second_at, query, grad, own_k, query_pair, grad_pair, key_pair,
        probs_low, own_probs_low, dscores, own_dscores, **_
    ):
        key_part = dot(dscores, query_pair, 1, 0)
        value_part = dot(probs_low, grad_pair, 1, 0)
        key_acc[first_at] += key_part[:, :E]
        key_acc[second_at] += key_part[:, E:]
        value_acc[first_at] += value_part[:, :E]
        value_acc[second_at] += value_part[:, E:]

        query_both = dot(key_pair, dscores, 0, 0)
        query_part = jnp.where(lane_row < boundary, query_both[:E], query_both[E:])
        query_part = (query_part + dot(own_k, own_dscores, 0, 0)) * SCALE
        for h in range(group):
            grads[:, h * E : (h + 1) * E] = query_part[:, h * rows : (h + 1) * rows].T.astype(BF16)
        grads[:, group * E : (group + 1) * E] = (dot(own_dscores, query, 1, 0) * SCALE).astype(BF16)
        grads[:, (group + 1) * E :] = dot(own_probs_low, grad, 1, 0).astype(BF16)

    ahead = products(packets[0], notes[0])
    for j in range(n):
        now = ahead
        if j + 1 < n:
            ahead = products(packets[j + 1], notes[j + 1])
        gradients(grads_out[j], **now, **soften(**now))

    for index in range(pieces if last else 0):
        for j in range(blocks):
            prompt, slot = slots[index][j]
            span = slice(slot * part, (slot + 1) * part)
            target = prefix_out[index]
            target[j, :, :E] = (key_acc[prompt, span, :] * SCALE).astype(target.dtype)
            target[j, :, E:] = value_acc[prompt, span, :].astype(target.dtype)


def attend(packets, notes, kv_in, sums, slots, out_types, prompts):
    n = len(packets)
    rows, packet_width = packets[0].shape
    group = (packet_width // E - 2) // 2
    first, last = not sums, bool(out_types)
    sums_shape = (prompts, PLEN, E)
    out_shape = [jax.ShapeDtypeStruct((rows, (group + 2) * E), BF16)] * n
    scratch_shapes = [pltpu.VMEM(sums_shape, BF16)] * 2
    if last:
        out_shape += [jax.ShapeDtypeStruct(kv_in[0].shape, kind) for kind in out_types]
        scratch_shapes += [pltpu.VMEM(sums_shape, F32)] * 2
    else:
        out_shape += [jax.ShapeDtypeStruct(sums_shape, F32)] * 2
    operands = [*packets, *notes, *kv_in, *sums]
    outs = pl.pallas_call(
        functools.partial(attend_kernel, slots, n, group, rows, first, last),
        out_shape=out_shape,
        in_specs=[VMEM] * len(operands),
        out_specs=[VMEM] * len(out_shape),
        scratch_shapes=scratch_shapes,
        compiler_params=params(32),
        cost_estimate=cost(20 * n * group * rows * (PLEN + rows) * E, 1024),
        name="attend_head",
    )(*operands)
    return outs[:n], outs[n:]


def total_kernel(n, keep_ref, *rest):
    parts, outs = rest[:-n], rest[-n:]
    for j in range(n):
        result = keep_ref[j]
        for part in parts:
            result = result + part[j].astype(F32)
        outs[j][...] = result.astype(BF16)


def total(keep, parts):
    n = keep.shape[0]
    return pl.pallas_call(
        functools.partial(total_kernel, n),
        out_shape=[jax.ShapeDtypeStruct(keep.shape[1:], BF16)] * n,
        in_specs=[VMEM] * (1 + len(parts)),
        out_specs=[VMEM] * n,
        compiler_params=params(),
        cost_estimate=cost(len(parts) * keep.size, (6 + 2 * len(parts)) * keep.size),
        name="total_prefix_grads",
    )(keep, *parts)


def prompt_kernel(n, *rest):
    shares, (kw_ref, vw_ref, out_ref, key_grad, value_grad) = rest[:n], rest[n:]

    @pl.when(pl.program_id(0) == 0)
    def _():
        head, _ = place()
        for j in range(n):
            key_grad[:, lanes(head ^ j, E)] = shares[j][:, :E]
            value_grad[:, lanes(head ^ j, E)] = shares[j][:, E:]

    out_ref[...] = (
        dot(key_grad[...], kw_ref[...], 1, 1) + dot(value_grad[...], vw_ref[...], 1, 1)
    ).astype(BF16)


def prompt_gradient(shares, key_weight, value_weight, chunk=1024):
    n = len(shares)
    rows = shares[0].shape[0]
    depth, width = key_weight.shape
    weight_spec = pl.BlockSpec((chunk, width), lambda i: (i, 0))
    return pl.pallas_call(
        functools.partial(prompt_kernel, n),
        grid=(depth // chunk,),
        out_shape=jax.ShapeDtypeStruct((rows, depth), BF16),
        in_specs=[pl.BlockSpec(shares[0].shape, lambda i: (0, 0))] * n
        + [weight_spec, weight_spec],
        out_specs=pl.BlockSpec((rows, chunk), lambda i: (0, i)),
        scratch_shapes=[pltpu.VMEM((rows, width), BF16)] * 2,
        compiler_params=params(),
        cost_estimate=cost(4 * rows * depth * width, 4 * depth * width + 2 * rows * depth),
        name="prompt_gradient",
    )(*shares, key_weight, value_weight)


def spread(number, bits):
    return sum(((number >> i) & 1) << bit for i, bit in enumerate(bits))


def per_device(
    n_prompt,
    n_resp,
    prompt_rows,
    key_weight,
    value_weight,
    queries,
    own_keys,
    own_values,
    out_grad,
    first_length,
    resp_prompt,
):
    devices = n_prompt * n_resp
    heads = own_keys.shape[1] // E
    every_bit = range(devices.bit_length() - 1)
    rest_bits = [bit for bit in GATHER_BITS if bit in every_bit]
    rest_bits += [bit for bit in every_bit if bit not in rest_bits and bit not in HEAD_BITS]
    member = [spread(j, HEAD_BITS) for j in range(heads)]

    def swap(x, offset):
        return lax.ppermute(x, ("prompt", "resp"), [(i, i ^ offset) for i in range(devices)])

    def swap_group(items):
        return [items[0]] + [swap(items[j], member[j]) for j in range(1, heads)]

    part = prompt_rows.shape[0]
    projected = project(
        first_length.reshape(1, 1), resp_prompt, prompt_rows, key_weight, value_weight, heads
    )
    projected, queries = lax.optimization_barrier((projected, queries))
    packed = pack(queries, out_grad, own_keys, own_values, heads)
    notes = swap_group(projected)
    notes, packed = lax.optimization_barrier((notes, packed))
    pieces = {0: jnp.stack([x[:part] for x in notes])}
    packets = swap_group(packed)
    for bit in rest_bits:
        for offset in list(pieces):
            pieces[offset | 1 << bit] = swap(pieces[offset], 1 << bit)
    offsets = list(pieces)

    filled = [0] * n_prompt
    slots = []
    for offset in offsets:
        places = []
        for j in range(heads):
            at = (offset ^ member[j]) // n_resp
            places.append((at, filled[at]))
            filled[at] += 1
        slots.append(tuple(places))

    first_out = 1 << rest_bits[-1]
    out_types = [BF16 if offset & first_out else F32 for offset in offsets]
    kv_in = [pieces[offset] for offset in offsets]
    slots = tuple(slots)
    early = heads - 1
    grads, sums = attend(packets[:early], notes[:early], kv_in, [], slots, [], n_prompt)
    last_grads, outs = attend(
        packets[early:], notes[early:], kv_in, sums, slots, out_types, n_prompt
    )
    sums = dict(zip(offsets, outs))
    arrived = {offset: [] for offset in offsets}
    for bit in reversed(rest_bits):
        sent = None
        for offset in reversed(offsets):
            if offset & 1 << bit:
                piece = sums.pop(offset)
                for part in arrived.pop(offset):
                    piece = piece + part.astype(F32)
                if bit == rest_bits[0]:
                    arrived[0][-1], last_grads = lax.optimization_barrier(
                        (arrived[0][-1], last_grads)
                    )
                if bit != rest_bits[-1] and offset == 1 << bit and sent is not None:
                    piece, ahead = lax.optimization_barrier((piece, arrived[sent][-1]))
                    arrived[sent][-1] = ahead
                arrived[offset ^ 1 << bit].append(swap(piece.astype(BF16), 1 << bit))
                sent = offset ^ 1 << bit
        offsets = list(sums)
    back = [swap(grads[j], member[j]) for j in range(1, early)]
    shares, back = lax.optimization_barrier((total(sums[0], arrived[0]), back))
    shares = swap_group(shares)
    back = [grads[0], *back, swap(last_grads[0], member[early])]
    query_grad, key_grad, value_grad = unpack(back, queries.shape[1], own_keys.shape[1])
    prompt_grad = prompt_gradient(shares, key_weight, value_weight)
    return (query_grad, key_grad, value_grad, prompt_grad)


def solution(mesh):
    both = P(("prompt", "resp"), None)
    return jax.shard_map(
        functools.partial(per_device, mesh.shape["prompt"], mesh.shape["resp"]),
        mesh=mesh,
        in_specs=(both, P(), P(), both, both, both, both, P(("prompt", "resp")), both),
        out_specs=(both, both, both, both),
        check_vma=False,
    )
```

time: 90.9 us -> 80 us (0.88)
  waiting for transfers between devices: 37.4 us -> 31.8 us
  Pallas kernels: 22.6 us -> 20.4 us
  starting transfers between devices: 26.1 us -> 24.3 us
  other arithmetic: 1.49 us -> 0.14 us
    ppermute x26, waiting for transfers between devices: 37.4 us -> 31.8 us  [swap(): lax.ppermute(x, ('prompt', 'resp'), [(i, i ^ offset) for i in range(devic...]
    ppermute x26, starting transfers between devices: 26.1 us -> 24.3 us  [swap(): lax.ppermute(x, ('prompt', 'resp'), [(i, i ^ offset) for i in range(devic...]
    another operation x2 -> x1, other arithmetic: 1.38 us -> 0.02 us  [per_device(): pieces = {0: jnp.stack([x[:part] for x in notes])}]
    pallas_call x2 -> x4, Pallas kernels: 15.9 us -> 14.8 us  [the longest x2 8.33 us: attend(): pl.pallas_call(functools.partial(attend_kernel, slots, n, group, rows, fi...]
  transfers between devices with their start and end apart: 26 -> 26, of which waited for: 10 -> 15; matrix products, arithmetic and copies ran while one was open for 1% -> 0% of each run, Pallas kernels for 2% -> 13%
where the time goes in v4:
time: 80 us; the launch traced here: 79.7 us
  waiting for transfers between devices  31.8 us (40%)
  starting transfers between devices  24.3 us (30%)
  Pallas kernels  20.4 us (25%)
  local copies, waits for them, and re-layouts  1.58 us (2%)
  between operations  1.48 us (2%)
    ppermute x26, waiting for transfers between devices, swap(): lax.ppermute(x, ('prompt', 'resp'), [(i, i ^ offset) for i in range(devic...  31.8 us
    ppermute x26, starting transfers between devices, swap(): lax.ppermute(x, ('prompt', 'resp'), [(i, i ^ offset) for i in range(devic...  24.3 us
    pallas_call x2, Pallas kernels, attend(): pl.pallas_call(functools.partial(attend_kernel, slots, n, group, rows, fi...  8.33 us
    pallas_call x1, Pallas kernels, project(): pl.pallas_call(functools.partial(project_kernel, n, steps), out_shape=[ja...  6.34 us
    pallas_call x1, Pallas kernels, prompt_gradient(): pl.pallas_call(functools.partial(prompt_kernel, n), grid=(depth // chunk,...  4.54 us
  transfers between devices with their start and end apart: 26, of which 15 were waited for; matrix products, arithmetic and copies ran while one was open for 0% of the time, Pallas kernels for 13%

profile of v4, /device:TPU:0, one launch (start us, length us, event | category | flops | bytes accessed | tf_op | source)
XLA Modules:
  0.0 79.7 jit_solution(1016551991072566316)
XLA Ops:
  1.3 6.3 %project_prefix.1 = (bf16[80,256]{1,0:T(8,128)(2,1)}, bf16[80,256]{1,0:T(8,128)(2,1)}, bf16[80,256]{1,0:T(8,128)(2,1)}, bf16[80,256]{1,0:T(8,128)(2,1)}) custom-call(s32[1,1]{1,0:T(1,128)} %bitcast.9.length_ref, s32[1,2]{1,0:T(1,128)} %prompts_ref.1, bf16[64,5120]{1,0:T(8,128)(2,1)} %x_ref.1, bf16[5120,512]{1,0:T(8,128)(2,1)} %rest_4_.1, ...), custom_call_target="tpu_custom_call" | custom-call | flops 671088640 | bytes 11141120 | tf_op jit(solution)/shard_map/project_prefix/pallas_call | solution.py:98
  7.7 3.0 %collective-permute-start = (bf16[80,256]{1,0:T(8,128)(2,1)}, bf16[80,256]{1,0:T(8,128)(2,1)S(1)}, u32[]{:S(2)}, u32[]{:S(2)}) collective-permute-start(bf16[80,256]{1,0:T(8,128)(2,1)} %get-tuple-element.61), channel_id=1, source_target_pairs={{0,8},{1,9},{2,10},{3,11},{4,12},{5,13},{6,14},{7,15},{8,0},{9,1},... | collective-permute-start | bytes 122888 | tf_op jit(solution)/shard_map/ppermute | solution.py:411
  10.7 1.5 %collective-permute-start.1 = (bf16[80,256]{1,0:T(8,128)(2,1)}, bf16[80,256]{1,0:T(8,128)(2,1)S(1)}, u32[]{:S(2)}, u32[]{:S(2)}) collective-permute-start(bf16[80,256]{1,0:T(8,128)(2,1)} %get-tuple-element.62), channel_id=1, source_target_pairs={{0,16},{1,17},{2,18},{3,19},{4,20},{5,21},{6,22},{7,23},{8,24},{9,... | collective-permute-start | bytes 122888 | tf_op jit(solution)/shard_map/ppermute | solution.py:411
  12.9 2.0 %collective-permute-done.1.rest_5_ = bf16[80,256]{1,0:T(8,128)(2,1)S(1)} collective-permute-done((bf16[80,256]{1,0:T(8,128)(2,1)}, bf16[80,256]{1,0:T(8,128)(2,1)S(1)}, u32[]{:S(2)}, u32[]{:S(2)}) %collective-permute-start.1) | collective-permute-done | bytes 40992 | tf_op jit(solution)/shard_map/ppermute | solution.py:411
  14.9 2.4 %collective-permute-done.2.rest_1_ = bf16[80,256]{1,0:T(8,128)(2,1)S(1)} collective-permute-done((bf16[80,256]{1,0:T(8,128)(2,1)}, bf16[80,256]{1,0:T(8,128)(2,1)S(1)}, u32[]{:S(2)}, u32[]{:S(2)}) %collective-permute-start.2) | collective-permute-done | bytes 40992 | tf_op jit(solution)/shard_map/ppermute | solution.py:411
  18.1 2.7 %collective-permute-start.5 = (bf16[4,64,256]{2,1,0:T(8,128)(2,1)S(1)}, bf16[4,64,256]{2,1,0:T(8,128)(2,1)S(1)}, u32[]{:S(2)}, u32[]{:S(2)}) collective-permute-start(bf16[4,64,256]{2,1,0:T(8,128)(2,1)S(1)} %pad_maximum_fusion.rest_6_.rest_2_), channel_id=1, source_target_pairs={{0,4},{1,5},{2,6},{3,7},{4,0},{5,1},{6,2},{7,3},{8,12},{9,13},{10,... | collective-permute-start | bytes 393224 | tf_op jit(solution)/shard_map/ppermute | solution.py:411
  21.8 1.6 %collective-permute-start.6 = (bf16[4,64,256]{2,1,0:T(8,128)(2,1)S(1)}, bf16[4,64,256]{2,1,0:T(8,128)(2,1)S(1)}, u32[]{:S(2)}, u32[]{:S(2)}) collective-permute-start(bf16[4,64,256]{2,1,0:T(8,128)(2,1)S(1)} %pad_maximum_fusion.rest_6_.rest_2_), channel_id=1, source_target_pairs={{0,2},{1,3},{2,0},{3,1},{4,6},{5,7},{6,4},{7,5},{8,10},{9,11},{10,... | collective-permute-start | bytes 393224 | tf_op jit(solution)/shard_map/ppermute | solution.py:411
  23.4 2.1 %collective-permute-done.5.rest_7_.rest_3_ = bf16[4,64,256]{2,1,0:T(8,128)(2,1)S(1)} collective-permute-done((bf16[4,64,256]{2,1,0:T(8,128)(2,1)S(1)}, bf16[4,64,256]{2,1,0:T(8,128)(2,1)S(1)}, u32[]{:S(2)}, u32[]{:S(2)}) %collective-permute-start.5) | collective-permute-done | bytes 131104 | tf_op jit(solution)/shard_map/ppermute | solution.py:411
  27.8 2.6 %collective-permute-done.7.rest_9_.rest_5_ = bf16[4,64,256]{2,1,0:T(8,128)(2,1)S(1)} collective-permute-done((bf16[4,64,256]{2,1,0:T(8,128)(2,1)S(1)}, bf16[4,64,256]{2,1,0:T(8,128)(2,1)S(1)}, u32[]{:S(2)}, u32[]{:S(2)}) %collective-permute-start.7) | collective-permute-done | bytes 131104 | tf_op jit(solution)/shard_map/ppermute | solution.py:411
  30.5 1.6 %collective-permute-start.12 = (bf16[128,1536]{1,0:T(8,128)(2,1)S(1)}, bf16[128,1536]{1,0:T(8,128)(2,1)S(1)}, u32[]{:S(2)}, u32[]{:S(2)}) collective-permute-start(bf16[128,1536]{1,0:T(8,128)(2,1)S(1)} %get-tuple-element.77), channel_id=1, source_target_pairs={{0,24},{1,25},{2,26},{3,27},{4,28},{5,29},{6,30},{7,31},{8,16},{9,... | collective-permute-start | bytes 1179656 | tf_op jit(solution)/shard_map/ppermute | solution.py:411
  32.9 5.9 %attend_head.2 = (bf16[128,896]{1,0:T(8,128)(2,1)S(1)}, bf16[128,896]{1,0:T(8,128)(2,1)S(1)}, bf16[128,896]{1,0:T(8,128)(2,1)S(1)}, f32[4,512,128]{2,1,0:T(8,128)S(1)}, f32[4,512,128]{2,1,0:T(8,128)S(1)}) custom-call(bf16[128,1536]{1,0:T(8,128)(2,1)S(1)} %get-tuple-element.69.rest_0_, bf16[128,1536]{1,0:T(8,128)(2,1)S(1)} %collective-permute-done.3.rest_1_, ...), custom_call_target="tpu_custom_call" | custom-call | flops 3145728000 | bytes 1024 | tf_op jit(solution)/shard_map/attend_head/pallas_call | solution.py:317
  38.8 4.1 %collective-permute-done.12.rest_0_ = bf16[128,1536]{1,0:T(8,128)(2,1)S(1)} collective-permute-done((bf16[128,1536]{1,0:T(8,128)(2,1)S(1)}, bf16[128,1536]{1,0:T(8,128)(2,1)S(1)}, u32[]{:S(2)}, u32[]{:S(2)}) %collective-permute-start.12) | collective-permute-done | bytes 393248 | tf_op jit(solution)/shard_map/ppermute | solution.py:411
  42.9 2.4 %attend_head.3 = (bf16[128,896]{1,0:T(8,128)(2,1)S(1)}, f32[4,64,256]{2,1,0:T(8,128)S(1)}, f32[4,64,256]{2,1,0:T(8,128)S(1)}, f32[4,64,256]{2,1,0:T(8,128)S(1)},...) custom-call(bf16[128,1536]{1,0:T(8,128)(2,1)S(1)} %collective-permut, ...), custom_call_target="tpu_custom_call" | custom-call | flops 1048576000 | bytes 1024 | tf_op jit(solution)/shard_map/attend_head/pallas_call | solution.py:317
  47.6 4.8 %collective-permute-done.16 = bf16[4,64,256]{2,1,0:T(8,128)(2,1)S(1)} collective-permute-done((bf16[4,64,256]{2,1,0:T(8,128)(2,1)S(1)}, bf16[4,64,256]{2,1,0:T(8,128)(2,1)S(1)}, u32[]{:S(2)}, u32[]{:S(2)}) %collective-permute-start.16) | collective-permute-done | bytes 131104 | tf_op jit(solution)/shard_map/ppermute | solution.py:411
  53.1 1.5 %collective-permute-start.20 = (bf16[128,896]{1,0:T(8,128)(2,1)S(1)}, bf16[128,896]{1,0:T(8,128)(2,1)S(1)}, u32[]{:S(2)}, u32[]{:S(2)}) collective-permute-start(bf16[128,896]{1,0:T(8,128)(2,1)S(1)} %get-tuple-element.96), channel_id=1, source_target_pairs={{0,8},{1,9},{2,10},{3,11},{4,12},{5,13},{6,14},{7,15},{8,0},{9,1},... | collective-permute-start | bytes 688136 | tf_op jit(solution)/shard_map/ppermute | solution.py:411
  54.6 1.5 %collective-permute-start.21 = (bf16[128,896]{1,0:T(8,128)(2,1)S(1)}, bf16[128,896]{1,0:T(8,128)(2,1)S(1)}, u32[]{:S(2)}, u32[]{:S(2)}) collective-permute-start(bf16[128,896]{1,0:T(8,128)(2,1)S(1)} %get-tuple-element.97), channel_id=1, source_target_pairs={{0,16},{1,17},{2,18},{3,19},{4,20},{5,21},{6,22},{7,23},{8,24},{9,... | collective-permute-start | bytes 688136 | tf_op jit(solution)/shard_map/ppermute | solution.py:411
  56.1 1.2 %collective-permute-done.17.rest_1_ = bf16[4,64,256]{2,1,0:T(8,128)(2,1)S(1)} collective-permute-done((bf16[4,64,256]{2,1,0:T(8,128)(2,1)S(1)}, bf16[4,64,256]{2,1,0:T(8,128)(2,1)S(1)}, u32[]{:S(2)}, u32[]{:S(2)}) %collective-permute-start.17) | collective-permute-done | bytes 131104 | tf_op jit(solution)/shard_map/ppermute | solution.py:411
  57.3 1.6 %collective-permute-start.22 = (bf16[128,896]{1,0:T(8,128)(2,1)S(1)}, bf16[128,896]{1,0:T(8,128)(2,1)S(1)}, u32[]{:S(2)}, u32[]{:S(2)}) collective-permute-start(bf16[128,896]{1,0:T(8,128)(2,1)S(1)} %get-tuple-element.100), channel_id=1, source_target_pairs={{0,24},{1,25},{2,26},{3,27},{4,28},{5,29},{6,30},{7,31},{8,16},{9,... | collective-permute-start | bytes 688136 | tf_op jit(solution)/shard_map/ppermute | solution.py:411
  59.0 1.5 %collective-permute-start.19 = (bf16[4,64,256]{2,1,0:T(8,128)(2,1)S(1)}, bf16[4,64,256]{2,1,0:T(8,128)(2,1)S(1)}, u32[]{:S(2)}, u32[]{:S(2)}) collective-permute-start(bf16[4,64,256]{2,1,0:T(8,128)(2,1)S(1)} %add_convert_fusion), channel_id=1, source_target_pairs={{0,4},{1,5},{2,6},{3,7},{4,0},{5,1},{6,2},{7,3},{8,12},{9,13},{10,... | collective-permute-start | bytes 393224 | tf_op jit(solution)/shard_map/ppermute | solution.py:411
  60.5 6.4 %collective-permute-done.19.rest_2_ = bf16[4,64,256]{2,1,0:T(8,128)(2,1)S(1)} collective-permute-done((bf16[4,64,256]{2,1,0:T(8,128)(2,1)S(1)}, bf16[4,64,256]{2,1,0:T(8,128)(2,1)S(1)}, u32[]{:S(2)}, u32[]{:S(2)}) %collective-permute-start.19) | collective-permute-done | bytes 131104 | tf_op jit(solution)/shard_map/ppermute | solution.py:411
  67.7 1.6 %collective-permute-start.24 = (bf16[64,256]{1,0:T(8,128)(2,1)S(1)}, bf16[64,256]{1,0:T(8,128)(2,1)S(1)}, u32[]{:S(2)}, u32[]{:S(2)}) collective-permute-start(bf16[64,256]{1,0:T(8,128)(2,1)S(1)} %get-tuple-element.106), channel_id=1, source_target_pairs={{0,16},{1,17},{2,18},{3,19},{4,20},{5,21},{6,22},{7,23},{8,24},{9,... | collective-permute-start | bytes 98312 | tf_op jit(solution)/shard_map/ppermute | solution.py:411
  69.3 1.4 %collective-permute-start.25 = (bf16[64,256]{1,0:T(8,128)(2,1)S(1)}, bf16[64,256]{1,0:T(8,128)(2,1)S(1)}, u32[]{:S(2)}, u32[]{:S(2)}) collective-permute-start(bf16[64,256]{1,0:T(8,128)(2,1)S(1)} %get-tuple-element.107), channel_id=1, source_target_pairs={{0,24},{1,25},{2,26},{3,27},{4,28},{5,29},{6,30},{7,31},{8,16},{9,... | collective-permute-start | bytes 98312 | tf_op jit(solution)/shard_map/ppermute | solution.py:411
  72.0 2.1 %collective-permute-done.25.rest_3_ = bf16[64,256]{1,0:T(8,128)(2,1)S(1)} collective-permute-done((bf16[64,256]{1,0:T(8,128)(2,1)S(1)}, bf16[64,256]{1,0:T(8,128)(2,1)S(1)}, u32[]{:S(2)}, u32[]{:S(2)}) %collective-permute-start.25) | collective-permute-done | bytes 32800 | tf_op jit(solution)/shard_map/ppermute | solution.py:411
  74.1 4.5 %prompt_gradient.1 = bf16[64,5120]{1,0:T(8,128)(2,1)} custom-call(bf16[64,256]{1,0:T(8,128)(2,1)S(1)} %get-tuple-element.104.rest_0_, bf16[64,256]{1,0:T(8,128)(2,1)S(1)} %collective-permute-done.23.rest_1_, bf16[64,256]{1,0:T(8,128)(2,1)S(1)} %collective-permute-done.24.rest_2_, bf16[64,256]{1,0:T(8,128)(2,1)S(1)} %collective-permute-done.25.rest_3_, ...), custom_call_target="tpu_custom_call" | custom-call | flops 671088640 | bytes 11141120 | tf_op jit(solution)/shard_map/prompt_gradient/pallas_call | solution.py:372
  (61 shorter events, 11.7 us)
Async XLA Ops:
  7.7 5.2 %collective-permute-start = (bf16[80,256]{1,0:T(8,128)(2,1)}, bf16[80,256]{1,0:T(8,128)(2,1)S(1)}, u32[]{:S(2)}, u32[]{:S(2)}) collective-permute-start(bf16[80,256]{1,0:T(8,128)(2,1)} %get-tuple-element.61), channel_id=1, source_target_pairs={{0,8},{1,9},{2,10},{3,11},{4,12},{5,13},{6,14},{7,15},{8,0},{9,1},... | collective-permute-start | bytes 122888 | tf_op jit(solution)/shard_map/ppermute | solution.py:411
  10.7 4.2 %collective-permute-start.1 = (bf16[80,256]{1,0:T(8,128)(2,1)}, bf16[80,256]{1,0:T(8,128)(2,1)S(1)}, u32[]{:S(2)}, u32[]{:S(2)}) collective-permute-start(bf16[80,256]{1,0:T(8,128)(2,1)} %get-tuple-element.62), channel_id=1, source_target_pairs={{0,16},{1,17},{2,18},{3,19},{4,20},{5,21},{6,22},{7,23},{8,24},{9,... | collective-permute-start | bytes 122888 | tf_op jit(solution)/shard_map/ppermute | solution.py:411
  12.2 5.1 %collective-permute-start.2 = (bf16[80,256]{1,0:T(8,128)(2,1)}, bf16[80,256]{1,0:T(8,128)(2,1)S(1)}, u32[]{:S(2)}, u32[]{:S(2)}) collective-permute-start(bf16[80,256]{1,0:T(8,128)(2,1)} %get-tuple-element.63), channel_id=1, source_target_pairs={{0,24},{1,25},{2,26},{3,27},{4,28},{5,29},{6,30},{7,31},{8,16},{9,... | collective-permute-start | bytes 122888 | tf_op jit(solution)/shard_map/ppermute | solution.py:411
  18.1 7.4 %collective-permute-start.5 = (bf16[4,64,256]{2,1,0:T(8,128)(2,1)S(1)}, bf16[4,64,256]{2,1,0:T(8,128)(2,1)S(1)}, u32[]{:S(2)}, u32[]{:S(2)}) collective-permute-start(bf16[4,64,256]{2,1,0:T(8,128)(2,1)S(1)} %pad_maximum_fusion.rest_6_.rest_2_), channel_id=1, source_target_pairs={{0,4},{1,5},{2,6},{3,7},{4,0},{5,1},{6,2},{7,3},{8,12},{9,13},{10,... | collective-permute-start | bytes 393224 | tf_op jit(solution)/shard_map/ppermute | solution.py:411
  20.8 11.3 %collective-permute-start.3 = (bf16[128,1536]{1,0:T(8,128)(2,1)S(1)}, bf16[128,1536]{1,0:T(8,128)(2,1)S(1)}, u32[]{:S(2)}, u32[]{:S(2)}) collective-permute-start(bf16[128,1536]{1,0:T(8,128)(2,1)S(1)} %get-tuple-element.70), channel_id=1, source_target_pairs={{0,8},{1,9},{2,10},{3,11},{4,12},{5,13},{6,14},{7,15},{8,0},{9,1},... | collective-permute-start | bytes 1179656 | tf_op jit(solution)/shard_map/ppermute | solution.py:411
  21.3 10.8 %collective-permute-start.4 = (bf16[128,1536]{1,0:T(8,128)(2,1)S(1)}, bf16[128,1536]{1,0:T(8,128)(2,1)S(1)}, u32[]{:S(2)}, u32[]{:S(2)}) collective-permute-start(bf16[128,1536]{1,0:T(8,128)(2,1)S(1)} %get-tuple-element.71), channel_id=1, source_target_pairs={{0,16},{1,17},{2,18},{3,19},{4,20},{5,21},{6,22},{7,23},{8,24},{9,... | collective-permute-start | bytes 1179656 | tf_op jit(solution)/shard_map/ppermute | solution.py:411
  21.8 5.5 %collective-permute-start.6 = (bf16[4,64,256]{2,1,0:T(8,128)(2,1)S(1)}, bf16[4,64,256]{2,1,0:T(8,128)(2,1)S(1)}, u32[]{:S(2)}, u32[]{:S(2)}) collective-permute-start(bf16[4,64,256]{2,1,0:T(8,128)(2,1)S(1)} %pad_maximum_fusion.rest_6_.rest_2_), channel_id=1, source_target_pairs={{0,2},{1,3},{2,0},{3,1},{4,6},{5,7},{6,4},{7,5},{8,10},{9,11},{10,... | collective-permute-start | bytes 393224 | tf_op jit(solution)/shard_map/ppermute | solution.py:411
  23.4 3.9 %collective-permute-start.8 = (bf16[4,64,256]{2,1,0:T(8,128)(2,1)S(1)}, bf16[4,64,256]{2,1,0:T(8,128)(2,1)S(1)}, u32[]{:S(2)}, u32[]{:S(2)}) collective-permute-start(bf16[4,64,256]{2,1,0:T(8,128)(2,1)S(1)} %pad_maximum_fusion.rest_6_.rest_2_), channel_id=1, source_target_pairs={{0,1},{1,0},{2,3},{3,2},{4,5},{5,4},{6,7},{7,6},{8,9},{9,8},{10,11... | collective-permute-start | bytes 393224 | tf_op jit(solution)/shard_map/ppermute | solution.py:411
  25.5 5.0 %collective-permute-start.7 = (bf16[4,64,256]{2,1,0:T(8,128)(2,1)S(1)}, bf16[4,64,256]{2,1,0:T(8,128)(2,1)S(1)}, u32[]{:S(2)}, u32[]{:S(2)}) collective-permute-start(bf16[4,64,256]{2,1,0:T(8,128)(2,1)S(1)} %collective-permute-done.5.rest_7_.rest_3_), channel_id=1, source_target_pairs={{0,2},{1,3},{2,0},{3,1},{4,6},{5,7},{6,4},{7,5},{8,10},{9,11},{10,... | collective-permute-start | bytes 393224 | tf_op jit(solution)/shard_map/ppermute | solution.py:411
  27.3 3.2 %collective-permute-start.10 = (bf16[4,64,256]{2,1,0:T(8,128)(2,1)S(1)}, bf16[4,64,256]{2,1,0:T(8,128)(2,1)S(1)}, u32[]{:S(2)}, u32[]{:S(2)}) collective-permute-start(bf16[4,64,256]{2,1,0:T(8,128)(2,1)S(1)} %collective-permute-done.6.rest_8_.rest_4_), channel_id=1, source_target_pairs={{0,1},{1,0},{2,3},{3,2},{4,5},{5,4},{6,7},{7,6},{8,9},{9,8},{10,11... | collective-permute-start | bytes 393224 | tf_op jit(solution)/shard_map/ppermute | solution.py:411
  27.3 4.8 %collective-permute-start.9 = (bf16[4,64,256]{2,1,0:T(8,128)(2,1)S(1)}, bf16[4,64,256]{2,1,0:T(8,128)(2,1)S(1)}, u32[]{:S(2)}, u32[]{:S(2)}) collective-permute-start(bf16[4,64,256]{2,1,0:T(8,128)(2,1)S(1)} %collective-permute-done.5.rest_7_.rest_3_), channel_id=1, source_target_pairs={{0,1},{1,0},{2,3},{3,2},{4,5},{5,4},{6,7},{7,6},{8,9},{9,8},{10,11... | collective-permute-start | bytes 393224 | tf_op jit(solution)/shard_map/ppermute | solution.py:411
  30.5 12.4 %collective-permute-start.12 = (bf16[128,1536]{1,0:T(8,128)(2,1)S(1)}, bf16[128,1536]{1,0:T(8,128)(2,1)S(1)}, u32[]{:S(2)}, u32[]{:S(2)}) collective-permute-start(bf16[128,1536]{1,0:T(8,128)(2,1)S(1)} %get-tuple-element.77), channel_id=1, source_target_pairs={{0,24},{1,25},{2,26},{3,27},{4,28},{5,29},{6,30},{7,31},{8,16},{9,... | collective-permute-start | bytes 1179656 | tf_op jit(solution)/shard_map/ppermute | solution.py:411
  45.4 2.2 %collective-permute-start.14 = (bf16[4,64,256]{2,1,0:T(8,128)(2,1)S(1)}, bf16[4,64,256]{2,1,0:T(8,128)(2,1)S(1)}, u32[]{:S(2)}, u32[]{:S(2)}) collective-permute-start(bf16[4,64,256]{2,1,0:T(8,128)(2,1)S(1)} %get-tuple-element.83), channel_id=1, source_target_pairs={{0,1},{1,0},{2,3},{3,2},{4,5},{5,4},{6,7},{7,6},{8,9},{9,8},{10,11... | collective-permute-start | bytes 393224 | tf_op jit(solution)/shard_map/ppermute | solution.py:411
  46.8 5.6 %collective-permute-start.16 = (bf16[4,64,256]{2,1,0:T(8,128)(2,1)S(1)}, bf16[4,64,256]{2,1,0:T(8,128)(2,1)S(1)}, u32[]{:S(2)}, u32[]{:S(2)}) collective-permute-start(bf16[4,64,256]{2,1,0:T(8,128)(2,1)S(1)} %add_convert_fusion.1), channel_id=1, source_target_pairs={{0,2},{1,3},{2,0},{3,1},{4,6},{5,7},{6,4},{7,5},{8,10},{9,11},{10,... | collective-permute-start | bytes 393224 | tf_op jit(solution)/shard_map/ppermute | solution.py:411
  52.4 5.0 %collective-permute-start.17 = (bf16[4,64,256]{2,1,0:T(8,128)(2,1)S(1)}, bf16[4,64,256]{2,1,0:T(8,128)(2,1)S(1)}, u32[]{:S(2)}, u32[]{:S(2)}) collective-permute-start(bf16[4,64,256]{2,1,0:T(8,128)(2,1)S(1)} %convert_add_fusion), channel_id=1, source_target_pairs={{0,2},{1,3},{2,0},{3,1},{4,6},{5,7},{6,4},{7,5},{8,10},{9,11},{10,... | collective-permute-start | bytes 393224 | tf_op jit(solution)/shard_map/ppermute | solution.py:411
  53.1 5.9 %collective-permute-start.18 = (bf16[4,64,256]{2,1,0:T(8,128)(2,1)S(1)}, bf16[4,64,256]{2,1,0:T(8,128)(2,1)S(1)}, u32[]{:S(2)}, u32[]{:S(2)}) collective-permute-start(bf16[4,64,256]{2,1,0:T(8,128)(2,1)S(1)} %get-tuple-element.90), channel_id=1, source_target_pairs={{0,1},{1,0},{2,3},{3,2},{4,5},{5,4},{6,7},{7,6},{8,9},{9,8},{10,11... | collective-permute-start | bytes 393224 | tf_op jit(solution)/shard_map/ppermute | solution.py:411
  53.1 13.9 %collective-permute-start.20 = (bf16[128,896]{1,0:T(8,128)(2,1)S(1)}, bf16[128,896]{1,0:T(8,128)(2,1)S(1)}, u32[]{:S(2)}, u32[]{:S(2)}) collective-permute-start(bf16[128,896]{1,0:T(8,128)(2,1)S(1)} %get-tuple-element.96), channel_id=1, source_target_pairs={{0,8},{1,9},{2,10},{3,11},{4,12},{5,13},{6,14},{7,15},{8,0},{9,1},... | collective-permute-start | bytes 688136 | tf_op jit(solution)/shard_map/ppermute | solution.py:411
  54.6 12.7 %collective-permute-start.21 = (bf16[128,896]{1,0:T(8,128)(2,1)S(1)}, bf16[128,896]{1,0:T(8,128)(2,1)S(1)}, u32[]{:S(2)}, u32[]{:S(2)}) collective-permute-start(bf16[128,896]{1,0:T(8,128)(2,1)S(1)} %get-tuple-element.97), channel_id=1, source_target_pairs={{0,16},{1,17},{2,18},{3,19},{4,20},{5,21},{6,22},{7,23},{8,24},{9,... | collective-permute-start | bytes 688136 | tf_op jit(solution)/shard_map/ppermute | solution.py:411
  56.1 4.4 %collective-permute-start.13 = (bf16[4,64,256]{2,1,0:T(8,128)(2,1)S(1)}, bf16[4,64,256]{2,1,0:T(8,128)(2,1)S(1)}, u32[]{:S(2)}, u32[]{:S(2)}) collective-permute-start(bf16[4,64,256]{2,1,0:T(8,128)(2,1)S(1)} %get-tuple-element.81), channel_id=1, source_target_pairs={{0,1},{1,0},{2,3},{3,2},{4,5},{5,4},{6,7},{7,6},{8,9},{9,8},{10,11... | collective-permute-start | bytes 393224 | tf_op jit(solution)/shard_map/ppermute | solution.py:411
  57.3 21.3 %collective-permute-start.22 = (bf16[128,896]{1,0:T(8,128)(2,1)S(1)}, bf16[128,896]{1,0:T(8,128)(2,1)S(1)}, u32[]{:S(2)}, u32[]{:S(2)}) collective-permute-start(bf16[128,896]{1,0:T(8,128)(2,1)S(1)} %get-tuple-element.100), channel_id=1, source_target_pairs={{0,24},{1,25},{2,26},{3,27},{4,28},{5,29},{6,30},{7,31},{8,16},{9,... | collective-permute-start | bytes 688136 | tf_op jit(solution)/shard_map/ppermute | solution.py:411
  59.0 7.9 %collective-permute-start.19 = (bf16[4,64,256]{2,1,0:T(8,128)(2,1)S(1)}, bf16[4,64,256]{2,1,0:T(8,128)(2,1)S(1)}, u32[]{:S(2)}, u32[]{:S(2)}) collective-permute-start(bf16[4,64,256]{2,1,0:T(8,128)(2,1)S(1)} %add_convert_fusion), channel_id=1, source_target_pairs={{0,4},{1,5},{2,6},{3,7},{4,0},{5,1},{6,2},{7,3},{8,12},{9,13},{10,... | collective-permute-start | bytes 393224 | tf_op jit(solution)/shard_map/ppermute | solution.py:411
  67.2 4.0 %collective-permute-start.23 = (bf16[64,256]{1,0:T(8,128)(2,1)S(1)}, bf16[64,256]{1,0:T(8,128)(2,1)S(1)}, u32[]{:S(2)}, u32[]{:S(2)}) collective-permute-start(bf16[64,256]{1,0:T(8,128)(2,1)S(1)} %get-tuple-element.105), channel_id=1, source_target_pairs={{0,8},{1,9},{2,10},{3,11},{4,12},{5,13},{6,14},{7,15},{8,0},{9,1},... | collective-permute-start | bytes 98312 | tf_op jit(solution)/shard_map/ppermute | solution.py:411
  67.7 4.3 %collective-permute-start.24 = (bf16[64,256]{1,0:T(8,128)(2,1)S(1)}, bf16[64,256]{1,0:T(8,128)(2,1)S(1)}, u32[]{:S(2)}, u32[]{:S(2)}) collective-permute-start(bf16[64,256]{1,0:T(8,128)(2,1)S(1)} %get-tuple-element.106), channel_id=1, source_target_pairs={{0,16},{1,17},{2,18},{3,19},{4,20},{5,21},{6,22},{7,23},{8,24},{9,... | collective-permute-start | bytes 98312 | tf_op jit(solution)/shard_map/ppermute | solution.py:411
  69.3 4.8 %collective-permute-start.25 = (bf16[64,256]{1,0:T(8,128)(2,1)S(1)}, bf16[64,256]{1,0:T(8,128)(2,1)S(1)}, u32[]{:S(2)}, u32[]{:S(2)}) collective-permute-start(bf16[64,256]{1,0:T(8,128)(2,1)S(1)} %get-tuple-element.107), channel_id=1, source_target_pairs={{0,24},{1,25},{2,26},{3,27},{4,28},{5,29},{6,30},{7,31},{8,16},{9,... | collective-permute-start | bytes 98312 | tf_op jit(solution)/shard_map/ppermute | solution.py:411
  (11 other events, 271.6 us)

commit v5 on v4

--- a/solution.py
+++ b/solution.py
@@ -48,7 +48,7 @@
 
 
 def project_kernel(n, steps, length_ref, prompts_ref, x_ref, kw_ref, vw_ref, *rest):
-    outs, (kw, vw, key_sum, value_sum, length, prompts, sems, note_sems) = rest[:n], rest[n:]
+    outs, (x, kw, vw, key_sum, value_sum, length, prompts, sems, note_sems) = rest[:n], rest[n:]
     chunk = kw.shape[0] // steps
     copies = []
     for step in range(steps):
@@ -63,16 +63,18 @@
         pltpu.make_async_copy(length_ref, length, note_sems.at[0]),
         pltpu.make_async_copy(prompts_ref, prompts, note_sems.at[1]),
     ]
-    for copy in copies + note_copies:
+    x_copy = pltpu.make_async_copy(x_ref, x, note_sems.at[2])
+    for copy in [copies[0], x_copy, *copies[1:], *note_copies]:
         copy.start()
+    x_copy.wait()
     keys = values = None
     for step in range(steps):
         span = slice(step * chunk, (step + 1) * chunk)
         copies[2 * step].wait()
-        part = dot(x_ref[:, span], kw[span, :], 1, 0)
+        part = dot(x[:, span], kw[span, :], 1, 0)
         keys = part if step == 0 else keys + part
         copies[2 * step + 1].wait()
-        part = dot(x_ref[:, span], vw[span, :], 1, 0)
+        part = dot(x[:, span], vw[span, :], 1, 0)
         values = part if step == 0 else values + part
     key_sum[...] = keys.astype(BF16)
     value_sum[...] = values.astype(BF16)
@@ -98,12 +100,13 @@
     return pl.pallas_call(
         functools.partial(project_kernel, n, steps),
         out_shape=[jax.ShapeDtypeStruct((rows + NOTE_ROWS, 2 * E), BF16)] * n,
-        in_specs=[ANY, ANY, VMEM, ANY, ANY],
+        in_specs=[ANY] * 5,
         out_specs=[VMEM] * n,
-        scratch_shapes=[pltpu.VMEM(key_weight.shape, BF16)] * 2
+        scratch_shapes=[pltpu.VMEM(prompt_rows.shape, BF16)]
+        + [pltpu.VMEM(key_weight.shape, BF16)] * 2
         + [pltpu.VMEM((rows, width), BF16)] * 2
         + [pltpu.SMEM(first_length.shape, jnp.int32), pltpu.SMEM(resp_prompt.shape, jnp.int32)]
-        + [pltpu.SemaphoreType.DMA((2 * steps,)), pltpu.SemaphoreType.DMA((2,))],
+        + [pltpu.SemaphoreType.DMA((2 * steps,)), pltpu.SemaphoreType.DMA((3,))],
         compiler_params=params(60),
         cost_estimate=cost(4 * rows * depth * width, 4 * depth * width + 2 * rows * depth),
         name="project_prefix",
@@ -300,16 +303,19 @@
             target[j, :, E:] = value_acc[prompt, span, :].astype(target.dtype)
 
 
-def attend(packets, notes, kv_in, sums, slots, out_types, prompts):
+def attend(packets, notes, kv_in, sums, slots, last, prompts):
     n = len(packets)
     rows, packet_width = packets[0].shape
     group = (packet_width // E - 2) // 2
-    first, last = not sums, bool(out_types)
+    first = not sums
     sums_shape = (prompts, PLEN, E)
     out_shape = [jax.ShapeDtypeStruct((rows, (group + 2) * E), BF16)] * n
     scratch_shapes = [pltpu.VMEM(sums_shape, BF16)] * 2
     if last:
-        out_shape += [jax.ShapeDtypeStruct(kv_in[0].shape, kind) for kind in out_types]
+        out_shape += [
+            jax.ShapeDtypeStruct(x.shape, BF16 if index % 2 else F32)
+            for index, x in enumerate(kv_in)
+        ]
         scratch_shapes += [pltpu.VMEM(sums_shape, F32)] * 2
     else:
         out_shape += [jax.ShapeDtypeStruct(sums_shape, F32)] * 2
@@ -321,7 +327,7 @@
         out_specs=[VMEM] * len(out_shape),
         scratch_shapes=scratch_shapes,
         compiler_params=params(32),
-        cost_estimate=cost(20 * n * group * rows * (PLEN + rows) * E, 1024),
+        cost_estimate=cost(0, 1024),
         name="attend_head",
     )(*operands)
     return outs[:n], outs[n:]
@@ -343,41 +349,42 @@
         out_shape=[jax.ShapeDtypeStruct(keep.shape[1:], BF16)] * n,
         in_specs=[VMEM] * (1 + len(parts)),
         out_specs=[VMEM] * n,
-        compiler_params=params(),
-        cost_estimate=cost(len(parts) * keep.size, (6 + 2 * len(parts)) * keep.size),
+        compiler_params=params(16),
+        cost_estimate=cost(0, 1 << 25),
         name="total_prefix_grads",
     )(keep, *parts)
 
 
-def prompt_kernel(n, *rest):
-    shares, (kw_ref, vw_ref, out_ref, key_grad, value_grad) = rest[:n], rest[n:]
-
-    @pl.when(pl.program_id(0) == 0)
-    def _():
-        head, _ = place()
-        for j in range(n):
-            key_grad[:, lanes(head ^ j, E)] = shares[j][:, :E]
-            value_grad[:, lanes(head ^ j, E)] = shares[j][:, E:]
-
-    out_ref[...] = (
-        dot(key_grad[...], kw_ref[...], 1, 1) + dot(value_grad[...], vw_ref[...], 1, 1)
-    ).astype(BF16)
+def prompt_kernel(n, chunk, *rest):
+    shares, (kw_ref, vw_ref, out_ref, key_grad, value_grad, out, sems) = rest[:n], rest[n:]
+    head, _ = place()
+    for j in range(n):
+        key_grad[:, lanes(head ^ j, E)] = shares[j][:, :E]
+        value_grad[:, lanes(head ^ j, E)] = shares[j][:, E:]
+    copies = []
+    for index in range(kw_ref.shape[0] // chunk):
+        span = slice(index * chunk, (index + 1) * chunk)
+        turned = dot(kw_ref[span, :], key_grad[...], 1, 1)
+        turned = turned + dot(vw_ref[span, :], value_grad[...], 1, 1)
+        out[:, span] = turned.T.astype(BF16)
+        copies.append(pltpu.make_async_copy(out.at[:, span], out_ref.at[:, span], sems.at[index]))
+        copies[-1].start()
+    for copy in copies:
+        copy.wait()
 
 
 def prompt_gradient(shares, key_weight, value_weight, chunk=1024):
     n = len(shares)
     rows = shares[0].shape[0]
     depth, width = key_weight.shape
-    weight_spec = pl.BlockSpec((chunk, width), lambda i: (i, 0))
     return pl.pallas_call(
-        functools.partial(prompt_kernel, n),
-        grid=(depth // chunk,),
+        functools.partial(prompt_kernel, n, chunk),
         out_shape=jax.ShapeDtypeStruct((rows, depth), BF16),
-        in_specs=[pl.BlockSpec(shares[0].shape, lambda i: (0, 0))] * n
-        + [weight_spec, weight_spec],
-        out_specs=pl.BlockSpec((rows, chunk), lambda i: (0, i)),
-        scratch_shapes=[pltpu.VMEM((rows, width), BF16)] * 2,
-        compiler_params=params(),
+        in_specs=[VMEM] * (n + 2),
+        out_specs=ANY,
+        scratch_shapes=[pltpu.VMEM((rows, width), BF16)] * 2
+        + [pltpu.VMEM((rows, depth), BF16), pltpu.SemaphoreType.DMA((depth // chunk,))],
+        compiler_params=params(32),
         cost_estimate=cost(4 * rows * depth * width, 4 * depth * width + 2 * rows * depth),
         name="prompt_gradient",
     )(*shares, key_weight, value_weight)
@@ -426,7 +433,8 @@
     for bit in rest_bits:
         for offset in list(pieces):
             pieces[offset | 1 << bit] = swap(pieces[offset], 1 << bit)
-    offsets = list(pieces)
+    core = 1 << rest_bits[-1]
+    offsets = [o ^ c for o in pieces if not o & core for c in (0, core)]
 
     filled = [0] * n_prompt
     slots = []
@@ -438,39 +446,25 @@
             filled[at] += 1
         slots.append(tuple(places))
 
-    first_out = 1 << rest_bits[-1]
-    out_types = [BF16 if offset & first_out else F32 for offset in offsets]
     kv_in = [pieces[offset] for offset in offsets]
     slots = tuple(slots)
     early = heads - 1
-    grads, sums = attend(packets[:early], notes[:early], kv_in, [], slots, [], n_prompt)
-    last_grads, outs = attend(
-        packets[early:], notes[early:], kv_in, sums, slots, out_types, n_prompt
-    )
-    sums = dict(zip(offsets, outs))
-    arrived = {offset: [] for offset in offsets}
-    for bit in reversed(rest_bits):
-        sent = None
-        for offset in reversed(offsets):
-            if offset & 1 << bit:
-                piece = sums.pop(offset)
-                for part in arrived.pop(offset):
-                    piece = piece + part.astype(F32)
-                if bit == rest_bits[0]:
-                    arrived[0][-1], last_grads = lax.optimization_barrier(
-                        (arrived[0][-1], last_grads)
-                    )
-                if bit != rest_bits[-1] and offset == 1 << bit and sent is not None:
-                    piece, ahead = lax.optimization_barrier((piece, arrived[sent][-1]))
-                    arrived[sent][-1] = ahead
-                arrived[offset ^ 1 << bit].append(swap(piece.astype(BF16), 1 << bit))
-                sent = offset ^ 1 << bit
-        offsets = list(sums)
-    back = [swap(grads[j], member[j]) for j in range(1, early)]
-    shares, back = lax.optimization_barrier((total(sums[0], arrived[0]), back))
-    shares = swap_group(shares)
-    back = [grads[0], *back, swap(last_grads[0], member[early])]
-    query_grad, key_grad, value_grad = unpack(back, queries.shape[1], own_keys.shape[1])
+    grads, sums = attend(packets[:early], notes[:early], kv_in, [], slots, False, n_prompt)
+    back = [grads[0]] + [swap(grads[j], member[j]) for j in range(1, early)]
+    last_grads, outs = attend(packets[early:], notes[early:], kv_in, sums, slots, True, n_prompt)
+
+    keep = outs[0::2]
+    sent = [swap(piece, core) for piece in outs[1::2]]
+    sent, last_grads = lax.optimization_barrier((sent, last_grads))
+    arrived = []
+    for index in range(1, len(keep)):
+        piece = (keep[index] + sent[index].astype(F32)).astype(BF16)
+        arrived.append(swap(piece, offsets[2 * index]))
+    back.append(swap(last_grads[0], member[early]))
+    shares = swap_group(total(keep[0], [sent[0], *arrived]))
+    unpacked = unpack(back, queries.shape[1], own_keys.shape[1])
+    shares, unpacked = lax.optimization_barrier((shares, unpacked))
+    query_grad, key_grad, value_grad = unpacked
     prompt_grad = prompt_gradient(shares, key_weight, value_weight)
     return (query_grad, key_grad, value_grad, prompt_grad)
 

time: 80 us -> 82.6 us (1.032)
  waiting for transfers between devices: 31.8 us -> 37.1 us
  starting transfers between devices: 24.3 us -> 21.6 us
    ppermute x26, waiting for transfers between devices: 31.8 us -> 37.1 us  [swap(): lax.ppermute(x, ('prompt', 'resp'), [(i, i ^ offset) for i in range(devic...]
    ppermute x26, starting transfers between devices: 24.3 us -> 21.6 us  [swap(): lax.ppermute(x, ('prompt', 'resp'), [(i, i ^ offset) for i in range(devic...]
    pallas_call x1, Pallas kernels: 4.54 us -> 3.68 us  [prompt_gradient(): pl.pallas_call(functools.partial(prompt_kernel, n, chunk), out_shape=jax....]
  transfers between devices with their start and end apart: 26 -> 26, of which waited for: 15 -> 13; matrix products, arithmetic and copies ran while one was open for 0% -> 0% of each run, Pallas kernels for 13% -> 9%
where the time goes in v5:
time: 82.6 us; the launch traced here: 82.4 us
  waiting for transfers between devices  37.1 us (45%)
  starting transfers between devices  21.6 us (26%)
  Pallas kernels  20.5 us (25%)
  local copies, waits for them, and re-layouts  1.58 us (2%)
  between operations  1.45 us (2%)
    ppermute x26, waiting for transfers between devices, swap(): lax.ppermute(x, ('prompt', 'resp'), [(i, i ^ offset) for i in range(devic...  37.1 us
    ppermute x26, starting transfers between devices, swap(): lax.ppermute(x, ('prompt', 'resp'), [(i, i ^ offset) for i in range(devic...  21.6 us
    pallas_call x2, Pallas kernels, attend(): pl.pallas_call(functools.partial(attend_kernel, slots, n, group, rows, fi...  8.39 us
    pallas_call x1, Pallas kernels, project(): pl.pallas_call(functools.partial(project_kernel, n, steps), out_shape=[ja...  7.13 us
    pallas_call x1, Pallas kernels, prompt_gradient(): pl.pallas_call(functools.partial(prompt_kernel, n, chunk), out_shape=jax....  3.68 us
  transfers between devices with their start and end apart: 26, of which 13 were waited for; matrix products, arithmetic and copies ran while one was open for 0% of the time, Pallas kernels for 9%

profile of v5, /device:TPU:0, one launch (start us, length us, event | category | flops | bytes accessed | tf_op | source)
XLA Modules:
  0.0 82.4 jit_solution(10539554603820525133)
XLA Ops:
  1.3 7.1 %project_prefix.1 = (bf16[80,256]{1,0:T(8,128)(2,1)}, bf16[80,256]{1,0:T(8,128)(2,1)}, bf16[80,256]{1,0:T(8,128)(2,1)}, bf16[80,256]{1,0:T(8,128)(2,1)}) custom-call(s32[1,1]{1,0:T(1,128)} %bitcast.9.length_ref, s32[1,2]{1,0:T(1,128)} %prompts_ref.1, bf16[64,5120]{1,0:T(8,128)(2,1)} %x_ref.1, bf16[5120,512]{1,0:T(8,128)(2,1)} %rest_4_.1, ...), custom_call_target="tpu_custom_call" | custom-call | flops 671088640 | bytes 11141120 | tf_op jit(solution)/shard_map/project_prefix/pallas_call | solution.py:100
  8.5 3.0 %collective-permute-start = (bf16[80,256]{1,0:T(8,128)(2,1)}, bf16[80,256]{1,0:T(8,128)(2,1)S(1)}, u32[]{:S(2)}, u32[]{:S(2)}) collective-permute-start(bf16[80,256]{1,0:T(8,128)(2,1)} %get-tuple-element.63), channel_id=1, source_target_pairs={{0,8},{1,9},{2,10},{3,11},{4,12},{5,13},{6,14},{7,15},{8,0},{9,1},... | collective-permute-start | bytes 122888 | tf_op jit(solution)/shard_map/ppermute | solution.py:418
  11.5 1.5 %collective-permute-start.1 = (bf16[80,256]{1,0:T(8,128)(2,1)}, bf16[80,256]{1,0:T(8,128)(2,1)S(1)}, u32[]{:S(2)}, u32[]{:S(2)}) collective-permute-start(bf16[80,256]{1,0:T(8,128)(2,1)} %get-tuple-element.64), channel_id=1, source_target_pairs={{0,16},{1,17},{2,18},{3,19},{4,20},{5,21},{6,22},{7,23},{8,24},{9,... | collective-permute-start | bytes 122888 | tf_op jit(solution)/shard_map/ppermute | solution.py:418
  13.7 2.0 %collective-permute-done.1.rest_5_ = bf16[80,256]{1,0:T(8,128)(2,1)S(1)} collective-permute-done((bf16[80,256]{1,0:T(8,128)(2,1)}, bf16[80,256]{1,0:T(8,128)(2,1)S(1)}, u32[]{:S(2)}, u32[]{:S(2)}) %collective-permute-start.1) | collective-permute-done | bytes 40992 | tf_op jit(solution)/shard_map/ppermute | solution.py:418
  15.7 2.4 %collective-permute-done.2.rest_1_ = bf16[80,256]{1,0:T(8,128)(2,1)S(1)} collective-permute-done((bf16[80,256]{1,0:T(8,128)(2,1)}, bf16[80,256]{1,0:T(8,128)(2,1)S(1)}, u32[]{:S(2)}, u32[]{:S(2)}) %collective-permute-start.2) | collective-permute-done | bytes 40992 | tf_op jit(solution)/shard_map/ppermute | solution.py:418
  18.9 1.6 %collective-permute-start.7 = (bf16[4,64,256]{2,1,0:T(8,128)(2,1)S(1)}, bf16[4,64,256]{2,1,0:T(8,128)(2,1)S(1)}, u32[]{:S(2)}, u32[]{:S(2)}) collective-permute-start(bf16[4,64,256]{2,1,0:T(8,128)(2,1)S(1)} %pad_maximum_fusion.rest_6_.rest_2_), channel_id=1, source_target_pairs={{0,2},{1,3},{2,0},{3,1},{4,6},{5,7},{6,4},{7,5},{8,10},{9,11},{10,... | collective-permute-start | bytes 393224 | tf_op jit(solution)/shard_map/ppermute | solution.py:418
  20.6 2.6 %collective-permute-start.5 = (bf16[4,64,256]{2,1,0:T(8,128)(2,1)S(1)}, bf16[4,64,256]{2,1,0:T(8,128)(2,1)S(1)}, u32[]{:S(2)}, u32[]{:S(2)}) collective-permute-start(bf16[4,64,256]{2,1,0:T(8,128)(2,1)S(1)} %pad_maximum_fusion.rest_6_.rest_2_), channel_id=1, source_target_pairs={{0,4},{1,5},{2,6},{3,7},{4,0},{5,1},{6,2},{7,3},{8,12},{9,13},{10,... | collective-permute-start | bytes 393224 | tf_op jit(solution)/shard_map/ppermute | solution.py:418
  24.6 2.0 %collective-permute-start.3 = (bf16[128,1536]{1,0:T(8,128)(2,1)S(1)}, bf16[128,1536]{1,0:T(8,128)(2,1)S(1)}, u32[]{:S(2)}, u32[]{:S(2)}) collective-permute-start(bf16[128,1536]{1,0:T(8,128)(2,1)S(1)} %get-tuple-element.71), channel_id=1, source_target_pairs={{0,24},{1,25},{2,26},{3,27},{4,28},{5,29},{6,30},{7,31},{8,16},{9,... | collective-permute-start | bytes 1179656 | tf_op jit(solution)/shard_map/ppermute | solution.py:418
  26.6 1.2 %collective-permute-done.5.rest_8_.rest_4_ = bf16[4,64,256]{2,1,0:T(8,128)(2,1)S(1)} collective-permute-done((bf16[4,64,256]{2,1,0:T(8,128)(2,1)S(1)}, bf16[4,64,256]{2,1,0:T(8,128)(2,1)S(1)}, u32[]{:S(2)}, u32[]{:S(2)}) %collective-permute-start.5) | collective-permute-done | bytes 131104 | tf_op jit(solution)/shard_map/ppermute | solution.py:418
  28.1 1.1 %collective-permute-done.8.rest_11_.rest_7_ = bf16[4,64,256]{2,1,0:T(8,128)(2,1)S(1)} collective-permute-done((bf16[4,64,256]{2,1,0:T(8,128)(2,1)S(1)}, bf16[4,64,256]{2,1,0:T(8,128)(2,1)S(1)}, u32[]{:S(2)}, u32[]{:S(2)}) %collective-permute-start.8) | collective-permute-done | bytes 131104 | tf_op jit(solution)/shard_map/ppermute | solution.py:418
  29.3 4.4 %collective-permute-done.9.rest_12_.rest_8_ = bf16[4,64,256]{2,1,0:T(8,128)(2,1)S(1)} collective-permute-done((bf16[4,64,256]{2,1,0:T(8,128)(2,1)S(1)}, bf16[4,64,256]{2,1,0:T(8,128)(2,1)S(1)}, u32[]{:S(2)}, u32[]{:S(2)}) %collective-permute-start.9) | collective-permute-done | bytes 131104 | tf_op jit(solution)/shard_map/ppermute | solution.py:418
  33.7 1.3 %collective-permute-done.10.rest_13_.rest_9_ = bf16[4,64,256]{2,1,0:T(8,128)(2,1)S(1)} collective-permute-done((bf16[4,64,256]{2,1,0:T(8,128)(2,1)S(1)}, bf16[4,64,256]{2,1,0:T(8,128)(2,1)S(1)}, u32[]{:S(2)}, u32[]{:S(2)}) %collective-permute-start.10) | collective-permute-done | bytes 131104 | tf_op jit(solution)/shard_map/ppermute | solution.py:418
  35.1 8.3 %collective-permute-done.12.rest_2_ = bf16[128,1536]{1,0:T(8,128)(2,1)S(1)} collective-permute-done((bf16[128,1536]{1,0:T(8,128)(2,1)S(1)}, bf16[128,1536]{1,0:T(8,128)(2,1)S(1)}, u32[]{:S(2)}, u32[]{:S(2)}) %collective-permute-start.12) | collective-permute-done | bytes 393248 | tf_op jit(solution)/shard_map/ppermute | solution.py:418
  44.1 6.0 %attend_head.2 = (bf16[128,896]{1,0:T(8,128)(2,1)S(1)}, bf16[128,896]{1,0:T(8,128)(2,1)S(1)}, bf16[128,896]{1,0:T(8,128)(2,1)S(1)}, f32[4,512,128]{2,1,0:T(8,128)S(1)}, f32[4,512,128]{2,1,0:T(8,128)S(1)}) custom-call(bf16[128,1536]{1,0:T(8,128)(2,1)S(1)} %get-tuple-element.76.rest_0_, bf16[128,1536]{1,0:T(8,128)(2,1)S(1)} %collective-permute-done.11.rest_1_, ...), custom_call_target="tpu_custom_call" | custom-call | bytes 1024 | tf_op jit(solution)/shard_map/attend_head/pallas_call | solution.py:323
  50.1 2.4 %attend_head.3 = (bf16[128,896]{1,0:T(8,128)(2,1)S(1)}, f32[4,64,256]{2,1,0:T(8,128)S(1)}, bf16[4,64,256]{2,1,0:T(8,128)(2,1)S(1)}, f32[4,64,256]{2,1,0:T(8,128)...) custom-call(bf16[128,1536]{1,0:T(8,128)(2,1)S(1)} %collective-permut, ...), custom_call_target="tpu_custom_call" | custom-call | bytes 1024 | tf_op jit(solution)/shard_map/attend_head/pallas_call | solution.py:323
  53.6 1.5 %collective-permute-start.23 = (bf16[128,896]{1,0:T(8,128)(2,1)S(1)}, bf16[128,896]{1,0:T(8,128)(2,1)S(1)}, u32[]{:S(2)}, u32[]{:S(2)}) collective-permute-start(bf16[128,896]{1,0:T(8,128)(2,1)S(1)} %get-tuple-element.99), channel_id=1, source_target_pairs={{0,8},{1,9},{2,10},{3,11},{4,12},{5,13},{6,14},{7,15},{8,0},{9,1},... | collective-permute-start | bytes 688136 | tf_op jit(solution)/shard_map/ppermute | solution.py:418
  56.6 1.5 %collective-permute-start.25 = (bf16[128,896]{1,0:T(8,128)(2,1)S(1)}, bf16[128,896]{1,0:T(8,128)(2,1)S(1)}, u32[]{:S(2)}, u32[]{:S(2)}) collective-permute-start(bf16[128,896]{1,0:T(8,128)(2,1)S(1)} %get-tuple-element.101), channel_id=1, source_target_pairs={{0,24},{1,25},{2,26},{3,27},{4,28},{5,29},{6,30},{7,31},{8,16},{9,... | collective-permute-start | bytes 688136 | tf_op jit(solution)/shard_map/ppermute | solution.py:418
  58.2 6.1 %collective-permute-done.17.rest_1_ = bf16[4,64,256]{2,1,0:T(8,128)(2,1)S(1)} collective-permute-done((bf16[4,64,256]{2,1,0:T(8,128)(2,1)S(1)}, bf16[4,64,256]{2,1,0:T(8,128)(2,1)S(1)}, u32[]{:S(2)}, u32[]{:S(2)}) %collective-permute-start.17) | collective-permute-done | bytes 131104 | tf_op jit(solution)/shard_map/ppermute | solution.py:418
  64.6 6.8 %collective-permute-done.19.rest_3_ = bf16[4,64,256]{2,1,0:T(8,128)(2,1)S(1)} collective-permute-done((bf16[4,64,256]{2,1,0:T(8,128)(2,1)S(1)}, bf16[4,64,256]{2,1,0:T(8,128)(2,1)S(1)}, u32[]{:S(2)}, u32[]{:S(2)}) %collective-permute-start.19) | collective-permute-done | bytes 131104 | tf_op jit(solution)/shard_map/ppermute | solution.py:418
  71.5 1.5 %collective-permute-start.20 = (bf16[64,256]{1,0:T(8,128)(2,1)S(1)}, bf16[64,256]{1,0:T(8,128)(2,1)S(1)}, u32[]{:S(2)}, u32[]{:S(2)}) collective-permute-start(bf16[64,256]{1,0:T(8,128)(2,1)S(1)} %get-tuple-element.95), channel_id=1, source_target_pairs={{0,8},{1,9},{2,10},{3,11},{4,12},{5,13},{6,14},{7,15},{8,0},{9,1},... | collective-permute-start | bytes 98312 | tf_op jit(solution)/shard_map/ppermute | solution.py:418
  73.8 1.2 %collective-permute-start.22 = (bf16[64,256]{1,0:T(8,128)(2,1)S(1)}, bf16[64,256]{1,0:T(8,128)(2,1)S(1)}, u32[]{:S(2)}, u32[]{:S(2)}) collective-permute-start(bf16[64,256]{1,0:T(8,128)(2,1)S(1)} %get-tuple-element.97), channel_id=1, source_target_pairs={{0,24},{1,25},{2,26},{3,27},{4,28},{5,29},{6,30},{7,31},{8,16},{9,... | collective-permute-start | bytes 98312 | tf_op jit(solution)/shard_map/ppermute | solution.py:418
  75.1 1.0 %unpack_rows.1 = (bf16[128,2560]{1,0:T(8,128)(2,1)}, bf16[128,512]{1,0:T(8,128)(2,1)}, bf16[128,512]{1,0:T(8,128)(2,1)}) custom-call(bf16[128,896]{1,0:T(8,128)(2,1)S(1)} %get-tuple-element.98.rest_0_, bf16[128,896]{1,0:T(8,128)(2,1)S(1)} %collective-permute-done.23.rest_1_, bf16[128,896]{1,0:T(8,128)(2,1)S(1)} %collective-permute-done.24.rest_2_, ...), custom_call_target="tpu_custom_call" | custom-call | bytes 1835008 | tf_op jit(solution)/shard_map/unpack_rows/pallas_call | solution.py:154
  76.9 1.8 %collective-permute-done.22.rest_3_ = bf16[64,256]{1,0:T(8,128)(2,1)S(1)} collective-permute-done((bf16[64,256]{1,0:T(8,128)(2,1)S(1)}, bf16[64,256]{1,0:T(8,128)(2,1)S(1)}, u32[]{:S(2)}, u32[]{:S(2)}) %collective-permute-start.22) | collective-permute-done | bytes 32800 | tf_op jit(solution)/shard_map/ppermute | solution.py:418
  78.7 3.7 %prompt_gradient.1 = bf16[64,5120]{1,0:T(8,128)(2,1)} custom-call(bf16[64,256]{1,0:T(8,128)(2,1)S(1)} %get-tuple-element.108.rest_0_, bf16[64,256]{1,0:T(8,128)(2,1)S(1)} %collective-permute-done.20.rest_1_, bf16[64,256]{1,0:T(8,128)(2,1)S(1)} %collective-permute-done.21.rest_2_, bf16[64,256]{1,0:T(8,128)(2,1)S(1)} %collective-permute-done.22.rest_3_, ...), custom_call_target="tpu_custom_call" | custom-call | flops 671088640 | bytes 11141120 | tf_op jit(solution)/shard_map/prompt_gradient/pallas_call | solution.py:380
  (58 shorter events, 8.8 us)
Async XLA Ops:
  8.5 5.2 %collective-permute-start = (bf16[80,256]{1,0:T(8,128)(2,1)}, bf16[80,256]{1,0:T(8,128)(2,1)S(1)}, u32[]{:S(2)}, u32[]{:S(2)}) collective-permute-start(bf16[80,256]{1,0:T(8,128)(2,1)} %get-tuple-element.63), channel_id=1, source_target_pairs={{0,8},{1,9},{2,10},{3,11},{4,12},{5,13},{6,14},{7,15},{8,0},{9,1},... | collective-permute-start | bytes 122888 | tf_op jit(solution)/shard_map/ppermute | solution.py:418
  11.5 4.2 %collective-permute-start.1 = (bf16[80,256]{1,0:T(8,128)(2,1)}, bf16[80,256]{1,0:T(8,128)(2,1)S(1)}, u32[]{:S(2)}, u32[]{:S(2)}) collective-permute-start(bf16[80,256]{1,0:T(8,128)(2,1)} %get-tuple-element.64), channel_id=1, source_target_pairs={{0,16},{1,17},{2,18},{3,19},{4,20},{5,21},{6,22},{7,23},{8,24},{9,... | collective-permute-start | bytes 122888 | tf_op jit(solution)/shard_map/ppermute | solution.py:418
  13.0 5.1 %collective-permute-start.2 = (bf16[80,256]{1,0:T(8,128)(2,1)}, bf16[80,256]{1,0:T(8,128)(2,1)S(1)}, u32[]{:S(2)}, u32[]{:S(2)}) collective-permute-start(bf16[80,256]{1,0:T(8,128)(2,1)} %get-tuple-element.65), channel_id=1, source_target_pairs={{0,24},{1,25},{2,26},{3,27},{4,28},{5,29},{6,30},{7,31},{8,16},{9,... | collective-permute-start | bytes 122888 | tf_op jit(solution)/shard_map/ppermute | solution.py:418
  18.9 5.7 %collective-permute-start.7 = (bf16[4,64,256]{2,1,0:T(8,128)(2,1)S(1)}, bf16[4,64,256]{2,1,0:T(8,128)(2,1)S(1)}, u32[]{:S(2)}, u32[]{:S(2)}) collective-permute-start(bf16[4,64,256]{2,1,0:T(8,128)(2,1)S(1)} %pad_maximum_fusion.rest_6_.rest_2_), channel_id=1, source_target_pairs={{0,2},{1,3},{2,0},{3,1},{4,6},{5,7},{6,4},{7,5},{8,10},{9,11},{10,... | collective-permute-start | bytes 393224 | tf_op jit(solution)/shard_map/ppermute | solution.py:418
  20.6 7.3 %collective-permute-start.5 = (bf16[4,64,256]{2,1,0:T(8,128)(2,1)S(1)}, bf16[4,64,256]{2,1,0:T(8,128)(2,1)S(1)}, u32[]{:S(2)}, u32[]{:S(2)}) collective-permute-start(bf16[4,64,256]{2,1,0:T(8,128)(2,1)S(1)} %pad_maximum_fusion.rest_6_.rest_2_), channel_id=1, source_target_pairs={{0,4},{1,5},{2,6},{3,7},{4,0},{5,1},{6,2},{7,3},{8,12},{9,13},{10,... | collective-permute-start | bytes 393224 | tf_op jit(solution)/shard_map/ppermute | solution.py:418
  23.1 4.7 %collective-permute-start.4 = (bf16[4,64,256]{2,1,0:T(8,128)(2,1)S(1)}, bf16[4,64,256]{2,1,0:T(8,128)(2,1)S(1)}, u32[]{:S(2)}, u32[]{:S(2)}) collective-permute-start(bf16[4,64,256]{2,1,0:T(8,128)(2,1)S(1)} %pad_maximum_fusion.rest_6_.rest_2_), channel_id=1, source_target_pairs={{0,1},{1,0},{2,3},{3,2},{4,5},{5,4},{6,7},{7,6},{8,9},{9,8},{10,11... | collective-permute-start | bytes 393224 | tf_op jit(solution)/shard_map/ppermute | solution.py:418
  23.1 11.9 %collective-permute-start.11 = (bf16[128,1536]{1,0:T(8,128)(2,1)S(1)}, bf16[128,1536]{1,0:T(8,128)(2,1)S(1)}, u32[]{:S(2)}, u32[]{:S(2)}) collective-permute-start(bf16[128,1536]{1,0:T(8,128)(2,1)S(1)} %get-tuple-element.77), channel_id=1, source_target_pairs={{0,8},{1,9},{2,10},{3,11},{4,12},{5,13},{6,14},{7,15},{8,0},{9,1},... | collective-permute-start | bytes 1179656 | tf_op jit(solution)/shard_map/ppermute | solution.py:418
  23.7 19.7 %collective-permute-start.12 = (bf16[128,1536]{1,0:T(8,128)(2,1)S(1)}, bf16[128,1536]{1,0:T(8,128)(2,1)S(1)}, u32[]{:S(2)}, u32[]{:S(2)}) collective-permute-start(bf16[128,1536]{1,0:T(8,128)(2,1)S(1)} %get-tuple-element.78), channel_id=1, source_target_pairs={{0,16},{1,17},{2,18},{3,19},{4,20},{5,21},{6,22},{7,23},{8,24},{9,... | collective-permute-start | bytes 1179656 | tf_op jit(solution)/shard_map/ppermute | solution.py:418
  24.6 25.5 %collective-permute-start.3 = (bf16[128,1536]{1,0:T(8,128)(2,1)S(1)}, bf16[128,1536]{1,0:T(8,128)(2,1)S(1)}, u32[]{:S(2)}, u32[]{:S(2)}) collective-permute-start(bf16[128,1536]{1,0:T(8,128)(2,1)S(1)} %get-tuple-element.71), channel_id=1, source_target_pairs={{0,24},{1,25},{2,26},{3,27},{4,28},{5,29},{6,30},{7,31},{8,16},{9,... | collective-permute-start | bytes 1179656 | tf_op jit(solution)/shard_map/ppermute | solution.py:418
  27.8 5.9 %collective-permute-start.9 = (bf16[4,64,256]{2,1,0:T(8,128)(2,1)S(1)}, bf16[4,64,256]{2,1,0:T(8,128)(2,1)S(1)}, u32[]{:S(2)}, u32[]{:S(2)}) collective-permute-start(bf16[4,64,256]{2,1,0:T(8,128)(2,1)S(1)} %collective-permute-done.5.rest_8_.rest_4_), channel_id=1, source_target_pairs={{0,2},{1,3},{2,0},{3,1},{4,6},{5,7},{6,4},{7,5},{8,10},{9,11},{10,... | collective-permute-start | bytes 393224 | tf_op jit(solution)/shard_map/ppermute | solution.py:418
  29.2 4.6 %collective-permute-start.6 = (bf16[4,64,256]{2,1,0:T(8,128)(2,1)S(1)}, bf16[4,64,256]{2,1,0:T(8,128)(2,1)S(1)}, u32[]{:S(2)}, u32[]{:S(2)}) collective-permute-start(bf16[4,64,256]{2,1,0:T(8,128)(2,1)S(1)} %collective-permute-done.5.rest_8_.rest_4_), channel_id=1, source_target_pairs={{0,1},{1,0},{2,3},{3,2},{4,5},{5,4},{6,7},{7,6},{8,9},{9,8},{10,11... | collective-permute-start | bytes 393224 | tf_op jit(solution)/shard_map/ppermute | solution.py:418
  52.5 2.6 %collective-permute-start.13 = (bf16[4,64,256]{2,1,0:T(8,128)(2,1)S(1)}, bf16[4,64,256]{2,1,0:T(8,128)(2,1)S(1)}, u32[]{:S(2)}, u32[]{:S(2)}) collective-permute-start(bf16[4,64,256]{2,1,0:T(8,128)(2,1)S(1)} %get-tuple-element.82), channel_id=1, source_target_pairs={{0,1},{1,0},{2,3},{3,2},{4,5},{5,4},{6,7},{7,6},{8,9},{9,8},{10,11... | collective-permute-start | bytes 393224 | tf_op jit(solution)/shard_map/ppermute | solution.py:418
  52.6 3.0 %collective-permute-start.14 = (bf16[4,64,256]{2,1,0:T(8,128)(2,1)S(1)}, bf16[4,64,256]{2,1,0:T(8,128)(2,1)S(1)}, u32[]{:S(2)}, u32[]{:S(2)}) collective-permute-start(bf16[4,64,256]{2,1,0:T(8,128)(2,1)S(1)} %get-tuple-element.83), channel_id=1, source_target_pairs={{0,1},{1,0},{2,3},{3,2},{4,5},{5,4},{6,7},{7,6},{8,9},{9,8},{10,11... | collective-permute-start | bytes 393224 | tf_op jit(solution)/shard_map/ppermute | solution.py:418
  53.1 2.5 %collective-permute-start.15 = (bf16[4,64,256]{2,1,0:T(8,128)(2,1)S(1)}, bf16[4,64,256]{2,1,0:T(8,128)(2,1)S(1)}, u32[]{:S(2)}, u32[]{:S(2)}) collective-permute-start(bf16[4,64,256]{2,1,0:T(8,128)(2,1)S(1)} %get-tuple-element.84), channel_id=1, source_target_pairs={{0,1},{1,0},{2,3},{3,2},{4,5},{5,4},{6,7},{7,6},{8,9},{9,8},{10,11... | collective-permute-start | bytes 393224 | tf_op jit(solution)/shard_map/ppermute | solution.py:418
  53.2 2.5 %collective-permute-start.16 = (bf16[4,64,256]{2,1,0:T(8,128)(2,1)S(1)}, bf16[4,64,256]{2,1,0:T(8,128)(2,1)S(1)}, u32[]{:S(2)}, u32[]{:S(2)}) collective-permute-start(bf16[4,64,256]{2,1,0:T(8,128)(2,1)S(1)} %get-tuple-element.85), channel_id=1, source_target_pairs={{0,1},{1,0},{2,3},{3,2},{4,5},{5,4},{6,7},{7,6},{8,9},{9,8},{10,11... | collective-permute-start | bytes 393224 | tf_op jit(solution)/shard_map/ppermute | solution.py:418
  53.6 20.2 %collective-permute-start.23 = (bf16[128,896]{1,0:T(8,128)(2,1)S(1)}, bf16[128,896]{1,0:T(8,128)(2,1)S(1)}, u32[]{:S(2)}, u32[]{:S(2)}) collective-permute-start(bf16[128,896]{1,0:T(8,128)(2,1)S(1)} %get-tuple-element.99), channel_id=1, source_target_pairs={{0,8},{1,9},{2,10},{3,11},{4,12},{5,13},{6,14},{7,15},{8,0},{9,1},... | collective-permute-start | bytes 688136 | tf_op jit(solution)/shard_map/ppermute | solution.py:418
  55.1 19.9 %collective-permute-start.24 = (bf16[128,896]{1,0:T(8,128)(2,1)S(1)}, bf16[128,896]{1,0:T(8,128)(2,1)S(1)}, u32[]{:S(2)}, u32[]{:S(2)}) collective-permute-start(bf16[128,896]{1,0:T(8,128)(2,1)S(1)} %get-tuple-element.100), channel_id=1, source_target_pairs={{0,16},{1,17},{2,18},{3,19},{4,20},{5,21},{6,22},{7,23},{8,24},{9,... | collective-permute-start | bytes 688136 | tf_op jit(solution)/shard_map/ppermute | solution.py:418
  55.7 8.6 %collective-permute-start.17 = (bf16[4,64,256]{2,1,0:T(8,128)(2,1)S(1)}, bf16[4,64,256]{2,1,0:T(8,128)(2,1)S(1)}, u32[]{:S(2)}, u32[]{:S(2)}) collective-permute-start(bf16[4,64,256]{2,1,0:T(8,128)(2,1)S(1)} %add_convert_fusion.2), channel_id=1, source_target_pairs={{0,4},{1,5},{2,6},{3,7},{4,0},{5,1},{6,2},{7,3},{8,12},{9,13},{10,... | collective-permute-start | bytes 393224 | tf_op jit(solution)/shard_map/ppermute | solution.py:418
  56.1 8.5 %collective-permute-start.18 = (bf16[4,64,256]{2,1,0:T(8,128)(2,1)S(1)}, bf16[4,64,256]{2,1,0:T(8,128)(2,1)S(1)}, u32[]{:S(2)}, u32[]{:S(2)}) collective-permute-start(bf16[4,64,256]{2,1,0:T(8,128)(2,1)S(1)} %add_convert_fusion.1), channel_id=1, source_target_pairs={{0,2},{1,3},{2,0},{3,1},{4,6},{5,7},{6,4},{7,5},{8,10},{9,11},{10,... | collective-permute-start | bytes 393224 | tf_op jit(solution)/shard_map/ppermute | solution.py:418
  56.6 18.4 %collective-permute-start.25 = (bf16[128,896]{1,0:T(8,128)(2,1)S(1)}, bf16[128,896]{1,0:T(8,128)(2,1)S(1)}, u32[]{:S(2)}, u32[]{:S(2)}) collective-permute-start(bf16[128,896]{1,0:T(8,128)(2,1)S(1)} %get-tuple-element.101), channel_id=1, source_target_pairs={{0,24},{1,25},{2,26},{3,27},{4,28},{5,29},{6,30},{7,31},{8,16},{9,... | collective-permute-start | bytes 688136 | tf_op jit(solution)/shard_map/ppermute | solution.py:418
  64.3 7.2 %collective-permute-start.19 = (bf16[4,64,256]{2,1,0:T(8,128)(2,1)S(1)}, bf16[4,64,256]{2,1,0:T(8,128)(2,1)S(1)}, u32[]{:S(2)}, u32[]{:S(2)}) collective-permute-start(bf16[4,64,256]{2,1,0:T(8,128)(2,1)S(1)} %add_convert_fusion), channel_id=1, source_target_pairs={{0,6},{1,7},{2,4},{3,5},{4,2},{5,3},{6,0},{7,1},{8,14},{9,15},{10,... | collective-permute-start | bytes 393224 | tf_op jit(solution)/shard_map/ppermute | solution.py:418
  71.5 4.6 %collective-permute-start.20 = (bf16[64,256]{1,0:T(8,128)(2,1)S(1)}, bf16[64,256]{1,0:T(8,128)(2,1)S(1)}, u32[]{:S(2)}, u32[]{:S(2)}) collective-permute-start(bf16[64,256]{1,0:T(8,128)(2,1)S(1)} %get-tuple-element.95), channel_id=1, source_target_pairs={{0,8},{1,9},{2,10},{3,11},{4,12},{5,13},{6,14},{7,15},{8,0},{9,1},... | collective-permute-start | bytes 98312 | tf_op jit(solution)/shard_map/ppermute | solution.py:418
  73.0 3.9 %collective-permute-start.21 = (bf16[64,256]{1,0:T(8,128)(2,1)S(1)}, bf16[64,256]{1,0:T(8,128)(2,1)S(1)}, u32[]{:S(2)}, u32[]{:S(2)}) collective-permute-start(bf16[64,256]{1,0:T(8,128)(2,1)S(1)} %get-tuple-element.96), channel_id=1, source_target_pairs={{0,16},{1,17},{2,18},{3,19},{4,20},{5,21},{6,22},{7,23},{8,24},{9,... | collective-permute-start | bytes 98312 | tf_op jit(solution)/shard_map/ppermute | solution.py:418
  73.8 4.8 %collective-permute-start.22 = (bf16[64,256]{1,0:T(8,128)(2,1)S(1)}, bf16[64,256]{1,0:T(8,128)(2,1)S(1)}, u32[]{:S(2)}, u32[]{:S(2)}) collective-permute-start(bf16[64,256]{1,0:T(8,128)(2,1)S(1)} %get-tuple-element.97), channel_id=1, source_target_pairs={{0,24},{1,25},{2,26},{3,27},{4,28},{5,29},{6,30},{7,31},{8,16},{9,... | collective-permute-start | bytes 98312 | tf_op jit(solution)/shard_map/ppermute | solution.py:418
  (10 other events, 263.4 us)

commit v6 on v5

--- a/solution.py
+++ b/solution.py
@@ -48,7 +48,7 @@
 
 
 def project_kernel(n, steps, length_ref, prompts_ref, x_ref, kw_ref, vw_ref, *rest):
-    outs, (x, kw, vw, key_sum, value_sum, length, prompts, sems, note_sems) = rest[:n], rest[n:]
+    outs, (kw, vw, key_sum, value_sum, length, prompts, sems, note_sems) = rest[:n], rest[n:]
     chunk = kw.shape[0] // steps
     copies = []
     for step in range(steps):
@@ -63,18 +63,16 @@
         pltpu.make_async_copy(length_ref, length, note_sems.at[0]),
         pltpu.make_async_copy(prompts_ref, prompts, note_sems.at[1]),
     ]
-    x_copy = pltpu.make_async_copy(x_ref, x, note_sems.at[2])
-    for copy in [copies[0], x_copy, *copies[1:], *note_copies]:
+    for copy in copies + note_copies:
         copy.start()
-    x_copy.wait()
     keys = values = None
     for step in range(steps):
         span = slice(step * chunk, (step + 1) * chunk)
         copies[2 * step].wait()
-        part = dot(x[:, span], kw[span, :], 1, 0)
+        part = dot(x_ref[:, span], kw[span, :], 1, 0)
         keys = part if step == 0 else keys + part
         copies[2 * step + 1].wait()
-        part = dot(x[:, span], vw[span, :], 1, 0)
+        part = dot(x_ref[:, span], vw[span, :], 1, 0)
         values = part if step == 0 else values + part
     key_sum[...] = keys.astype(BF16)
     value_sum[...] = values.astype(BF16)
@@ -100,13 +98,12 @@
     return pl.pallas_call(
         functools.partial(project_kernel, n, steps),
         out_shape=[jax.ShapeDtypeStruct((rows + NOTE_ROWS, 2 * E), BF16)] * n,
-        in_specs=[ANY] * 5,
+        in_specs=[ANY, ANY, VMEM, ANY, ANY],
         out_specs=[VMEM] * n,
-        scratch_shapes=[pltpu.VMEM(prompt_rows.shape, BF16)]
-        + [pltpu.VMEM(key_weight.shape, BF16)] * 2
+        scratch_shapes=[pltpu.VMEM(key_weight.shape, BF16)] * 2
         + [pltpu.VMEM((rows, width), BF16)] * 2
         + [pltpu.SMEM(first_length.shape, jnp.int32), pltpu.SMEM(resp_prompt.shape, jnp.int32)]
-        + [pltpu.SemaphoreType.DMA((2 * steps,)), pltpu.SemaphoreType.DMA((3,))],
+        + [pltpu.SemaphoreType.DMA((2 * steps,)), pltpu.SemaphoreType.DMA((2,))],
         compiler_params=params(60),
         cost_estimate=cost(4 * rows * depth * width, 4 * depth * width + 2 * rows * depth),
         name="project_prefix",
@@ -418,7 +415,7 @@
         return lax.ppermute(x, ("prompt", "resp"), [(i, i ^ offset) for i in range(devices)])
 
     def swap_group(items):
-        return [items[0]] + [swap(items[j], member[j]) for j in range(1, heads)]
+        return [items[0]] + [swap(items[j], member[j]) for j in range(1, len(items))]
 
     part = prompt_rows.shape[0]
     projected = project(
@@ -429,10 +426,13 @@
     notes = swap_group(projected)
     notes, packed = lax.optimization_barrier((notes, packed))
     pieces = {0: jnp.stack([x[:part] for x in notes])}
-    packets = swap_group(packed)
+    packets = swap_group(packed[:-1])
     for bit in rest_bits:
         for offset in list(pieces):
             pieces[offset | 1 << bit] = swap(pieces[offset], 1 << bit)
+        if len(pieces) == 2:
+            pieces[1 << bit], late = lax.optimization_barrier((pieces[1 << bit], packed[-1]))
+            packets.append(swap(late, member[-1]))
     core = 1 << rest_bits[-1]
     offsets = [o ^ c for o in pieces if not o & core for c in (0, core)]
 
@@ -453,15 +453,25 @@
     back = [grads[0]] + [swap(grads[j], member[j]) for j in range(1, early)]
     last_grads, outs = attend(packets[early:], notes[early:], kv_in, sums, slots, True, n_prompt)
 
-    keep = outs[0::2]
     sent = [swap(piece, core) for piece in outs[1::2]]
     sent, last_grads = lax.optimization_barrier((sent, last_grads))
-    arrived = []
-    for index in range(1, len(keep)):
-        piece = (keep[index] + sent[index].astype(F32)).astype(BF16)
-        arrived.append(swap(piece, offsets[2 * index]))
+    sums = dict(zip(offsets[0::2], outs[0::2]))
+    arrived = {offset: [part] for offset, part in zip(sums, sent)}
+    for bit in reversed(rest_bits[:-1]):
+        first = None
+        for offset in sorted(sums, reverse=True):
+            if offset & 1 << bit:
+                piece = sums.pop(offset)
+                for part in arrived.pop(offset):
+                    piece = piece + part.astype(F32)
+                if offset == 1 << bit and first is not None:
+                    piece, arrived[first][-1] = lax.optimization_barrier(
+                        (piece, arrived[first][-1])
+                    )
+                arrived[offset ^ 1 << bit].append(swap(piece.astype(BF16), 1 << bit))
+                first = offset ^ 1 << bit if first is None else first
     back.append(swap(last_grads[0], member[early]))
-    shares = swap_group(total(keep[0], [sent[0], *arrived]))
+    shares = swap_group(total(sums[0], arrived[0]))
     unpacked = unpack(back, queries.shape[1], own_keys.shape[1])
     shares, unpacked = lax.optimization_barrier((shares, unpacked))
     query_grad, key_grad, value_grad = unpacked

time: 82.6 us -> 79.7 us (0.965)
  waiting for transfers between devices: 37.1 us -> 35.2 us
    ppermute x26, waiting for transfers between devices: 37.1 us -> 35.2 us  [swap(): lax.ppermute(x, ('prompt', 'resp'), [(i, i ^ offset) for i in range(devic...]
  transfers between devices with their start and end apart: 26 -> 26, of which waited for: 13 -> 14; matrix products, arithmetic and copies ran while one was open for 0% -> 0% of each run, Pallas kernels for 9% -> 9%
where the time goes in v6:
time: 79.7 us; the launch traced here: 79.5 us
  waiting for transfers between devices  35.2 us (44%)
  starting transfers between devices  21.2 us (27%)
  Pallas kernels  19.9 us (25%)
  local copies, waits for them, and re-layouts  1.58 us (2%)
  between operations  1.46 us (2%)
    ppermute x26, waiting for transfers between devices, swap(): lax.ppermute(x, ('prompt', 'resp'), [(i, i ^ offset) for i in range(devic...  35.2 us
    ppermute x26, starting transfers between devices, swap(): lax.ppermute(x, ('prompt', 'resp'), [(i, i ^ offset) for i in range(devic...  21.2 us
    pallas_call x2, Pallas kernels, attend(): pl.pallas_call(functools.partial(attend_kernel, slots, n, group, rows, fi...  8.38 us
    pallas_call x1, Pallas kernels, project(): pl.pallas_call(functools.partial(project_kernel, n, steps), out_shape=[ja...  6.59 us
    pallas_call x1, Pallas kernels, prompt_gradient(): pl.pallas_call(functools.partial(prompt_kernel, n, chunk), out_shape=jax....  3.68 us
  transfers between devices with their start and end apart: 26, of which 14 were waited for; matrix products, arithmetic and copies ran while one was open for 0% of the time, Pallas kernels for 9%

profile of v6, /device:TPU:0, one launch (start us, length us, event | category | flops | bytes accessed | tf_op | source)
XLA Modules:
  0.0 79.5 jit_solution(15840953065867180973)
XLA Ops:
  1.3 6.6 %project_prefix.1 = (bf16[80,256]{1,0:T(8,128)(2,1)}, bf16[80,256]{1,0:T(8,128)(2,1)}, bf16[80,256]{1,0:T(8,128)(2,1)}, bf16[80,256]{1,0:T(8,128)(2,1)}) custom-call(s32[1,1]{1,0:T(1,128)} %bitcast.9.length_ref, s32[1,2]{1,0:T(1,128)} %prompts_ref.1, bf16[64,5120]{1,0:T(8,128)(2,1)} %x_ref.1, bf16[5120,512]{1,0:T(8,128)(2,1)} %rest_4_.1, ...), custom_call_target="tpu_custom_call" | custom-call | flops 671088640 | bytes 11141120 | tf_op jit(solution)/shard_map/project_prefix/pallas_call | solution.py:98
  7.9 3.0 %collective-permute-start = (bf16[80,256]{1,0:T(8,128)(2,1)}, bf16[80,256]{1,0:T(8,128)(2,1)S(1)}, u32[]{:S(2)}, u32[]{:S(2)}) collective-permute-start(bf16[80,256]{1,0:T(8,128)(2,1)} %get-tuple-element.67), channel_id=1, source_target_pairs={{0,8},{1,9},{2,10},{3,11},{4,12},{5,13},{6,14},{7,15},{8,0},{9,1},... | collective-permute-start | bytes 122888 | tf_op jit(solution)/shard_map/ppermute | solution.py:415
  10.9 1.5 %collective-permute-start.1 = (bf16[80,256]{1,0:T(8,128)(2,1)}, bf16[80,256]{1,0:T(8,128)(2,1)S(1)}, u32[]{:S(2)}, u32[]{:S(2)}) collective-permute-start(bf16[80,256]{1,0:T(8,128)(2,1)} %get-tuple-element.68), channel_id=1, source_target_pairs={{0,16},{1,17},{2,18},{3,19},{4,20},{5,21},{6,22},{7,23},{8,24},{9,... | collective-permute-start | bytes 122888 | tf_op jit(solution)/shard_map/ppermute | solution.py:415
  13.1 2.0 %collective-permute-done.1.rest_5_ = bf16[80,256]{1,0:T(8,128)(2,1)S(1)} collective-permute-done((bf16[80,256]{1,0:T(8,128)(2,1)}, bf16[80,256]{1,0:T(8,128)(2,1)S(1)}, u32[]{:S(2)}, u32[]{:S(2)}) %collective-permute-start.1) | collective-permute-done | bytes 40992 | tf_op jit(solution)/shard_map/ppermute | solution.py:415
  15.2 2.4 %collective-permute-done.2.rest_1_ = bf16[80,256]{1,0:T(8,128)(2,1)S(1)} collective-permute-done((bf16[80,256]{1,0:T(8,128)(2,1)}, bf16[80,256]{1,0:T(8,128)(2,1)S(1)}, u32[]{:S(2)}, u32[]{:S(2)}) %collective-permute-start.2) | collective-permute-done | bytes 40992 | tf_op jit(solution)/shard_map/ppermute | solution.py:415
  18.4 2.7 %collective-permute-start.3 = (bf16[4,64,256]{2,1,0:T(8,128)(2,1)S(1)}, bf16[4,64,256]{2,1,0:T(8,128)(2,1)S(1)}, u32[]{:S(2)}, u32[]{:S(2)}) collective-permute-start(bf16[4,64,256]{2,1,0:T(8,128)(2,1)S(1)} %pad_maximum_fusion.rest_6_.rest_2_), channel_id=1, source_target_pairs={{0,4},{1,5},{2,6},{3,7},{4,0},{5,1},{6,2},{7,3},{8,12},{9,13},{10,... | collective-permute-start | bytes 393224 | tf_op jit(solution)/shard_map/ppermute | solution.py:415
  21.0 1.6 %collective-permute-start.7 = (bf16[4,64,256]{2,1,0:T(8,128)(2,1)S(1)}, bf16[4,64,256]{2,1,0:T(8,128)(2,1)S(1)}, u32[]{:S(2)}, u32[]{:S(2)}) collective-permute-start(bf16[4,64,256]{2,1,0:T(8,128)(2,1)S(1)} %pad_maximum_fusion.rest_6_.rest_2_), channel_id=1, source_target_pairs={{0,2},{1,3},{2,0},{3,1},{4,6},{5,7},{6,4},{7,5},{8,10},{9,11},{10,... | collective-permute-start | bytes 393224 | tf_op jit(solution)/shard_map/ppermute | solution.py:415
  23.7 2.2 %collective-permute-done.3.rest_8_.rest_4_ = bf16[4,64,256]{2,1,0:T(8,128)(2,1)S(1)} collective-permute-done((bf16[4,64,256]{2,1,0:T(8,128)(2,1)S(1)}, bf16[4,64,256]{2,1,0:T(8,128)(2,1)S(1)}, u32[]{:S(2)}, u32[]{:S(2)}) %collective-permute-start.3) | collective-permute-done | bytes 131104 | tf_op jit(solution)/shard_map/ppermute | solution.py:415
  26.6 1.0 %collective-permute-start.9 = (bf16[4,64,256]{2,1,0:T(8,128)(2,1)S(1)}, bf16[4,64,256]{2,1,0:T(8,128)(2,1)S(1)}, u32[]{:S(2)}, u32[]{:S(2)}) collective-permute-start(bf16[4,64,256]{2,1,0:T(8,128)(2,1)S(1)} %collective-permute-done.3.rest_8_.rest_4_), channel_id=1, source_target_pairs={{0,2},{1,3},{2,0},{3,1},{4,6},{5,7},{6,4},{7,5},{8,10},{9,11},{10,... | collective-permute-start | bytes 393224 | tf_op jit(solution)/shard_map/ppermute | solution.py:415
  28.1 4.4 %collective-permute-done.9.rest_12_.rest_8_ = bf16[4,64,256]{2,1,0:T(8,128)(2,1)S(1)} collective-permute-done((bf16[4,64,256]{2,1,0:T(8,128)(2,1)S(1)}, bf16[4,64,256]{2,1,0:T(8,128)(2,1)S(1)}, u32[]{:S(2)}, u32[]{:S(2)}) %collective-permute-start.9) | collective-permute-done | bytes 131104 | tf_op jit(solution)/shard_map/ppermute | solution.py:415
  32.5 1.3 %collective-permute-done.10.rest_13_.rest_9_ = bf16[4,64,256]{2,1,0:T(8,128)(2,1)S(1)} collective-permute-done((bf16[4,64,256]{2,1,0:T(8,128)(2,1)S(1)}, bf16[4,64,256]{2,1,0:T(8,128)(2,1)S(1)}, u32[]{:S(2)}, u32[]{:S(2)}) %collective-permute-start.10) | collective-permute-done | bytes 131104 | tf_op jit(solution)/shard_map/ppermute | solution.py:415
  34.5 8.3 %collective-permute-done.12.rest_2_ = bf16[128,1536]{1,0:T(8,128)(2,1)S(1)} collective-permute-done((bf16[128,1536]{1,0:T(8,128)(2,1)S(1)}, bf16[128,1536]{1,0:T(8,128)(2,1)S(1)}, u32[]{:S(2)}, u32[]{:S(2)}) %collective-permute-start.12) | collective-permute-done | bytes 393248 | tf_op jit(solution)/shard_map/ppermute | solution.py:415
  43.6 6.0 %attend_head.2 = (bf16[128,896]{1,0:T(8,128)(2,1)S(1)}, bf16[128,896]{1,0:T(8,128)(2,1)S(1)}, bf16[128,896]{1,0:T(8,128)(2,1)S(1)}, f32[4,512,128]{2,1,0:T(8,128)S(1)}, f32[4,512,128]{2,1,0:T(8,128)S(1)}) custom-call(bf16[128,1536]{1,0:T(8,128)(2,1)S(1)} %get-tuple-element.82.rest_0_, bf16[128,1536]{1,0:T(8,128)(2,1)S(1)} %collective-permute-done.11.rest_1_, ...), custom_call_target="tpu_custom_call" | custom-call | bytes 1024 | tf_op jit(solution)/shard_map/attend_head/pallas_call | solution.py:320
  49.6 2.4 %attend_head.3 = (bf16[128,896]{1,0:T(8,128)(2,1)S(1)}, f32[4,64,256]{2,1,0:T(8,128)S(1)}, bf16[4,64,256]{2,1,0:T(8,128)(2,1)S(1)}, f32[4,64,256]{2,1,0:T(8,128)...) custom-call(bf16[128,1536]{1,0:T(8,128)(2,1)S(1)} %collective-permut, ...), custom_call_target="tpu_custom_call" | custom-call | bytes 1024 | tf_op jit(solution)/shard_map/attend_head/pallas_call | solution.py:320
  53.1 1.5 %collective-permute-start.23 = (bf16[128,896]{1,0:T(8,128)(2,1)S(1)}, bf16[128,896]{1,0:T(8,128)(2,1)S(1)}, u32[]{:S(2)}, u32[]{:S(2)}) collective-permute-start(bf16[128,896]{1,0:T(8,128)(2,1)S(1)} %get-tuple-element.107), channel_id=1, source_target_pairs={{0,8},{1,9},{2,10},{3,11},{4,12},{5,13},{6,14},{7,15},{8,0},{9,1},... | collective-permute-start | bytes 688136 | tf_op jit(solution)/shard_map/ppermute | solution.py:415
  55.7 1.5 %collective-permute-start.25 = (bf16[128,896]{1,0:T(8,128)(2,1)S(1)}, bf16[128,896]{1,0:T(8,128)(2,1)S(1)}, u32[]{:S(2)}, u32[]{:S(2)}) collective-permute-start(bf16[128,896]{1,0:T(8,128)(2,1)S(1)} %get-tuple-element.109), channel_id=1, source_target_pairs={{0,24},{1,25},{2,26},{3,27},{4,28},{5,29},{6,30},{7,31},{8,16},{9,... | collective-permute-start | bytes 688136 | tf_op jit(solution)/shard_map/ppermute | solution.py:415
  57.2 3.0 %collective-permute-done.17 = bf16[4,64,256]{2,1,0:T(8,128)(2,1)S(1)} collective-permute-done((bf16[4,64,256]{2,1,0:T(8,128)(2,1)S(1)}, bf16[4,64,256]{2,1,0:T(8,128)(2,1)S(1)}, u32[]{:S(2)}, u32[]{:S(2)}) %collective-permute-start.17) | collective-permute-done | bytes 131104 | tf_op jit(solution)/shard_map/ppermute | solution.py:415
  61.1 5.0 %collective-permute-done.18.rest_1_ = bf16[4,64,256]{2,1,0:T(8,128)(2,1)S(1)} collective-permute-done((bf16[4,64,256]{2,1,0:T(8,128)(2,1)S(1)}, bf16[4,64,256]{2,1,0:T(8,128)(2,1)S(1)}, u32[]{:S(2)}, u32[]{:S(2)}) %collective-permute-start.18) | collective-permute-done | bytes 131104 | tf_op jit(solution)/shard_map/ppermute | solution.py:415
  66.1 2.6 %collective-permute-done.19.rest_2_ = bf16[4,64,256]{2,1,0:T(8,128)(2,1)S(1)} collective-permute-done((bf16[4,64,256]{2,1,0:T(8,128)(2,1)S(1)}, bf16[4,64,256]{2,1,0:T(8,128)(2,1)S(1)}, u32[]{:S(2)}, u32[]{:S(2)}) %collective-permute-start.19) | collective-permute-done | bytes 131104 | tf_op jit(solution)/shard_map/ppermute | solution.py:415
  68.7 1.8 %collective-permute-start.20 = (bf16[64,256]{1,0:T(8,128)(2,1)S(1)}, bf16[64,256]{1,0:T(8,128)(2,1)S(1)}, u32[]{:S(2)}, u32[]{:S(2)}) collective-permute-start(bf16[64,256]{1,0:T(8,128)(2,1)S(1)} %get-tuple-element.103), channel_id=1, source_target_pairs={{0,8},{1,9},{2,10},{3,11},{4,12},{5,13},{6,14},{7,15},{8,0},{9,1},... | collective-permute-start | bytes 98312 | tf_op jit(solution)/shard_map/ppermute | solution.py:415
  71.0 1.3 %collective-permute-start.22 = (bf16[64,256]{1,0:T(8,128)(2,1)S(1)}, bf16[64,256]{1,0:T(8,128)(2,1)S(1)}, u32[]{:S(2)}, u32[]{:S(2)}) collective-permute-start(bf16[64,256]{1,0:T(8,128)(2,1)S(1)} %get-tuple-element.105), channel_id=1, source_target_pairs={{0,24},{1,25},{2,26},{3,27},{4,28},{5,29},{6,30},{7,31},{8,16},{9,... | collective-permute-start | bytes 98312 | tf_op jit(solution)/shard_map/ppermute | solution.py:415
  73.3 1.1 %collective-permute-done.21.rest_2_ = bf16[64,256]{1,0:T(8,128)(2,1)S(1)} collective-permute-done((bf16[64,256]{1,0:T(8,128)(2,1)S(1)}, bf16[64,256]{1,0:T(8,128)(2,1)S(1)}, u32[]{:S(2)}, u32[]{:S(2)}) %collective-permute-start.21) | collective-permute-done | bytes 32800 | tf_op jit(solution)/shard_map/ppermute | solution.py:415
  74.4 1.3 %collective-permute-done.22.rest_3_ = bf16[64,256]{1,0:T(8,128)(2,1)S(1)} collective-permute-done((bf16[64,256]{1,0:T(8,128)(2,1)S(1)}, bf16[64,256]{1,0:T(8,128)(2,1)S(1)}, u32[]{:S(2)}, u32[]{:S(2)}) %collective-permute-start.22) | collective-permute-done | bytes 32800 | tf_op jit(solution)/shard_map/ppermute | solution.py:415
  75.8 3.7 %prompt_gradient.1 = bf16[64,5120]{1,0:T(8,128)(2,1)} custom-call(bf16[64,256]{1,0:T(8,128)(2,1)S(1)} %get-tuple-element.116.rest_0_, bf16[64,256]{1,0:T(8,128)(2,1)S(1)} %collective-permute-done.20.rest_1_, bf16[64,256]{1,0:T(8,128)(2,1)S(1)} %collective-permute-done.21.rest_2_, bf16[64,256]{1,0:T(8,128)(2,1)S(1)} %collective-permute-done.22.rest_3_, ...), custom_call_target="tpu_custom_call" | custom-call | flops 671088640 | bytes 11141120 | tf_op jit(solution)/shard_map/prompt_gradient/pallas_call | solution.py:377
  (58 shorter events, 9.8 us)
Async XLA Ops:
  7.9 5.2 %collective-permute-start = (bf16[80,256]{1,0:T(8,128)(2,1)}, bf16[80,256]{1,0:T(8,128)(2,1)S(1)}, u32[]{:S(2)}, u32[]{:S(2)}) collective-permute-start(bf16[80,256]{1,0:T(8,128)(2,1)} %get-tuple-element.67), channel_id=1, source_target_pairs={{0,8},{1,9},{2,10},{3,11},{4,12},{5,13},{6,14},{7,15},{8,0},{9,1},... | collective-permute-start | bytes 122888 | tf_op jit(solution)/shard_map/ppermute | solution.py:415
  10.9 4.2 %collective-permute-start.1 = (bf16[80,256]{1,0:T(8,128)(2,1)}, bf16[80,256]{1,0:T(8,128)(2,1)S(1)}, u32[]{:S(2)}, u32[]{:S(2)}) collective-permute-start(bf16[80,256]{1,0:T(8,128)(2,1)} %get-tuple-element.68), channel_id=1, source_target_pairs={{0,16},{1,17},{2,18},{3,19},{4,20},{5,21},{6,22},{7,23},{8,24},{9,... | collective-permute-start | bytes 122888 | tf_op jit(solution)/shard_map/ppermute | solution.py:415
  12.5 5.1 %collective-permute-start.2 = (bf16[80,256]{1,0:T(8,128)(2,1)}, bf16[80,256]{1,0:T(8,128)(2,1)S(1)}, u32[]{:S(2)}, u32[]{:S(2)}) collective-permute-start(bf16[80,256]{1,0:T(8,128)(2,1)} %get-tuple-element.69), channel_id=1, source_target_pairs={{0,24},{1,25},{2,26},{3,27},{4,28},{5,29},{6,30},{7,31},{8,16},{9,... | collective-permute-start | bytes 122888 | tf_op jit(solution)/shard_map/ppermute | solution.py:415
  18.4 7.5 %collective-permute-start.3 = (bf16[4,64,256]{2,1,0:T(8,128)(2,1)S(1)}, bf16[4,64,256]{2,1,0:T(8,128)(2,1)S(1)}, u32[]{:S(2)}, u32[]{:S(2)}) collective-permute-start(bf16[4,64,256]{2,1,0:T(8,128)(2,1)S(1)} %pad_maximum_fusion.rest_6_.rest_2_), channel_id=1, source_target_pairs={{0,4},{1,5},{2,6},{3,7},{4,0},{5,1},{6,2},{7,3},{8,12},{9,13},{10,... | collective-permute-start | bytes 393224 | tf_op jit(solution)/shard_map/ppermute | solution.py:415
  21.0 5.5 %collective-permute-start.7 = (bf16[4,64,256]{2,1,0:T(8,128)(2,1)S(1)}, bf16[4,64,256]{2,1,0:T(8,128)(2,1)S(1)}, u32[]{:S(2)}, u32[]{:S(2)}) collective-permute-start(bf16[4,64,256]{2,1,0:T(8,128)(2,1)S(1)} %pad_maximum_fusion.rest_6_.rest_2_), channel_id=1, source_target_pairs={{0,2},{1,3},{2,0},{3,1},{4,6},{5,7},{6,4},{7,5},{8,10},{9,11},{10,... | collective-permute-start | bytes 393224 | tf_op jit(solution)/shard_map/ppermute | solution.py:415
  22.6 4.0 %collective-permute-start.5 = (bf16[4,64,256]{2,1,0:T(8,128)(2,1)S(1)}, bf16[4,64,256]{2,1,0:T(8,128)(2,1)S(1)}, u32[]{:S(2)}, u32[]{:S(2)}) collective-permute-start(bf16[4,64,256]{2,1,0:T(8,128)(2,1)S(1)} %pad_maximum_fusion.rest_6_.rest_2_), channel_id=1, source_target_pairs={{0,1},{1,0},{2,3},{3,2},{4,5},{5,4},{6,7},{7,6},{8,9},{9,8},{10,11... | collective-permute-start | bytes 393224 | tf_op jit(solution)/shard_map/ppermute | solution.py:415
  22.6 11.9 %collective-permute-start.11 = (bf16[128,1536]{1,0:T(8,128)(2,1)S(1)}, bf16[128,1536]{1,0:T(8,128)(2,1)S(1)}, u32[]{:S(2)}, u32[]{:S(2)}) collective-permute-start(bf16[128,1536]{1,0:T(8,128)(2,1)S(1)} %get-tuple-element.83), channel_id=1, source_target_pairs={{0,8},{1,9},{2,10},{3,11},{4,12},{5,13},{6,14},{7,15},{8,0},{9,1},... | collective-permute-start | bytes 1179656 | tf_op jit(solution)/shard_map/ppermute | solution.py:415
  23.1 19.7 %collective-permute-start.12 = (bf16[128,1536]{1,0:T(8,128)(2,1)S(1)}, bf16[128,1536]{1,0:T(8,128)(2,1)S(1)}, u32[]{:S(2)}, u32[]{:S(2)}) collective-permute-start(bf16[128,1536]{1,0:T(8,128)(2,1)S(1)} %get-tuple-element.84), channel_id=1, source_target_pairs={{0,16},{1,17},{2,18},{3,19},{4,20},{5,21},{6,22},{7,23},{8,24},{9,... | collective-permute-start | bytes 1179656 | tf_op jit(solution)/shard_map/ppermute | solution.py:415
  25.8 23.8 %collective-permute-start.4 = (bf16[128,1536]{1,0:T(8,128)(2,1)S(1)}, bf16[128,1536]{1,0:T(8,128)(2,1)S(1)}, u32[]{:S(2)}, u32[]{:S(2)}) collective-permute-start(bf16[128,1536]{1,0:T(8,128)(2,1)S(1)} %get-tuple-element.80), channel_id=1, source_target_pairs={{0,24},{1,25},{2,26},{3,27},{4,28},{5,29},{6,30},{7,31},{8,16},{9,... | collective-permute-start | bytes 1179656 | tf_op jit(solution)/shard_map/ppermute | solution.py:415
  26.6 5.9 %collective-permute-start.9 = (bf16[4,64,256]{2,1,0:T(8,128)(2,1)S(1)}, bf16[4,64,256]{2,1,0:T(8,128)(2,1)S(1)}, u32[]{:S(2)}, u32[]{:S(2)}) collective-permute-start(bf16[4,64,256]{2,1,0:T(8,128)(2,1)S(1)} %collective-permute-done.3.rest_8_.rest_4_), channel_id=1, source_target_pairs={{0,2},{1,3},{2,0},{3,1},{4,6},{5,7},{6,4},{7,5},{8,10},{9,11},{10,... | collective-permute-start | bytes 393224 | tf_op jit(solution)/shard_map/ppermute | solution.py:415
  27.9 4.6 %collective-permute-start.6 = (bf16[4,64,256]{2,1,0:T(8,128)(2,1)S(1)}, bf16[4,64,256]{2,1,0:T(8,128)(2,1)S(1)}, u32[]{:S(2)}, u32[]{:S(2)}) collective-permute-start(bf16[4,64,256]{2,1,0:T(8,128)(2,1)S(1)} %collective-permute-done.3.rest_8_.rest_4_), channel_id=1, source_target_pairs={{0,1},{1,0},{2,3},{3,2},{4,5},{5,4},{6,7},{7,6},{8,9},{9,8},{10,11... | collective-permute-start | bytes 393224 | tf_op jit(solution)/shard_map/ppermute | solution.py:415
  52.0 2.6 %collective-permute-start.13 = (bf16[4,64,256]{2,1,0:T(8,128)(2,1)S(1)}, bf16[4,64,256]{2,1,0:T(8,128)(2,1)S(1)}, u32[]{:S(2)}, u32[]{:S(2)}) collective-permute-start(bf16[4,64,256]{2,1,0:T(8,128)(2,1)S(1)} %get-tuple-element.88), channel_id=1, source_target_pairs={{0,1},{1,0},{2,3},{3,2},{4,5},{5,4},{6,7},{7,6},{8,9},{9,8},{10,11... | collective-permute-start | bytes 393224 | tf_op jit(solution)/shard_map/ppermute | solution.py:415
  52.1 3.0 %collective-permute-start.14 = (bf16[4,64,256]{2,1,0:T(8,128)(2,1)S(1)}, bf16[4,64,256]{2,1,0:T(8,128)(2,1)S(1)}, u32[]{:S(2)}, u32[]{:S(2)}) collective-permute-start(bf16[4,64,256]{2,1,0:T(8,128)(2,1)S(1)} %get-tuple-element.89), channel_id=1, source_target_pairs={{0,1},{1,0},{2,3},{3,2},{4,5},{5,4},{6,7},{7,6},{8,9},{9,8},{10,11... | collective-permute-start | bytes 393224 | tf_op jit(solution)/shard_map/ppermute | solution.py:415
  52.6 2.5 %collective-permute-start.15 = (bf16[4,64,256]{2,1,0:T(8,128)(2,1)S(1)}, bf16[4,64,256]{2,1,0:T(8,128)(2,1)S(1)}, u32[]{:S(2)}, u32[]{:S(2)}) collective-permute-start(bf16[4,64,256]{2,1,0:T(8,128)(2,1)S(1)} %get-tuple-element.90), channel_id=1, source_target_pairs={{0,1},{1,0},{2,3},{3,2},{4,5},{5,4},{6,7},{7,6},{8,9},{9,8},{10,11... | collective-permute-start | bytes 393224 | tf_op jit(solution)/shard_map/ppermute | solution.py:415
  52.7 2.4 %collective-permute-start.16 = (bf16[4,64,256]{2,1,0:T(8,128)(2,1)S(1)}, bf16[4,64,256]{2,1,0:T(8,128)(2,1)S(1)}, u32[]{:S(2)}, u32[]{:S(2)}) collective-permute-start(bf16[4,64,256]{2,1,0:T(8,128)(2,1)S(1)} %get-tuple-element.91), channel_id=1, source_target_pairs={{0,1},{1,0},{2,3},{3,2},{4,5},{5,4},{6,7},{7,6},{8,9},{9,8},{10,11... | collective-permute-start | bytes 393224 | tf_op jit(solution)/shard_map/ppermute | solution.py:415
  53.1 17.9 %collective-permute-start.23 = (bf16[128,896]{1,0:T(8,128)(2,1)S(1)}, bf16[128,896]{1,0:T(8,128)(2,1)S(1)}, u32[]{:S(2)}, u32[]{:S(2)}) collective-permute-start(bf16[128,896]{1,0:T(8,128)(2,1)S(1)} %get-tuple-element.107), channel_id=1, source_target_pairs={{0,8},{1,9},{2,10},{3,11},{4,12},{5,13},{6,14},{7,15},{8,0},{9,1},... | collective-permute-start | bytes 688136 | tf_op jit(solution)/shard_map/ppermute | solution.py:415
  54.6 17.7 %collective-permute-start.24 = (bf16[128,896]{1,0:T(8,128)(2,1)S(1)}, bf16[128,896]{1,0:T(8,128)(2,1)S(1)}, u32[]{:S(2)}, u32[]{:S(2)}) collective-permute-start(bf16[128,896]{1,0:T(8,128)(2,1)S(1)} %get-tuple-element.108), channel_id=1, source_target_pairs={{0,16},{1,17},{2,18},{3,19},{4,20},{5,21},{6,22},{7,23},{8,24},{9,... | collective-permute-start | bytes 688136 | tf_op jit(solution)/shard_map/ppermute | solution.py:415
  55.1 5.0 %collective-permute-start.17 = (bf16[4,64,256]{2,1,0:T(8,128)(2,1)S(1)}, bf16[4,64,256]{2,1,0:T(8,128)(2,1)S(1)}, u32[]{:S(2)}, u32[]{:S(2)}) collective-permute-start(bf16[4,64,256]{2,1,0:T(8,128)(2,1)S(1)} %add_convert_fusion.1), channel_id=1, source_target_pairs={{0,2},{1,3},{2,0},{3,1},{4,6},{5,7},{6,4},{7,5},{8,10},{9,11},{10,... | collective-permute-start | bytes 393224 | tf_op jit(solution)/shard_map/ppermute | solution.py:415
  55.7 16.6 %collective-permute-start.25 = (bf16[128,896]{1,0:T(8,128)(2,1)S(1)}, bf16[128,896]{1,0:T(8,128)(2,1)S(1)}, u32[]{:S(2)}, u32[]{:S(2)}) collective-permute-start(bf16[128,896]{1,0:T(8,128)(2,1)S(1)} %get-tuple-element.109), channel_id=1, source_target_pairs={{0,24},{1,25},{2,26},{3,27},{4,28},{5,29},{6,30},{7,31},{8,16},{9,... | collective-permute-start | bytes 688136 | tf_op jit(solution)/shard_map/ppermute | solution.py:415
  60.2 5.9 %collective-permute-start.18 = (bf16[4,64,256]{2,1,0:T(8,128)(2,1)S(1)}, bf16[4,64,256]{2,1,0:T(8,128)(2,1)S(1)}, u32[]{:S(2)}, u32[]{:S(2)}) collective-permute-start(bf16[4,64,256]{2,1,0:T(8,128)(2,1)S(1)} %convert_add_fusion), channel_id=1, source_target_pairs={{0,2},{1,3},{2,0},{3,1},{4,6},{5,7},{6,4},{7,5},{8,10},{9,11},{10,... | collective-permute-start | bytes 393224 | tf_op jit(solution)/shard_map/ppermute | solution.py:415
  60.7 8.0 %collective-permute-start.19 = (bf16[4,64,256]{2,1,0:T(8,128)(2,1)S(1)}, bf16[4,64,256]{2,1,0:T(8,128)(2,1)S(1)}, u32[]{:S(2)}, u32[]{:S(2)}) collective-permute-start(bf16[4,64,256]{2,1,0:T(8,128)(2,1)S(1)} %add_convert_fusion), channel_id=1, source_target_pairs={{0,4},{1,5},{2,6},{3,7},{4,0},{5,1},{6,2},{7,3},{8,12},{9,13},{10,... | collective-permute-start | bytes 393224 | tf_op jit(solution)/shard_map/ppermute | solution.py:415
  68.7 4.6 %collective-permute-start.20 = (bf16[64,256]{1,0:T(8,128)(2,1)S(1)}, bf16[64,256]{1,0:T(8,128)(2,1)S(1)}, u32[]{:S(2)}, u32[]{:S(2)}) collective-permute-start(bf16[64,256]{1,0:T(8,128)(2,1)S(1)} %get-tuple-element.103), channel_id=1, source_target_pairs={{0,8},{1,9},{2,10},{3,11},{4,12},{5,13},{6,14},{7,15},{8,0},{9,1},... | collective-permute-start | bytes 98312 | tf_op jit(solution)/shard_map/ppermute | solution.py:415
  70.5 3.9 %collective-permute-start.21 = (bf16[64,256]{1,0:T(8,128)(2,1)S(1)}, bf16[64,256]{1,0:T(8,128)(2,1)S(1)}, u32[]{:S(2)}, u32[]{:S(2)}) collective-permute-start(bf16[64,256]{1,0:T(8,128)(2,1)S(1)} %get-tuple-element.104), channel_id=1, source_target_pairs={{0,16},{1,17},{2,18},{3,19},{4,20},{5,21},{6,22},{7,23},{8,24},{9,... | collective-permute-start | bytes 98312 | tf_op jit(solution)/shard_map/ppermute | solution.py:415
  71.0 4.8 %collective-permute-start.22 = (bf16[64,256]{1,0:T(8,128)(2,1)S(1)}, bf16[64,256]{1,0:T(8,128)(2,1)S(1)}, u32[]{:S(2)}, u32[]{:S(2)}) collective-permute-start(bf16[64,256]{1,0:T(8,128)(2,1)S(1)} %get-tuple-element.105), channel_id=1, source_target_pairs={{0,24},{1,25},{2,26},{3,27},{4,28},{5,29},{6,30},{7,31},{8,16},{9,... | collective-permute-start | bytes 98312 | tf_op jit(solution)/shard_map/ppermute | solution.py:415
  (10 other events, 253.7 us)

commit v7 on v6

v7 whole, which is shorter than its diff:
```python
import functools
import math

import jax
import jax.numpy as jnp
from jax import lax
from jax.experimental import pallas as pl
from jax.experimental.pallas import tpu as pltpu
from jax.sharding import PartitionSpec as P

E = 128
PLEN = 512
SCALE = E ** (-0.5)
EXP2_SCALE = SCALE * math.log2(math.e)
HIDDEN = -1e30
BF16 = jnp.bfloat16
F32 = jnp.float32
NOTE_ROWS = 32
CORE, X, Y = 0, 3, 4
GATHER_BITS = (2, 1)
MEMBERS = (0, 1 << CORE, 1 << X, 1 << X | 1 << CORE)

SMEM = pl.BlockSpec(memory_space=pltpu.SMEM)
ANY = pl.BlockSpec(memory_space=pl.ANY)
VMEM = pl.BlockSpec(memory_space=pltpu.VMEM)


def params(mebibytes=40):
    return pltpu.CompilerParams(vmem_limit_bytes=mebibytes * 1024 * 1024)


def cost(flops, bytes_accessed, transcendentals=0):
    return pl.CostEstimate(
        flops=int(flops), bytes_accessed=int(bytes_accessed), transcendentals=int(transcendentals)
    )


def lanes(index, width):
    return pl.ds(pl.multiple_of(index * width, 128), width)


def dot(a, b, a_dim, b_dim):
    return lax.dot_general(a, b, (((a_dim,), (b_dim,)), ((), ())), preferred_element_type=F32)


def crossed(offset, core):
    change = ((offset >> X) ^ (offset >> Y)) & core
    return offset ^ (change << X | change << Y)


def place():
    prompt = lax.axis_index("prompt")
    device = prompt * lax.axis_size("resp") + lax.axis_index("resp")
    core, x, y = ((device >> bit) & 1 for bit in (CORE, X, Y))
    own, other = jnp.where(core == 0, x, 2 + y), jnp.where(core == 0, 2 + y, x)
    return (own, other, own ^ 1, other ^ 1), core, prompt


def project_kernel(steps, note_ref, other_note_ref, x_ref, other_ref, kw_ref, vw_ref, *rest):
    keep_ref, send_ref, rows_in, weights, sums, sems, row_sems = rest
    heads, core, _ = place()
    width = weights.shape[1] // 2
    chunk = weights.shape[0] // steps
    copies = []
    for step in range(steps):
        span = slice(step * chunk, (step + 1) * chunk)
        for index, source in enumerate((kw_ref, vw_ref)):
            copies.append(
                pltpu.make_async_copy(
                    source.at[span, lanes(core, width)],
                    weights.at[span, index * width : (index + 1) * width],
                    sems.at[len(copies)],
                )
            )
    part = x_ref.shape[0]
    row_copies = [
        pltpu.make_async_copy(source, rows_in.at[at : at + part, :], row_sems.at[index])
        for index, (source, at) in enumerate(((x_ref, 0), (other_ref, part)))
    ]
    for copy in row_copies + copies[:4]:
        copy.start()
    for copy in row_copies:
        copy.wait()
    total = None
    for step in range(steps):
        span = slice(step * chunk, (step + 1) * chunk)
        copies[2 * step].wait()
        copies[2 * step + 1].wait()
        for copy in copies[2 * step + 4 : 2 * step + 6]:
            copy.start()
        product = dot(rows_in[:, span], weights[span, :], 1, 0)
        total = product if step == 0 else total + product
    sums[...] = total.astype(BF16)
    lane = lax.broadcasted_iota(jnp.int32, (NOTE_ROWS, 2 * E), 1)
    row = lax.broadcasted_iota(jnp.int32, (NOTE_ROWS, 2 * E), 0)
    note = jnp.where(
        row < NOTE_ROWS // 4,
        jnp.where(lane < E, note_ref[0], note_ref[1]),
        jnp.where(
            row < NOTE_ROWS // 2,
            note_ref[2],
            jnp.where(
                row < 3 * (NOTE_ROWS // 4),
                jnp.where(lane < E, other_note_ref[0], other_note_ref[1]),
                other_note_ref[2],
            ),
        ),
    )
    note = note.astype(F32).astype(BF16)
    rows = sums.shape[0]
    for out, head in ((keep_ref, heads[0] & 1), (send_ref, heads[2] & 1)):
        out[:rows, :E] = sums[:, lanes(head, E)]
        out[:rows, E:] = sums[:, lanes(head + 2, E)]
        out[rows:, :] = note


def project(note, other_note, prompt_rows, other_rows, key_weight, value_weight, steps=5):
    rows = 2 * prompt_rows.shape[0]
    depth, width = key_weight.shape
    return pl.pallas_call(
        functools.partial(project_kernel, steps),
        out_shape=[jax.ShapeDtypeStruct((rows + NOTE_ROWS, 2 * E), BF16)] * 2,
        in_specs=[SMEM, SMEM] + [ANY] * 4,
        out_specs=[VMEM] * 2,
        scratch_shapes=[
            pltpu.VMEM((rows, depth), BF16),
            pltpu.VMEM((depth, width), BF16),
            pltpu.VMEM((rows, width), BF16),
            pltpu.SemaphoreType.DMA((2 * steps,)),
            pltpu.SemaphoreType.DMA((2,)),
        ],
        compiler_params=params(50),
        cost_estimate=cost(2 * rows * depth * width, 2 * depth * width + 2 * rows * depth),
        name="project_prefix",
    )(note, other_note, prompt_rows, other_rows, key_weight, value_weight)


def pack_kernel(q_ref, g_ref, k_ref, v_ref, *outs):
    heads, _, _ = place()
    for head, out in zip(heads, outs):
        start = 0
        for source in (q_ref, g_ref, k_ref, v_ref):
            width = source.shape[1] // len(outs)
            out[:, start : start + width] = source[:, lanes(head, width)]
            start += width


def pack(queries, out_grad, own_keys, own_values):
    rows = queries.shape[0]
    n = len(MEMBERS)
    width = (2 * queries.shape[1] + 2 * own_keys.shape[1]) // n
    return pl.pallas_call(
        pack_kernel,
        out_shape=[jax.ShapeDtypeStruct((rows, width), BF16)] * n,
        in_specs=[VMEM] * 4,
        out_specs=[VMEM] * n,
        compiler_params=params(62),
        cost_estimate=cost(0, 4 * n * rows * width),
        name="pack_rows",
    )(queries, out_grad, own_keys, own_values)


def unpack_kernel(n, *rest):
    packets, targets = rest[:n], rest[n:]
    heads, _, _ = place()
    for head, packet in zip(heads, packets):
        start = 0
        for target in targets:
            width = target.shape[1] // n
            target[:, lanes(head, width)] = packet[:, start : start + width]
            start += width


def unpack(packets, q_width, kv_width):
    n = len(packets)
    rows = packets[0].shape[0]
    return pl.pallas_call(
        functools.partial(unpack_kernel, n),
        out_shape=[
            jax.ShapeDtypeStruct((rows, width), BF16) for width in (q_width, kv_width, kv_width)
        ],
        in_specs=[VMEM] * n,
        out_specs=[VMEM] * 3,
        compiler_params=params(16),
        cost_estimate=cost(0, 4 * rows * (q_width + 2 * kv_width)),
        name="unpack_rows",
    )(*packets)


def attend_kernel(slots, group, rows, resp_bits, *rest):
    rest = list(rest)

    def take(count):
        taken = rest[:count]
        del rest[:count]
        return taken

    pieces = len(slots)
    n = len(MEMBERS)
    packets = take(n)
    notes = take(2)
    kv_in = take(pieces)
    grads_out = take(n)
    prefix_out = take(pieces)
    keys, values, key_acc, value_acc = rest
    blocks, part, _ = kv_in[0].shape
    _, core, prompt_place = place()

    for index in range(pieces):
        for j in range(blocks):
            prompt, slot = slots[index][j]
            span = slice(slot * part, (slot + 1) * part)
            keys[prompt, span, :] = kv_in[index][j, :, :E]
            values[prompt, span, :] = kv_in[index][j, :, E:]
    key_acc[...] = jnp.zeros_like(key_acc)
    value_acc[...] = jnp.zeros_like(value_acc)

    total_rows = group * rows
    row_in_column = lax.broadcasted_iota(jnp.int32, (total_rows, E), 0) & (rows - 1)
    row_in_lane = lax.broadcasted_iota(jnp.int32, (rows, total_rows), 1) & (rows - 1)
    own_key = lax.broadcasted_iota(jnp.int32, (rows, total_rows), 0)
    lane_row = lax.broadcasted_iota(jnp.int32, (E, total_rows), 1) & (rows - 1)

    def products(j):
        packet = packets[j]
        note = notes[j // 2][2 * part :, :].astype(F32)
        step = NOTE_ROWS // 4
        at = 2 * step * (j % 2)
        boundary, first_at, second_at = (
            jnp.max(block).astype(jnp.int32)
            for block in (
                note[at : at + step, :E],
                note[at : at + step, E:],
                note[at + step : at + 2 * step, E:],
            )
        )
        first_at, second_at = (
            crossed((prompt ^ prompt_place) << resp_bits, core) >> resp_bits
            for prompt in (first_at, second_at)
        )
        heads = [packet[:, h * E : (h + 1) * E] for h in range(2 * group + 2)]
        query = jnp.concatenate(heads[:group], axis=0)
        grad = jnp.concatenate(heads[group : 2 * group], axis=0)
        own_k, own_v = heads[2 * group], heads[2 * group + 1]
        in_first = row_in_column < boundary

        def split(x):
            x = x.astype(F32)
            return jnp.concatenate(
                [jnp.where(in_first, x, 0.0), jnp.where(in_first, 0.0, x)], axis=1
            ).astype(BF16)

        query_pair = split(query)
        grad_pair = split(grad)
        key_pair = jnp.concatenate([keys[first_at], keys[second_at]], axis=1)
        value_pair = jnp.concatenate([values[first_at], values[second_at]], axis=1)

        visible = (own_key <= row_in_lane) & ((own_key >= boundary) == (row_in_lane >= boundary))
        return dict(
            boundary=boundary,
            first_at=first_at,
            second_at=second_at,
            query=query,
            grad=grad,
            own_k=own_k,
            query_pair=query_pair,
            grad_pair=grad_pair,
            key_pair=key_pair,
            scores=dot(key_pair, query_pair, 1, 1),
            own_scores=jnp.where(visible, dot(own_k, query, 1, 1), HIDDEN),
            dprobs=dot(value_pair, grad_pair, 1, 1),
            own_dprobs=dot(own_v, grad, 1, 1),
        )

    def soften(scores, own_scores, dprobs, own_dprobs, **_):
        top = jnp.maximum(
            jnp.max(scores, axis=0, keepdims=True), jnp.max(own_scores, axis=0, keepdims=True)
        )
        weight = jnp.exp2((scores - top) * EXP2_SCALE)
        own_weight = jnp.exp2((own_scores - top) * EXP2_SCALE)
        inverse = 1.0 / (
            jnp.sum(weight, axis=0, keepdims=True) + jnp.sum(own_weight, axis=0, keepdims=True)
        )
        probs = weight * inverse
        own_probs = own_weight * inverse
        probs_low = probs.astype(BF16)
        own_probs_low = own_probs.astype(BF16)
        delta = jnp.sum(probs_low.astype(F32) * dprobs, axis=0, keepdims=True) + jnp.sum(
            own_probs_low.astype(F32) * own_dprobs, axis=0, keepdims=True
        )
        return dict(
            probs_low=probs_low,
            own_probs_low=own_probs_low,
            dscores=(probs * (dprobs - delta)).astype(BF16),
            own_dscores=(own_probs * (own_dprobs - delta)).astype(BF16),
        )

    def gradients(
        grads, boundary, first_at, second_at, query, grad, own_k, query_pair, grad_pair, key_pair,
        probs_low, own_probs_low, dscores, own_dscores, **_
    ):
        key_part = dot(dscores, query_pair, 1, 0)
        value_part = dot(probs_low, grad_pair, 1, 0)
        key_acc[first_at] += key_part[:, :E]
        key_acc[second_at] += key_part[:, E:]
        value_acc[first_at] += value_part[:, :E]
        value_acc[second_at] += value_part[:, E:]

        query_both = dot(key_pair, dscores, 0, 0)
        query_part = jnp.where(lane_row < boundary, query_both[:E], query_both[E:])
        query_part = (query_part + dot(own_k, own_dscores, 0, 0)) * SCALE
        for h in range(group):
            grads[:, h * E : (h + 1) * E] = query_part[:, h * rows : (h + 1) * rows].T.astype(BF16)
        grads[:, group * E : (group + 1) * E] = (dot(own_dscores, query, 1, 0) * SCALE).astype(BF16)
        grads[:, (group + 1) * E :] = dot(own_probs_low, grad, 1, 0).astype(BF16)

    ahead = products(0)
    for j in range(n):
        now = ahead
        if j + 1 < n:
            ahead = products(j + 1)
        gradients(grads_out[j], **now, **soften(**now))

    for index in range(pieces):
        for j in range(blocks):
            prompt, slot = slots[index][j]
            span = slice(slot * part, (slot + 1) * part)
            target = prefix_out[index]
            target[j, :, :E] = (key_acc[prompt, span, :] * SCALE).astype(target.dtype)
            target[j, :, E:] = value_acc[prompt, span, :].astype(target.dtype)


def attend(packets, notes, kv_in, slots, prompts, resp_bits):
    rows, packet_width = packets[0].shape
    group = (packet_width // E - 2) // 2
    sums_shape = (prompts, PLEN, E)
    out_shape = [jax.ShapeDtypeStruct((rows, (group + 2) * E), BF16)] * len(packets)
    out_shape += [
        jax.ShapeDtypeStruct(x.shape, BF16 if 2 * index >= len(kv_in) else F32)
        for index, x in enumerate(kv_in)
    ]
    operands = [*packets, *notes, *kv_in]
    outs = pl.pallas_call(
        functools.partial(attend_kernel, slots, group, rows, resp_bits),
        out_shape=out_shape,
        in_specs=[VMEM] * len(operands),
        out_specs=[VMEM] * len(out_shape),
        scratch_shapes=[pltpu.VMEM(sums_shape, BF16)] * 2 + [pltpu.VMEM(sums_shape, F32)] * 2,
        compiler_params=params(32),
        cost_estimate=cost(
            20 * len(packets) * group * rows * (PLEN + rows) * E, 1 << 24
        ),
        name="attend_head",
    )(*operands)
    return outs[: len(packets)], outs[len(packets) :]


def total_kernel(keep_ref, *rest):
    parts, (own_ref, other_ref, away_ref) = rest[:-3], rest[-3:]
    for j, out in enumerate((own_ref, other_ref, away_ref.at[0], away_ref.at[1])):
        result = keep_ref[j]
        for part in parts:
            result = result + part[j].astype(F32)
        out[...] = result.astype(BF16)


def total(keep, parts):
    _, rows, width = keep.shape
    return pl.pallas_call(
        total_kernel,
        out_shape=[
            jax.ShapeDtypeStruct(shape, BF16)
            for shape in ((rows, width), (rows, width), (2, rows, width))
        ],
        in_specs=[VMEM] * (1 + len(parts)),
        out_specs=[VMEM] * 3,
        compiler_params=params(16),
        cost_estimate=cost(0, 1 << 25),
        name="total_prefix_grads",
    )(keep, *parts)


def prompt_kernel(n, chunk, *rest):
    shares, (kw_ref, vw_ref, out_ref, key_grad, value_grad, out, sems) = rest[:n], rest[n:]
    heads, _, _ = place()
    for head, share in zip(heads, shares):
        key_grad[:, lanes(head, E)] = share[:, :E]
        value_grad[:, lanes(head, E)] = share[:, E:]
    copies = []
    for index in range(kw_ref.shape[0] // chunk):
        span = slice(index * chunk, (index + 1) * chunk)
        turned = dot(kw_ref[span, :], key_grad[...], 1, 1)
        turned = turned + dot(vw_ref[span, :], value_grad[...], 1, 1)
        out[:, span] = turned.T.astype(BF16)
        copies.append(pltpu.make_async_copy(out.at[:, span], out_ref.at[:, span], sems.at[index]))
        copies[-1].start()
    for copy in copies:
        copy.wait()


def prompt_gradient(shares, key_weight, value_weight, chunk=1024):
    n = len(shares)
    rows = shares[0].shape[0]
    depth, width = key_weight.shape
    return pl.pallas_call(
        functools.partial(prompt_kernel, n, chunk),
        out_shape=jax.ShapeDtypeStruct((rows, depth), BF16),
        in_specs=[VMEM] * (n + 2),
        out_specs=ANY,
        scratch_shapes=[pltpu.VMEM((rows, width), BF16)] * 2
        + [pltpu.VMEM((rows, depth), BF16), pltpu.SemaphoreType.DMA((depth // chunk,))],
        compiler_params=params(32),
        cost_estimate=cost(4 * rows * depth * width, 4 * depth * width + 2 * rows * depth),
        name="prompt_gradient",
    )(*shares, key_weight, value_weight)


def per_device(
    n_prompt,
    n_resp,
    prompt_rows,
    key_weight,
    value_weight,
    queries,
    own_keys,
    own_values,
    out_grad,
    first_length,
    resp_prompt,
):
    devices = n_prompt * n_resp
    every_bit = range(devices.bit_length() - 1)
    line_bits = [bit for bit in GATHER_BITS if bit in every_bit]
    line_bits += [bit for bit in every_bit if bit not in (CORE, X, Y, *line_bits)]
    part = prompt_rows.shape[0]

    def fetch(x, offset):
        pairs = [(i ^ crossed(offset, i >> CORE & 1), i) for i in range(devices)]
        return lax.ppermute(x, ("prompt", "resp"), pairs)

    def give(x, offset):
        pairs = [(i, i ^ crossed(offset, i >> CORE & 1)) for i in range(devices)]
        return lax.ppermute(x, ("prompt", "resp"), pairs)

    other_rows = fetch(prompt_rows, MEMBERS[1])
    note = jnp.concatenate([first_length, resp_prompt.reshape(-1)])
    other_note = fetch(note, MEMBERS[1])
    packed = pack(queries, out_grad, own_keys, own_values)
    packed, other_rows = lax.optimization_barrier((packed, other_rows))
    packets = [packed[0], fetch(packed[1], MEMBERS[1]), fetch(packed[2], MEMBERS[2])]
    keep, send = project(note, other_note, prompt_rows, other_rows, key_weight, value_weight)
    send, packets[2] = lax.optimization_barrier((send, packets[2]))
    notes = [keep, fetch(send, MEMBERS[2])]
    notes[1], late = lax.optimization_barrier((notes[1], packed[3]))
    packets.append(fetch(late, MEMBERS[3]))

    pieces = {0: jnp.concatenate([x[: 2 * part] for x in notes]).reshape(len(MEMBERS), part, -1)}
    for bit in line_bits:
        for offset in list(pieces):
            pieces[offset | 1 << bit] = fetch(pieces[offset], 1 << bit)
    line = list(pieces)
    for offset in line:
        piece = pieces[offset]
        if offset == 0:
            piece, packets[3] = lax.optimization_barrier((piece, packets[3]))
        pieces[offset | 1 << Y] = fetch(piece, 1 << Y)

    filled = [0] * n_prompt
    slots = []
    for offset in pieces:
        places = []
        for member in MEMBERS:
            at = (offset ^ member) // n_resp
            places.append((at, filled[at]))
            filled[at] += 1
        slots.append(tuple(places))
    kv_in = list(pieces.values())
    resp_bits = n_resp.bit_length() - 1
    grads, outs = attend(packets, notes, kv_in, tuple(slots), n_prompt, resp_bits)

    sums = dict(zip(line, outs))
    arrived = {o: [give(x, 1 << Y)] for o, x in zip(line, outs[len(line) :])}
    far = sorted(line, reverse=True)[: len(line) // 2]
    ready, grads = lax.optimization_barrier(([arrived[o][0] for o in far], grads))
    for offset, x in zip(far, ready):
        arrived[offset] = [x]
    for bit in reversed(line_bits):
        first = None
        for offset in sorted(sums, reverse=True):
            if offset & 1 << bit:
                piece = sums.pop(offset)
                for x in arrived.pop(offset):
                    piece = piece + x.astype(F32)
                if offset == 1 << bit and first is not None:
                    piece, arrived[first][-1] = lax.optimization_barrier(
                        (piece, arrived[first][-1])
                    )
                arrived[offset ^ 1 << bit].append(give(piece.astype(BF16), 1 << bit))
                first = offset ^ 1 << bit if first is None else first
    back = [grads[0]] + [give(grads[j], MEMBERS[j]) for j in range(1, len(MEMBERS))]
    (own, other, away), back = lax.optimization_barrier((total(sums[0], arrived[0]), back))
    near = give(away, MEMBERS[2])
    shares = [own, give(other, MEMBERS[1]), near[0], give(near[1], MEMBERS[1])]
    unpacked = unpack(back, queries.shape[1], own_keys.shape[1])
    shares, unpacked = lax.optimization_barrier((shares, unpacked))
    query_grad, key_grad, value_grad = unpacked
    prompt_grad = prompt_gradient(shares, key_weight, value_weight)
    return (query_grad, key_grad, value_grad, prompt_grad)


def solution(mesh):
    both = P(("prompt", "resp"), None)
    return jax.shard_map(
        functools.partial(per_device, mesh.shape["prompt"], mesh.shape["resp"]),
        mesh=mesh,
        in_specs=(both, P(), P(), both, both, both, both, P(("prompt", "resp")), both),
        out_specs=(both, both, both, both),
        check_vma=False,
    )
```

time: 79.7 us -> 80.4 us (level)
  waiting for transfers between devices: 35.2 us -> 30.2 us
  starting transfers between devices: 21.2 us -> 26 us
    ppermute x26, waiting for transfers between devices: 35.2 us -> 30.2 us  [the longest x13 16.1 us: fetch(): return lax.ppermute(x, ('prompt', 'resp'), pairs)]
    ppermute x26, starting transfers between devices: 21.2 us -> 26 us  [the longest x13 15 us: fetch(): return lax.ppermute(x, ('prompt', 'resp'), pairs)]
    pallas_call x5 -> x4, Pallas kernels: 15.2 us -> 15.6 us  [the longest x1 7.74 us: attend(): pl.pallas_call(functools.partial(attend_kernel, slots, group, rows, resp_...]
  transfers between devices with their start and end apart: 26 -> 26, of which waited for: 14 -> 14; matrix products, arithmetic and copies ran while one was open for 0% -> 1% of each run, Pallas kernels for 9% -> 11%
where the time goes in v7:
time: 80.4 us; the launch traced here: 80.1 us
  waiting for transfers between devices  30.2 us (38%)
  starting transfers between devices  26 us (32%)
  Pallas kernels  20.3 us (25%)
  between operations  1.62 us (2%)
  local copies, waits for them, and re-layouts  1.14 us (1%)
  other arithmetic  0.85 us (1%)
    ppermute x13, waiting for transfers between devices, fetch(): return lax.ppermute(x, ('prompt', 'resp'), pairs)  16.1 us
    ppermute x13, starting transfers between devices, fetch(): return lax.ppermute(x, ('prompt', 'resp'), pairs)  15 us
    ppermute x13, waiting for transfers between devices, give(): return lax.ppermute(x, ('prompt', 'resp'), pairs)  14 us
    ppermute x13, starting transfers between devices, give(): return lax.ppermute(x, ('prompt', 'resp'), pairs)  11.1 us
    pallas_call x1, Pallas kernels, attend(): pl.pallas_call(functools.partial(attend_kernel, slots, group, rows, resp_...  7.74 us
    pallas_call x1, Pallas kernels, project(): pl.pallas_call(functools.partial(project_kernel, steps), out_shape=[jax.S...  5.16 us
    pallas_call x1, Pallas kernels, prompt_gradient(): pl.pallas_call(functools.partial(prompt_kernel, n, chunk), out_shape=jax....  3.68 us
    pallas_call x1, Pallas kernels, pack(): pl.pallas_call(pack_kernel, out_shape=[jax.ShapeDtypeStruct((rows, width)...  2.63 us
  transfers between devices with their start and end apart: 26, of which 14 were waited for; matrix products, arithmetic and copies ran while one was open for 1% of the time, Pallas kernels for 11%

profile of v7, /device:TPU:0, one launch (start us, length us, event | category | flops | bytes accessed | tf_op | source)
XLA Modules:
  0.0 80.1 jit_solution(17964399937428271952)
XLA Ops:
  1.1 2.6 %pack_rows.1 = (bf16[128,1536]{1,0:T(8,128)(2,1)}, bf16[128,1536]{1,0:T(8,128)(2,1)}, bf16[128,1536]{1,0:T(8,128)(2,1)}, bf16[128,1536]{1,0:T(8,128)(2,1)}) custom-call(bf16[128,2560]{1,0:T(8,128)(2,1)} %q_ref.1, bf16[128,2560]{1,0:T(8,128)(2,1)} %g_ref.1, bf16[128,512]{1,0:T(8,128)(2,1)} %k_ref.1, bf16[128,512]{1,0:T(8,128)(2,1)} %v_ref.1), custom_call_target="tpu_custom_call" | custom-call | bytes 3145728 | tf_op jit(solution)/shard_map/pack_rows/pallas_call | solution.py:152
  3.8 2.5 %collective-permute-start.3 = (bf16[128,1536]{1,0:T(8,128)(2,1)}, bf16[128,1536]{1,0:T(8,128)(2,1)S(1)}, u32[]{:S(2)}, u32[]{:S(2)}) collective-permute-start(bf16[128,1536]{1,0:T(8,128)(2,1)} %get-tuple-element.69), channel_id=1, source_target_pairs={{8,0},{17,1},{10,2},{19,3},{12,4},{21,5},{14,6},{23,7},{0,8},{25,9... | collective-permute-start | bytes 1179656 | tf_op jit(solution)/shard_map/ppermute | solution.py:439
  9.9 5.2 %project_prefix.1 = (bf16[160,256]{1,0:T(8,128)(2,1)S(1)}, bf16[160,256]{1,0:T(8,128)(2,1)S(1)}) custom-call(s32[3]{0:T(128)S(1)} %pad_add_fusion.note_ref, s32[3]{0:T(128)S(1)} %collective-permute-done.2.other_note_ref, bf16[64,5120]{1,0:T(8,128)(2,1)S(1)} %copy-done, bf16[64,5120]{1,0:T(8,128)(2,1)S(1)} %collective-permute-done.other_ref, ...), custom_call_target="tpu_custom_call" | custom-call | flops 671088640 | bytes 6553600 | tf_op jit(solution)/shard_map/project_prefix/pallas_call | solution.py:120
  15.1 1.5 %collective-permute-start.4 = (bf16[160,256]{1,0:T(8,128)(2,1)S(1)}, bf16[160,256]{1,0:T(8,128)(2,1)S(1)}, u32[]{:S(2)}, u32[]{:S(2)}) collective-permute-start(bf16[160,256]{1,0:T(8,128)(2,1)S(1)} %get-tuple-element.72), channel_id=1, source_target_pairs={{8,0},{17,1},{10,2},{19,3},{12,4},{21,5},{14,6},{23,7},{0,8},{25,9... | collective-permute-start | bytes 245768 | tf_op jit(solution)/shard_map/ppermute | solution.py:439
  16.6 3.0 %collective-permute-done.4.rest_5_ = bf16[160,256]{1,0:T(8,128)(2,1)S(1)} collective-permute-done((bf16[160,256]{1,0:T(8,128)(2,1)S(1)}, bf16[160,256]{1,0:T(8,128)(2,1)S(1)}, u32[]{:S(2)}, u32[]{:S(2)}) %collective-permute-start.4) | collective-permute-done | bytes 81952 | tf_op jit(solution)/shard_map/ppermute | solution.py:439
  20.1 2.7 %collective-permute-start.6 = (bf16[4,64,256]{2,1,0:T(8,128)(2,1)S(1)}, bf16[4,64,256]{2,1,0:T(8,128)(2,1)S(1)}, u32[]{:S(2)}, u32[]{:S(2)}) collective-permute-start(bf16[4,64,256]{2,1,0:T(8,128)(2,1)S(1)} %bitcast.10), channel_id=1, source_target_pairs={{4,0},{5,1},{6,2},{7,3},{0,4},{1,5},{2,6},{3,7},{12,8},{13,9},{14,... | collective-permute-start | bytes 393224 | tf_op jit(solution)/shard_map/ppermute | solution.py:439
  23.6 1.6 %collective-permute-start.7 = (bf16[4,64,256]{2,1,0:T(8,128)(2,1)S(1)}, bf16[4,64,256]{2,1,0:T(8,128)(2,1)S(1)}, u32[]{:S(2)}, u32[]{:S(2)}) collective-permute-start(bf16[4,64,256]{2,1,0:T(8,128)(2,1)S(1)} %bitcast.11), channel_id=1, source_target_pairs={{2,0},{3,1},{0,2},{1,3},{6,4},{7,5},{4,6},{5,7},{10,8},{11,9},{8,1... | collective-permute-start | bytes 393224 | tf_op jit(solution)/shard_map/ppermute | solution.py:439
  25.2 5.1 %collective-permute-done.6.rest_7_ = bf16[4,64,256]{2,1,0:T(8,128)(2,1)S(1)} collective-permute-done((bf16[4,64,256]{2,1,0:T(8,128)(2,1)S(1)}, bf16[4,64,256]{2,1,0:T(8,128)(2,1)S(1)}, u32[]{:S(2)}, u32[]{:S(2)}) %collective-permute-start.6) | collective-permute-done | bytes 131104 | tf_op jit(solution)/shard_map/ppermute | solution.py:439
  33.0 2.8 %collective-permute-done.8.rest_9_ = bf16[4,64,256]{2,1,0:T(8,128)(2,1)S(1)} collective-permute-done((bf16[4,64,256]{2,1,0:T(8,128)(2,1)S(1)}, bf16[4,64,256]{2,1,0:T(8,128)(2,1)S(1)}, u32[]{:S(2)}, u32[]{:S(2)}) %collective-permute-start.8) | collective-permute-done | bytes 131104 | tf_op jit(solution)/shard_map/ppermute | solution.py:439
  36.2 1.5 %collective-permute-start.9 = (bf16[4,64,256]{2,1,0:T(8,128)(2,1)S(1)}, bf16[4,64,256]{2,1,0:T(8,128)(2,1)S(1)}, u32[]{:S(2)}, u32[]{:S(2)}) collective-permute-start(bf16[4,64,256]{2,1,0:T(8,128)(2,1)S(1)} %bitcast.12), channel_id=1, source_target_pairs={{16,0},{9,1},{18,2},{11,3},{20,4},{13,5},{22,6},{15,7},{24,8},{1,9... | collective-permute-start | bytes 393224 | tf_op jit(solution)/shard_map/ppermute | solution.py:439
  37.8 2.9 %collective-permute-done.12.rest_13_ = bf16[4,64,256]{2,1,0:T(8,128)(2,1)S(1)} collective-permute-done((bf16[4,64,256]{2,1,0:T(8,128)(2,1)S(1)}, bf16[4,64,256]{2,1,0:T(8,128)(2,1)S(1)}, u32[]{:S(2)}, u32[]{:S(2)}) %collective-permute-start.12) | collective-permute-done | bytes 131104 | tf_op jit(solution)/shard_map/ppermute | solution.py:439
  40.7 1.4 %collective-permute-done.9.rest_10_ = bf16[4,64,256]{2,1,0:T(8,128)(2,1)S(1)} collective-permute-done((bf16[4,64,256]{2,1,0:T(8,128)(2,1)S(1)}, bf16[4,64,256]{2,1,0:T(8,128)(2,1)S(1)}, u32[]{:S(2)}, u32[]{:S(2)}) %collective-permute-start.9) | collective-permute-done | bytes 131104 | tf_op jit(solution)/shard_map/ppermute | solution.py:439
  42.1 7.7 %attend_head.1 = (bf16[128,896]{1,0:T(8,128)(2,1)S(1)}, bf16[128,896]{1,0:T(8,128)(2,1)S(1)}, bf16[128,896]{1,0:T(8,128)(2,1)S(1)}, bf16[128,896]{1,0:T(8,128)(2...) custom-call(bf16[128,1536]{1,0:T(8,128)(2,1)S(1)} %copy-done.1, ...), custom_call_target="tpu_custom_call" | custom-call | flops 4194304000 | bytes 16777216 | tf_op jit(solution)/shard_map/attend_head/pallas_call | solution.py:343
  50.6 1.4 %collective-permute-start.16 = (bf16[4,64,256]{2,1,0:T(8,128)(2,1)S(1)}, bf16[4,64,256]{2,1,0:T(8,128)(2,1)S(1)}, u32[]{:S(2)}, u32[]{:S(2)}) collective-permute-start(bf16[4,64,256]{2,1,0:T(8,128)(2,1)S(1)} %get-tuple-element.84), channel_id=1, source_target_pairs={{0,16},{1,9},{2,18},{3,11},{4,20},{5,13},{6,22},{7,15},{8,24},{9,1... | collective-permute-start | bytes 393224 | tf_op jit(solution)/shard_map/ppermute | solution.py:443
  52.6 1.4 %collective-permute-start.14 = (bf16[4,64,256]{2,1,0:T(8,128)(2,1)S(1)}, bf16[4,64,256]{2,1,0:T(8,128)(2,1)S(1)}, u32[]{:S(2)}, u32[]{:S(2)}) collective-permute-start(bf16[4,64,256]{2,1,0:T(8,128)(2,1)S(1)} %get-tuple-element.81), channel_id=1, source_target_pairs={{0,16},{1,9},{2,18},{3,11},{4,20},{5,13},{6,22},{7,15},{8,24},{9,1... | collective-permute-start | bytes 393224 | tf_op jit(solution)/shard_map/ppermute | solution.py:443
  54.9 1.4 %collective-permute-done.16 = bf16[4,64,256]{2,1,0:T(8,128)(2,1)S(1)} collective-permute-done((bf16[4,64,256]{2,1,0:T(8,128)(2,1)S(1)}, bf16[4,64,256]{2,1,0:T(8,128)(2,1)S(1)}, u32[]{:S(2)}, u32[]{:S(2)}) %collective-permute-start.16) | collective-permute-done | bytes 131104 | tf_op jit(solution)/shard_map/ppermute | solution.py:443
  57.8 1.3 %collective-permute-done.14 = bf16[4,64,256]{2,1,0:T(8,128)(2,1)S(1)} collective-permute-done((bf16[4,64,256]{2,1,0:T(8,128)(2,1)S(1)}, bf16[4,64,256]{2,1,0:T(8,128)(2,1)S(1)}, u32[]{:S(2)}, u32[]{:S(2)}) %collective-permute-start.14) | collective-permute-done | bytes 131104 | tf_op jit(solution)/shard_map/ppermute | solution.py:443
  59.2 2.2 %collective-permute-done.17 = bf16[4,64,256]{2,1,0:T(8,128)(2,1)S(1)} collective-permute-done((bf16[4,64,256]{2,1,0:T(8,128)(2,1)S(1)}, bf16[4,64,256]{2,1,0:T(8,128)(2,1)S(1)}, u32[]{:S(2)}, u32[]{:S(2)}) %collective-permute-start.17) | collective-permute-done | bytes 131104 | tf_op jit(solution)/shard_map/ppermute | solution.py:443
  62.2 3.4 %collective-permute-start.19 = (bf16[4,64,256]{2,1,0:T(8,128)(2,1)S(1)}, bf16[4,64,256]{2,1,0:T(8,128)(2,1)S(1)}, u32[]{:S(2)}, u32[]{:S(2)}) collective-permute-start(bf16[4,64,256]{2,1,0:T(8,128)(2,1)S(1)} %add_convert_fusion), channel_id=1, source_target_pairs={{0,4},{1,5},{2,6},{3,7},{4,0},{5,1},{6,2},{7,3},{8,12},{9,13},{10,... | collective-permute-start | bytes 393224 | tf_op jit(solution)/shard_map/ppermute | solution.py:443
  65.6 2.6 %collective-permute-done.18.rest_1_ = bf16[4,64,256]{2,1,0:T(8,128)(2,1)S(1)} collective-permute-done((bf16[4,64,256]{2,1,0:T(8,128)(2,1)S(1)}, bf16[4,64,256]{2,1,0:T(8,128)(2,1)S(1)}, u32[]{:S(2)}, u32[]{:S(2)}) %collective-permute-start.18) | collective-permute-done | bytes 131104 | tf_op jit(solution)/shard_map/ppermute | solution.py:443
  68.2 2.4 %collective-permute-done.19.rest_2_ = bf16[4,64,256]{2,1,0:T(8,128)(2,1)S(1)} collective-permute-done((bf16[4,64,256]{2,1,0:T(8,128)(2,1)S(1)}, bf16[4,64,256]{2,1,0:T(8,128)(2,1)S(1)}, u32[]{:S(2)}, u32[]{:S(2)}) %collective-permute-start.19) | collective-permute-done | bytes 131104 | tf_op jit(solution)/shard_map/ppermute | solution.py:443
  70.7 1.3 %collective-permute-start.24 = (bf16[2,64,256]{2,1,0:T(8,128)(2,1)S(1)}, bf16[2,64,256]{2,1,0:T(8,128)(2,1)S(1)}, u32[]{:S(2)}, u32[]{:S(2)}) collective-permute-start(bf16[2,64,256]{2,1,0:T(8,128)(2,1)S(1)} %get-tuple-element.103), channel_id=1, source_target_pairs={{0,8},{1,17},{2,10},{3,19},{4,12},{5,21},{6,14},{7,23},{8,0},{9,25... | collective-permute-start | bytes 196616 | tf_op jit(solution)/shard_map/ppermute | solution.py:443
  72.0 3.0 %collective-permute-done.24 = bf16[2,64,256]{2,1,0:T(8,128)(2,1)S(1)} collective-permute-done((bf16[2,64,256]{2,1,0:T(8,128)(2,1)S(1)}, bf16[2,64,256]{2,1,0:T(8,128)(2,1)S(1)}, u32[]{:S(2)}, u32[]{:S(2)}) %collective-permute-start.24) | collective-permute-done | bytes 65568 | tf_op jit(solution)/shard_map/ppermute | solution.py:443
  76.3 3.7 %prompt_gradient.1 = bf16[64,5120]{1,0:T(8,128)(2,1)} custom-call(bf16[64,256]{1,0:T(8,128)(2,1)S(1)} %get-tuple-element.114.rest_0_, bf16[64,256]{1,0:T(8,128)(2,1)S(1)} %collective-permute-done.23.rest_1_, bf16[64,256]{1,0:T(8,128)(2,1)S(1)} %get-tuple-element.116.rest_2_, bf16[64,256]{1,0:T(8,128)(2,1)S(1)} %collective-permute-done.25.rest_3_, ...), custom_call_target="tpu_custom_call" | custom-call | flops 671088640 | bytes 11141120 | tf_op jit(solution)/shard_map/prompt_gradient/pallas_call | solution.py:405
  (60 shorter events, 13.8 us)
Async XLA Ops:
  0.6 3.2 %collective-permute-start = (bf16[64,5120]{1,0:T(8,128)(2,1)}, bf16[64,5120]{1,0:T(8,128)(2,1)S(1)}, u32[]{:S(2)}, u32[]{:S(2)}) collective-permute-start(bf16[64,5120]{1,0:T(8,128)(2,1)} %x_ref.1), channel_id=1, source_target_pairs={{1,0},{0,1},{3,2},{2,3},{5,4},{4,5},{7,6},{6,7},{9,8},{8,9},{11,10... | collective-permute-start | bytes 1966088 | tf_op jit(solution)/shard_map/ppermute | solution.py:439
  3.8 11.3 %collective-permute-start.3 = (bf16[128,1536]{1,0:T(8,128)(2,1)}, bf16[128,1536]{1,0:T(8,128)(2,1)S(1)}, u32[]{:S(2)}, u32[]{:S(2)}) collective-permute-start(bf16[128,1536]{1,0:T(8,128)(2,1)} %get-tuple-element.69), channel_id=1, source_target_pairs={{8,0},{17,1},{10,2},{19,3},{12,4},{21,5},{14,6},{23,7},{0,8},{25,9... | collective-permute-start | bytes 1179656 | tf_op jit(solution)/shard_map/ppermute | solution.py:439
  15.1 4.5 %collective-permute-start.4 = (bf16[160,256]{1,0:T(8,128)(2,1)S(1)}, bf16[160,256]{1,0:T(8,128)(2,1)S(1)}, u32[]{:S(2)}, u32[]{:S(2)}) collective-permute-start(bf16[160,256]{1,0:T(8,128)(2,1)S(1)} %get-tuple-element.72), channel_id=1, source_target_pairs={{8,0},{17,1},{10,2},{19,3},{12,4},{21,5},{14,6},{23,7},{0,8},{25,9... | collective-permute-start | bytes 245768 | tf_op jit(solution)/shard_map/ppermute | solution.py:439
  19.6 16.7 %collective-permute-start.5 = (bf16[128,1536]{1,0:T(8,128)(2,1)S(1)}, bf16[128,1536]{1,0:T(8,128)(2,1)S(1)}, u32[]{:S(2)}, u32[]{:S(2)}) collective-permute-start(bf16[128,1536]{1,0:T(8,128)(2,1)S(1)} %copy-done.3), channel_id=1, source_target_pairs={{9,0},{16,1},{11,2},{18,3},{13,4},{20,5},{15,6},{22,7},{1,8},{24,9... | collective-permute-start | bytes 1179656 | tf_op jit(solution)/shard_map/ppermute | solution.py:439
  20.1 10.1 %collective-permute-start.6 = (bf16[4,64,256]{2,1,0:T(8,128)(2,1)S(1)}, bf16[4,64,256]{2,1,0:T(8,128)(2,1)S(1)}, u32[]{:S(2)}, u32[]{:S(2)}) collective-permute-start(bf16[4,64,256]{2,1,0:T(8,128)(2,1)S(1)} %bitcast.10), channel_id=1, source_target_pairs={{4,0},{5,1},{6,2},{7,3},{0,4},{1,5},{2,6},{3,7},{12,8},{13,9},{14,... | collective-permute-start | bytes 393224 | tf_op jit(solution)/shard_map/ppermute | solution.py:439
  22.8 15.0 %collective-permute-start.1 = (bf16[128,1536]{1,0:T(8,128)(2,1)S(1)}, bf16[128,1536]{1,0:T(8,128)(2,1)S(1)}, u32[]{:S(2)}, u32[]{:S(2)}) collective-permute-start(bf16[128,1536]{1,0:T(8,128)(2,1)S(1)} %copy-done.2), channel_id=1, source_target_pairs={{1,0},{0,1},{3,2},{2,3},{5,4},{4,5},{7,6},{6,7},{9,8},{8,9},{11,10... | collective-permute-start | bytes 1179656 | tf_op jit(solution)/shard_map/ppermute | solution.py:439
  23.6 8.1 %collective-permute-start.7 = (bf16[4,64,256]{2,1,0:T(8,128)(2,1)S(1)}, bf16[4,64,256]{2,1,0:T(8,128)(2,1)S(1)}, u32[]{:S(2)}, u32[]{:S(2)}) collective-permute-start(bf16[4,64,256]{2,1,0:T(8,128)(2,1)S(1)} %bitcast.11), channel_id=1, source_target_pairs={{2,0},{3,1},{0,2},{1,3},{6,4},{7,5},{4,6},{5,7},{10,8},{11,9},{8,1... | collective-permute-start | bytes 393224 | tf_op jit(solution)/shard_map/ppermute | solution.py:439
  30.3 5.5 %collective-permute-start.8 = (bf16[4,64,256]{2,1,0:T(8,128)(2,1)S(1)}, bf16[4,64,256]{2,1,0:T(8,128)(2,1)S(1)}, u32[]{:S(2)}, u32[]{:S(2)}) collective-permute-start(bf16[4,64,256]{2,1,0:T(8,128)(2,1)S(1)} %collective-permute-done.6.rest_7_), channel_id=1, source_target_pairs={{2,0},{3,1},{0,2},{1,3},{6,4},{7,5},{4,6},{5,7},{10,8},{11,9},{8,1... | collective-permute-start | bytes 393224 | tf_op jit(solution)/shard_map/ppermute | solution.py:439
  31.0 6.8 %collective-permute-start.10 = (bf16[4,64,256]{2,1,0:T(8,128)(2,1)S(1)}, bf16[4,64,256]{2,1,0:T(8,128)(2,1)S(1)}, u32[]{:S(2)}, u32[]{:S(2)}) collective-permute-start(bf16[4,64,256]{2,1,0:T(8,128)(2,1)S(1)} %collective-permute-done.6.rest_7_), channel_id=1, source_target_pairs={{16,0},{9,1},{18,2},{11,3},{20,4},{13,5},{22,6},{15,7},{24,8},{1,9... | collective-permute-start | bytes 393224 | tf_op jit(solution)/shard_map/ppermute | solution.py:439
  31.7 6.1 %collective-permute-start.11 = (bf16[4,64,256]{2,1,0:T(8,128)(2,1)S(1)}, bf16[4,64,256]{2,1,0:T(8,128)(2,1)S(1)}, u32[]{:S(2)}, u32[]{:S(2)}) collective-permute-start(bf16[4,64,256]{2,1,0:T(8,128)(2,1)S(1)} %collective-permute-done.7.rest_8_), channel_id=1, source_target_pairs={{16,0},{9,1},{18,2},{11,3},{20,4},{13,5},{22,6},{15,7},{24,8},{1,9... | collective-permute-start | bytes 393224 | tf_op jit(solution)/shard_map/ppermute | solution.py:439
  35.8 5.0 %collective-permute-start.12 = (bf16[4,64,256]{2,1,0:T(8,128)(2,1)S(1)}, bf16[4,64,256]{2,1,0:T(8,128)(2,1)S(1)}, u32[]{:S(2)}, u32[]{:S(2)}) collective-permute-start(bf16[4,64,256]{2,1,0:T(8,128)(2,1)S(1)} %collective-permute-done.8.rest_9_), channel_id=1, source_target_pairs={{16,0},{9,1},{18,2},{11,3},{20,4},{13,5},{22,6},{15,7},{24,8},{1,9... | collective-permute-start | bytes 393224 | tf_op jit(solution)/shard_map/ppermute | solution.py:439
  36.2 5.9 %collective-permute-start.9 = (bf16[4,64,256]{2,1,0:T(8,128)(2,1)S(1)}, bf16[4,64,256]{2,1,0:T(8,128)(2,1)S(1)}, u32[]{:S(2)}, u32[]{:S(2)}) collective-permute-start(bf16[4,64,256]{2,1,0:T(8,128)(2,1)S(1)} %bitcast.12), channel_id=1, source_target_pairs={{16,0},{9,1},{18,2},{11,3},{20,4},{13,5},{22,6},{15,7},{24,8},{1,9... | collective-permute-start | bytes 393224 | tf_op jit(solution)/shard_map/ppermute | solution.py:439
  49.9 5.0 %collective-permute-start.15 = (bf16[4,64,256]{2,1,0:T(8,128)(2,1)S(1)}, bf16[4,64,256]{2,1,0:T(8,128)(2,1)S(1)}, u32[]{:S(2)}, u32[]{:S(2)}) collective-permute-start(bf16[4,64,256]{2,1,0:T(8,128)(2,1)S(1)} %get-tuple-element.83), channel_id=1, source_target_pairs={{0,16},{1,9},{2,18},{3,11},{4,20},{5,13},{6,22},{7,15},{8,24},{9,1... | collective-permute-start | bytes 393224 | tf_op jit(solution)/shard_map/ppermute | solution.py:443
  50.6 5.7 %collective-permute-start.16 = (bf16[4,64,256]{2,1,0:T(8,128)(2,1)S(1)}, bf16[4,64,256]{2,1,0:T(8,128)(2,1)S(1)}, u32[]{:S(2)}, u32[]{:S(2)}) collective-permute-start(bf16[4,64,256]{2,1,0:T(8,128)(2,1)S(1)} %get-tuple-element.84), channel_id=1, source_target_pairs={{0,16},{1,9},{2,18},{3,11},{4,20},{5,13},{6,22},{7,15},{8,24},{9,1... | collective-permute-start | bytes 393224 | tf_op jit(solution)/shard_map/ppermute | solution.py:443
  52.0 10.2 %collective-permute-start.13 = (bf16[4,64,256]{2,1,0:T(8,128)(2,1)S(1)}, bf16[4,64,256]{2,1,0:T(8,128)(2,1)S(1)}, u32[]{:S(2)}, u32[]{:S(2)}) collective-permute-start(bf16[4,64,256]{2,1,0:T(8,128)(2,1)S(1)} %get-tuple-element.79), channel_id=1, source_target_pairs={{0,16},{1,9},{2,18},{3,11},{4,20},{5,13},{6,22},{7,15},{8,24},{9,1... | collective-permute-start | bytes 393224 | tf_op jit(solution)/shard_map/ppermute | solution.py:443
  52.6 6.5 %collective-permute-start.14 = (bf16[4,64,256]{2,1,0:T(8,128)(2,1)S(1)}, bf16[4,64,256]{2,1,0:T(8,128)(2,1)S(1)}, u32[]{:S(2)}, u32[]{:S(2)}) collective-permute-start(bf16[4,64,256]{2,1,0:T(8,128)(2,1)S(1)} %get-tuple-element.81), channel_id=1, source_target_pairs={{0,16},{1,9},{2,18},{3,11},{4,20},{5,13},{6,22},{7,15},{8,24},{9,1... | collective-permute-start | bytes 393224 | tf_op jit(solution)/shard_map/ppermute | solution.py:443
  56.3 5.0 %collective-permute-start.17 = (bf16[4,64,256]{2,1,0:T(8,128)(2,1)S(1)}, bf16[4,64,256]{2,1,0:T(8,128)(2,1)S(1)}, u32[]{:S(2)}, u32[]{:S(2)}) collective-permute-start(bf16[4,64,256]{2,1,0:T(8,128)(2,1)S(1)} %add_convert_fusion.1), channel_id=1, source_target_pairs={{0,2},{1,3},{2,0},{3,1},{4,6},{5,7},{6,4},{7,5},{8,10},{9,11},{10,... | collective-permute-start | bytes 393224 | tf_op jit(solution)/shard_map/ppermute | solution.py:443
  57.1 13.5 %collective-permute-start.20 = (bf16[128,896]{1,0:T(8,128)(2,1)S(1)}, bf16[128,896]{1,0:T(8,128)(2,1)S(1)}, u32[]{:S(2)}, u32[]{:S(2)}) collective-permute-start(bf16[128,896]{1,0:T(8,128)(2,1)S(1)} %get-tuple-element.98), channel_id=1, source_target_pairs={{0,1},{1,0},{2,3},{3,2},{4,5},{5,4},{6,7},{7,6},{8,9},{9,8},{10,11... | collective-permute-start | bytes 688136 | tf_op jit(solution)/shard_map/ppermute | solution.py:443
  57.1 13.5 %collective-permute-start.21 = (bf16[128,896]{1,0:T(8,128)(2,1)S(1)}, bf16[128,896]{1,0:T(8,128)(2,1)S(1)}, u32[]{:S(2)}, u32[]{:S(2)}) collective-permute-start(bf16[128,896]{1,0:T(8,128)(2,1)S(1)} %get-tuple-element.99), channel_id=1, source_target_pairs={{0,8},{1,17},{2,10},{3,19},{4,12},{5,21},{6,14},{7,23},{8,0},{9,25... | collective-permute-start | bytes 688136 | tf_op jit(solution)/shard_map/ppermute | solution.py:443
  59.1 11.5 %collective-permute-start.22 = (bf16[128,896]{1,0:T(8,128)(2,1)S(1)}, bf16[128,896]{1,0:T(8,128)(2,1)S(1)}, u32[]{:S(2)}, u32[]{:S(2)}) collective-permute-start(bf16[128,896]{1,0:T(8,128)(2,1)S(1)} %get-tuple-element.100), channel_id=1, source_target_pairs={{0,9},{1,16},{2,11},{3,18},{4,13},{5,20},{6,15},{7,22},{8,1},{9,24... | collective-permute-start | bytes 688136 | tf_op jit(solution)/shard_map/ppermute | solution.py:443
  61.4 6.8 %collective-permute-start.18 = (bf16[4,64,256]{2,1,0:T(8,128)(2,1)S(1)}, bf16[4,64,256]{2,1,0:T(8,128)(2,1)S(1)}, u32[]{:S(2)}, u32[]{:S(2)}) collective-permute-start(bf16[4,64,256]{2,1,0:T(8,128)(2,1)S(1)} %convert_add_fusion), channel_id=1, source_target_pairs={{0,2},{1,3},{2,0},{3,1},{4,6},{5,7},{6,4},{7,5},{8,10},{9,11},{10,... | collective-permute-start | bytes 393224 | tf_op jit(solution)/shard_map/ppermute | solution.py:443
  62.2 8.4 %collective-permute-start.19 = (bf16[4,64,256]{2,1,0:T(8,128)(2,1)S(1)}, bf16[4,64,256]{2,1,0:T(8,128)(2,1)S(1)}, u32[]{:S(2)}, u32[]{:S(2)}) collective-permute-start(bf16[4,64,256]{2,1,0:T(8,128)(2,1)S(1)} %add_convert_fusion), channel_id=1, source_target_pairs={{0,4},{1,5},{2,6},{3,7},{4,0},{5,1},{6,2},{7,3},{8,12},{9,13},{10,... | collective-permute-start | bytes 393224 | tf_op jit(solution)/shard_map/ppermute | solution.py:443
  70.7 4.3 %collective-permute-start.24 = (bf16[2,64,256]{2,1,0:T(8,128)(2,1)S(1)}, bf16[2,64,256]{2,1,0:T(8,128)(2,1)S(1)}, u32[]{:S(2)}, u32[]{:S(2)}) collective-permute-start(bf16[2,64,256]{2,1,0:T(8,128)(2,1)S(1)} %get-tuple-element.103), channel_id=1, source_target_pairs={{0,8},{1,17},{2,10},{3,19},{4,12},{5,21},{6,14},{7,23},{8,0},{9,25... | collective-permute-start | bytes 196616 | tf_op jit(solution)/shard_map/ppermute | solution.py:443
  72.0 4.1 %collective-permute-start.23 = (bf16[64,256]{1,0:T(8,128)(2,1)S(1)}, bf16[64,256]{1,0:T(8,128)(2,1)S(1)}, u32[]{:S(2)}, u32[]{:S(2)}) collective-permute-start(bf16[64,256]{1,0:T(8,128)(2,1)S(1)} %get-tuple-element.102), channel_id=1, source_target_pairs={{0,1},{1,0},{2,3},{3,2},{4,5},{5,4},{6,7},{7,6},{8,9},{9,8},{10,11... | collective-permute-start | bytes 98312 | tf_op jit(solution)/shard_map/ppermute | solution.py:443
  (10 other events, 282.7 us)

commit v8 on v7

--- a/solution.py
+++ b/solution.py
@@ -15,7 +15,7 @@
 HIDDEN = -1e30
 BF16 = jnp.bfloat16
 F32 = jnp.float32
-NOTE_ROWS = 32
+NOTE_ROWS = 16
 CORE, X, Y = 0, 3, 4
 GATHER_BITS = (2, 1)
 MEMBERS = (0, 1 << CORE, 1 << X, 1 << X | 1 << CORE)
@@ -56,7 +56,7 @@
     return (own, other, own ^ 1, other ^ 1), core, prompt
 
 
-def project_kernel(steps, note_ref, other_note_ref, x_ref, other_ref, kw_ref, vw_ref, *rest):
+def project_kernel(steps, x_ref, other_ref, kw_ref, vw_ref, *rest):
     keep_ref, send_ref, rows_in, weights, sums, sems, row_sems = rest
     heads, core, _ = place()
     width = weights.shape[1] // 2
@@ -77,7 +77,7 @@
         pltpu.make_async_copy(source, rows_in.at[at : at + part, :], row_sems.at[index])
         for index, (source, at) in enumerate(((x_ref, 0), (other_ref, part)))
     ]
-    for copy in row_copies + copies[:4]:
+    for copy in row_copies + copies[:8]:
         copy.start()
     for copy in row_copies:
         copy.wait()
@@ -86,41 +86,23 @@
         span = slice(step * chunk, (step + 1) * chunk)
         copies[2 * step].wait()
         copies[2 * step + 1].wait()
-        for copy in copies[2 * step + 4 : 2 * step + 6]:
+        for copy in copies[2 * step + 8 : 2 * step + 10]:
             copy.start()
         product = dot(rows_in[:, span], weights[span, :], 1, 0)
         total = product if step == 0 else total + product
     sums[...] = total.astype(BF16)
-    lane = lax.broadcasted_iota(jnp.int32, (NOTE_ROWS, 2 * E), 1)
-    row = lax.broadcasted_iota(jnp.int32, (NOTE_ROWS, 2 * E), 0)
-    note = jnp.where(
-        row < NOTE_ROWS // 4,
-        jnp.where(lane < E, note_ref[0], note_ref[1]),
-        jnp.where(
-            row < NOTE_ROWS // 2,
-            note_ref[2],
-            jnp.where(
-                row < 3 * (NOTE_ROWS // 4),
-                jnp.where(lane < E, other_note_ref[0], other_note_ref[1]),
-                other_note_ref[2],
-            ),
-        ),
-    )
-    note = note.astype(F32).astype(BF16)
-    rows = sums.shape[0]
     for out, head in ((keep_ref, heads[0] & 1), (send_ref, heads[2] & 1)):
-        out[:rows, :E] = sums[:, lanes(head, E)]
-        out[:rows, E:] = sums[:, lanes(head + 2, E)]
-        out[rows:, :] = note
-
-
-def project(note, other_note, prompt_rows, other_rows, key_weight, value_weight, steps=5):
+        out[:, :E] = sums[:, lanes(head, E)]
+        out[:, E:] = sums[:, lanes(head + 2, E)]
+
+
+def project(prompt_rows, other_rows, key_weight, value_weight, steps=10):
     rows = 2 * prompt_rows.shape[0]
     depth, width = key_weight.shape
     return pl.pallas_call(
         functools.partial(project_kernel, steps),
-        out_shape=[jax.ShapeDtypeStruct((rows + NOTE_ROWS, 2 * E), BF16)] * 2,
-        in_specs=[SMEM, SMEM] + [ANY] * 4,
+        out_shape=[jax.ShapeDtypeStruct((rows, 2 * E), BF16)] * 2,
+        in_specs=[ANY] * 4,
         out_specs=[VMEM] * 2,
         scratch_shapes=[
             pltpu.VMEM((rows, depth), BF16),
@@ -132,32 +114,40 @@
         compiler_params=params(50),
         cost_estimate=cost(2 * rows * depth * width, 2 * depth * width + 2 * rows * depth),
         name="project_prefix",
-    )(note, other_note, prompt_rows, other_rows, key_weight, value_weight)
-
-
-def pack_kernel(q_ref, g_ref, k_ref, v_ref, *outs):
+    )(prompt_rows, other_rows, key_weight, value_weight)
+
+
+def pack_kernel(length_ref, prompts_ref, q_ref, g_ref, k_ref, v_ref, *outs):
     heads, _, _ = place()
+    row = lax.broadcasted_iota(jnp.int32, (q_ref.shape[0], E), 0)
+    note = jnp.where(
+        row < NOTE_ROWS,
+        length_ref[0],
+        jnp.where(row < 2 * NOTE_ROWS, prompts_ref[0, 0], prompts_ref[0, 1]),
+    )
+    note = note.astype(F32).astype(BF16)
     for head, out in zip(heads, outs):
         start = 0
         for source in (q_ref, g_ref, k_ref, v_ref):
             width = source.shape[1] // len(outs)
             out[:, start : start + width] = source[:, lanes(head, width)]
             start += width
-
-
-def pack(queries, out_grad, own_keys, own_values):
+        out[:, start:] = note
+
+
+def pack(first_length, resp_prompt, queries, out_grad, own_keys, own_values):
     rows = queries.shape[0]
     n = len(MEMBERS)
-    width = (2 * queries.shape[1] + 2 * own_keys.shape[1]) // n
+    width = (2 * queries.shape[1] + 2 * own_keys.shape[1]) // n + E
     return pl.pallas_call(
         pack_kernel,
         out_shape=[jax.ShapeDtypeStruct((rows, width), BF16)] * n,
-        in_specs=[VMEM] * 4,
+        in_specs=[SMEM] * 2 + [VMEM] * 4,
         out_specs=[VMEM] * n,
-        compiler_params=params(62),
+        compiler_params=params(16),
         cost_estimate=cost(0, 4 * n * rows * width),
         name="pack_rows",
-    )(queries, out_grad, own_keys, own_values)
+    )(first_length, resp_prompt, queries, out_grad, own_keys, own_values)
 
 
 def unpack_kernel(n, *rest):
@@ -195,13 +185,15 @@
         del rest[:count]
         return taken
 
+    def unstack(near, stacks):
+        return near + [stack.at[index] for stack in stacks for index in range(stack.shape[0])]
+
     pieces = len(slots)
     n = len(MEMBERS)
     packets = take(n)
-    notes = take(2)
-    kv_in = take(pieces)
+    kv_in = unstack(take(pieces // 2), take(2))
     grads_out = take(n)
-    prefix_out = take(pieces)
+    prefix_out = unstack(take(pieces // 2), take(2))
     keys, values, key_acc, value_acc = rest
     blocks, part, _ = kv_in[0].shape
     _, core, prompt_place = place()
@@ -223,16 +215,9 @@
 
     def products(j):
         packet = packets[j]
-        note = notes[j // 2][2 * part :, :].astype(F32)
-        step = NOTE_ROWS // 4
-        at = 2 * step * (j % 2)
         boundary, first_at, second_at = (
-            jnp.max(block).astype(jnp.int32)
-            for block in (
-                note[at : at + step, :E],
-                note[at : at + step, E:],
-                note[at + step : at + 2 * step, E:],
-            )
+            jnp.max(packet[at : at + NOTE_ROWS, -E:].astype(F32)).astype(jnp.int32)
+            for at in (0, NOTE_ROWS, 2 * NOTE_ROWS)
         )
         first_at, second_at = (
             crossed((prompt ^ prompt_place) << resp_bits, core) >> resp_bits
@@ -330,16 +315,14 @@
             target[j, :, E:] = value_acc[prompt, span, :].astype(target.dtype)
 
 
-def attend(packets, notes, kv_in, slots, prompts, resp_bits):
+def attend(packets, line, stacks, slots, prompts, resp_bits):
     rows, packet_width = packets[0].shape
-    group = (packet_width // E - 2) // 2
+    group = (packet_width // E - 3) // 2
     sums_shape = (prompts, PLEN, E)
     out_shape = [jax.ShapeDtypeStruct((rows, (group + 2) * E), BF16)] * len(packets)
-    out_shape += [
-        jax.ShapeDtypeStruct(x.shape, BF16 if 2 * index >= len(kv_in) else F32)
-        for index, x in enumerate(kv_in)
-    ]
-    operands = [*packets, *notes, *kv_in]
+    out_shape += [jax.ShapeDtypeStruct(x.shape, F32) for x in line]
+    out_shape += [jax.ShapeDtypeStruct(x.shape, BF16) for x in stacks]
+    operands = [*packets, *line, *stacks]
     outs = pl.pallas_call(
         functools.partial(attend_kernel, slots, group, rows, resp_bits),
         out_shape=out_shape,
@@ -352,7 +335,7 @@
         ),
         name="attend_head",
     )(*operands)
-    return outs[: len(packets)], outs[len(packets) :]
+    return outs[: len(packets)], outs[len(packets) : -2], outs[-2:]
 
 
 def total_kernel(keep_ref, *rest):
@@ -443,47 +426,47 @@
         return lax.ppermute(x, ("prompt", "resp"), pairs)
 
     other_rows = fetch(prompt_rows, MEMBERS[1])
-    note = jnp.concatenate([first_length, resp_prompt.reshape(-1)])
-    other_note = fetch(note, MEMBERS[1])
-    packed = pack(queries, out_grad, own_keys, own_values)
-    packed, other_rows = lax.optimization_barrier((packed, other_rows))
-    packets = [packed[0], fetch(packed[1], MEMBERS[1]), fetch(packed[2], MEMBERS[2])]
-    keep, send = project(note, other_note, prompt_rows, other_rows, key_weight, value_weight)
-    send, packets[2] = lax.optimization_barrier((send, packets[2]))
-    notes = [keep, fetch(send, MEMBERS[2])]
-    notes[1], late = lax.optimization_barrier((notes[1], packed[3]))
-    packets.append(fetch(late, MEMBERS[3]))
-
-    pieces = {0: jnp.concatenate([x[: 2 * part] for x in notes]).reshape(len(MEMBERS), part, -1)}
+    keep, send = project(prompt_rows, other_rows, key_weight, value_weight)
+    send, queries = lax.optimization_barrier((send, queries))
+    packed = pack(first_length, resp_prompt, queries, out_grad, own_keys, own_values)
+    arriving = fetch(send, MEMBERS[2])
+    joined = jnp.concatenate([keep, arriving]).reshape(len(MEMBERS), part, -1)
+    joined, packed = lax.optimization_barrier((joined, packed))
+    packets = [packed[0]] + [fetch(packed[j], MEMBERS[j]) for j in range(1, len(MEMBERS))]
+
+    pieces = {0: joined}
     for bit in line_bits:
         for offset in list(pieces):
             pieces[offset | 1 << bit] = fetch(pieces[offset], 1 << bit)
-    line = list(pieces)
-    for offset in line:
-        piece = pieces[offset]
-        if offset == 0:
-            piece, packets[3] = lax.optimization_barrier((piece, packets[3]))
-        pieces[offset | 1 << Y] = fetch(piece, 1 << Y)
+    offsets = list(pieces)
+    half = len(offsets) // 2
+    stacks = [
+        jnp.stack([pieces[offset] for offset in some])
+        for some in (offsets[:half], offsets[half:])
+    ]
+    stacks[1], packets = lax.optimization_barrier((stacks[1], packets))
+    stacks = [fetch(x, 1 << Y) for x in stacks]
 
     filled = [0] * n_prompt
     slots = []
-    for offset in pieces:
+    for offset in offsets + [offset | 1 << Y for offset in offsets]:
         places = []
         for member in MEMBERS:
             at = (offset ^ member) // n_resp
             places.append((at, filled[at]))
             filled[at] += 1
         slots.append(tuple(places))
-    kv_in = list(pieces.values())
     resp_bits = n_resp.bit_length() - 1
-    grads, outs = attend(packets, notes, kv_in, tuple(slots), n_prompt, resp_bits)
-
-    sums = dict(zip(line, outs))
-    arrived = {o: [give(x, 1 << Y)] for o, x in zip(line, outs[len(line) :])}
-    far = sorted(line, reverse=True)[: len(line) // 2]
-    ready, grads = lax.optimization_barrier(([arrived[o][0] for o in far], grads))
-    for offset, x in zip(far, ready):
-        arrived[offset] = [x]
+    grads, sums, back_stacks = attend(
+        packets, list(pieces.values()), stacks, tuple(slots), n_prompt, resp_bits
+    )
+
+    sums = dict(zip(offsets, sums))
+    far = give(back_stacks[1], 1 << Y)
+    near = give(back_stacks[0], 1 << Y)
+    far, grads = lax.optimization_barrier((far, grads))
+    arrived = {offset: [near[index]] for index, offset in enumerate(offsets[:half])}
+    arrived.update({offset: [far[index]] for index, offset in enumerate(offsets[half:])})
     for bit in reversed(line_bits):
         first = None
         for offset in sorted(sums, reverse=True):

time: 80.4 us -> 75.5 us (0.939)
  waiting for transfers between devices: 30.2 us -> 27.4 us
  Pallas kernels: 20.3 us -> 17.7 us
  starting transfers between devices: 26 us -> 27.2 us
    ppermute x13 -> x11, waiting for transfers between devices: 14 us -> 11.6 us  [give(): return lax.ppermute(x, ('prompt', 'resp'), pairs)]
    ppermute x13 -> x11, starting transfers between devices: 11.1 us -> 13.3 us  [give(): return lax.ppermute(x, ('prompt', 'resp'), pairs)]
    pallas_call x1, Pallas kernels: 2.63 us -> 0.71 us  [pack(): pl.pallas_call(pack_kernel, out_shape=[jax.ShapeDtypeStruct((rows, width)...]
    ppermute x13 -> x10, starting transfers between devices: 15 us -> 13.9 us  [fetch(): return lax.ppermute(x, ('prompt', 'resp'), pairs)]
    ppermute x13 -> x10, waiting for transfers between devices: 16.1 us -> 15.7 us  [fetch(): return lax.ppermute(x, ('prompt', 'resp'), pairs)]
  transfers between devices with their start and end apart: 26 -> 21, of which waited for: 14 -> 12; matrix products, arithmetic and copies ran while one was open for 1% -> 0% of each run, Pallas kernels for 11% -> 2%
where the time goes in v8:
time: 75.5 us; the launch traced here: 75.2 us
  waiting for transfers between devices  27.4 us (36%)
  starting transfers between devices  27.2 us (36%)
  Pallas kernels  17.7 us (23%)
  between operations  1.68 us (2%)
  local copies, waits for them, and re-layouts  1.14 us (2%)
    ppermute x10, waiting for transfers between devices, fetch(): return lax.ppermute(x, ('prompt', 'resp'), pairs)  15.7 us
    ppermute x10, starting transfers between devices, fetch(): return lax.ppermute(x, ('prompt', 'resp'), pairs)  13.9 us
    ppermute x11, starting transfers between devices, give(): return lax.ppermute(x, ('prompt', 'resp'), pairs)  13.3 us
    ppermute x11, waiting for transfers between devices, give(): return lax.ppermute(x, ('prompt', 'resp'), pairs)  11.6 us
    pallas_call x1, Pallas kernels, attend(): pl.pallas_call(functools.partial(attend_kernel, slots, group, rows, resp_...  7.88 us
    pallas_call x1, Pallas kernels, project(): pl.pallas_call(functools.partial(project_kernel, steps), out_shape=[jax.S...  4.37 us
    pallas_call x1, Pallas kernels, prompt_gradient(): pl.pallas_call(functools.partial(prompt_kernel, n, chunk), out_shape=jax....  3.69 us
  transfers between devices with their start and end apart: 21, of which 12 were waited for; matrix products, arithmetic and copies ran while one was open for 0% of the time, Pallas kernels for 2%

profile of v8, /device:TPU:0, one launch (start us, length us, event | category | flops | bytes accessed | tf_op | source)
XLA Modules:
  0.0 75.2 jit_solution(6999962742625816286)
XLA Ops:
  1.2 1.9 %collective-permute-done.other_ref = bf16[64,5120]{1,0:T(8,128)(2,1)S(1)} collective-permute-done((bf16[64,5120]{1,0:T(8,128)(2,1)}, bf16[64,5120]{1,0:T(8,128)(2,1)S(1)}, u32[]{:S(2)}, u32[]{:S(2)}) %collective-permute-start) | collective-permute-done | bytes 655392 | tf_op jit(solution)/shard_map/ppermute | solution.py:422
  3.1 1.1 %copy-done = bf16[64,5120]{1,0:T(8,128)(2,1)S(1)} copy-done((bf16[64,5120]{1,0:T(8,128)(2,1)S(1)}, bf16[64,5120]{1,0:T(8,128)(2,1)}, u32[]{:S(2)}) %copy-start) | copy-done | bytes 655384
  4.2 4.4 %project_prefix.1 = (bf16[128,256]{1,0:T(8,128)(2,1)S(1)}, bf16[128,256]{1,0:T(8,128)(2,1)S(1)}) custom-call(bf16[64,5120]{1,0:T(8,128)(2,1)S(1)} %copy-done, bf16[64,5120]{1,0:T(8,128)(2,1)S(1)} %collective-permute-done.other_ref, bf16[5120,512]{1,0:T(8,128)(2,1)} %rest_4_.1, bf16[5120,512]{1,0:T(8,128)(2,1)} %rest_5_.1), custom_call_target="tpu_custom_call" | custom-call | flops 671088640 | bytes 6553600 | tf_op jit(solution)/shard_map/project_prefix/pallas_call | solution.py:102
  8.6 2.9 %collective-permute-start.1 = (bf16[128,256]{1,0:T(8,128)(2,1)S(1)}, bf16[128,256]{1,0:T(8,128)(2,1)S(1)}, u32[]{:S(2)}, u32[]{:S(2)}) collective-permute-start(bf16[128,256]{1,0:T(8,128)(2,1)S(1)} %get-tuple-element.61), channel_id=1, source_target_pairs={{8,0},{17,1},{10,2},{19,3},{12,4},{21,5},{14,6},{23,7},{0,8},{25,9... | collective-permute-start | bytes 196616 | tf_op jit(solution)/shard_map/ppermute | solution.py:422
  13.8 2.1 %collective-permute-start.6 = (bf16[128,1664]{1,0:T(8,128)(2,1)S(1)}, bf16[128,1664]{1,0:T(8,128)(2,1)S(1)}, u32[]{:S(2)}, u32[]{:S(2)}) collective-permute-start(bf16[128,1664]{1,0:T(8,128)(2,1)S(1)} %get-tuple-element.70), channel_id=1, source_target_pairs={{8,0},{17,1},{10,2},{19,3},{12,4},{21,5},{14,6},{23,7},{0,8},{25,9... | collective-permute-start | bytes 1277960 | tf_op jit(solution)/shard_map/ppermute | solution.py:422
  16.0 2.8 %collective-permute-start.3 = (bf16[4,64,256]{2,1,0:T(8,128)(2,1)S(1)}, bf16[4,64,256]{2,1,0:T(8,128)(2,1)S(1)}, u32[]{:S(2)}, u32[]{:S(2)}) collective-permute-start(bf16[4,64,256]{2,1,0:T(8,128)(2,1)S(1)} %bitcast.26), channel_id=1, source_target_pairs={{4,0},{5,1},{6,2},{7,3},{0,4},{1,5},{2,6},{3,7},{12,8},{13,9},{14,... | collective-permute-start | bytes 393224 | tf_op jit(solution)/shard_map/ppermute | solution.py:422
  18.8 1.6 %collective-permute-start.2 = (bf16[4,64,256]{2,1,0:T(8,128)(2,1)S(1)}, bf16[4,64,256]{2,1,0:T(8,128)(2,1)S(1)}, u32[]{:S(2)}, u32[]{:S(2)}) collective-permute-start(bf16[4,64,256]{2,1,0:T(8,128)(2,1)S(1)} %bitcast.27), channel_id=1, source_target_pairs={{2,0},{3,1},{0,2},{1,3},{6,4},{7,5},{4,6},{5,7},{10,8},{11,9},{8,1... | collective-permute-start | bytes 393224 | tf_op jit(solution)/shard_map/ppermute | solution.py:422
  20.4 5.3 %collective-permute-done.3.rest_5_ = bf16[4,64,256]{2,1,0:T(8,128)(2,1)S(1)} collective-permute-done((bf16[4,64,256]{2,1,0:T(8,128)(2,1)S(1)}, bf16[4,64,256]{2,1,0:T(8,128)(2,1)S(1)}, u32[]{:S(2)}, u32[]{:S(2)}) %collective-permute-start.3) | collective-permute-done | bytes 131104 | tf_op jit(solution)/shard_map/ppermute | solution.py:422
  26.4 1.6 %collective-permute-start.8 = (bf16[2,4,64,256]{3,2,1,0:T(8,128)(2,1)S(1)}, bf16[2,4,64,256]{3,2,1,0:T(8,128)(2,1)S(1)}, u32[]{:S(2)}, u32[]{:S(2)}) collective-permute-start(bf16[2,4,64,256]{3,2,1,0:T(8,128)(2,1)S(1)} %pad_maximum_fusion.1), channel_id=1, source_target_pairs={{16,0},{9,1},{18,2},{11,3},{20,4},{13,5},{22,6},{15,7},{24,8},{1,9... | collective-permute-start | bytes 786440 | tf_op jit(solution)/shard_map/ppermute | solution.py:422
  28.0 2.8 %collective-permute-done.4.rest_7_ = bf16[4,64,256]{2,1,0:T(8,128)(2,1)S(1)} collective-permute-done((bf16[4,64,256]{2,1,0:T(8,128)(2,1)S(1)}, bf16[4,64,256]{2,1,0:T(8,128)(2,1)S(1)}, u32[]{:S(2)}, u32[]{:S(2)}) %collective-permute-start.4) | collective-permute-done | bytes 131104 | tf_op jit(solution)/shard_map/ppermute | solution.py:422
  30.9 1.6 %collective-permute-start.9 = (bf16[2,4,64,256]{3,2,1,0:T(8,128)(2,1)S(1)}, bf16[2,4,64,256]{3,2,1,0:T(8,128)(2,1)S(1)}, u32[]{:S(2)}, u32[]{:S(2)}) collective-permute-start(bf16[2,4,64,256]{3,2,1,0:T(8,128)(2,1)S(1)} %pad_maximum_fusion), channel_id=1, source_target_pairs={{16,0},{9,1},{18,2},{11,3},{20,4},{13,5},{22,6},{15,7},{24,8},{1,9... | collective-permute-start | bytes 786440 | tf_op jit(solution)/shard_map/ppermute | solution.py:422
  32.9 4.4 %collective-permute-done.9.rest_9_ = bf16[2,4,64,256]{3,2,1,0:T(8,128)(2,1)S(1)} collective-permute-done((bf16[2,4,64,256]{3,2,1,0:T(8,128)(2,1)S(1)}, bf16[2,4,64,256]{3,2,1,0:T(8,128)(2,1)S(1)}, u32[]{:S(2)}, u32[]{:S(2)}) %collective-permute-start.9) | collective-permute-done | bytes 262176 | tf_op jit(solution)/shard_map/ppermute | solution.py:422
  37.3 7.9 %attend_head.1 = (bf16[128,896]{1,0:T(8,128)(2,1)S(1)}, bf16[128,896]{1,0:T(8,128)(2,1)S(1)}, bf16[128,896]{1,0:T(8,128)(2,1)S(1)}, bf16[128,896]{1,0:T(8,128)(2...) custom-call(bf16[128,1664]{1,0:T(8,128)(2,1)S(1)} %get-tuple-element, ...), custom_call_target="tpu_custom_call" | custom-call | flops 4194304000 | bytes 16777216 | tf_op jit(solution)/shard_map/attend_head/pallas_call | solution.py:326
  45.2 1.6 %collective-permute-start.11 = (bf16[2,4,64,256]{3,2,1,0:T(8,128)(2,1)S(1)}, bf16[2,4,64,256]{3,2,1,0:T(8,128)(2,1)S(1)}, u32[]{:S(2)}, u32[]{:S(2)}) collective-permute-start(bf16[2,4,64,256]{3,2,1,0:T(8,128)(2,1)S(1)} %get-tuple-element.80), channel_id=1, source_target_pairs={{0,16},{1,9},{2,18},{3,11},{4,20},{5,13},{6,22},{7,15},{8,24},{9,1... | collective-permute-start | bytes 786440 | tf_op jit(solution)/shard_map/ppermute | solution.py:426
  47.3 4.3 %collective-permute-done.11 = bf16[2,4,64,256]{3,2,1,0:T(8,128)(2,1)S(1)} collective-permute-done((bf16[2,4,64,256]{3,2,1,0:T(8,128)(2,1)S(1)}, bf16[2,4,64,256]{3,2,1,0:T(8,128)(2,1)S(1)}, u32[]{:S(2)}, u32[]{:S(2)}) %collective-permute-start.11) | collective-permute-done | bytes 262176 | tf_op jit(solution)/shard_map/ppermute | solution.py:426
  51.6 1.1 %collective-permute-start.12 = (bf16[4,64,256]{2,1,0:T(8,128)(2,1)S(1)}, bf16[4,64,256]{2,1,0:T(8,128)(2,1)S(1)}, u32[]{:S(2)}, u32[]{:S(2)}) collective-permute-start(bf16[4,64,256]{2,1,0:T(8,128)(2,1)S(1)} %fusion.2), channel_id=1, source_target_pairs={{0,2},{1,3},{2,0},{3,1},{4,6},{5,7},{6,4},{7,5},{8,10},{9,11},{10,... | collective-permute-start | bytes 393224 | tf_op jit(solution)/shard_map/ppermute | solution.py:426
  52.8 1.5 %collective-permute-start.16 = (bf16[128,896]{1,0:T(8,128)(2,1)S(1)}, bf16[128,896]{1,0:T(8,128)(2,1)S(1)}, u32[]{:S(2)}, u32[]{:S(2)}) collective-permute-start(bf16[128,896]{1,0:T(8,128)(2,1)S(1)} %get-tuple-element.95), channel_id=1, source_target_pairs={{0,8},{1,17},{2,10},{3,19},{4,12},{5,21},{6,14},{7,23},{8,0},{9,25... | collective-permute-start | bytes 688136 | tf_op jit(solution)/shard_map/ppermute | solution.py:426
  54.3 1.4 %collective-permute-start.17 = (bf16[128,896]{1,0:T(8,128)(2,1)S(1)}, bf16[128,896]{1,0:T(8,128)(2,1)S(1)}, u32[]{:S(2)}, u32[]{:S(2)}) collective-permute-start(bf16[128,896]{1,0:T(8,128)(2,1)S(1)} %get-tuple-element.96), channel_id=1, source_target_pairs={{0,9},{1,16},{2,11},{3,18},{4,13},{5,20},{6,15},{7,22},{8,1},{9,24... | collective-permute-start | bytes 688136 | tf_op jit(solution)/shard_map/ppermute | solution.py:426
  57.8 3.4 %collective-permute-start.14 = (bf16[4,64,256]{2,1,0:T(8,128)(2,1)S(1)}, bf16[4,64,256]{2,1,0:T(8,128)(2,1)S(1)}, u32[]{:S(2)}, u32[]{:S(2)}) collective-permute-start(bf16[4,64,256]{2,1,0:T(8,128)(2,1)S(1)} %fusion.1), channel_id=1, source_target_pairs={{0,4},{1,5},{2,6},{3,7},{4,0},{5,1},{6,2},{7,3},{8,12},{9,13},{10,... | collective-permute-start | bytes 393224 | tf_op jit(solution)/shard_map/ppermute | solution.py:426
  61.2 2.6 %collective-permute-done.13.rest_1_ = bf16[4,64,256]{2,1,0:T(8,128)(2,1)S(1)} collective-permute-done((bf16[4,64,256]{2,1,0:T(8,128)(2,1)S(1)}, bf16[4,64,256]{2,1,0:T(8,128)(2,1)S(1)}, u32[]{:S(2)}, u32[]{:S(2)}) %collective-permute-start.13) | collective-permute-done | bytes 131104 | tf_op jit(solution)/shard_map/ppermute | solution.py:426
  63.8 1.3 %collective-permute-done.14.rest_2_ = bf16[4,64,256]{2,1,0:T(8,128)(2,1)S(1)} collective-permute-done((bf16[4,64,256]{2,1,0:T(8,128)(2,1)S(1)}, bf16[4,64,256]{2,1,0:T(8,128)(2,1)S(1)}, u32[]{:S(2)}, u32[]{:S(2)}) %collective-permute-start.14) | collective-permute-done | bytes 131104 | tf_op jit(solution)/shard_map/ppermute | solution.py:426
  65.2 2.7 %collective-permute-start.19 = (bf16[2,64,256]{2,1,0:T(8,128)(2,1)S(1)}, bf16[2,64,256]{2,1,0:T(8,128)(2,1)S(1)}, u32[]{:S(2)}, u32[]{:S(2)}) collective-permute-start(bf16[2,64,256]{2,1,0:T(8,128)(2,1)S(1)} %get-tuple-element.99), channel_id=1, source_target_pairs={{0,8},{1,17},{2,10},{3,19},{4,12},{5,21},{6,14},{7,23},{8,0},{9,25... | collective-permute-start | bytes 196616 | tf_op jit(solution)/shard_map/ppermute | solution.py:426
  67.9 2.2 %collective-permute-done.19 = bf16[2,64,256]{2,1,0:T(8,128)(2,1)S(1)} collective-permute-done((bf16[2,64,256]{2,1,0:T(8,128)(2,1)S(1)}, bf16[2,64,256]{2,1,0:T(8,128)(2,1)S(1)}, u32[]{:S(2)}, u32[]{:S(2)}) %collective-permute-start.19) | collective-permute-done | bytes 65568 | tf_op jit(solution)/shard_map/ppermute | solution.py:426
  71.4 3.7 %prompt_gradient.1 = bf16[64,5120]{1,0:T(8,128)(2,1)} custom-call(bf16[64,256]{1,0:T(8,128)(2,1)S(1)} %get-tuple-element.110.rest_0_, bf16[64,256]{1,0:T(8,128)(2,1)S(1)} %collective-permute-done.18.rest_1_, bf16[64,256]{1,0:T(8,128)(2,1)S(1)} %get-tuple-element.112.rest_2_, bf16[64,256]{1,0:T(8,128)(2,1)S(1)} %collective-permute-done.20.rest_3_, ...), custom_call_target="tpu_custom_call" | custom-call | flops 671088640 | bytes 11141120 | tf_op jit(solution)/shard_map/prompt_gradient/pallas_call | solution.py:388
  (54 shorter events, 7.4 us)
Async XLA Ops:
  0.6 2.5 %collective-permute-start = (bf16[64,5120]{1,0:T(8,128)(2,1)}, bf16[64,5120]{1,0:T(8,128)(2,1)S(1)}, u32[]{:S(2)}, u32[]{:S(2)}) collective-permute-start(bf16[64,5120]{1,0:T(8,128)(2,1)} %x_ref.1), channel_id=1, source_target_pairs={{1,0},{0,1},{3,2},{2,3},{5,4},{4,5},{7,6},{6,7},{9,8},{8,9},{11,10... | collective-permute-start | bytes 1966088 | tf_op jit(solution)/shard_map/ppermute | solution.py:422
  8.6 5.2 %collective-permute-start.1 = (bf16[128,256]{1,0:T(8,128)(2,1)S(1)}, bf16[128,256]{1,0:T(8,128)(2,1)S(1)}, u32[]{:S(2)}, u32[]{:S(2)}) collective-permute-start(bf16[128,256]{1,0:T(8,128)(2,1)S(1)} %get-tuple-element.61), channel_id=1, source_target_pairs={{8,0},{17,1},{10,2},{19,3},{12,4},{21,5},{14,6},{23,7},{0,8},{25,9... | collective-permute-start | bytes 196616 | tf_op jit(solution)/shard_map/ppermute | solution.py:422
  13.8 17.1 %collective-permute-start.5 = (bf16[128,1664]{1,0:T(8,128)(2,1)S(1)}, bf16[128,1664]{1,0:T(8,128)(2,1)S(1)}, u32[]{:S(2)}, u32[]{:S(2)}) collective-permute-start(bf16[128,1664]{1,0:T(8,128)(2,1)S(1)} %get-tuple-element.69), channel_id=1, source_target_pairs={{1,0},{0,1},{3,2},{2,3},{5,4},{4,5},{7,6},{6,7},{9,8},{8,9},{11,10... | collective-permute-start | bytes 1277960 | tf_op jit(solution)/shard_map/ppermute | solution.py:422
  13.8 17.0 %collective-permute-start.6 = (bf16[128,1664]{1,0:T(8,128)(2,1)S(1)}, bf16[128,1664]{1,0:T(8,128)(2,1)S(1)}, u32[]{:S(2)}, u32[]{:S(2)}) collective-permute-start(bf16[128,1664]{1,0:T(8,128)(2,1)S(1)} %get-tuple-element.70), channel_id=1, source_target_pairs={{8,0},{17,1},{10,2},{19,3},{12,4},{21,5},{14,6},{23,7},{0,8},{25,9... | collective-permute-start | bytes 1277960 | tf_op jit(solution)/shard_map/ppermute | solution.py:422
  15.9 14.9 %collective-permute-start.7 = (bf16[128,1664]{1,0:T(8,128)(2,1)S(1)}, bf16[128,1664]{1,0:T(8,128)(2,1)S(1)}, u32[]{:S(2)}, u32[]{:S(2)}) collective-permute-start(bf16[128,1664]{1,0:T(8,128)(2,1)S(1)} %get-tuple-element.71), channel_id=1, source_target_pairs={{9,0},{16,1},{11,2},{18,3},{13,4},{20,5},{15,6},{22,7},{1,8},{24,9... | collective-permute-start | bytes 1277960 | tf_op jit(solution)/shard_map/ppermute | solution.py:422
  16.0 9.7 %collective-permute-start.3 = (bf16[4,64,256]{2,1,0:T(8,128)(2,1)S(1)}, bf16[4,64,256]{2,1,0:T(8,128)(2,1)S(1)}, u32[]{:S(2)}, u32[]{:S(2)}) collective-permute-start(bf16[4,64,256]{2,1,0:T(8,128)(2,1)S(1)} %bitcast.26), channel_id=1, source_target_pairs={{4,0},{5,1},{6,2},{7,3},{0,4},{1,5},{2,6},{3,7},{12,8},{13,9},{14,... | collective-permute-start | bytes 393224 | tf_op jit(solution)/shard_map/ppermute | solution.py:422
  18.8 7.6 %collective-permute-start.2 = (bf16[4,64,256]{2,1,0:T(8,128)(2,1)S(1)}, bf16[4,64,256]{2,1,0:T(8,128)(2,1)S(1)}, u32[]{:S(2)}, u32[]{:S(2)}) collective-permute-start(bf16[4,64,256]{2,1,0:T(8,128)(2,1)S(1)} %bitcast.27), channel_id=1, source_target_pairs={{2,0},{3,1},{0,2},{1,3},{6,4},{7,5},{4,6},{5,7},{10,8},{11,9},{8,1... | collective-permute-start | bytes 393224 | tf_op jit(solution)/shard_map/ppermute | solution.py:422
  25.7 5.0 %collective-permute-start.4 = (bf16[4,64,256]{2,1,0:T(8,128)(2,1)S(1)}, bf16[4,64,256]{2,1,0:T(8,128)(2,1)S(1)}, u32[]{:S(2)}, u32[]{:S(2)}) collective-permute-start(bf16[4,64,256]{2,1,0:T(8,128)(2,1)S(1)} %collective-permute-done.3.rest_5_), channel_id=1, source_target_pairs={{2,0},{3,1},{0,2},{1,3},{6,4},{7,5},{4,6},{5,7},{10,8},{11,9},{8,1... | collective-permute-start | bytes 393224 | tf_op jit(solution)/shard_map/ppermute | solution.py:422
  26.4 6.4 %collective-permute-start.8 = (bf16[2,4,64,256]{3,2,1,0:T(8,128)(2,1)S(1)}, bf16[2,4,64,256]{3,2,1,0:T(8,128)(2,1)S(1)}, u32[]{:S(2)}, u32[]{:S(2)}) collective-permute-start(bf16[2,4,64,256]{3,2,1,0:T(8,128)(2,1)S(1)} %pad_maximum_fusion.1), channel_id=1, source_target_pairs={{16,0},{9,1},{18,2},{11,3},{20,4},{13,5},{22,6},{15,7},{24,8},{1,9... | collective-permute-start | bytes 786440 | tf_op jit(solution)/shard_map/ppermute | solution.py:422
  30.8 40.6 %slice-start = ((s8[5242880]{0:T(1024)(128)(4,1)}), s8[4194304]{0:T(1024)(128)(4,1)S(1)}, s32[]{:S(2)}) async-start(s8[5242880]{0:T(1024)(128)(4,1)} %bitcast.22), calls=%async_computation | async-start | bytes 8388608
  30.8 40.6 %slice-start.2 = ((s8[5242880]{0:T(1024)(128)(4,1)}), s8[4194304]{0:T(1024)(128)(4,1)S(1)}, s32[]{:S(2)}) async-start(s8[5242880]{0:T(1024)(128)(4,1)} %bitcast.24), calls=%async_computation.2 | async-start | bytes 8388608
  30.8 40.6 %slice-start.1 = ((s8[5242880]{0:T(1024)(128)(4,1)}), s8[1048576]{0:T(1024)(128)(4,1)S(1)}, s32[]{:S(2)}) async-start(s8[5242880]{0:T(1024)(128)(4,1)} %bitcast.22), calls=%async_computation.1 | async-start | bytes 2097152
  30.9 6.4 %collective-permute-start.9 = (bf16[2,4,64,256]{3,2,1,0:T(8,128)(2,1)S(1)}, bf16[2,4,64,256]{3,2,1,0:T(8,128)(2,1)S(1)}, u32[]{:S(2)}, u32[]{:S(2)}) collective-permute-start(bf16[2,4,64,256]{3,2,1,0:T(8,128)(2,1)S(1)} %pad_maximum_fusion), channel_id=1, source_target_pairs={{16,0},{9,1},{18,2},{11,3},{20,4},{13,5},{22,6},{15,7},{24,8},{1,9... | collective-permute-start | bytes 786440 | tf_op jit(solution)/shard_map/ppermute | solution.py:422
  45.2 6.4 %collective-permute-start.11 = (bf16[2,4,64,256]{3,2,1,0:T(8,128)(2,1)S(1)}, bf16[2,4,64,256]{3,2,1,0:T(8,128)(2,1)S(1)}, u32[]{:S(2)}, u32[]{:S(2)}) collective-permute-start(bf16[2,4,64,256]{3,2,1,0:T(8,128)(2,1)S(1)} %get-tuple-element.80), channel_id=1, source_target_pairs={{0,16},{1,9},{2,18},{3,11},{4,20},{5,13},{6,22},{7,15},{8,24},{9,1... | collective-permute-start | bytes 786440 | tf_op jit(solution)/shard_map/ppermute | solution.py:426
  46.8 11.0 %collective-permute-start.10 = (bf16[2,4,64,256]{3,2,1,0:T(8,128)(2,1)S(1)}, bf16[2,4,64,256]{3,2,1,0:T(8,128)(2,1)S(1)}, u32[]{:S(2)}, u32[]{:S(2)}) collective-permute-start(bf16[2,4,64,256]{3,2,1,0:T(8,128)(2,1)S(1)} %get-tuple-element.78), channel_id=1, source_target_pairs={{0,16},{1,9},{2,18},{3,11},{4,20},{5,13},{6,22},{7,15},{8,24},{9,1... | collective-permute-start | bytes 786440 | tf_op jit(solution)/shard_map/ppermute | solution.py:426
  51.6 5.0 %collective-permute-start.12 = (bf16[4,64,256]{2,1,0:T(8,128)(2,1)S(1)}, bf16[4,64,256]{2,1,0:T(8,128)(2,1)S(1)}, u32[]{:S(2)}, u32[]{:S(2)}) collective-permute-start(bf16[4,64,256]{2,1,0:T(8,128)(2,1)S(1)} %fusion.2), channel_id=1, source_target_pairs={{0,2},{1,3},{2,0},{3,1},{4,6},{5,7},{6,4},{7,5},{8,10},{9,11},{10,... | collective-permute-start | bytes 393224 | tf_op jit(solution)/shard_map/ppermute | solution.py:426
  52.8 12.4 %collective-permute-start.15 = (bf16[128,896]{1,0:T(8,128)(2,1)S(1)}, bf16[128,896]{1,0:T(8,128)(2,1)S(1)}, u32[]{:S(2)}, u32[]{:S(2)}) collective-permute-start(bf16[128,896]{1,0:T(8,128)(2,1)S(1)} %get-tuple-element.94), channel_id=1, source_target_pairs={{0,1},{1,0},{2,3},{3,2},{4,5},{5,4},{6,7},{7,6},{8,9},{9,8},{10,11... | collective-permute-start | bytes 688136 | tf_op jit(solution)/shard_map/ppermute | solution.py:426
  52.8 12.4 %collective-permute-start.16 = (bf16[128,896]{1,0:T(8,128)(2,1)S(1)}, bf16[128,896]{1,0:T(8,128)(2,1)S(1)}, u32[]{:S(2)}, u32[]{:S(2)}) collective-permute-start(bf16[128,896]{1,0:T(8,128)(2,1)S(1)} %get-tuple-element.95), channel_id=1, source_target_pairs={{0,8},{1,17},{2,10},{3,19},{4,12},{5,21},{6,14},{7,23},{8,0},{9,25... | collective-permute-start | bytes 688136 | tf_op jit(solution)/shard_map/ppermute | solution.py:426
  54.3 10.9 %collective-permute-start.17 = (bf16[128,896]{1,0:T(8,128)(2,1)S(1)}, bf16[128,896]{1,0:T(8,128)(2,1)S(1)}, u32[]{:S(2)}, u32[]{:S(2)}) collective-permute-start(bf16[128,896]{1,0:T(8,128)(2,1)S(1)} %get-tuple-element.96), channel_id=1, source_target_pairs={{0,9},{1,16},{2,11},{3,18},{4,13},{5,20},{6,15},{7,22},{8,1},{9,24... | collective-permute-start | bytes 688136 | tf_op jit(solution)/shard_map/ppermute | solution.py:426
  56.7 7.1 %collective-permute-start.13 = (bf16[4,64,256]{2,1,0:T(8,128)(2,1)S(1)}, bf16[4,64,256]{2,1,0:T(8,128)(2,1)S(1)}, u32[]{:S(2)}, u32[]{:S(2)}) collective-permute-start(bf16[4,64,256]{2,1,0:T(8,128)(2,1)S(1)} %convert_add_fusion.2), channel_id=1, source_target_pairs={{0,2},{1,3},{2,0},{3,1},{4,6},{5,7},{6,4},{7,5},{8,10},{9,11},{10,... | collective-permute-start | bytes 393224 | tf_op jit(solution)/shard_map/ppermute | solution.py:426
  57.8 7.3 %collective-permute-start.14 = (bf16[4,64,256]{2,1,0:T(8,128)(2,1)S(1)}, bf16[4,64,256]{2,1,0:T(8,128)(2,1)S(1)}, u32[]{:S(2)}, u32[]{:S(2)}) collective-permute-start(bf16[4,64,256]{2,1,0:T(8,128)(2,1)S(1)} %fusion.1), channel_id=1, source_target_pairs={{0,4},{1,5},{2,6},{3,7},{4,0},{5,1},{6,2},{7,3},{8,12},{9,13},{10,... | collective-permute-start | bytes 393224 | tf_op jit(solution)/shard_map/ppermute | solution.py:426
  65.2 5.0 %collective-permute-start.19 = (bf16[2,64,256]{2,1,0:T(8,128)(2,1)S(1)}, bf16[2,64,256]{2,1,0:T(8,128)(2,1)S(1)}, u32[]{:S(2)}, u32[]{:S(2)}) collective-permute-start(bf16[2,64,256]{2,1,0:T(8,128)(2,1)S(1)} %get-tuple-element.99), channel_id=1, source_target_pairs={{0,8},{1,17},{2,10},{3,19},{4,12},{5,21},{6,14},{7,23},{8,0},{9,25... | collective-permute-start | bytes 196616 | tf_op jit(solution)/shard_map/ppermute | solution.py:426
  67.9 3.3 %collective-permute-start.18 = (bf16[64,256]{1,0:T(8,128)(2,1)S(1)}, bf16[64,256]{1,0:T(8,128)(2,1)S(1)}, u32[]{:S(2)}, u32[]{:S(2)}) collective-permute-start(bf16[64,256]{1,0:T(8,128)(2,1)S(1)} %get-tuple-element.98), channel_id=1, source_target_pairs={{0,1},{1,0},{2,3},{3,2},{4,5},{5,4},{6,7},{7,6},{8,9},{9,8},{10,11... | collective-permute-start | bytes 98312 | tf_op jit(solution)/shard_map/ppermute | solution.py:426
  70.1 1.2 %collective-permute-start.20 = (bf16[64,256]{1,0:T(8,128)(2,1)S(1)}, bf16[64,256]{1,0:T(8,128)(2,1)S(1)}, u32[]{:S(2)}, u32[]{:S(2)}) collective-permute-start(bf16[64,256]{1,0:T(8,128)(2,1)S(1)} %get-tuple-element.114), channel_id=1, source_target_pairs={{0,1},{1,0},{2,3},{3,2},{4,5},{5,4},{6,7},{7,6},{8,9},{9,8},{10,11... | collective-permute-start | bytes 98312 | tf_op jit(solution)/shard_map/ppermute | solution.py:426
  (7 other events, 81.6 us)

commit v9 on v8

--- a/solution.py
+++ b/solution.py
@@ -191,7 +191,7 @@
     pieces = len(slots)
     n = len(MEMBERS)
     packets = take(n)
-    kv_in = unstack(take(pieces // 2), take(2))
+    kv_in = unstack(take(pieces // 2), take(3))
     grads_out = take(n)
     prefix_out = unstack(take(pieces // 2), take(2))
     keys, values, key_acc, value_acc = rest
@@ -237,74 +237,67 @@
 
         query_pair = split(query)
         grad_pair = split(grad)
-        key_pair = jnp.concatenate([keys[first_at], keys[second_at]], axis=1)
-        value_pair = jnp.concatenate([values[first_at], values[second_at]], axis=1)
-
+        spans = [slice(at, at + E) for at in range(0, PLEN, E)]
+        key_pairs, value_pairs = (
+            [jnp.concatenate([x[first_at, span], x[second_at, span]], axis=1) for span in spans]
+            for x in (keys, values)
+        )
         visible = (own_key <= row_in_lane) & ((own_key >= boundary) == (row_in_lane >= boundary))
+        scores = [dot(key_pair, query_pair, 1, 1) for key_pair in key_pairs]
+        scores.append(jnp.where(visible, dot(own_k, query, 1, 1), HIDDEN))
         return dict(
             boundary=boundary,
-            first_at=first_at,
-            second_at=second_at,
-            query=query,
-            grad=grad,
-            own_k=own_k,
-            query_pair=query_pair,
-            grad_pair=grad_pair,
-            key_pair=key_pair,
-            scores=dot(key_pair, query_pair, 1, 1),
-            own_scores=jnp.where(visible, dot(own_k, query, 1, 1), HIDDEN),
-            dprobs=dot(value_pair, grad_pair, 1, 1),
-            own_dprobs=dot(own_v, grad, 1, 1),
+            places=[(first_at, second_at, span) for span in spans],
+            keys=key_pairs + [own_k],
+            values=value_pairs + [own_v],
+            queries=[query_pair] * len(spans) + [query],
+            grads=[grad_pair] * len(spans) + [grad],
+            scores=scores,
         )
 
-    def soften(scores, own_scores, dprobs, own_dprobs, **_):
-        top = jnp.maximum(
-            jnp.max(scores, axis=0, keepdims=True), jnp.max(own_scores, axis=0, keepdims=True)
-        )
-        weight = jnp.exp2((scores - top) * EXP2_SCALE)
-        own_weight = jnp.exp2((own_scores - top) * EXP2_SCALE)
-        inverse = 1.0 / (
-            jnp.sum(weight, axis=0, keepdims=True) + jnp.sum(own_weight, axis=0, keepdims=True)
-        )
-        probs = weight * inverse
-        own_probs = own_weight * inverse
-        probs_low = probs.astype(BF16)
-        own_probs_low = own_probs.astype(BF16)
-        delta = jnp.sum(probs_low.astype(F32) * dprobs, axis=0, keepdims=True) + jnp.sum(
-            own_probs_low.astype(F32) * own_dprobs, axis=0, keepdims=True
-        )
-        return dict(
-            probs_low=probs_low,
-            own_probs_low=own_probs_low,
-            dscores=(probs * (dprobs - delta)).astype(BF16),
-            own_dscores=(own_probs * (own_dprobs - delta)).astype(BF16),
-        )
-
-    def gradients(
-        grads, boundary, first_at, second_at, query, grad, own_k, query_pair, grad_pair, key_pair,
-        probs_low, own_probs_low, dscores, own_dscores, **_
-    ):
-        key_part = dot(dscores, query_pair, 1, 0)
-        value_part = dot(probs_low, grad_pair, 1, 0)
-        key_acc[first_at] += key_part[:, :E]
-        key_acc[second_at] += key_part[:, E:]
-        value_acc[first_at] += value_part[:, :E]
-        value_acc[second_at] += value_part[:, E:]
-
-        query_both = dot(key_pair, dscores, 0, 0)
-        query_part = jnp.where(lane_row < boundary, query_both[:E], query_both[E:])
-        query_part = (query_part + dot(own_k, own_dscores, 0, 0)) * SCALE
+    def gradients(out, boundary, places, keys, values, queries, grads, scores):
+        top = functools.reduce(jnp.maximum, [jnp.max(x, axis=0, keepdims=True) for x in scores])
+        weights, dprobs = [], []
+        for x, value, grad in zip(scores, values, grads):
+            dprobs.append(dot(value, grad, 1, 1))
+            weights.append(jnp.exp2((x - top) * EXP2_SCALE))
+        inverse = 1.0 / sum(jnp.sum(x, axis=0, keepdims=True) for x in weights)
+        probs = []
+        delta = 0.0
+        for index, (weight, dprob, grad) in enumerate(zip(weights, dprobs, grads)):
+            probs.append(weight * inverse)
+            low = probs[-1].astype(BF16)
+            delta = delta + jnp.sum(low.astype(F32) * dprob, axis=0, keepdims=True)
+            part = dot(low, grad, 1, 0)
+            if index < len(places):
+                first_at, second_at, span = places[index]
+                value_acc[first_at, span] += part[:, :E]
+                value_acc[second_at, span] += part[:, E:]
+            else:
+                out[:, (group + 1) * E :] = part.astype(BF16)
+        both = own = None
+        for index, (prob, dprob, key, query) in enumerate(zip(probs, dprobs, keys, queries)):
+            dscore = (prob * (dprob - delta)).astype(BF16)
+            part = dot(dscore, query, 1, 0)
+            turned = dot(key, dscore, 0, 0)
+            if index < len(places):
+                first_at, second_at, span = places[index]
+                key_acc[first_at, span] += part[:, :E]
+                key_acc[second_at, span] += part[:, E:]
+                both = turned if both is None else both + turned
+            else:
+                out[:, group * E : (group + 1) * E] = (part * SCALE).astype(BF16)
+                own = turned
+        whole = (jnp.where(lane_row < boundary, both[:E], both[E:]) + own) * SCALE
         for h in range(group):
-            grads[:, h * E : (h + 1) * E] = query_part[:, h * rows : (h + 1) * rows].T.astype(BF16)
-        grads[:, group * E : (group + 1) * E] = (dot(own_dscores, query, 1, 0) * SCALE).astype(BF16)
-        grads[:, (group + 1) * E :] = dot(own_probs_low, grad, 1, 0).astype(BF16)
+            out[:, h * E : (h + 1) * E] = whole[:, h * rows : (h + 1) * rows].T.astype(BF16)
 
     ahead = products(0)
     for j in range(n):
         now = ahead
         if j + 1 < n:
             ahead = products(j + 1)
-        gradients(grads_out[j], **now, **soften(**now))
+        gradients(grads_out[j], **now)
 
     for index in range(pieces):
         for j in range(blocks):
@@ -321,7 +314,8 @@
     sums_shape = (prompts, PLEN, E)
     out_shape = [jax.ShapeDtypeStruct((rows, (group + 2) * E), BF16)] * len(packets)
     out_shape += [jax.ShapeDtypeStruct(x.shape, F32) for x in line]
-    out_shape += [jax.ShapeDtypeStruct(x.shape, BF16) for x in stacks]
+    half = len(line) // 2
+    out_shape += [jax.ShapeDtypeStruct((half, *line[0].shape), BF16)] * 2
     operands = [*packets, *line, *stacks]
     outs = pl.pallas_call(
         functools.partial(attend_kernel, slots, group, rows, resp_bits),
@@ -339,8 +333,8 @@
 
 
 def total_kernel(keep_ref, *rest):
-    parts, (own_ref, other_ref, away_ref) = rest[:-3], rest[-3:]
-    for j, out in enumerate((own_ref, other_ref, away_ref.at[0], away_ref.at[1])):
+    parts, outs = rest[: -len(MEMBERS)], rest[-len(MEMBERS) :]
+    for j, out in enumerate(outs):
         result = keep_ref[j]
         for part in parts:
             result = result + part[j].astype(F32)
@@ -348,54 +342,66 @@
 
 
 def total(keep, parts):
-    _, rows, width = keep.shape
     return pl.pallas_call(
         total_kernel,
-        out_shape=[
-            jax.ShapeDtypeStruct(shape, BF16)
-            for shape in ((rows, width), (rows, width), (2, rows, width))
-        ],
+        out_shape=[jax.ShapeDtypeStruct(keep.shape[1:], BF16)] * len(MEMBERS),
         in_specs=[VMEM] * (1 + len(parts)),
-        out_specs=[VMEM] * 3,
+        out_specs=[VMEM] * len(MEMBERS),
         compiler_params=params(16),
         cost_estimate=cost(0, 1 << 25),
         name="total_prefix_grads",
     )(keep, *parts)
 
 
-def prompt_kernel(n, chunk, *rest):
-    shares, (kw_ref, vw_ref, out_ref, key_grad, value_grad, out, sems) = rest[:n], rest[n:]
+def prompt_kernel(chunk, members, first, *rest):
+    rest = list(rest)
+    shares = [rest.pop(0) for _ in members]
+    kw_ref, vw_ref = rest.pop(0), rest.pop(0)
+    start_ref = None if first else rest.pop(0)
+    out_ref, *scratch = rest
     heads, _, _ = place()
-    for head, share in zip(heads, shares):
-        key_grad[:, lanes(head, E)] = share[:, :E]
-        value_grad[:, lanes(head, E)] = share[:, E:]
+    key_grad, value_grad = (
+        jnp.concatenate([share[:, at : at + E] for share in shares], axis=1) for at in (0, E)
+    )
     copies = []
     for index in range(kw_ref.shape[0] // chunk):
         span = slice(index * chunk, (index + 1) * chunk)
-        turned = dot(kw_ref[span, :], key_grad[...], 1, 1)
-        turned = turned + dot(vw_ref[span, :], value_grad[...], 1, 1)
-        out[:, span] = turned.T.astype(BF16)
+        key_part, value_part = (
+            jnp.concatenate([weight[span, lanes(heads[j], E)] for j in members], axis=1)
+            for weight in (kw_ref, vw_ref)
+        )
+        turned = dot(key_part, key_grad, 1, 1) + dot(value_part, value_grad, 1, 1)
+        if first:
+            out_ref[span, :] = turned
+            continue
+        out, sems = scratch
+        out[:, span] = (turned + start_ref[span, :]).T.astype(BF16)
         copies.append(pltpu.make_async_copy(out.at[:, span], out_ref.at[:, span], sems.at[index]))
         copies[-1].start()
     for copy in copies:
         copy.wait()
 
 
-def prompt_gradient(shares, key_weight, value_weight, chunk=1024):
-    n = len(shares)
+def prompt_gradient(members, shares, key_weight, value_weight, start=None, chunk=1024):
+    first = start is None
     rows = shares[0].shape[0]
     depth, width = key_weight.shape
+    operands = [*shares, key_weight, value_weight] + ([] if first else [start])
+    out = jax.ShapeDtypeStruct((depth, rows), F32)
+    if not first:
+        out = jax.ShapeDtypeStruct((rows, depth), BF16)
     return pl.pallas_call(
-        functools.partial(prompt_kernel, n, chunk),
-        out_shape=jax.ShapeDtypeStruct((rows, depth), BF16),
-        in_specs=[VMEM] * (n + 2),
-        out_specs=ANY,
-        scratch_shapes=[pltpu.VMEM((rows, width), BF16)] * 2
-        + [pltpu.VMEM((rows, depth), BF16), pltpu.SemaphoreType.DMA((depth // chunk,))],
-        compiler_params=params(32),
-        cost_estimate=cost(4 * rows * depth * width, 4 * depth * width + 2 * rows * depth),
+        functools.partial(prompt_kernel, chunk, members, first),
+        out_shape=out,
+        in_specs=[VMEM] * len(operands),
+        out_specs=VMEM if first else ANY,
+        scratch_shapes=[]
+        if first
+        else [pltpu.VMEM((rows, depth), BF16), pltpu.SemaphoreType.DMA((depth // chunk,))],
+        compiler_params=params(24),
+        cost_estimate=cost(2 * rows * depth * width, 2 * depth * width + 2 * rows * depth),
         name="prompt_gradient",
-    )(*shares, key_weight, value_weight)
+    )(*operands)
 
 
 def per_device(
@@ -439,17 +445,17 @@
         for offset in list(pieces):
             pieces[offset | 1 << bit] = fetch(pieces[offset], 1 << bit)
     offsets = list(pieces)
-    half = len(offsets) // 2
-    stacks = [
-        jnp.stack([pieces[offset] for offset in some])
-        for some in (offsets[:half], offsets[half:])
-    ]
-    stacks[1], packets = lax.optimization_barrier((stacks[1], packets))
+    long = 1 << line_bits[0]
+    some = [offset for offset in offsets if not offset & long]
+    many = [offset for offset in offsets if offset & long]
+    groups = [some, many[:-1], many[-1:]]
+    stacks = [jnp.stack([pieces[offset] for offset in group]) for group in groups]
+    stacks[2], packets = lax.optimization_barrier((stacks[2], packets))
     stacks = [fetch(x, 1 << Y) for x in stacks]
 
     filled = [0] * n_prompt
     slots = []
-    for offset in offsets + [offset | 1 << Y for offset in offsets]:
+    for offset in offsets + [offset | 1 << Y for group in groups for offset in group]:
         places = []
         for member in MEMBERS:
             at = (offset ^ member) // n_resp
@@ -465,8 +471,11 @@
     far = give(back_stacks[1], 1 << Y)
     near = give(back_stacks[0], 1 << Y)
     far, grads = lax.optimization_barrier((far, grads))
-    arrived = {offset: [near[index]] for index, offset in enumerate(offsets[:half])}
-    arrived.update({offset: [far[index]] for index, offset in enumerate(offsets[half:])})
+    arrived = {
+        offset: [stack[index]]
+        for group, stack in ((some, near), (many, far))
+        for index, offset in enumerate(group)
+    }
     for bit in reversed(line_bits):
         first = None
         for offset in sorted(sums, reverse=True):
@@ -481,13 +490,13 @@
                 arrived[offset ^ 1 << bit].append(give(piece.astype(BF16), 1 << bit))
                 first = offset ^ 1 << bit if first is None else first
     back = [grads[0]] + [give(grads[j], MEMBERS[j]) for j in range(1, len(MEMBERS))]
-    (own, other, away), back = lax.optimization_barrier((total(sums[0], arrived[0]), back))
-    near = give(away, MEMBERS[2])
-    shares = [own, give(other, MEMBERS[1]), near[0], give(near[1], MEMBERS[1])]
+    blocks, back = lax.optimization_barrier((total(sums[0], arrived[0]), back))
+    shares = [blocks[0]] + [give(blocks[j], MEMBERS[j]) for j in range(1, len(MEMBERS))]
+    start = prompt_gradient((0, 1), shares[:2], key_weight, value_weight)
     unpacked = unpack(back, queries.shape[1], own_keys.shape[1])
-    shares, unpacked = lax.optimization_barrier((shares, unpacked))
+    start, unpacked = lax.optimization_barrier((start, unpacked))
     query_grad, key_grad, value_grad = unpacked
-    prompt_grad = prompt_gradient(shares, key_weight, value_weight)
+    prompt_grad = prompt_gradient((2, 3), shares[2:], key_weight, value_weight, start)
     return (query_grad, key_grad, value_grad, prompt_grad)
 
 

time: 75.5 us -> 75.5 us (level)
  Pallas kernels: 17.7 us -> 19 us
    pallas_call x1, Pallas kernels: 7.88 us -> 9.04 us  [attend(): pl.pallas_call(functools.partial(attend_kernel, slots, group, rows, resp_...]
    ppermute x11, starting transfers between devices: 13.3 us -> 12.2 us  [give(): return lax.ppermute(x, ('prompt', 'resp'), pairs)]
    ppermute x10 -> x11, starting transfers between devices: 13.9 us -> 14.4 us  [fetch(): return lax.ppermute(x, ('prompt', 'resp'), pairs)]
    ppermute x10 -> x11, waiting for transfers between devices: 15.7 us -> 15.3 us  [fetch(): return lax.ppermute(x, ('prompt', 'resp'), pairs)]
    pallas_call x2 -> x3, Pallas kernels: 3.75 us -> 3.87 us  [the longest x2 3.81 us: prompt_gradient(): pl.pallas_call(functools.partial(prompt_kernel, chunk, members, first), o...]
  transfers between devices with their start and end apart: 21 -> 22, of which waited for: 12 -> 10; matrix products, arithmetic and copies ran while one was open for 0% -> 0% of each run, Pallas kernels for 2% -> 4%
where the time goes in v9:
time: 75.5 us; the launch traced here: 75.3 us
  waiting for transfers between devices  26.7 us (35%)
  starting transfers between devices  26.6 us (35%)
  Pallas kernels  19 us (25%)
  between operations  1.7 us (2%)
  local copies, waits for them, and re-layouts  1.14 us (2%)
    ppermute x11, waiting for transfers between devices, fetch(): return lax.ppermute(x, ('prompt', 'resp'), pairs)  15.3 us
    ppermute x11, starting transfers between devices, fetch(): return lax.ppermute(x, ('prompt', 'resp'), pairs)  14.4 us
    ppermute x11, starting transfers between devices, give(): return lax.ppermute(x, ('prompt', 'resp'), pairs)  12.2 us
    ppermute x11, waiting for transfers between devices, give(): return lax.ppermute(x, ('prompt', 'resp'), pairs)  11.4 us
    pallas_call x1, Pallas kernels, attend(): pl.pallas_call(functools.partial(attend_kernel, slots, group, rows, resp_...  9.04 us
    pallas_call x1, Pallas kernels, project(): pl.pallas_call(functools.partial(project_kernel, steps), out_shape=[jax.S...  4.37 us
    pallas_call x2, Pallas kernels, prompt_gradient(): pl.pallas_call(functools.partial(prompt_kernel, chunk, members, first), o...  3.81 us
  transfers between devices with their start and end apart: 22, of which 10 were waited for; matrix products, arithmetic and copies ran while one was open for 0% of the time, Pallas kernels for 4%

profile of v9, /device:TPU:0, one launch (start us, length us, event | category | flops | bytes accessed | tf_op | source)
XLA Modules:
  0.0 75.3 jit_solution(8120734158957801811)
XLA Ops:
  1.2 1.9 %collective-permute-done.other_ref = bf16[64,5120]{1,0:T(8,128)(2,1)S(1)} collective-permute-done((bf16[64,5120]{1,0:T(8,128)(2,1)}, bf16[64,5120]{1,0:T(8,128)(2,1)S(1)}, u32[]{:S(2)}, u32[]{:S(2)}) %collective-permute-start) | collective-permute-done | bytes 655392 | tf_op jit(solution)/shard_map/ppermute | solution.py:428
  4.2 4.4 %project_prefix.1 = (bf16[128,256]{1,0:T(8,128)(2,1)S(1)}, bf16[128,256]{1,0:T(8,128)(2,1)S(1)}) custom-call(bf16[64,5120]{1,0:T(8,128)(2,1)S(1)} %copy-done, bf16[64,5120]{1,0:T(8,128)(2,1)S(1)} %collective-permute-done.other_ref, bf16[5120,512]{1,0:T(8,128)(2,1)} %rest_2_.3, bf16[5120,512]{1,0:T(8,128)(2,1)} %rest_3_.3), custom_call_target="tpu_custom_call" | custom-call | flops 671088640 | bytes 6553600 | tf_op jit(solution)/shard_map/project_prefix/pallas_call | solution.py:102
  8.6 2.9 %collective-permute-start.1 = (bf16[128,256]{1,0:T(8,128)(2,1)S(1)}, bf16[128,256]{1,0:T(8,128)(2,1)S(1)}, u32[]{:S(2)}, u32[]{:S(2)}) collective-permute-start(bf16[128,256]{1,0:T(8,128)(2,1)S(1)} %get-tuple-element.60), channel_id=1, source_target_pairs={{8,0},{17,1},{10,2},{19,3},{12,4},{21,5},{14,6},{23,7},{0,8},{25,9... | collective-permute-start | bytes 196616 | tf_op jit(solution)/shard_map/ppermute | solution.py:428
  13.8 2.1 %collective-permute-start.5 = (bf16[128,1664]{1,0:T(8,128)(2,1)S(1)}, bf16[128,1664]{1,0:T(8,128)(2,1)S(1)}, u32[]{:S(2)}, u32[]{:S(2)}) collective-permute-start(bf16[128,1664]{1,0:T(8,128)(2,1)S(1)} %get-tuple-element.69), channel_id=1, source_target_pairs={{8,0},{17,1},{10,2},{19,3},{12,4},{21,5},{14,6},{23,7},{0,8},{25,9... | collective-permute-start | bytes 1277960 | tf_op jit(solution)/shard_map/ppermute | solution.py:428
  16.0 2.8 %collective-permute-start.2 = (bf16[4,64,256]{2,1,0:T(8,128)(2,1)S(1)}, bf16[4,64,256]{2,1,0:T(8,128)(2,1)S(1)}, u32[]{:S(2)}, u32[]{:S(2)}) collective-permute-start(bf16[4,64,256]{2,1,0:T(8,128)(2,1)S(1)} %bitcast.22), channel_id=1, source_target_pairs={{4,0},{5,1},{6,2},{7,3},{0,4},{1,5},{2,6},{3,7},{12,8},{13,9},{14,... | collective-permute-start | bytes 393224 | tf_op jit(solution)/shard_map/ppermute | solution.py:428
  18.8 1.6 %collective-permute-start.7 = (bf16[4,64,256]{2,1,0:T(8,128)(2,1)S(1)}, bf16[4,64,256]{2,1,0:T(8,128)(2,1)S(1)}, u32[]{:S(2)}, u32[]{:S(2)}) collective-permute-start(bf16[4,64,256]{2,1,0:T(8,128)(2,1)S(1)} %bitcast.23), channel_id=1, source_target_pairs={{2,0},{3,1},{0,2},{1,3},{6,4},{7,5},{4,6},{5,7},{10,8},{11,9},{8,1... | collective-permute-start | bytes 393224 | tf_op jit(solution)/shard_map/ppermute | solution.py:428
  20.4 5.3 %collective-permute-done.2.rest_5_ = bf16[4,64,256]{2,1,0:T(8,128)(2,1)S(1)} collective-permute-done((bf16[4,64,256]{2,1,0:T(8,128)(2,1)S(1)}, bf16[4,64,256]{2,1,0:T(8,128)(2,1)S(1)}, u32[]{:S(2)}, u32[]{:S(2)}) %collective-permute-start.2) | collective-permute-done | bytes 131104 | tf_op jit(solution)/shard_map/ppermute | solution.py:428
  26.4 1.6 %collective-permute-start.8 = (bf16[2,4,64,256]{3,2,1,0:T(8,128)(2,1)S(1)}, bf16[2,4,64,256]{3,2,1,0:T(8,128)(2,1)S(1)}, u32[]{:S(2)}, u32[]{:S(2)}) collective-permute-start(bf16[2,4,64,256]{3,2,1,0:T(8,128)(2,1)S(1)} %pad_maximum_fusion), channel_id=1, source_target_pairs={{16,0},{9,1},{18,2},{11,3},{20,4},{13,5},{22,6},{15,7},{24,8},{1,9... | collective-permute-start | bytes 786440 | tf_op jit(solution)/shard_map/ppermute | solution.py:428
  28.0 2.8 %collective-permute-done.3.rest_7_ = bf16[4,64,256]{2,1,0:T(8,128)(2,1)S(1)} collective-permute-done((bf16[4,64,256]{2,1,0:T(8,128)(2,1)S(1)}, bf16[4,64,256]{2,1,0:T(8,128)(2,1)S(1)}, u32[]{:S(2)}, u32[]{:S(2)}) %collective-permute-start.3) | collective-permute-done | bytes 131104 | tf_op jit(solution)/shard_map/ppermute | solution.py:428
  30.8 1.5 %collective-permute-start.9 = (bf16[1,4,64,256]{3,2,1,0:T(8,128)(2,1)S(1)}, bf16[1,4,64,256]{3,2,1,0:T(8,128)(2,1)S(1)}, u32[]{:S(2)}, u32[]{:S(2)}) collective-permute-start(bf16[1,4,64,256]{3,2,1,0:T(8,128)(2,1)S(1)} %bitcast.27), channel_id=1, source_target_pairs={{16,0},{9,1},{18,2},{11,3},{20,4},{13,5},{22,6},{15,7},{24,8},{1,9... | collective-permute-start | bytes 393224 | tf_op jit(solution)/shard_map/ppermute | solution.py:428
  32.9 2.8 %collective-permute-done.9.rest_9_ = bf16[1,4,64,256]{3,2,1,0:T(8,128)(2,1)S(1)} collective-permute-done((bf16[1,4,64,256]{3,2,1,0:T(8,128)(2,1)S(1)}, bf16[1,4,64,256]{3,2,1,0:T(8,128)(2,1)S(1)}, u32[]{:S(2)}, u32[]{:S(2)}) %collective-permute-start.9) | collective-permute-done | bytes 131104 | tf_op jit(solution)/shard_map/ppermute | solution.py:428
  35.7 1.6 %collective-permute-done.10.rest_10_ = bf16[1,4,64,256]{3,2,1,0:T(8,128)(2,1)S(1)} collective-permute-done((bf16[1,4,64,256]{3,2,1,0:T(8,128)(2,1)S(1)}, bf16[1,4,64,256]{3,2,1,0:T(8,128)(2,1)S(1)}, u32[]{:S(2)}, u32[]{:S(2)}) %collective-permute-start.10) | collective-permute-done | bytes 131104 | tf_op jit(solution)/shard_map/ppermute | solution.py:428
  37.4 9.0 %attend_head.1 = (bf16[128,896]{1,0:T(8,128)(2,1)S(1)}, bf16[128,896]{1,0:T(8,128)(2,1)S(1)}, bf16[128,896]{1,0:T(8,128)(2,1)S(1)}, bf16[128,896]{1,0:T(8,128)(2...) custom-call(bf16[128,1664]{1,0:T(8,128)(2,1)S(1)} %get-tuple-element, ...), custom_call_target="tpu_custom_call" | custom-call | flops 4194304000 | bytes 16777216 | tf_op jit(solution)/shard_map/attend_head/pallas_call | solution.py:320
  46.4 1.3 %collective-permute-start.12 = (bf16[2,4,64,256]{3,2,1,0:T(8,128)(2,1)S(1)}, bf16[2,4,64,256]{3,2,1,0:T(8,128)(2,1)S(1)}, u32[]{:S(2)}, u32[]{:S(2)}) collective-permute-start(bf16[2,4,64,256]{3,2,1,0:T(8,128)(2,1)S(1)} %get-tuple-element.80), channel_id=1, source_target_pairs={{0,16},{1,9},{2,18},{3,11},{4,20},{5,13},{6,22},{7,15},{8,24},{9,1... | collective-permute-start | bytes 786440 | tf_op jit(solution)/shard_map/ppermute | solution.py:432
  48.5 4.3 %collective-permute-done.12 = bf16[2,4,64,256]{3,2,1,0:T(8,128)(2,1)S(1)} collective-permute-done((bf16[2,4,64,256]{3,2,1,0:T(8,128)(2,1)S(1)}, bf16[2,4,64,256]{3,2,1,0:T(8,128)(2,1)S(1)}, u32[]{:S(2)}, u32[]{:S(2)}) %collective-permute-start.12) | collective-permute-done | bytes 262176 | tf_op jit(solution)/shard_map/ppermute | solution.py:432
  52.9 1.1 %collective-permute-start.13 = (bf16[4,64,256]{2,1,0:T(8,128)(2,1)S(1)}, bf16[4,64,256]{2,1,0:T(8,128)(2,1)S(1)}, u32[]{:S(2)}, u32[]{:S(2)}) collective-permute-start(bf16[4,64,256]{2,1,0:T(8,128)(2,1)S(1)} %fusion.2), channel_id=1, source_target_pairs={{0,2},{1,3},{2,0},{3,1},{4,6},{5,7},{6,4},{7,5},{8,10},{9,11},{10,... | collective-permute-start | bytes 393224 | tf_op jit(solution)/shard_map/ppermute | solution.py:432
  54.0 1.5 %collective-permute-start.17 = (bf16[128,896]{1,0:T(8,128)(2,1)S(1)}, bf16[128,896]{1,0:T(8,128)(2,1)S(1)}, u32[]{:S(2)}, u32[]{:S(2)}) collective-permute-start(bf16[128,896]{1,0:T(8,128)(2,1)S(1)} %get-tuple-element.95), channel_id=1, source_target_pairs={{0,8},{1,17},{2,10},{3,19},{4,12},{5,21},{6,14},{7,23},{8,0},{9,25... | collective-permute-start | bytes 688136 | tf_op jit(solution)/shard_map/ppermute | solution.py:432
  56.7 1.3 %collective-permute-done.13 = bf16[4,64,256]{2,1,0:T(8,128)(2,1)S(1)} collective-permute-done((bf16[4,64,256]{2,1,0:T(8,128)(2,1)S(1)}, bf16[4,64,256]{2,1,0:T(8,128)(2,1)S(1)}, u32[]{:S(2)}, u32[]{:S(2)}) %collective-permute-start.13) | collective-permute-done | bytes 131104 | tf_op jit(solution)/shard_map/ppermute | solution.py:432
  59.0 3.4 %collective-permute-start.15 = (bf16[4,64,256]{2,1,0:T(8,128)(2,1)S(1)}, bf16[4,64,256]{2,1,0:T(8,128)(2,1)S(1)}, u32[]{:S(2)}, u32[]{:S(2)}) collective-permute-start(bf16[4,64,256]{2,1,0:T(8,128)(2,1)S(1)} %fusion.1), channel_id=1, source_target_pairs={{0,4},{1,5},{2,6},{3,7},{4,0},{5,1},{6,2},{7,3},{8,12},{9,13},{10,... | collective-permute-start | bytes 393224 | tf_op jit(solution)/shard_map/ppermute | solution.py:432
  62.5 1.9 %collective-permute-done.14.rest_1_ = bf16[4,64,256]{2,1,0:T(8,128)(2,1)S(1)} collective-permute-done((bf16[4,64,256]{2,1,0:T(8,128)(2,1)S(1)}, bf16[4,64,256]{2,1,0:T(8,128)(2,1)S(1)}, u32[]{:S(2)}, u32[]{:S(2)}) %collective-permute-start.14) | collective-permute-done | bytes 131104 | tf_op jit(solution)/shard_map/ppermute | solution.py:432
  64.4 3.9 %collective-permute-done.15.rest_2_ = bf16[4,64,256]{2,1,0:T(8,128)(2,1)S(1)} collective-permute-done((bf16[4,64,256]{2,1,0:T(8,128)(2,1)S(1)}, bf16[4,64,256]{2,1,0:T(8,128)(2,1)S(1)}, u32[]{:S(2)}, u32[]{:S(2)}) %collective-permute-start.15) | collective-permute-done | bytes 131104 | tf_op jit(solution)/shard_map/ppermute | solution.py:432
  69.0 1.2 %collective-permute-start.21 = (bf16[64,256]{1,0:T(8,128)(2,1)S(1)}, bf16[64,256]{1,0:T(8,128)(2,1)S(1)}, u32[]{:S(2)}, u32[]{:S(2)}) collective-permute-start(bf16[64,256]{1,0:T(8,128)(2,1)S(1)} %get-tuple-element.110), channel_id=1, source_target_pairs={{0,9},{1,16},{2,11},{3,18},{4,13},{5,20},{6,15},{7,22},{8,1},{9,24... | collective-permute-start | bytes 98312 | tf_op jit(solution)/shard_map/ppermute | solution.py:432
  71.3 1.5 %prompt_gradient.2.rest_4_ = f32[5120,64]{1,0:T(8,128)S(1)} custom-call(bf16[64,256]{1,0:T(8,128)(2,1)S(1)} %get-tuple-element.97.rest_0_, bf16[64,256]{1,0:T(8,128)(2,1)S(1)} %collective-permute-done.19.rest_1_, bf16[5120,512]{1,0:T(8,128)(2,1)S(1)} %bitcast.19, bf16[5120,512]{1,0:T(8,128)(2,1)S(1)} %bitcast.21), custom_call_target="tpu_custom_call" | custom-call | flops 335544320 | bytes 5898240 | tf_op jit(solution)/shard_map/prompt_gradient/pallas_call | solution.py:393
  72.8 2.3 %prompt_gradient.3 = bf16[64,5120]{1,0:T(8,128)(2,1)} custom-call(bf16[64,256]{1,0:T(8,128)(2,1)S(1)} %collective-permute-done.20.rest_0_, bf16[64,256]{1,0:T(8,128)(2,1)S(1)} %collective-permute-done.21.rest_1_, bf16[5120,512]{1,0:T(8,128)(2,1)S(1)} %bitcast.19, bf16[5120,512]{1,0:T(8,128)(2,1)S(1)} %bitcast.21, f32[5120,64]{1,0:T(8,128)S(1)} %prompt_gradient.2.rest_4_), custom_call_target="tpu_custom_call" | custom-call | flops 335544320 | bytes 5898240 | tf_op jit(solution)/shard_map/prompt_gradient/pallas_call | solution.py:393
  (55 shorter events, 9.4 us)
Async XLA Ops:
  0.6 2.5 %collective-permute-start = (bf16[64,5120]{1,0:T(8,128)(2,1)}, bf16[64,5120]{1,0:T(8,128)(2,1)S(1)}, u32[]{:S(2)}, u32[]{:S(2)}) collective-permute-start(bf16[64,5120]{1,0:T(8,128)(2,1)} %x_ref.1), channel_id=1, source_target_pairs={{1,0},{0,1},{3,2},{2,3},{5,4},{4,5},{7,6},{6,7},{9,8},{8,9},{11,10... | collective-permute-start | bytes 1966088 | tf_op jit(solution)/shard_map/ppermute | solution.py:428
  8.6 5.2 %collective-permute-start.1 = (bf16[128,256]{1,0:T(8,128)(2,1)S(1)}, bf16[128,256]{1,0:T(8,128)(2,1)S(1)}, u32[]{:S(2)}, u32[]{:S(2)}) collective-permute-start(bf16[128,256]{1,0:T(8,128)(2,1)S(1)} %get-tuple-element.60), channel_id=1, source_target_pairs={{8,0},{17,1},{10,2},{19,3},{12,4},{21,5},{14,6},{23,7},{0,8},{25,9... | collective-permute-start | bytes 196616 | tf_op jit(solution)/shard_map/ppermute | solution.py:428
  13.8 18.5 %collective-permute-start.4 = (bf16[128,1664]{1,0:T(8,128)(2,1)S(1)}, bf16[128,1664]{1,0:T(8,128)(2,1)S(1)}, u32[]{:S(2)}, u32[]{:S(2)}) collective-permute-start(bf16[128,1664]{1,0:T(8,128)(2,1)S(1)} %get-tuple-element.68), channel_id=1, source_target_pairs={{1,0},{0,1},{3,2},{2,3},{5,4},{4,5},{7,6},{6,7},{9,8},{8,9},{11,10... | collective-permute-start | bytes 1277960 | tf_op jit(solution)/shard_map/ppermute | solution.py:428
  13.8 18.4 %collective-permute-start.5 = (bf16[128,1664]{1,0:T(8,128)(2,1)S(1)}, bf16[128,1664]{1,0:T(8,128)(2,1)S(1)}, u32[]{:S(2)}, u32[]{:S(2)}) collective-permute-start(bf16[128,1664]{1,0:T(8,128)(2,1)S(1)} %get-tuple-element.69), channel_id=1, source_target_pairs={{8,0},{17,1},{10,2},{19,3},{12,4},{21,5},{14,6},{23,7},{0,8},{25,9... | collective-permute-start | bytes 1277960 | tf_op jit(solution)/shard_map/ppermute | solution.py:428
  15.9 16.4 %collective-permute-start.6 = (bf16[128,1664]{1,0:T(8,128)(2,1)S(1)}, bf16[128,1664]{1,0:T(8,128)(2,1)S(1)}, u32[]{:S(2)}, u32[]{:S(2)}) collective-permute-start(bf16[128,1664]{1,0:T(8,128)(2,1)S(1)} %get-tuple-element.70), channel_id=1, source_target_pairs={{9,0},{16,1},{11,2},{18,3},{13,4},{20,5},{15,6},{22,7},{1,8},{24,9... | collective-permute-start | bytes 1277960 | tf_op jit(solution)/shard_map/ppermute | solution.py:428
  16.0 9.7 %collective-permute-start.2 = (bf16[4,64,256]{2,1,0:T(8,128)(2,1)S(1)}, bf16[4,64,256]{2,1,0:T(8,128)(2,1)S(1)}, u32[]{:S(2)}, u32[]{:S(2)}) collective-permute-start(bf16[4,64,256]{2,1,0:T(8,128)(2,1)S(1)} %bitcast.22), channel_id=1, source_target_pairs={{4,0},{5,1},{6,2},{7,3},{0,4},{1,5},{2,6},{3,7},{12,8},{13,9},{14,... | collective-permute-start | bytes 393224 | tf_op jit(solution)/shard_map/ppermute | solution.py:428
  18.8 7.6 %collective-permute-start.7 = (bf16[4,64,256]{2,1,0:T(8,128)(2,1)S(1)}, bf16[4,64,256]{2,1,0:T(8,128)(2,1)S(1)}, u32[]{:S(2)}, u32[]{:S(2)}) collective-permute-start(bf16[4,64,256]{2,1,0:T(8,128)(2,1)S(1)} %bitcast.23), channel_id=1, source_target_pairs={{2,0},{3,1},{0,2},{1,3},{6,4},{7,5},{4,6},{5,7},{10,8},{11,9},{8,1... | collective-permute-start | bytes 393224 | tf_op jit(solution)/shard_map/ppermute | solution.py:428
  25.7 5.0 %collective-permute-start.3 = (bf16[4,64,256]{2,1,0:T(8,128)(2,1)S(1)}, bf16[4,64,256]{2,1,0:T(8,128)(2,1)S(1)}, u32[]{:S(2)}, u32[]{:S(2)}) collective-permute-start(bf16[4,64,256]{2,1,0:T(8,128)(2,1)S(1)} %collective-permute-done.2.rest_5_), channel_id=1, source_target_pairs={{2,0},{3,1},{0,2},{1,3},{6,4},{7,5},{4,6},{5,7},{10,8},{11,9},{8,1... | collective-permute-start | bytes 393224 | tf_op jit(solution)/shard_map/ppermute | solution.py:428
  26.4 9.3 %collective-permute-start.8 = (bf16[2,4,64,256]{3,2,1,0:T(8,128)(2,1)S(1)}, bf16[2,4,64,256]{3,2,1,0:T(8,128)(2,1)S(1)}, u32[]{:S(2)}, u32[]{:S(2)}) collective-permute-start(bf16[2,4,64,256]{3,2,1,0:T(8,128)(2,1)S(1)} %pad_maximum_fusion), channel_id=1, source_target_pairs={{16,0},{9,1},{18,2},{11,3},{20,4},{13,5},{22,6},{15,7},{24,8},{1,9... | collective-permute-start | bytes 786440 | tf_op jit(solution)/shard_map/ppermute | solution.py:428
  30.8 5.0 %collective-permute-start.9 = (bf16[1,4,64,256]{3,2,1,0:T(8,128)(2,1)S(1)}, bf16[1,4,64,256]{3,2,1,0:T(8,128)(2,1)S(1)}, u32[]{:S(2)}, u32[]{:S(2)}) collective-permute-start(bf16[1,4,64,256]{3,2,1,0:T(8,128)(2,1)S(1)} %bitcast.27), channel_id=1, source_target_pairs={{16,0},{9,1},{18,2},{11,3},{20,4},{13,5},{22,6},{15,7},{24,8},{1,9... | collective-permute-start | bytes 393224 | tf_op jit(solution)/shard_map/ppermute | solution.py:428
  32.3 38.9 %slice-start = ((s8[5242880]{0:T(1024)(128)(4,1)}), s8[4194304]{0:T(1024)(128)(4,1)S(1)}, s32[]{:S(2)}) async-start(s8[5242880]{0:T(1024)(128)(4,1)} %bitcast.18), calls=%async_computation | async-start | bytes 8388608
  32.3 38.9 %slice-start.2 = ((s8[5242880]{0:T(1024)(128)(4,1)}), s8[4194304]{0:T(1024)(128)(4,1)S(1)}, s32[]{:S(2)}) async-start(s8[5242880]{0:T(1024)(128)(4,1)} %bitcast.20), calls=%async_computation.2 | async-start | bytes 8388608
  32.3 5.0 %collective-permute-start.10 = (bf16[1,4,64,256]{3,2,1,0:T(8,128)(2,1)S(1)}, bf16[1,4,64,256]{3,2,1,0:T(8,128)(2,1)S(1)}, u32[]{:S(2)}, u32[]{:S(2)}) collective-permute-start(bf16[1,4,64,256]{3,2,1,0:T(8,128)(2,1)S(1)} %bitcast.28), channel_id=1, source_target_pairs={{16,0},{9,1},{18,2},{11,3},{20,4},{13,5},{22,6},{15,7},{24,8},{1,9... | collective-permute-start | bytes 393224 | tf_op jit(solution)/shard_map/ppermute | solution.py:428
  46.4 6.4 %collective-permute-start.12 = (bf16[2,4,64,256]{3,2,1,0:T(8,128)(2,1)S(1)}, bf16[2,4,64,256]{3,2,1,0:T(8,128)(2,1)S(1)}, u32[]{:S(2)}, u32[]{:S(2)}) collective-permute-start(bf16[2,4,64,256]{3,2,1,0:T(8,128)(2,1)S(1)} %get-tuple-element.80), channel_id=1, source_target_pairs={{0,16},{1,9},{2,18},{3,11},{4,20},{5,13},{6,22},{7,15},{8,24},{9,1... | collective-permute-start | bytes 786440 | tf_op jit(solution)/shard_map/ppermute | solution.py:432
  47.8 8.9 %collective-permute-start.11 = (bf16[2,4,64,256]{3,2,1,0:T(8,128)(2,1)S(1)}, bf16[2,4,64,256]{3,2,1,0:T(8,128)(2,1)S(1)}, u32[]{:S(2)}, u32[]{:S(2)}) collective-permute-start(bf16[2,4,64,256]{3,2,1,0:T(8,128)(2,1)S(1)} %get-tuple-element.77), channel_id=1, source_target_pairs={{0,16},{1,9},{2,18},{3,11},{4,20},{5,13},{6,22},{7,15},{8,24},{9,1... | collective-permute-start | bytes 786440 | tf_op jit(solution)/shard_map/ppermute | solution.py:432
  52.9 5.0 %collective-permute-start.13 = (bf16[4,64,256]{2,1,0:T(8,128)(2,1)S(1)}, bf16[4,64,256]{2,1,0:T(8,128)(2,1)S(1)}, u32[]{:S(2)}, u32[]{:S(2)}) collective-permute-start(bf16[4,64,256]{2,1,0:T(8,128)(2,1)S(1)} %fusion.2), channel_id=1, source_target_pairs={{0,2},{1,3},{2,0},{3,1},{4,6},{5,7},{6,4},{7,5},{8,10},{9,11},{10,... | collective-permute-start | bytes 393224 | tf_op jit(solution)/shard_map/ppermute | solution.py:432
  54.0 14.3 %collective-permute-start.16 = (bf16[128,896]{1,0:T(8,128)(2,1)S(1)}, bf16[128,896]{1,0:T(8,128)(2,1)S(1)}, u32[]{:S(2)}, u32[]{:S(2)}) collective-permute-start(bf16[128,896]{1,0:T(8,128)(2,1)S(1)} %get-tuple-element.94), channel_id=1, source_target_pairs={{0,1},{1,0},{2,3},{3,2},{4,5},{5,4},{6,7},{7,6},{8,9},{9,8},{10,11... | collective-permute-start | bytes 688136 | tf_op jit(solution)/shard_map/ppermute | solution.py:432
  54.0 14.3 %collective-permute-start.17 = (bf16[128,896]{1,0:T(8,128)(2,1)S(1)}, bf16[128,896]{1,0:T(8,128)(2,1)S(1)}, u32[]{:S(2)}, u32[]{:S(2)}) collective-permute-start(bf16[128,896]{1,0:T(8,128)(2,1)S(1)} %get-tuple-element.95), channel_id=1, source_target_pairs={{0,8},{1,17},{2,10},{3,19},{4,12},{5,21},{6,14},{7,23},{8,0},{9,25... | collective-permute-start | bytes 688136 | tf_op jit(solution)/shard_map/ppermute | solution.py:432
  55.5 12.8 %collective-permute-start.18 = (bf16[128,896]{1,0:T(8,128)(2,1)S(1)}, bf16[128,896]{1,0:T(8,128)(2,1)S(1)}, u32[]{:S(2)}, u32[]{:S(2)}) collective-permute-start(bf16[128,896]{1,0:T(8,128)(2,1)S(1)} %get-tuple-element.96), channel_id=1, source_target_pairs={{0,9},{1,16},{2,11},{3,18},{4,13},{5,20},{6,15},{7,22},{8,1},{9,24... | collective-permute-start | bytes 688136 | tf_op jit(solution)/shard_map/ppermute | solution.py:432
  57.9 6.4 %collective-permute-start.14 = (bf16[4,64,256]{2,1,0:T(8,128)(2,1)S(1)}, bf16[4,64,256]{2,1,0:T(8,128)(2,1)S(1)}, u32[]{:S(2)}, u32[]{:S(2)}) collective-permute-start(bf16[4,64,256]{2,1,0:T(8,128)(2,1)S(1)} %convert_add_fusion.2), channel_id=1, source_target_pairs={{0,2},{1,3},{2,0},{3,1},{4,6},{5,7},{6,4},{7,5},{8,10},{9,11},{10,... | collective-permute-start | bytes 393224 | tf_op jit(solution)/shard_map/ppermute | solution.py:432
  59.0 9.2 %collective-permute-start.15 = (bf16[4,64,256]{2,1,0:T(8,128)(2,1)S(1)}, bf16[4,64,256]{2,1,0:T(8,128)(2,1)S(1)}, u32[]{:S(2)}, u32[]{:S(2)}) collective-permute-start(bf16[4,64,256]{2,1,0:T(8,128)(2,1)S(1)} %fusion.1), channel_id=1, source_target_pairs={{0,4},{1,5},{2,6},{3,7},{4,0},{5,1},{6,2},{7,3},{8,12},{9,13},{10,... | collective-permute-start | bytes 393224 | tf_op jit(solution)/shard_map/ppermute | solution.py:432
  68.3 2.9 %collective-permute-start.19 = (bf16[64,256]{1,0:T(8,128)(2,1)S(1)}, bf16[64,256]{1,0:T(8,128)(2,1)S(1)}, u32[]{:S(2)}, u32[]{:S(2)}) collective-permute-start(bf16[64,256]{1,0:T(8,128)(2,1)S(1)} %get-tuple-element.98), channel_id=1, source_target_pairs={{0,1},{1,0},{2,3},{3,2},{4,5},{5,4},{6,7},{7,6},{8,9},{9,8},{10,11... | collective-permute-start | bytes 98312 | tf_op jit(solution)/shard_map/ppermute | solution.py:432
  68.4 4.4 %collective-permute-start.20 = (bf16[64,256]{1,0:T(8,128)(2,1)S(1)}, bf16[64,256]{1,0:T(8,128)(2,1)S(1)}, u32[]{:S(2)}, u32[]{:S(2)}) collective-permute-start(bf16[64,256]{1,0:T(8,128)(2,1)S(1)} %get-tuple-element.109), channel_id=1, source_target_pairs={{0,8},{1,17},{2,10},{3,19},{4,12},{5,21},{6,14},{7,23},{8,0},{9,25... | collective-permute-start | bytes 98312 | tf_op jit(solution)/shard_map/ppermute | solution.py:432
  69.0 3.8 %collective-permute-start.21 = (bf16[64,256]{1,0:T(8,128)(2,1)S(1)}, bf16[64,256]{1,0:T(8,128)(2,1)S(1)}, u32[]{:S(2)}, u32[]{:S(2)}) collective-permute-start(bf16[64,256]{1,0:T(8,128)(2,1)S(1)} %get-tuple-element.110), channel_id=1, source_target_pairs={{0,9},{1,16},{2,11},{3,18},{4,13},{5,20},{6,15},{7,22},{8,1},{9,24... | collective-permute-start | bytes 98312 | tf_op jit(solution)/shard_map/ppermute | solution.py:432
  (8 other events, 118.9 us)

commit v10 on v8

--- a/solution.py
+++ b/solution.py
@@ -193,7 +193,7 @@
     packets = take(n)
     kv_in = unstack(take(pieces // 2), take(2))
     grads_out = take(n)
-    prefix_out = unstack(take(pieces // 2), take(2))
+    prefix_out = unstack(take(pieces // 2), take(3))
     keys, values, key_acc, value_acc = rest
     blocks, part, _ = kv_in[0].shape
     _, core, prompt_place = place()
@@ -321,7 +321,9 @@
     sums_shape = (prompts, PLEN, E)
     out_shape = [jax.ShapeDtypeStruct((rows, (group + 2) * E), BF16)] * len(packets)
     out_shape += [jax.ShapeDtypeStruct(x.shape, F32) for x in line]
-    out_shape += [jax.ShapeDtypeStruct(x.shape, BF16) for x in stacks]
+    out_shape += [
+        jax.ShapeDtypeStruct((count, *line[0].shape), BF16) for count in (1, len(line) - 2, 1)
+    ]
     operands = [*packets, *line, *stacks]
     outs = pl.pallas_call(
         functools.partial(attend_kernel, slots, group, rows, resp_bits),
@@ -335,12 +337,12 @@
         ),
         name="attend_head",
     )(*operands)
-    return outs[: len(packets)], outs[len(packets) : -2], outs[-2:]
+    return outs[: len(packets)], outs[len(packets) : -3], outs[-3:]
 
 
 def total_kernel(keep_ref, *rest):
-    parts, (own_ref, other_ref, away_ref) = rest[:-3], rest[-3:]
-    for j, out in enumerate((own_ref, other_ref, away_ref.at[0], away_ref.at[1])):
+    parts, outs = rest[: -len(MEMBERS)], rest[-len(MEMBERS) :]
+    for j, out in enumerate(outs):
         result = keep_ref[j]
         for part in parts:
             result = result + part[j].astype(F32)
@@ -348,54 +350,66 @@
 
 
 def total(keep, parts):
-    _, rows, width = keep.shape
     return pl.pallas_call(
         total_kernel,
-        out_shape=[
-            jax.ShapeDtypeStruct(shape, BF16)
-            for shape in ((rows, width), (rows, width), (2, rows, width))
-        ],
+        out_shape=[jax.ShapeDtypeStruct(keep.shape[1:], BF16)] * len(MEMBERS),
         in_specs=[VMEM] * (1 + len(parts)),
-        out_specs=[VMEM] * 3,
+        out_specs=[VMEM] * len(MEMBERS),
         compiler_params=params(16),
         cost_estimate=cost(0, 1 << 25),
         name="total_prefix_grads",
     )(keep, *parts)
 
 
-def prompt_kernel(n, chunk, *rest):
-    shares, (kw_ref, vw_ref, out_ref, key_grad, value_grad, out, sems) = rest[:n], rest[n:]
+def prompt_kernel(chunk, members, first, *rest):
+    rest = list(rest)
+    shares = [rest.pop(0) for _ in members]
+    kw_ref, vw_ref = rest.pop(0), rest.pop(0)
+    start_ref = None if first else rest.pop(0)
+    out_ref, *scratch = rest
     heads, _, _ = place()
-    for head, share in zip(heads, shares):
-        key_grad[:, lanes(head, E)] = share[:, :E]
-        value_grad[:, lanes(head, E)] = share[:, E:]
+    key_grad, value_grad = (
+        jnp.concatenate([share[:, at : at + E] for share in shares], axis=1) for at in (0, E)
+    )
     copies = []
     for index in range(kw_ref.shape[0] // chunk):
         span = slice(index * chunk, (index + 1) * chunk)
-        turned = dot(kw_ref[span, :], key_grad[...], 1, 1)
-        turned = turned + dot(vw_ref[span, :], value_grad[...], 1, 1)
-        out[:, span] = turned.T.astype(BF16)
+        key_part, value_part = (
+            jnp.concatenate([weight[span, lanes(heads[j], E)] for j in members], axis=1)
+            for weight in (kw_ref, vw_ref)
+        )
+        turned = dot(key_part, key_grad, 1, 1) + dot(value_part, value_grad, 1, 1)
+        if first:
+            out_ref[span, :] = turned
+            continue
+        out, sems = scratch
+        out[:, span] = (turned + start_ref[span, :]).T.astype(BF16)
         copies.append(pltpu.make_async_copy(out.at[:, span], out_ref.at[:, span], sems.at[index]))
         copies[-1].start()
     for copy in copies:
         copy.wait()
 
 
-def prompt_gradient(shares, key_weight, value_weight, chunk=1024):
-    n = len(shares)
+def prompt_gradient(members, shares, key_weight, value_weight, start=None, chunk=1024):
+    first = start is None
     rows = shares[0].shape[0]
     depth, width = key_weight.shape
+    operands = [*shares, key_weight, value_weight] + ([] if first else [start])
+    out = jax.ShapeDtypeStruct((depth, rows), F32)
+    if not first:
+        out = jax.ShapeDtypeStruct((rows, depth), BF16)
     return pl.pallas_call(
-        functools.partial(prompt_kernel, n, chunk),
-        out_shape=jax.ShapeDtypeStruct((rows, depth), BF16),
-        in_specs=[VMEM] * (n + 2),
-        out_specs=ANY,
-        scratch_shapes=[pltpu.VMEM((rows, width), BF16)] * 2
-        + [pltpu.VMEM((rows, depth), BF16), pltpu.SemaphoreType.DMA((depth // chunk,))],
-        compiler_params=params(32),
-        cost_estimate=cost(4 * rows * depth * width, 4 * depth * width + 2 * rows * depth),
+        functools.partial(prompt_kernel, chunk, members, first),
+        out_shape=out,
+        in_specs=[VMEM] * len(operands),
+        out_specs=VMEM if first else ANY,
+        scratch_shapes=[]
+        if first
+        else [pltpu.VMEM((rows, depth), BF16), pltpu.SemaphoreType.DMA((depth // chunk,))],
+        compiler_params=params(24),
+        cost_estimate=cost(2 * rows * depth * width, 2 * depth * width + 2 * rows * depth),
         name="prompt_gradient",
-    )(*shares, key_weight, value_weight)
+    )(*operands)
 
 
 def per_device(
@@ -439,10 +453,8 @@
         for offset in list(pieces):
             pieces[offset | 1 << bit] = fetch(pieces[offset], 1 << bit)
     offsets = list(pieces)
-    half = len(offsets) // 2
     stacks = [
-        jnp.stack([pieces[offset] for offset in some])
-        for some in (offsets[:half], offsets[half:])
+        jnp.stack([pieces[offset] for offset in some]) for some in (offsets[:-1], offsets[-1:])
     ]
     stacks[1], packets = lax.optimization_barrier((stacks[1], packets))
     stacks = [fetch(x, 1 << Y) for x in stacks]
@@ -462,32 +474,29 @@
     )
 
     sums = dict(zip(offsets, sums))
-    far = give(back_stacks[1], 1 << Y)
+    far = give(back_stacks[2], 1 << Y)
+    middle = give(back_stacks[1], 1 << Y)
     near = give(back_stacks[0], 1 << Y)
     far, grads = lax.optimization_barrier((far, grads))
-    arrived = {offset: [near[index]] for index, offset in enumerate(offsets[:half])}
-    arrived.update({offset: [far[index]] for index, offset in enumerate(offsets[half:])})
+    back = [grads[0]] + [give(grads[j], MEMBERS[j]) for j in range(1, len(MEMBERS))]
+    arrived = {offset: [middle[index]] for index, offset in enumerate(offsets[1:-1])}
+    arrived.update({offsets[0]: [near[0]], offsets[-1]: [far[0]]})
     for bit in reversed(line_bits):
-        first = None
         for offset in sorted(sums, reverse=True):
             if offset & 1 << bit:
                 piece = sums.pop(offset)
                 for x in arrived.pop(offset):
                     piece = piece + x.astype(F32)
-                if offset == 1 << bit and first is not None:
-                    piece, arrived[first][-1] = lax.optimization_barrier(
-                        (piece, arrived[first][-1])
-                    )
+                if offset == 1 << bit and bit != line_bits[0]:
+                    piece, back[2] = lax.optimization_barrier((piece, back[2]))
                 arrived[offset ^ 1 << bit].append(give(piece.astype(BF16), 1 << bit))
-                first = offset ^ 1 << bit if first is None else first
-    back = [grads[0]] + [give(grads[j], MEMBERS[j]) for j in range(1, len(MEMBERS))]
-    (own, other, away), back = lax.optimization_barrier((total(sums[0], arrived[0]), back))
-    near = give(away, MEMBERS[2])
-    shares = [own, give(other, MEMBERS[1]), near[0], give(near[1], MEMBERS[1])]
     unpacked = unpack(back, queries.shape[1], own_keys.shape[1])
-    shares, unpacked = lax.optimization_barrier((shares, unpacked))
+    arrived[0], unpacked = lax.optimization_barrier((arrived[0], unpacked))
     query_grad, key_grad, value_grad = unpacked
-    prompt_grad = prompt_gradient(shares, key_weight, value_weight)
+    blocks = total(sums[0], arrived[0])
+    shares = [blocks[0]] + [give(blocks[j], MEMBERS[j]) for j in range(1, len(MEMBERS))]
+    start = prompt_gradient((0, 1), shares[:2], key_weight, value_weight)
+    prompt_grad = prompt_gradient((2, 3), shares[2:], key_weight, value_weight, start)
     return (query_grad, key_grad, value_grad, prompt_grad)
 
 

time: 75.5 us -> 72.6 us (0.962)
  starting transfers between devices: 27.2 us -> 23.4 us
  waiting for transfers between devices: 27.4 us -> 28.3 us
    ppermute x11 -> x12, starting transfers between devices: 13.3 us -> 9.69 us  [give(): return lax.ppermute(x, ('prompt', 'resp'), pairs)]
    ppermute x11 -> x12, waiting for transfers between devices: 11.6 us -> 13.2 us  [give(): return lax.ppermute(x, ('prompt', 'resp'), pairs)]
    pallas_call x2 -> x3, Pallas kernels: 3.75 us -> 3.87 us  [the longest x2 3.81 us: prompt_gradient(): pl.pallas_call(functools.partial(prompt_kernel, chunk, members, first), o...]
  transfers between devices with their start and end apart: 21 -> 22, of which waited for: 12 -> 15; matrix products, arithmetic and copies ran while one was open for 0% -> 0% of each run, Pallas kernels for 2% -> 4%
where the time goes in v10:
time: 72.6 us; the launch traced here: 72.4 us
  waiting for transfers between devices  28.3 us (39%)
  starting transfers between devices  23.4 us (32%)
  Pallas kernels  17.8 us (25%)
  between operations  1.62 us (2%)
  local copies, waits for them, and re-layouts  1.12 us (2%)
    ppermute x10, waiting for transfers between devices, fetch(): return lax.ppermute(x, ('prompt', 'resp'), pairs)  15.1 us
    ppermute x10, starting transfers between devices, fetch(): return lax.ppermute(x, ('prompt', 'resp'), pairs)  13.7 us
    ppermute x12, waiting for transfers between devices, give(): return lax.ppermute(x, ('prompt', 'resp'), pairs)  13.2 us
    ppermute x12, starting transfers between devices, give(): return lax.ppermute(x, ('prompt', 'resp'), pairs)  9.69 us
    pallas_call x1, Pallas kernels, attend(): pl.pallas_call(functools.partial(attend_kernel, slots, group, rows, resp_...  7.88 us
    pallas_call x1, Pallas kernels, project(): pl.pallas_call(functools.partial(project_kernel, steps), out_shape=[jax.S...  4.37 us
    pallas_call x2, Pallas kernels, prompt_gradient(): pl.pallas_call(functools.partial(prompt_kernel, chunk, members, first), o...  3.81 us
  transfers between devices with their start and end apart: 22, of which 15 were waited for; matrix products, arithmetic and copies ran while one was open for 0% of the time, Pallas kernels for 4%

profile of v10, /device:TPU:0, one launch (start us, length us, event | category | flops | bytes accessed | tf_op | source)
XLA Modules:
  0.0 72.4 jit_solution(11066200231652040577)
XLA Ops:
  1.2 1.9 %collective-permute-done.other_ref = bf16[64,5120]{1,0:T(8,128)(2,1)S(1)} collective-permute-done((bf16[64,5120]{1,0:T(8,128)(2,1)}, bf16[64,5120]{1,0:T(8,128)(2,1)S(1)}, u32[]{:S(2)}, u32[]{:S(2)}) %collective-permute-start) | collective-permute-done | bytes 655392 | tf_op jit(solution)/shard_map/ppermute | solution.py:436
  4.2 4.4 %project_prefix.1 = (bf16[128,256]{1,0:T(8,128)(2,1)S(1)}, bf16[128,256]{1,0:T(8,128)(2,1)S(1)}) custom-call(bf16[64,5120]{1,0:T(8,128)(2,1)S(1)} %copy-done, bf16[64,5120]{1,0:T(8,128)(2,1)S(1)} %collective-permute-done.other_ref, bf16[5120,512]{1,0:T(8,128)(2,1)} %rest_2_.3, bf16[5120,512]{1,0:T(8,128)(2,1)} %rest_3_.3), custom_call_target="tpu_custom_call" | custom-call | flops 671088640 | bytes 6553600 | tf_op jit(solution)/shard_map/project_prefix/pallas_call | solution.py:102
  8.6 2.9 %collective-permute-start.1 = (bf16[128,256]{1,0:T(8,128)(2,1)S(1)}, bf16[128,256]{1,0:T(8,128)(2,1)S(1)}, u32[]{:S(2)}, u32[]{:S(2)}) collective-permute-start(bf16[128,256]{1,0:T(8,128)(2,1)S(1)} %get-tuple-element.55), channel_id=1, source_target_pairs={{8,0},{17,1},{10,2},{19,3},{12,4},{21,5},{14,6},{23,7},{0,8},{25,9... | collective-permute-start | bytes 196616 | tf_op jit(solution)/shard_map/ppermute | solution.py:436
  13.8 2.2 %collective-permute-start.7 = (bf16[4,64,256]{2,1,0:T(8,128)(2,1)S(1)}, bf16[4,64,256]{2,1,0:T(8,128)(2,1)S(1)}, u32[]{:S(2)}, u32[]{:S(2)}) collective-permute-start(bf16[4,64,256]{2,1,0:T(8,128)(2,1)S(1)} %bitcast.23), channel_id=1, source_target_pairs={{2,0},{3,1},{0,2},{1,3},{6,4},{7,5},{4,6},{5,7},{10,8},{11,9},{8,1... | collective-permute-start | bytes 393224 | tf_op jit(solution)/shard_map/ppermute | solution.py:436
  15.9 2.6 %collective-permute-start.2 = (bf16[4,64,256]{2,1,0:T(8,128)(2,1)S(1)}, bf16[4,64,256]{2,1,0:T(8,128)(2,1)S(1)}, u32[]{:S(2)}, u32[]{:S(2)}) collective-permute-start(bf16[4,64,256]{2,1,0:T(8,128)(2,1)S(1)} %bitcast.24), channel_id=1, source_target_pairs={{4,0},{5,1},{6,2},{7,3},{0,4},{1,5},{2,6},{3,7},{12,8},{13,9},{14,... | collective-permute-start | bytes 393224 | tf_op jit(solution)/shard_map/ppermute | solution.py:436
  18.5 1.5 %collective-permute-start.5 = (bf16[128,1664]{1,0:T(8,128)(2,1)S(1)}, bf16[128,1664]{1,0:T(8,128)(2,1)S(1)}, u32[]{:S(2)}, u32[]{:S(2)}) collective-permute-start(bf16[128,1664]{1,0:T(8,128)(2,1)S(1)} %get-tuple-element.64), channel_id=1, source_target_pairs={{8,0},{17,1},{10,2},{19,3},{12,4},{21,5},{14,6},{23,7},{0,8},{25,9... | collective-permute-start | bytes 1277960 | tf_op jit(solution)/shard_map/ppermute | solution.py:436
  20.4 3.4 %collective-permute-done.2.rest_5_ = bf16[4,64,256]{2,1,0:T(8,128)(2,1)S(1)} collective-permute-done((bf16[4,64,256]{2,1,0:T(8,128)(2,1)S(1)}, bf16[4,64,256]{2,1,0:T(8,128)(2,1)S(1)}, u32[]{:S(2)}, u32[]{:S(2)}) %collective-permute-start.2) | collective-permute-done | bytes 131104 | tf_op jit(solution)/shard_map/ppermute | solution.py:436
  23.8 1.6 %collective-permute-start.8 = (bf16[3,4,64,256]{3,2,1,0:T(8,128)(2,1)S(1)}, bf16[3,4,64,256]{3,2,1,0:T(8,128)(2,1)S(1)}, u32[]{:S(2)}, u32[]{:S(2)}) collective-permute-start(bf16[3,4,64,256]{3,2,1,0:T(8,128)(2,1)S(1)} %pad_maximum_fusion), channel_id=1, source_target_pairs={{16,0},{9,1},{18,2},{11,3},{20,4},{13,5},{22,6},{15,7},{24,8},{1,9... | collective-permute-start | bytes 1179656 | tf_op jit(solution)/shard_map/ppermute | solution.py:436
  25.9 4.5 %collective-permute-done.3.rest_7_ = bf16[4,64,256]{2,1,0:T(8,128)(2,1)S(1)} collective-permute-done((bf16[4,64,256]{2,1,0:T(8,128)(2,1)S(1)}, bf16[4,64,256]{2,1,0:T(8,128)(2,1)S(1)}, u32[]{:S(2)}, u32[]{:S(2)}) %collective-permute-start.3) | collective-permute-done | bytes 131104 | tf_op jit(solution)/shard_map/ppermute | solution.py:436
  31.2 1.6 %collective-permute-start.9 = (bf16[1,4,64,256]{3,2,1,0:T(8,128)(2,1)S(1)}, bf16[1,4,64,256]{3,2,1,0:T(8,128)(2,1)S(1)}, u32[]{:S(2)}, u32[]{:S(2)}) collective-permute-start(bf16[1,4,64,256]{3,2,1,0:T(8,128)(2,1)S(1)} %bitcast.30), channel_id=1, source_target_pairs={{16,0},{9,1},{18,2},{11,3},{20,4},{13,5},{22,6},{15,7},{24,8},{1,9... | collective-permute-start | bytes 393224 | tf_op jit(solution)/shard_map/ppermute | solution.py:436
  32.8 2.2 %collective-permute-done.8.rest_8_ = bf16[3,4,64,256]{3,2,1,0:T(8,128)(2,1)S(1)} collective-permute-done((bf16[3,4,64,256]{3,2,1,0:T(8,128)(2,1)S(1)}, bf16[3,4,64,256]{3,2,1,0:T(8,128)(2,1)S(1)}, u32[]{:S(2)}, u32[]{:S(2)}) %collective-permute-start.8) | collective-permute-done | bytes 393248 | tf_op jit(solution)/shard_map/ppermute | solution.py:436
  35.0 1.4 %collective-permute-done.9.rest_9_ = bf16[1,4,64,256]{3,2,1,0:T(8,128)(2,1)S(1)} collective-permute-done((bf16[1,4,64,256]{3,2,1,0:T(8,128)(2,1)S(1)}, bf16[1,4,64,256]{3,2,1,0:T(8,128)(2,1)S(1)}, u32[]{:S(2)}, u32[]{:S(2)}) %collective-permute-start.9) | collective-permute-done | bytes 131104 | tf_op jit(solution)/shard_map/ppermute | solution.py:436
  36.4 7.9 %attend_head.1 = (bf16[128,896]{1,0:T(8,128)(2,1)S(1)}, bf16[128,896]{1,0:T(8,128)(2,1)S(1)}, bf16[128,896]{1,0:T(8,128)(2,1)S(1)}, bf16[128,896]{1,0:T(8,128)(2...) custom-call(bf16[128,1664]{1,0:T(8,128)(2,1)S(1)} %get-tuple-element, ...), custom_call_target="tpu_custom_call" | custom-call | flops 4194304000 | bytes 16777216 | tf_op jit(solution)/shard_map/attend_head/pallas_call | solution.py:328
  44.3 1.6 %collective-permute-start.12 = (bf16[1,4,64,256]{3,2,1,0:T(8,128)(2,1)S(1)}, bf16[1,4,64,256]{3,2,1,0:T(8,128)(2,1)S(1)}, u32[]{:S(2)}, u32[]{:S(2)}) collective-permute-start(bf16[1,4,64,256]{3,2,1,0:T(8,128)(2,1)S(1)} %get-tuple-element.74), channel_id=1, source_target_pairs={{0,16},{1,9},{2,18},{3,11},{4,20},{5,13},{6,22},{7,15},{8,24},{9,1... | collective-permute-start | bytes 393224 | tf_op jit(solution)/shard_map/ppermute | solution.py:440
  46.4 2.9 %collective-permute-done.12 = bf16[1,4,64,256]{3,2,1,0:T(8,128)(2,1)S(1)} collective-permute-done((bf16[1,4,64,256]{3,2,1,0:T(8,128)(2,1)S(1)}, bf16[1,4,64,256]{3,2,1,0:T(8,128)(2,1)S(1)}, u32[]{:S(2)}, u32[]{:S(2)}) %collective-permute-start.12) | collective-permute-done | bytes 131104 | tf_op jit(solution)/shard_map/ppermute | solution.py:440
  49.8 1.5 %collective-permute-start.10 = (bf16[1,4,64,256]{3,2,1,0:T(8,128)(2,1)S(1)}, bf16[1,4,64,256]{3,2,1,0:T(8,128)(2,1)S(1)}, u32[]{:S(2)}, u32[]{:S(2)}) collective-permute-start(bf16[1,4,64,256]{3,2,1,0:T(8,128)(2,1)S(1)} %get-tuple-element.71), channel_id=1, source_target_pairs={{0,16},{1,9},{2,18},{3,11},{4,20},{5,13},{6,22},{7,15},{8,24},{9,1... | collective-permute-start | bytes 393224 | tf_op jit(solution)/shard_map/ppermute | solution.py:440
  51.4 1.5 %collective-permute-start.13 = (bf16[128,896]{1,0:T(8,128)(2,1)S(1)}, bf16[128,896]{1,0:T(8,128)(2,1)S(1)}, u32[]{:S(2)}, u32[]{:S(2)}) collective-permute-start(bf16[128,896]{1,0:T(8,128)(2,1)S(1)} %get-tuple-element.79), channel_id=1, source_target_pairs={{0,8},{1,17},{2,10},{3,19},{4,12},{5,21},{6,14},{7,23},{8,0},{9,25... | collective-permute-start | bytes 688136 | tf_op jit(solution)/shard_map/ppermute | solution.py:440
  52.9 1.5 %collective-permute-done.15 = bf16[4,64,256]{2,1,0:T(8,128)(2,1)S(1)} collective-permute-done((bf16[4,64,256]{2,1,0:T(8,128)(2,1)S(1)}, bf16[4,64,256]{2,1,0:T(8,128)(2,1)S(1)}, u32[]{:S(2)}, u32[]{:S(2)}) %collective-permute-start.15) | collective-permute-done | bytes 131104 | tf_op jit(solution)/shard_map/ppermute | solution.py:440
  54.9 2.5 %collective-permute-done.13.rest_2_ = bf16[128,896]{1,0:T(8,128)(2,1)S(1)} collective-permute-done((bf16[128,896]{1,0:T(8,128)(2,1)S(1)}, bf16[128,896]{1,0:T(8,128)(2,1)S(1)}, u32[]{:S(2)}, u32[]{:S(2)}) %collective-permute-start.13) | collective-permute-done | bytes 229408 | tf_op jit(solution)/shard_map/ppermute | solution.py:440
  57.4 1.6 %collective-permute-start.14 = (bf16[4,64,256]{2,1,0:T(8,128)(2,1)S(1)}, bf16[4,64,256]{2,1,0:T(8,128)(2,1)S(1)}, u32[]{:S(2)}, u32[]{:S(2)}) collective-permute-start(bf16[4,64,256]{2,1,0:T(8,128)(2,1)S(1)} %convert_add_fusion.2), channel_id=1, source_target_pairs={{0,2},{1,3},{2,0},{3,1},{4,6},{5,7},{6,4},{7,5},{8,10},{9,11},{10,... | collective-permute-start | bytes 393224 | tf_op jit(solution)/shard_map/ppermute | solution.py:440
  60.8 3.6 %collective-permute-done.16.rest_2_ = bf16[4,64,256]{2,1,0:T(8,128)(2,1)S(1)} collective-permute-done((bf16[4,64,256]{2,1,0:T(8,128)(2,1)S(1)}, bf16[4,64,256]{2,1,0:T(8,128)(2,1)S(1)}, u32[]{:S(2)}, u32[]{:S(2)}) %collective-permute-start.16) | collective-permute-done | bytes 131104 | tf_op jit(solution)/shard_map/ppermute | solution.py:440
  65.0 1.6 %collective-permute-start.19 = (bf16[64,256]{1,0:T(8,128)(2,1)S(1)}, bf16[64,256]{1,0:T(8,128)(2,1)S(1)}, u32[]{:S(2)}, u32[]{:S(2)}) collective-permute-start(bf16[64,256]{1,0:T(8,128)(2,1)S(1)} %get-tuple-element.98), channel_id=1, source_target_pairs={{0,8},{1,17},{2,10},{3,19},{4,12},{5,21},{6,14},{7,23},{8,0},{9,25... | collective-permute-start | bytes 98312 | tf_op jit(solution)/shard_map/ppermute | solution.py:440
  67.1 1.5 %prompt_gradient.2.rest_4_ = f32[5120,64]{1,0:T(8,128)S(1)} custom-call(bf16[64,256]{1,0:T(8,128)(2,1)S(1)} %get-tuple-element.100.rest_0_, bf16[64,256]{1,0:T(8,128)(2,1)S(1)} %collective-permute-done.21.rest_1_, bf16[5120,512]{1,0:T(8,128)(2,1)S(1)} %bitcast.20, bf16[5120,512]{1,0:T(8,128)(2,1)S(1)} %bitcast.22), custom_call_target="tpu_custom_call" | custom-call | flops 335544320 | bytes 5898240 | tf_op jit(solution)/shard_map/prompt_gradient/pallas_call | solution.py:401
  69.9 2.3 %prompt_gradient.3 = bf16[64,5120]{1,0:T(8,128)(2,1)} custom-call(bf16[64,256]{1,0:T(8,128)(2,1)S(1)} %collective-permute-done.19.rest_0_, bf16[64,256]{1,0:T(8,128)(2,1)S(1)} %collective-permute-done.20.rest_1_, bf16[5120,512]{1,0:T(8,128)(2,1)S(1)} %bitcast.20, bf16[5120,512]{1,0:T(8,128)(2,1)S(1)} %bitcast.22, f32[5120,64]{1,0:T(8,128)S(1)} %prompt_gradient.2.rest_4_), custom_call_target="tpu_custom_call" | custom-call | flops 335544320 | bytes 5898240 | tf_op jit(solution)/shard_map/prompt_gradient/pallas_call | solution.py:401
  (54 shorter events, 10.7 us)
Async XLA Ops:
  0.6 2.5 %collective-permute-start = (bf16[64,5120]{1,0:T(8,128)(2,1)}, bf16[64,5120]{1,0:T(8,128)(2,1)S(1)}, u32[]{:S(2)}, u32[]{:S(2)}) collective-permute-start(bf16[64,5120]{1,0:T(8,128)(2,1)} %x_ref.1), channel_id=1, source_target_pairs={{1,0},{0,1},{3,2},{2,3},{5,4},{4,5},{7,6},{6,7},{9,8},{8,9},{11,10... | collective-permute-start | bytes 1966088 | tf_op jit(solution)/shard_map/ppermute | solution.py:436
  8.6 5.2 %collective-permute-start.1 = (bf16[128,256]{1,0:T(8,128)(2,1)S(1)}, bf16[128,256]{1,0:T(8,128)(2,1)S(1)}, u32[]{:S(2)}, u32[]{:S(2)}) collective-permute-start(bf16[128,256]{1,0:T(8,128)(2,1)S(1)} %get-tuple-element.55), channel_id=1, source_target_pairs={{8,0},{17,1},{10,2},{19,3},{12,4},{21,5},{14,6},{23,7},{0,8},{25,9... | collective-permute-start | bytes 196616 | tf_op jit(solution)/shard_map/ppermute | solution.py:436
  13.8 6.6 %collective-permute-start.7 = (bf16[4,64,256]{2,1,0:T(8,128)(2,1)S(1)}, bf16[4,64,256]{2,1,0:T(8,128)(2,1)S(1)}, u32[]{:S(2)}, u32[]{:S(2)}) collective-permute-start(bf16[4,64,256]{2,1,0:T(8,128)(2,1)S(1)} %bitcast.23), channel_id=1, source_target_pairs={{2,0},{3,1},{0,2},{1,3},{6,4},{7,5},{4,6},{5,7},{10,8},{11,9},{8,1... | collective-permute-start | bytes 393224 | tf_op jit(solution)/shard_map/ppermute | solution.py:436
  15.9 7.9 %collective-permute-start.2 = (bf16[4,64,256]{2,1,0:T(8,128)(2,1)S(1)}, bf16[4,64,256]{2,1,0:T(8,128)(2,1)S(1)}, u32[]{:S(2)}, u32[]{:S(2)}) collective-permute-start(bf16[4,64,256]{2,1,0:T(8,128)(2,1)S(1)} %bitcast.24), channel_id=1, source_target_pairs={{4,0},{5,1},{6,2},{7,3},{0,4},{1,5},{2,6},{3,7},{12,8},{13,9},{14,... | collective-permute-start | bytes 393224 | tf_op jit(solution)/shard_map/ppermute | solution.py:436
  18.5 11.9 %collective-permute-start.4 = (bf16[128,1664]{1,0:T(8,128)(2,1)S(1)}, bf16[128,1664]{1,0:T(8,128)(2,1)S(1)}, u32[]{:S(2)}, u32[]{:S(2)}) collective-permute-start(bf16[128,1664]{1,0:T(8,128)(2,1)S(1)} %get-tuple-element.63), channel_id=1, source_target_pairs={{1,0},{0,1},{3,2},{2,3},{5,4},{4,5},{7,6},{6,7},{9,8},{8,9},{11,10... | collective-permute-start | bytes 1277960 | tf_op jit(solution)/shard_map/ppermute | solution.py:436
  18.5 11.9 %collective-permute-start.5 = (bf16[128,1664]{1,0:T(8,128)(2,1)S(1)}, bf16[128,1664]{1,0:T(8,128)(2,1)S(1)}, u32[]{:S(2)}, u32[]{:S(2)}) collective-permute-start(bf16[128,1664]{1,0:T(8,128)(2,1)S(1)} %get-tuple-element.64), channel_id=1, source_target_pairs={{8,0},{17,1},{10,2},{19,3},{12,4},{21,5},{14,6},{23,7},{0,8},{25,9... | collective-permute-start | bytes 1277960 | tf_op jit(solution)/shard_map/ppermute | solution.py:436
  20.0 11.2 %collective-permute-start.6 = (bf16[128,1664]{1,0:T(8,128)(2,1)S(1)}, bf16[128,1664]{1,0:T(8,128)(2,1)S(1)}, u32[]{:S(2)}, u32[]{:S(2)}) collective-permute-start(bf16[128,1664]{1,0:T(8,128)(2,1)S(1)} %get-tuple-element.65), channel_id=1, source_target_pairs={{9,0},{16,1},{11,2},{18,3},{13,4},{20,5},{15,6},{22,7},{1,8},{24,9... | collective-permute-start | bytes 1277960 | tf_op jit(solution)/shard_map/ppermute | solution.py:436
  23.8 11.1 %collective-permute-start.8 = (bf16[3,4,64,256]{3,2,1,0:T(8,128)(2,1)S(1)}, bf16[3,4,64,256]{3,2,1,0:T(8,128)(2,1)S(1)}, u32[]{:S(2)}, u32[]{:S(2)}) collective-permute-start(bf16[3,4,64,256]{3,2,1,0:T(8,128)(2,1)S(1)} %pad_maximum_fusion), channel_id=1, source_target_pairs={{16,0},{9,1},{18,2},{11,3},{20,4},{13,5},{22,6},{15,7},{24,8},{1,9... | collective-permute-start | bytes 1179656 | tf_op jit(solution)/shard_map/ppermute | solution.py:436
  25.4 5.0 %collective-permute-start.3 = (bf16[4,64,256]{2,1,0:T(8,128)(2,1)S(1)}, bf16[4,64,256]{2,1,0:T(8,128)(2,1)S(1)}, u32[]{:S(2)}, u32[]{:S(2)}) collective-permute-start(bf16[4,64,256]{2,1,0:T(8,128)(2,1)S(1)} %collective-permute-done.2.rest_5_), channel_id=1, source_target_pairs={{2,0},{3,1},{0,2},{1,3},{6,4},{7,5},{4,6},{5,7},{10,8},{11,9},{8,1... | collective-permute-start | bytes 393224 | tf_op jit(solution)/shard_map/ppermute | solution.py:436
  31.2 35.9 %slice-start.1 = ((s8[5242880]{0:T(1024)(128)(4,1)}), s8[1048576]{0:T(1024)(128)(4,1)S(1)}, s32[]{:S(2)}) async-start(s8[5242880]{0:T(1024)(128)(4,1)} %bitcast.19), calls=%async_computation.1 | async-start | bytes 2097152
  31.2 35.9 %slice-start.3 = ((s8[5242880]{0:T(1024)(128)(4,1)}), s8[1048576]{0:T(1024)(128)(4,1)S(1)}, s32[]{:S(2)}) async-start(s8[5242880]{0:T(1024)(128)(4,1)} %bitcast.21), calls=%async_computation.3 | async-start | bytes 2097152
  31.2 5.1 %collective-permute-start.9 = (bf16[1,4,64,256]{3,2,1,0:T(8,128)(2,1)S(1)}, bf16[1,4,64,256]{3,2,1,0:T(8,128)(2,1)S(1)}, u32[]{:S(2)}, u32[]{:S(2)}) collective-permute-start(bf16[1,4,64,256]{3,2,1,0:T(8,128)(2,1)S(1)} %bitcast.30), channel_id=1, source_target_pairs={{16,0},{9,1},{18,2},{11,3},{20,4},{13,5},{22,6},{15,7},{24,8},{1,9... | collective-permute-start | bytes 393224 | tf_op jit(solution)/shard_map/ppermute | solution.py:436
  44.3 5.0 %collective-permute-start.12 = (bf16[1,4,64,256]{3,2,1,0:T(8,128)(2,1)S(1)}, bf16[1,4,64,256]{3,2,1,0:T(8,128)(2,1)S(1)}, u32[]{:S(2)}, u32[]{:S(2)}) collective-permute-start(bf16[1,4,64,256]{3,2,1,0:T(8,128)(2,1)S(1)} %get-tuple-element.74), channel_id=1, source_target_pairs={{0,16},{1,9},{2,18},{3,11},{4,20},{5,13},{6,22},{7,15},{8,24},{9,1... | collective-permute-start | bytes 393224 | tf_op jit(solution)/shard_map/ppermute | solution.py:440
  45.8 8.5 %collective-permute-start.11 = (bf16[2,4,64,256]{3,2,1,0:T(8,128)(2,1)S(1)}, bf16[2,4,64,256]{3,2,1,0:T(8,128)(2,1)S(1)}, u32[]{:S(2)}, u32[]{:S(2)}) collective-permute-start(bf16[2,4,64,256]{3,2,1,0:T(8,128)(2,1)S(1)} %get-tuple-element.73), channel_id=1, source_target_pairs={{0,16},{1,9},{2,18},{3,11},{4,20},{5,13},{6,22},{7,15},{8,24},{9,1... | collective-permute-start | bytes 786440 | tf_op jit(solution)/shard_map/ppermute | solution.py:440
  49.3 5.0 %collective-permute-start.15 = (bf16[4,64,256]{2,1,0:T(8,128)(2,1)S(1)}, bf16[4,64,256]{2,1,0:T(8,128)(2,1)S(1)}, u32[]{:S(2)}, u32[]{:S(2)}) collective-permute-start(bf16[4,64,256]{2,1,0:T(8,128)(2,1)S(1)} %fusion), channel_id=1, source_target_pairs={{0,2},{1,3},{2,0},{3,1},{4,6},{5,7},{6,4},{7,5},{8,10},{9,11},{10,... | collective-permute-start | bytes 393224 | tf_op jit(solution)/shard_map/ppermute | solution.py:440
  49.8 11.0 %collective-permute-start.10 = (bf16[1,4,64,256]{3,2,1,0:T(8,128)(2,1)S(1)}, bf16[1,4,64,256]{3,2,1,0:T(8,128)(2,1)S(1)}, u32[]{:S(2)}, u32[]{:S(2)}) collective-permute-start(bf16[1,4,64,256]{3,2,1,0:T(8,128)(2,1)S(1)} %get-tuple-element.71), channel_id=1, source_target_pairs={{0,16},{1,9},{2,18},{3,11},{4,20},{5,13},{6,22},{7,15},{8,24},{9,1... | collective-permute-start | bytes 393224 | tf_op jit(solution)/shard_map/ppermute | solution.py:440
  51.4 6.0 %collective-permute-start.13 = (bf16[128,896]{1,0:T(8,128)(2,1)S(1)}, bf16[128,896]{1,0:T(8,128)(2,1)S(1)}, u32[]{:S(2)}, u32[]{:S(2)}) collective-permute-start(bf16[128,896]{1,0:T(8,128)(2,1)S(1)} %get-tuple-element.79), channel_id=1, source_target_pairs={{0,8},{1,17},{2,10},{3,19},{4,12},{5,21},{6,14},{7,23},{8,0},{9,25... | collective-permute-start | bytes 688136 | tf_op jit(solution)/shard_map/ppermute | solution.py:440
  52.9 6.1 %collective-permute-start.17 = (bf16[128,896]{1,0:T(8,128)(2,1)S(1)}, bf16[128,896]{1,0:T(8,128)(2,1)S(1)}, u32[]{:S(2)}, u32[]{:S(2)}) collective-permute-start(bf16[128,896]{1,0:T(8,128)(2,1)S(1)} %get-tuple-element.85), channel_id=1, source_target_pairs={{0,1},{1,0},{2,3},{3,2},{4,5},{5,4},{6,7},{7,6},{8,9},{9,8},{10,11... | collective-permute-start | bytes 688136 | tf_op jit(solution)/shard_map/ppermute | solution.py:440
  54.4 5.4 %collective-permute-start.18 = (bf16[128,896]{1,0:T(8,128)(2,1)S(1)}, bf16[128,896]{1,0:T(8,128)(2,1)S(1)}, u32[]{:S(2)}, u32[]{:S(2)}) collective-permute-start(bf16[128,896]{1,0:T(8,128)(2,1)S(1)} %get-tuple-element.87), channel_id=1, source_target_pairs={{0,9},{1,16},{2,11},{3,18},{4,13},{5,20},{6,15},{7,22},{8,1},{9,24... | collective-permute-start | bytes 688136 | tf_op jit(solution)/shard_map/ppermute | solution.py:440
  54.4 10.0 %collective-permute-start.16 = (bf16[4,64,256]{2,1,0:T(8,128)(2,1)S(1)}, bf16[4,64,256]{2,1,0:T(8,128)(2,1)S(1)}, u32[]{:S(2)}, u32[]{:S(2)}) collective-permute-start(bf16[4,64,256]{2,1,0:T(8,128)(2,1)S(1)} %fusion.2), channel_id=1, source_target_pairs={{0,4},{1,5},{2,6},{3,7},{4,0},{5,1},{6,2},{7,3},{8,12},{9,13},{10,... | collective-permute-start | bytes 393224 | tf_op jit(solution)/shard_map/ppermute | solution.py:440
  57.4 7.5 %collective-permute-start.14 = (bf16[4,64,256]{2,1,0:T(8,128)(2,1)S(1)}, bf16[4,64,256]{2,1,0:T(8,128)(2,1)S(1)}, u32[]{:S(2)}, u32[]{:S(2)}) collective-permute-start(bf16[4,64,256]{2,1,0:T(8,128)(2,1)S(1)} %convert_add_fusion.2), channel_id=1, source_target_pairs={{0,2},{1,3},{2,0},{3,1},{4,6},{5,7},{6,4},{7,5},{8,10},{9,11},{10,... | collective-permute-start | bytes 393224 | tf_op jit(solution)/shard_map/ppermute | solution.py:440
  65.0 2.1 %collective-permute-start.21 = (bf16[64,256]{1,0:T(8,128)(2,1)S(1)}, bf16[64,256]{1,0:T(8,128)(2,1)S(1)}, u32[]{:S(2)}, u32[]{:S(2)}) collective-permute-start(bf16[64,256]{1,0:T(8,128)(2,1)S(1)} %get-tuple-element.101), channel_id=1, source_target_pairs={{0,1},{1,0},{2,3},{3,2},{4,5},{5,4},{6,7},{7,6},{8,9},{9,8},{10,11... | collective-permute-start | bytes 98312 | tf_op jit(solution)/shard_map/ppermute | solution.py:440
  65.0 4.0 %collective-permute-start.19 = (bf16[64,256]{1,0:T(8,128)(2,1)S(1)}, bf16[64,256]{1,0:T(8,128)(2,1)S(1)}, u32[]{:S(2)}, u32[]{:S(2)}) collective-permute-start(bf16[64,256]{1,0:T(8,128)(2,1)S(1)} %get-tuple-element.98), channel_id=1, source_target_pairs={{0,8},{1,17},{2,10},{3,19},{4,12},{5,21},{6,14},{7,23},{8,0},{9,25... | collective-permute-start | bytes 98312 | tf_op jit(solution)/shard_map/ppermute | solution.py:440
  66.6 3.3 %collective-permute-start.20 = (bf16[64,256]{1,0:T(8,128)(2,1)S(1)}, bf16[64,256]{1,0:T(8,128)(2,1)S(1)}, u32[]{:S(2)}, u32[]{:S(2)}) collective-permute-start(bf16[64,256]{1,0:T(8,128)(2,1)S(1)} %get-tuple-element.99), channel_id=1, source_target_pairs={{0,9},{1,16},{2,11},{3,18},{4,13},{5,20},{6,15},{7,22},{8,1},{9,24... | collective-permute-start | bytes 98312 | tf_op jit(solution)/shard_map/ppermute | solution.py:440
  (8 other events, 112.8 us)

commit v11 on v10

--- a/solution.py
+++ b/solution.py
@@ -56,9 +56,8 @@
     return (own, other, own ^ 1, other ^ 1), core, prompt
 
 
-def project_kernel(steps, x_ref, other_ref, kw_ref, vw_ref, *rest):
-    keep_ref, send_ref, rows_in, weights, sums, sems, row_sems = rest
-    heads, core, _ = place()
+def project_kernel(steps, x_ref, kw_ref, vw_ref, out_ref, weights, sems):
+    _, core, _ = place()
     width = weights.shape[1] // 2
     chunk = weights.shape[0] // steps
     copies = []
@@ -72,15 +71,8 @@
                     sems.at[len(copies)],
                 )
             )
-    part = x_ref.shape[0]
-    row_copies = [
-        pltpu.make_async_copy(source, rows_in.at[at : at + part, :], row_sems.at[index])
-        for index, (source, at) in enumerate(((x_ref, 0), (other_ref, part)))
-    ]
-    for copy in row_copies + copies[:8]:
+    for copy in copies[:8]:
         copy.start()
-    for copy in row_copies:
-        copy.wait()
     total = None
     for step in range(steps):
         span = slice(step * chunk, (step + 1) * chunk)
@@ -88,33 +80,52 @@
         copies[2 * step + 1].wait()
         for copy in copies[2 * step + 8 : 2 * step + 10]:
             copy.start()
-        product = dot(rows_in[:, span], weights[span, :], 1, 0)
+        product = dot(x_ref[:, span], weights[span, :], 1, 0)
         total = product if step == 0 else total + product
-    sums[...] = total.astype(BF16)
-    for out, head in ((keep_ref, heads[0] & 1), (send_ref, heads[2] & 1)):
-        out[:, :E] = sums[:, lanes(head, E)]
-        out[:, E:] = sums[:, lanes(head + 2, E)]
-
-
-def project(prompt_rows, other_rows, key_weight, value_weight, steps=10):
-    rows = 2 * prompt_rows.shape[0]
+    out_ref[...] = total.astype(BF16)
+
+
+def project(prompt_rows, key_weight, value_weight, steps=10):
+    rows = prompt_rows.shape[0]
     depth, width = key_weight.shape
     return pl.pallas_call(
         functools.partial(project_kernel, steps),
-        out_shape=[jax.ShapeDtypeStruct((rows, 2 * E), BF16)] * 2,
-        in_specs=[ANY] * 4,
+        out_shape=[
+            jax.ShapeDtypeStruct((rows, width), BF16),
+            jax.ShapeDtypeStruct((depth, width), BF16),
+        ],
+        in_specs=[VMEM, ANY, ANY],
         out_specs=[VMEM] * 2,
-        scratch_shapes=[
-            pltpu.VMEM((rows, depth), BF16),
-            pltpu.VMEM((depth, width), BF16),
-            pltpu.VMEM((rows, width), BF16),
-            pltpu.SemaphoreType.DMA((2 * steps,)),
-            pltpu.SemaphoreType.DMA((2,)),
-        ],
-        compiler_params=params(50),
+        scratch_shapes=[pltpu.SemaphoreType.DMA((2 * steps,))],
+        compiler_params=params(44),
         cost_estimate=cost(2 * rows * depth * width, 2 * depth * width + 2 * rows * depth),
-        name="project_prefix",
-    )(prompt_rows, other_rows, key_weight, value_weight)
+        name="project_own",
+    )(prompt_rows, key_weight, value_weight)
+
+
+def project_other_kernel(x_ref, weights, first_ref, keep_ref, send_ref, second_ref):
+    heads, _, _ = place()
+    second_ref[...] = dot(x_ref[...], weights[...], 1, 0).astype(BF16)
+    part = x_ref.shape[0]
+    for out, head in ((keep_ref, heads[0] & 1), (send_ref, heads[2] & 1)):
+        for index, source in enumerate((first_ref, second_ref)):
+            span = slice(index * part, (index + 1) * part)
+            out[span, :E] = source[:, lanes(head, E)]
+            out[span, E:] = source[:, lanes(head + 2, E)]
+
+
+def project_other(other_rows, weights, first):
+    rows, depth = other_rows.shape
+    return pl.pallas_call(
+        project_other_kernel,
+        out_shape=[jax.ShapeDtypeStruct((2 * rows, 2 * E), BF16)] * 2,
+        in_specs=[VMEM] * 3,
+        out_specs=[VMEM] * 2,
+        scratch_shapes=[pltpu.VMEM(first.shape, BF16)],
+        compiler_params=params(16),
+        cost_estimate=cost(2 * rows * depth * first.shape[1], 2 * weights.size),
+        name="project_other",
+    )(other_rows, weights, first)
 
 
 def pack_kernel(length_ref, prompts_ref, q_ref, g_ref, k_ref, v_ref, *outs):
@@ -440,7 +451,8 @@
         return lax.ppermute(x, ("prompt", "resp"), pairs)
 
     other_rows = fetch(prompt_rows, MEMBERS[1])
-    keep, send = project(prompt_rows, other_rows, key_weight, value_weight)
+    first, weights = project(prompt_rows, key_weight, value_weight)
+    keep, send = project_other(other_rows, weights, first)
     send, queries = lax.optimization_barrier((send, queries))
     packed = pack(first_length, resp_prompt, queries, out_grad, own_keys, own_values)
     arriving = fetch(send, MEMBERS[2])
@@ -452,6 +464,10 @@
     for bit in line_bits:
         for offset in list(pieces):
             pieces[offset | 1 << bit] = fetch(pieces[offset], 1 << bit)
+            if len(pieces) == 2:
+                pieces[1 << bit], packets[2] = lax.optimization_barrier(
+                    (pieces[1 << bit], packets[2])
+                )
     offsets = list(pieces)
     stacks = [
         jnp.stack([pieces[offset] for offset in some]) for some in (offsets[:-1], offsets[-1:])
@@ -477,18 +493,20 @@
     far = give(back_stacks[2], 1 << Y)
     middle = give(back_stacks[1], 1 << Y)
     near = give(back_stacks[0], 1 << Y)
-    far, grads = lax.optimization_barrier((far, grads))
+    middle, grads = lax.optimization_barrier((middle, grads))
     back = [grads[0]] + [give(grads[j], MEMBERS[j]) for j in range(1, len(MEMBERS))]
     arrived = {offset: [middle[index]] for index, offset in enumerate(offsets[1:-1])}
     arrived.update({offsets[0]: [near[0]], offsets[-1]: [far[0]]})
+    line_ahead = offsets[-1] ^ 1 << line_bits[-1]
     for bit in reversed(line_bits):
         for offset in sorted(sums, reverse=True):
             if offset & 1 << bit:
                 piece = sums.pop(offset)
                 for x in arrived.pop(offset):
                     piece = piece + x.astype(F32)
-                if offset == 1 << bit and bit != line_bits[0]:
-                    piece, back[2] = lax.optimization_barrier((piece, back[2]))
+                if offset == 1 << bit and bit == line_bits[-1]:
+                    ahead = arrived[line_ahead]
+                    piece, ahead[-1] = lax.optimization_barrier((piece, ahead[-1]))
                 arrived[offset ^ 1 << bit].append(give(piece.astype(BF16), 1 << bit))
     unpacked = unpack(back, queries.shape[1], own_keys.shape[1])
     arrived[0], unpacked = lax.optimization_barrier((arrived[0], unpacked))

time: 72.6 us -> 70.5 us (0.971)
  waiting for transfers between devices: 28.3 us -> 20.5 us
  starting transfers between devices: 23.4 us -> 28 us
    ppermute x12, waiting for transfers between devices: 13.2 us -> 8.33 us  [give(): return lax.ppermute(x, ('prompt', 'resp'), pairs)]
    ppermute x12, starting transfers between devices: 9.69 us -> 14.1 us  [give(): return lax.ppermute(x, ('prompt', 'resp'), pairs)]
    ppermute x10, waiting for transfers between devices: 15.1 us -> 12.2 us  [fetch(): return lax.ppermute(x, ('prompt', 'resp'), pairs)]
    pallas_call x0 -> x1, Pallas kernels: none -> 1.03 us  [project_other(): pl.pallas_call(project_other_kernel, out_shape=[jax.ShapeDtypeStruct((2 *...]
  transfers between devices with their start and end apart: 22 -> 22, of which waited for: 15 -> 11; matrix products, arithmetic and copies ran while one was open for 0% -> 0% of each run, Pallas kernels for 4% -> 10%
where the time goes in v11:
time: 70.5 us; the launch traced here: 69.8 us
  starting transfers between devices  28 us (40%)
  waiting for transfers between devices  20.5 us (29%)
  Pallas kernels  18.3 us (26%)
  between operations  1.65 us (2%)
  local copies, waits for them, and re-layouts  1.13 us (2%)
    ppermute x12, starting transfers between devices, give(): return lax.ppermute(x, ('prompt', 'resp'), pairs)  14.1 us
    ppermute x10, starting transfers between devices, fetch(): return lax.ppermute(x, ('prompt', 'resp'), pairs)  13.9 us
    ppermute x10, waiting for transfers between devices, fetch(): return lax.ppermute(x, ('prompt', 'resp'), pairs)  12.2 us
    ppermute x12, waiting for transfers between devices, give(): return lax.ppermute(x, ('prompt', 'resp'), pairs)  8.33 us
    pallas_call x1, Pallas kernels, attend(): pl.pallas_call(functools.partial(attend_kernel, slots, group, rows, resp_...  7.88 us
    pallas_call x1, Pallas kernels, project(): pl.pallas_call(functools.partial(project_kernel, steps), out_shape=[jax.S...  3.83 us
    pallas_call x2, Pallas kernels, prompt_gradient(): pl.pallas_call(functools.partial(prompt_kernel, chunk, members, first), o...  3.81 us
  transfers between devices with their start and end apart: 22, of which 11 were waited for; matrix products, arithmetic and copies ran while one was open for 0% of the time, Pallas kernels for 10%

profile of v11, /device:TPU:0, one launch (start us, length us, event | category | flops | bytes accessed | tf_op | source)
XLA Modules:
  0.0 69.8 jit_solution(14477553739447163562)
XLA Ops:
  1.1 1.1 %copy-done.2 = bf16[64,5120]{1,0:T(8,128)(2,1)S(1)} copy-done((bf16[64,5120]{1,0:T(8,128)(2,1)S(1)}, bf16[64,5120]{1,0:T(8,128)(2,1)}, u32[]{:S(2)}) %copy-start.2) | copy-done | bytes 655384
  2.2 3.8 %project_own.1 = (bf16[64,512]{1,0:T(8,128)(2,1)S(1)}, bf16[5120,512]{1,0:T(8,128)(2,1)S(1)}) custom-call(bf16[64,5120]{1,0:T(8,128)(2,1)S(1)} %copy-done.2, bf16[5120,512]{1,0:T(8,128)(2,1)} %rest_2_.3, bf16[5120,512]{1,0:T(8,128)(2,1)} %rest_3_.3), custom_call_target="tpu_custom_call" | custom-call | flops 335544320 | bytes 5898240 | tf_op jit(solution)/shard_map/project_own/pallas_call | solution.py:91
  7.2 2.6 %collective-permute-start.1 = (bf16[128,256]{1,0:T(8,128)(2,1)S(1)}, bf16[128,256]{1,0:T(8,128)(2,1)S(1)}, u32[]{:S(2)}, u32[]{:S(2)}) collective-permute-start(bf16[128,256]{1,0:T(8,128)(2,1)S(1)} %get-tuple-element.61), channel_id=1, source_target_pairs={{8,0},{17,1},{10,2},{19,3},{12,4},{21,5},{14,6},{23,7},{0,8},{25,9... | collective-permute-start | bytes 196616 | tf_op jit(solution)/shard_map/ppermute | solution.py:447
  12.0 2.1 %collective-permute-start.3 = (bf16[128,1664]{1,0:T(8,128)(2,1)S(1)}, bf16[128,1664]{1,0:T(8,128)(2,1)S(1)}, u32[]{:S(2)}, u32[]{:S(2)}) collective-permute-start(bf16[128,1664]{1,0:T(8,128)(2,1)S(1)} %get-tuple-element.68), channel_id=1, source_target_pairs={{8,0},{17,1},{10,2},{19,3},{12,4},{21,5},{14,6},{23,7},{0,8},{25,9... | collective-permute-start | bytes 1277960 | tf_op jit(solution)/shard_map/ppermute | solution.py:447
  14.1 2.6 %collective-permute-start.2 = (bf16[4,64,256]{2,1,0:T(8,128)(2,1)S(1)}, bf16[4,64,256]{2,1,0:T(8,128)(2,1)S(1)}, u32[]{:S(2)}, u32[]{:S(2)}) collective-permute-start(bf16[4,64,256]{2,1,0:T(8,128)(2,1)S(1)} %bitcast.19), channel_id=1, source_target_pairs={{4,0},{5,1},{6,2},{7,3},{0,4},{1,5},{2,6},{3,7},{12,8},{13,9},{14,... | collective-permute-start | bytes 393224 | tf_op jit(solution)/shard_map/ppermute | solution.py:447
  16.7 1.6 %collective-permute-start.7 = (bf16[4,64,256]{2,1,0:T(8,128)(2,1)S(1)}, bf16[4,64,256]{2,1,0:T(8,128)(2,1)S(1)}, u32[]{:S(2)}, u32[]{:S(2)}) collective-permute-start(bf16[4,64,256]{2,1,0:T(8,128)(2,1)S(1)} %bitcast.20), channel_id=1, source_target_pairs={{2,0},{3,1},{0,2},{1,3},{6,4},{7,5},{4,6},{5,7},{10,8},{11,9},{8,1... | collective-permute-start | bytes 393224 | tf_op jit(solution)/shard_map/ppermute | solution.py:447
  18.3 1.6 %collective-permute-start.6 = (bf16[128,1664]{1,0:T(8,128)(2,1)S(1)}, bf16[128,1664]{1,0:T(8,128)(2,1)S(1)}, u32[]{:S(2)}, u32[]{:S(2)}) collective-permute-start(bf16[128,1664]{1,0:T(8,128)(2,1)S(1)} %get-tuple-element.73), channel_id=1, source_target_pairs={{9,0},{16,1},{11,2},{18,3},{13,4},{20,5},{15,6},{22,7},{1,8},{24,9... | collective-permute-start | bytes 1277960 | tf_op jit(solution)/shard_map/ppermute | solution.py:447
  19.9 2.7 %collective-permute-done.2.rest_5_ = bf16[4,64,256]{2,1,0:T(8,128)(2,1)S(1)} collective-permute-done((bf16[4,64,256]{2,1,0:T(8,128)(2,1)S(1)}, bf16[4,64,256]{2,1,0:T(8,128)(2,1)S(1)}, u32[]{:S(2)}, u32[]{:S(2)}) %collective-permute-start.2) | collective-permute-done | bytes 131104 | tf_op jit(solution)/shard_map/ppermute | solution.py:447
  23.5 1.4 %collective-permute-start.4 = (bf16[4,64,256]{2,1,0:T(8,128)(2,1)S(1)}, bf16[4,64,256]{2,1,0:T(8,128)(2,1)S(1)}, u32[]{:S(2)}, u32[]{:S(2)}) collective-permute-start(bf16[4,64,256]{2,1,0:T(8,128)(2,1)S(1)} %collective-permute-done.2.rest_5_), channel_id=1, source_target_pairs={{2,0},{3,1},{0,2},{1,3},{6,4},{7,5},{4,6},{5,7},{10,8},{11,9},{8,1... | collective-permute-start | bytes 393224 | tf_op jit(solution)/shard_map/ppermute | solution.py:447
  25.8 3.3 %collective-permute-done.4.rest_7_ = bf16[4,64,256]{2,1,0:T(8,128)(2,1)S(1)} collective-permute-done((bf16[4,64,256]{2,1,0:T(8,128)(2,1)S(1)}, bf16[4,64,256]{2,1,0:T(8,128)(2,1)S(1)}, u32[]{:S(2)}, u32[]{:S(2)}) %collective-permute-start.4) | collective-permute-done | bytes 131104 | tf_op jit(solution)/shard_map/ppermute | solution.py:447
  30.1 4.1 %collective-permute-done.9.rest_9_ = bf16[1,4,64,256]{3,2,1,0:T(8,128)(2,1)S(1)} collective-permute-done((bf16[1,4,64,256]{3,2,1,0:T(8,128)(2,1)S(1)}, bf16[1,4,64,256]{3,2,1,0:T(8,128)(2,1)S(1)}, u32[]{:S(2)}, u32[]{:S(2)}) %collective-permute-start.9) | collective-permute-done | bytes 131104 | tf_op jit(solution)/shard_map/ppermute | solution.py:447
  34.2 7.9 %attend_head.1 = (bf16[128,896]{1,0:T(8,128)(2,1)S(1)}, bf16[128,896]{1,0:T(8,128)(2,1)S(1)}, bf16[128,896]{1,0:T(8,128)(2,1)S(1)}, bf16[128,896]{1,0:T(8,128)(2...) custom-call(bf16[128,1664]{1,0:T(8,128)(2,1)S(1)} %get-tuple-element, ...), custom_call_target="tpu_custom_call" | custom-call | flops 4194304000 | bytes 16777216 | tf_op jit(solution)/shard_map/attend_head/pallas_call | solution.py:339
  43.0 1.2 %collective-permute-start.11 = (bf16[2,4,64,256]{3,2,1,0:T(8,128)(2,1)S(1)}, bf16[2,4,64,256]{3,2,1,0:T(8,128)(2,1)S(1)}, u32[]{:S(2)}, u32[]{:S(2)}) collective-permute-start(bf16[2,4,64,256]{3,2,1,0:T(8,128)(2,1)S(1)} %get-tuple-element.81), channel_id=1, source_target_pairs={{0,16},{1,9},{2,18},{3,11},{4,20},{5,13},{6,22},{7,15},{8,24},{9,1... | collective-permute-start | bytes 786440 | tf_op jit(solution)/shard_map/ppermute | solution.py:451
  45.0 2.1 %collective-permute-done.12 = bf16[1,4,64,256]{3,2,1,0:T(8,128)(2,1)S(1)} collective-permute-done((bf16[1,4,64,256]{3,2,1,0:T(8,128)(2,1)S(1)}, bf16[1,4,64,256]{3,2,1,0:T(8,128)(2,1)S(1)}, u32[]{:S(2)}, u32[]{:S(2)}) %collective-permute-start.12) | collective-permute-done | bytes 131104 | tf_op jit(solution)/shard_map/ppermute | solution.py:451
  47.1 1.5 %collective-permute-start.13 = (bf16[4,64,256]{2,1,0:T(8,128)(2,1)S(1)}, bf16[4,64,256]{2,1,0:T(8,128)(2,1)S(1)}, u32[]{:S(2)}, u32[]{:S(2)}) collective-permute-start(bf16[4,64,256]{2,1,0:T(8,128)(2,1)S(1)} %fusion.2), channel_id=1, source_target_pairs={{0,2},{1,3},{2,0},{3,1},{4,6},{5,7},{6,4},{7,5},{8,10},{9,11},{10,... | collective-permute-start | bytes 393224 | tf_op jit(solution)/shard_map/ppermute | solution.py:451
  48.7 1.3 %collective-permute-done.11 = bf16[2,4,64,256]{3,2,1,0:T(8,128)(2,1)S(1)} collective-permute-done((bf16[2,4,64,256]{3,2,1,0:T(8,128)(2,1)S(1)}, bf16[2,4,64,256]{3,2,1,0:T(8,128)(2,1)S(1)}, u32[]{:S(2)}, u32[]{:S(2)}) %collective-permute-start.11) | collective-permute-done | bytes 262176 | tf_op jit(solution)/shard_map/ppermute | solution.py:451
  50.9 1.2 %collective-permute-start.18 = (bf16[128,896]{1,0:T(8,128)(2,1)S(1)}, bf16[128,896]{1,0:T(8,128)(2,1)S(1)}, u32[]{:S(2)}, u32[]{:S(2)}) collective-permute-start(bf16[128,896]{1,0:T(8,128)(2,1)S(1)} %get-tuple-element.95), channel_id=1, source_target_pairs={{0,9},{1,16},{2,11},{3,18},{4,13},{5,20},{6,15},{7,22},{8,1},{9,24... | collective-permute-start | bytes 688136 | tf_op jit(solution)/shard_map/ppermute | solution.py:451
  52.2 4.0 %collective-permute-start.15 = (bf16[4,64,256]{2,1,0:T(8,128)(2,1)S(1)}, bf16[4,64,256]{2,1,0:T(8,128)(2,1)S(1)}, u32[]{:S(2)}, u32[]{:S(2)}) collective-permute-start(bf16[4,64,256]{2,1,0:T(8,128)(2,1)S(1)} %fusion.1), channel_id=1, source_target_pairs={{0,4},{1,5},{2,6},{3,7},{4,0},{5,1},{6,2},{7,3},{8,12},{9,13},{10,... | collective-permute-start | bytes 393224 | tf_op jit(solution)/shard_map/ppermute | solution.py:451
  56.3 2.0 %collective-permute-start.14 = (bf16[4,64,256]{2,1,0:T(8,128)(2,1)S(1)}, bf16[4,64,256]{2,1,0:T(8,128)(2,1)S(1)}, u32[]{:S(2)}, u32[]{:S(2)}) collective-permute-start(bf16[4,64,256]{2,1,0:T(8,128)(2,1)S(1)} %convert_add_fusion.2), channel_id=1, source_target_pairs={{0,2},{1,3},{2,0},{3,1},{4,6},{5,7},{6,4},{7,5},{8,10},{9,11},{10,... | collective-permute-start | bytes 393224 | tf_op jit(solution)/shard_map/ppermute | solution.py:451
  59.3 3.8 %collective-permute-done.15.rest_2_ = bf16[4,64,256]{2,1,0:T(8,128)(2,1)S(1)} collective-permute-done((bf16[4,64,256]{2,1,0:T(8,128)(2,1)S(1)}, bf16[4,64,256]{2,1,0:T(8,128)(2,1)S(1)}, u32[]{:S(2)}, u32[]{:S(2)}) %collective-permute-start.15) | collective-permute-done | bytes 131104 | tf_op jit(solution)/shard_map/ppermute | solution.py:451
  63.7 1.0 %collective-permute-start.20 = (bf16[64,256]{1,0:T(8,128)(2,1)S(1)}, bf16[64,256]{1,0:T(8,128)(2,1)S(1)}, u32[]{:S(2)}, u32[]{:S(2)}) collective-permute-start(bf16[64,256]{1,0:T(8,128)(2,1)S(1)} %get-tuple-element.107), channel_id=1, source_target_pairs={{0,9},{1,16},{2,11},{3,18},{4,13},{5,20},{6,15},{7,22},{8,1},{9,24... | collective-permute-start | bytes 98312 | tf_op jit(solution)/shard_map/ppermute | solution.py:451
  64.8 1.5 %prompt_gradient.2.rest_4_ = f32[5120,64]{1,0:T(8,128)S(1)} custom-call(bf16[64,256]{1,0:T(8,128)(2,1)S(1)} %get-tuple-element.108.rest_0_, bf16[64,256]{1,0:T(8,128)(2,1)S(1)} %collective-permute-done.21.rest_1_, bf16[5120,512]{1,0:T(8,128)(2,1)S(1)} %bitcast.16, bf16[5120,512]{1,0:T(8,128)(2,1)S(1)} %bitcast.18), custom_call_target="tpu_custom_call" | custom-call | flops 335544320 | bytes 5898240 | tf_op jit(solution)/shard_map/prompt_gradient/pallas_call | solution.py:412
  66.3 1.0 %collective-permute-done.19.rest_0_ = bf16[64,256]{1,0:T(8,128)(2,1)S(1)} collective-permute-done((bf16[64,256]{1,0:T(8,128)(2,1)S(1)}, bf16[64,256]{1,0:T(8,128)(2,1)S(1)}, u32[]{:S(2)}, u32[]{:S(2)}) %collective-permute-start.19) | collective-permute-done | bytes 32800 | tf_op jit(solution)/shard_map/ppermute | solution.py:451
  67.3 2.3 %prompt_gradient.3 = bf16[64,5120]{1,0:T(8,128)(2,1)} custom-call(bf16[64,256]{1,0:T(8,128)(2,1)S(1)} %collective-permute-done.19.rest_0_, bf16[64,256]{1,0:T(8,128)(2,1)S(1)} %collective-permute-done.20.rest_1_, bf16[5120,512]{1,0:T(8,128)(2,1)S(1)} %bitcast.16, bf16[5120,512]{1,0:T(8,128)(2,1)S(1)} %bitcast.18, f32[5120,64]{1,0:T(8,128)S(1)} %prompt_gradient.2.rest_4_), custom_call_target="tpu_custom_call" | custom-call | flops 335544320 | bytes 5898240 | tf_op jit(solution)/shard_map/prompt_gradient/pallas_call | solution.py:412
  (55 shorter events, 10.3 us)
Async XLA Ops:
  0.6 5.5 %collective-permute-start = (bf16[64,5120]{1,0:T(8,128)(2,1)}, bf16[64,5120]{1,0:T(8,128)(2,1)S(1)}, u32[]{:S(2)}, u32[]{:S(2)}) collective-permute-start(bf16[64,5120]{1,0:T(8,128)(2,1)} %x_ref.1), channel_id=1, source_target_pairs={{1,0},{0,1},{3,2},{2,3},{5,4},{4,5},{7,6},{6,7},{9,8},{8,9},{11,10... | collective-permute-start | bytes 1966088 | tf_op jit(solution)/shard_map/ppermute | solution.py:447
  7.2 4.8 %collective-permute-start.1 = (bf16[128,256]{1,0:T(8,128)(2,1)S(1)}, bf16[128,256]{1,0:T(8,128)(2,1)S(1)}, u32[]{:S(2)}, u32[]{:S(2)}) collective-permute-start(bf16[128,256]{1,0:T(8,128)(2,1)S(1)} %get-tuple-element.61), channel_id=1, source_target_pairs={{8,0},{17,1},{10,2},{19,3},{12,4},{21,5},{14,6},{23,7},{0,8},{25,9... | collective-permute-start | bytes 196616 | tf_op jit(solution)/shard_map/ppermute | solution.py:447
  12.0 10.6 %collective-permute-start.3 = (bf16[128,1664]{1,0:T(8,128)(2,1)S(1)}, bf16[128,1664]{1,0:T(8,128)(2,1)S(1)}, u32[]{:S(2)}, u32[]{:S(2)}) collective-permute-start(bf16[128,1664]{1,0:T(8,128)(2,1)S(1)} %get-tuple-element.68), channel_id=1, source_target_pairs={{8,0},{17,1},{10,2},{19,3},{12,4},{21,5},{14,6},{23,7},{0,8},{25,9... | collective-permute-start | bytes 1277960 | tf_op jit(solution)/shard_map/ppermute | solution.py:447
  14.1 8.5 %collective-permute-start.2 = (bf16[4,64,256]{2,1,0:T(8,128)(2,1)S(1)}, bf16[4,64,256]{2,1,0:T(8,128)(2,1)S(1)}, u32[]{:S(2)}, u32[]{:S(2)}) collective-permute-start(bf16[4,64,256]{2,1,0:T(8,128)(2,1)S(1)} %bitcast.19), channel_id=1, source_target_pairs={{4,0},{5,1},{6,2},{7,3},{0,4},{1,5},{2,6},{3,7},{12,8},{13,9},{14,... | collective-permute-start | bytes 393224 | tf_op jit(solution)/shard_map/ppermute | solution.py:447
  16.7 6.2 %collective-permute-start.7 = (bf16[4,64,256]{2,1,0:T(8,128)(2,1)S(1)}, bf16[4,64,256]{2,1,0:T(8,128)(2,1)S(1)}, u32[]{:S(2)}, u32[]{:S(2)}) collective-permute-start(bf16[4,64,256]{2,1,0:T(8,128)(2,1)S(1)} %bitcast.20), channel_id=1, source_target_pairs={{2,0},{3,1},{0,2},{1,3},{6,4},{7,5},{4,6},{5,7},{10,8},{11,9},{8,1... | collective-permute-start | bytes 393224 | tf_op jit(solution)/shard_map/ppermute | solution.py:447
  18.3 6.7 %collective-permute-start.5 = (bf16[128,1664]{1,0:T(8,128)(2,1)S(1)}, bf16[128,1664]{1,0:T(8,128)(2,1)S(1)}, u32[]{:S(2)}, u32[]{:S(2)}) collective-permute-start(bf16[128,1664]{1,0:T(8,128)(2,1)S(1)} %get-tuple-element.71), channel_id=1, source_target_pairs={{1,0},{0,1},{3,2},{2,3},{5,4},{4,5},{7,6},{6,7},{9,8},{8,9},{11,10... | collective-permute-start | bytes 1277960 | tf_op jit(solution)/shard_map/ppermute | solution.py:447
  18.3 7.6 %collective-permute-start.6 = (bf16[128,1664]{1,0:T(8,128)(2,1)S(1)}, bf16[128,1664]{1,0:T(8,128)(2,1)S(1)}, u32[]{:S(2)}, u32[]{:S(2)}) collective-permute-start(bf16[128,1664]{1,0:T(8,128)(2,1)S(1)} %get-tuple-element.73), channel_id=1, source_target_pairs={{9,0},{16,1},{11,2},{18,3},{13,4},{20,5},{15,6},{22,7},{1,8},{24,9... | collective-permute-start | bytes 1277960 | tf_op jit(solution)/shard_map/ppermute | solution.py:447
  22.9 11.3 %collective-permute-start.8 = (bf16[3,4,64,256]{3,2,1,0:T(8,128)(2,1)S(1)}, bf16[3,4,64,256]{3,2,1,0:T(8,128)(2,1)S(1)}, u32[]{:S(2)}, u32[]{:S(2)}) collective-permute-start(bf16[3,4,64,256]{3,2,1,0:T(8,128)(2,1)S(1)} %pad_maximum_fusion), channel_id=1, source_target_pairs={{16,0},{9,1},{18,2},{11,3},{20,4},{13,5},{22,6},{15,7},{24,8},{1,9... | collective-permute-start | bytes 1179656 | tf_op jit(solution)/shard_map/ppermute | solution.py:447
  23.5 5.6 %collective-permute-start.4 = (bf16[4,64,256]{2,1,0:T(8,128)(2,1)S(1)}, bf16[4,64,256]{2,1,0:T(8,128)(2,1)S(1)}, u32[]{:S(2)}, u32[]{:S(2)}) collective-permute-start(bf16[4,64,256]{2,1,0:T(8,128)(2,1)S(1)} %collective-permute-done.2.rest_5_), channel_id=1, source_target_pairs={{2,0},{3,1},{0,2},{1,3},{6,4},{7,5},{4,6},{5,7},{10,8},{11,9},{8,1... | collective-permute-start | bytes 393224 | tf_op jit(solution)/shard_map/ppermute | solution.py:447
  29.2 35.6 %slice-start.1 = ((s8[5242880]{0:T(1024)(128)(4,1)}), s8[1048576]{0:T(1024)(128)(4,1)S(1)}, s32[]{:S(2)}) async-start(s8[5242880]{0:T(1024)(128)(4,1)} %bitcast.15), calls=%async_computation.1 | async-start | bytes 2097152
  29.2 35.6 %slice-start.3 = ((s8[5242880]{0:T(1024)(128)(4,1)}), s8[1048576]{0:T(1024)(128)(4,1)S(1)}, s32[]{:S(2)}) async-start(s8[5242880]{0:T(1024)(128)(4,1)} %bitcast.17), calls=%async_computation.3 | async-start | bytes 2097152
  29.2 5.0 %collective-permute-start.9 = (bf16[1,4,64,256]{3,2,1,0:T(8,128)(2,1)S(1)}, bf16[1,4,64,256]{3,2,1,0:T(8,128)(2,1)S(1)}, u32[]{:S(2)}, u32[]{:S(2)}) collective-permute-start(bf16[1,4,64,256]{3,2,1,0:T(8,128)(2,1)S(1)} %bitcast.26), channel_id=1, source_target_pairs={{16,0},{9,1},{18,2},{11,3},{20,4},{13,5},{22,6},{15,7},{24,8},{1,9... | collective-permute-start | bytes 393224 | tf_op jit(solution)/shard_map/ppermute | solution.py:447
  42.1 5.0 %collective-permute-start.12 = (bf16[1,4,64,256]{3,2,1,0:T(8,128)(2,1)S(1)}, bf16[1,4,64,256]{3,2,1,0:T(8,128)(2,1)S(1)}, u32[]{:S(2)}, u32[]{:S(2)}) collective-permute-start(bf16[1,4,64,256]{3,2,1,0:T(8,128)(2,1)S(1)} %get-tuple-element.88), channel_id=1, source_target_pairs={{0,16},{1,9},{2,18},{3,11},{4,20},{5,13},{6,22},{7,15},{8,24},{9,1... | collective-permute-start | bytes 393224 | tf_op jit(solution)/shard_map/ppermute | solution.py:451
  43.0 6.9 %collective-permute-start.11 = (bf16[2,4,64,256]{3,2,1,0:T(8,128)(2,1)S(1)}, bf16[2,4,64,256]{3,2,1,0:T(8,128)(2,1)S(1)}, u32[]{:S(2)}, u32[]{:S(2)}) collective-permute-start(bf16[2,4,64,256]{3,2,1,0:T(8,128)(2,1)S(1)} %get-tuple-element.81), channel_id=1, source_target_pairs={{0,16},{1,9},{2,18},{3,11},{4,20},{5,13},{6,22},{7,15},{8,24},{9,1... | collective-permute-start | bytes 786440 | tf_op jit(solution)/shard_map/ppermute | solution.py:451
  44.2 15.1 %collective-permute-start.10 = (bf16[1,4,64,256]{3,2,1,0:T(8,128)(2,1)S(1)}, bf16[1,4,64,256]{3,2,1,0:T(8,128)(2,1)S(1)}, u32[]{:S(2)}, u32[]{:S(2)}) collective-permute-start(bf16[1,4,64,256]{3,2,1,0:T(8,128)(2,1)S(1)} %get-tuple-element.79), channel_id=1, source_target_pairs={{0,16},{1,9},{2,18},{3,11},{4,20},{5,13},{6,22},{7,15},{8,24},{9,1... | collective-permute-start | bytes 393224 | tf_op jit(solution)/shard_map/ppermute | solution.py:451
  47.1 5.0 %collective-permute-start.13 = (bf16[4,64,256]{2,1,0:T(8,128)(2,1)S(1)}, bf16[4,64,256]{2,1,0:T(8,128)(2,1)S(1)}, u32[]{:S(2)}, u32[]{:S(2)}) collective-permute-start(bf16[4,64,256]{2,1,0:T(8,128)(2,1)S(1)} %fusion.2), channel_id=1, source_target_pairs={{0,2},{1,3},{2,0},{3,1},{4,6},{5,7},{6,4},{7,5},{8,10},{9,11},{10,... | collective-permute-start | bytes 393224 | tf_op jit(solution)/shard_map/ppermute | solution.py:451
  49.9 6.3 %collective-permute-start.16 = (bf16[128,896]{1,0:T(8,128)(2,1)S(1)}, bf16[128,896]{1,0:T(8,128)(2,1)S(1)}, u32[]{:S(2)}, u32[]{:S(2)}) collective-permute-start(bf16[128,896]{1,0:T(8,128)(2,1)S(1)} %get-tuple-element.93), channel_id=1, source_target_pairs={{0,1},{1,0},{2,3},{3,2},{4,5},{5,4},{6,7},{7,6},{8,9},{9,8},{10,11... | collective-permute-start | bytes 688136 | tf_op jit(solution)/shard_map/ppermute | solution.py:451
  49.9 8.4 %collective-permute-start.17 = (bf16[128,896]{1,0:T(8,128)(2,1)S(1)}, bf16[128,896]{1,0:T(8,128)(2,1)S(1)}, u32[]{:S(2)}, u32[]{:S(2)}) collective-permute-start(bf16[128,896]{1,0:T(8,128)(2,1)S(1)} %get-tuple-element.94), channel_id=1, source_target_pairs={{0,8},{1,17},{2,10},{3,19},{4,12},{5,21},{6,14},{7,23},{8,0},{9,25... | collective-permute-start | bytes 688136 | tf_op jit(solution)/shard_map/ppermute | solution.py:451
  50.9 7.4 %collective-permute-start.18 = (bf16[128,896]{1,0:T(8,128)(2,1)S(1)}, bf16[128,896]{1,0:T(8,128)(2,1)S(1)}, u32[]{:S(2)}, u32[]{:S(2)}) collective-permute-start(bf16[128,896]{1,0:T(8,128)(2,1)S(1)} %get-tuple-element.95), channel_id=1, source_target_pairs={{0,9},{1,16},{2,11},{3,18},{4,13},{5,20},{6,15},{7,22},{8,1},{9,24... | collective-permute-start | bytes 688136 | tf_op jit(solution)/shard_map/ppermute | solution.py:451
  52.2 10.9 %collective-permute-start.15 = (bf16[4,64,256]{2,1,0:T(8,128)(2,1)S(1)}, bf16[4,64,256]{2,1,0:T(8,128)(2,1)S(1)}, u32[]{:S(2)}, u32[]{:S(2)}) collective-permute-start(bf16[4,64,256]{2,1,0:T(8,128)(2,1)S(1)} %fusion.1), channel_id=1, source_target_pairs={{0,4},{1,5},{2,6},{3,7},{4,0},{5,1},{6,2},{7,3},{8,12},{9,13},{10,... | collective-permute-start | bytes 393224 | tf_op jit(solution)/shard_map/ppermute | solution.py:451
  56.3 6.9 %collective-permute-start.14 = (bf16[4,64,256]{2,1,0:T(8,128)(2,1)S(1)}, bf16[4,64,256]{2,1,0:T(8,128)(2,1)S(1)}, u32[]{:S(2)}, u32[]{:S(2)}) collective-permute-start(bf16[4,64,256]{2,1,0:T(8,128)(2,1)S(1)} %convert_add_fusion.2), channel_id=1, source_target_pairs={{0,2},{1,3},{2,0},{3,1},{4,6},{5,7},{6,4},{7,5},{8,10},{9,11},{10,... | collective-permute-start | bytes 393224 | tf_op jit(solution)/shard_map/ppermute | solution.py:451
  63.3 1.5 %collective-permute-start.21 = (bf16[64,256]{1,0:T(8,128)(2,1)S(1)}, bf16[64,256]{1,0:T(8,128)(2,1)S(1)}, u32[]{:S(2)}, u32[]{:S(2)}) collective-permute-start(bf16[64,256]{1,0:T(8,128)(2,1)S(1)} %get-tuple-element.109), channel_id=1, source_target_pairs={{0,1},{1,0},{2,3},{3,2},{4,5},{5,4},{6,7},{7,6},{8,9},{9,8},{10,11... | collective-permute-start | bytes 98312 | tf_op jit(solution)/shard_map/ppermute | solution.py:451
  63.3 4.0 %collective-permute-start.19 = (bf16[64,256]{1,0:T(8,128)(2,1)S(1)}, bf16[64,256]{1,0:T(8,128)(2,1)S(1)}, u32[]{:S(2)}, u32[]{:S(2)}) collective-permute-start(bf16[64,256]{1,0:T(8,128)(2,1)S(1)} %get-tuple-element.106), channel_id=1, source_target_pairs={{0,8},{1,17},{2,10},{3,19},{4,12},{5,21},{6,14},{7,23},{8,0},{9,25... | collective-permute-start | bytes 98312 | tf_op jit(solution)/shard_map/ppermute | solution.py:451
  63.7 3.6 %collective-permute-start.20 = (bf16[64,256]{1,0:T(8,128)(2,1)S(1)}, bf16[64,256]{1,0:T(8,128)(2,1)S(1)}, u32[]{:S(2)}, u32[]{:S(2)}) collective-permute-start(bf16[64,256]{1,0:T(8,128)(2,1)S(1)} %get-tuple-element.107), channel_id=1, source_target_pairs={{0,9},{1,16},{2,11},{3,18},{4,13},{5,20},{6,15},{7,22},{8,1},{9,24... | collective-permute-start | bytes 98312 | tf_op jit(solution)/shard_map/ppermute | solution.py:451
  (8 other events, 93.8 us)

commit v12 on v11

--- a/solution.py
+++ b/solution.py
@@ -188,7 +188,47 @@
     )(*packets)
 
 
-def attend_kernel(slots, group, rows, resp_bits, *rest):
+def unstack(near, stacks):
+    return near + [stack.at[index] for stack in stacks for index in range(stack.shape[0])]
+
+
+def open_packet(packet, group, resp_bits):
+    _, core, prompt_place = place()
+    rows = packet.shape[0]
+    boundary, first_at, second_at = (
+        jnp.max(packet[at : at + NOTE_ROWS, -E:].astype(F32)).astype(jnp.int32)
+        for at in (0, NOTE_ROWS, 2 * NOTE_ROWS)
+    )
+    first_at, second_at = (
+        crossed((prompt ^ prompt_place) << resp_bits, core) >> resp_bits
+        for prompt in (first_at, second_at)
+    )
+    heads = [packet[:, h * E : (h + 1) * E] for h in range(2 * group + 2)]
+    query = jnp.concatenate(heads[:group], axis=0)
+    grad = jnp.concatenate(heads[group : 2 * group], axis=0)
+    row_in_column = lax.broadcasted_iota(jnp.int32, (group * rows, E), 0) & (rows - 1)
+    in_first = row_in_column < boundary
+
+    def split(x):
+        x = x.astype(F32)
+        return jnp.concatenate(
+            [jnp.where(in_first, x, 0.0), jnp.where(in_first, 0.0, x)], axis=1
+        ).astype(BF16)
+
+    return dict(
+        boundary=boundary,
+        first_at=first_at,
+        second_at=second_at,
+        query=query,
+        grad=grad,
+        own_k=heads[2 * group],
+        own_v=heads[2 * group + 1],
+        query_pair=split(query),
+        grad_pair=split(grad),
+    )
+
+
+def scores_kernel(slots, group, rows, resp_bits, *rest):
     rest = list(rest)
 
     def take(count):
@@ -196,18 +236,12 @@
         del rest[:count]
         return taken
 
-    def unstack(near, stacks):
-        return near + [stack.at[index] for stack in stacks for index in range(stack.shape[0])]
-
     pieces = len(slots)
     n = len(MEMBERS)
     packets = take(n)
     kv_in = unstack(take(pieces // 2), take(2))
-    grads_out = take(n)
-    prefix_out = unstack(take(pieces // 2), take(3))
-    keys, values, key_acc, value_acc = rest
+    probs_out, dscores_out, keys, far_out, far_key, far_value, values = rest
     blocks, part, _ = kv_in[0].shape
-    _, core, prompt_place = place()
 
     for index in range(pieces):
         for j in range(blocks):
@@ -215,57 +249,25 @@
             span = slice(slot * part, (slot + 1) * part)
             keys[prompt, span, :] = kv_in[index][j, :, :E]
             values[prompt, span, :] = kv_in[index][j, :, E:]
-    key_acc[...] = jnp.zeros_like(key_acc)
-    value_acc[...] = jnp.zeros_like(value_acc)
+    far_key[...] = jnp.zeros_like(far_key)
+    far_value[...] = jnp.zeros_like(far_value)
 
     total_rows = group * rows
-    row_in_column = lax.broadcasted_iota(jnp.int32, (total_rows, E), 0) & (rows - 1)
     row_in_lane = lax.broadcasted_iota(jnp.int32, (rows, total_rows), 1) & (rows - 1)
     own_key = lax.broadcasted_iota(jnp.int32, (rows, total_rows), 0)
-    lane_row = lax.broadcasted_iota(jnp.int32, (E, total_rows), 1) & (rows - 1)
 
     def products(j):
-        packet = packets[j]
-        boundary, first_at, second_at = (
-            jnp.max(packet[at : at + NOTE_ROWS, -E:].astype(F32)).astype(jnp.int32)
-            for at in (0, NOTE_ROWS, 2 * NOTE_ROWS)
-        )
-        first_at, second_at = (
-            crossed((prompt ^ prompt_place) << resp_bits, core) >> resp_bits
-            for prompt in (first_at, second_at)
-        )
-        heads = [packet[:, h * E : (h + 1) * E] for h in range(2 * group + 2)]
-        query = jnp.concatenate(heads[:group], axis=0)
-        grad = jnp.concatenate(heads[group : 2 * group], axis=0)
-        own_k, own_v = heads[2 * group], heads[2 * group + 1]
-        in_first = row_in_column < boundary
-
-        def split(x):
-            x = x.astype(F32)
-            return jnp.concatenate(
-                [jnp.where(in_first, x, 0.0), jnp.where(in_first, 0.0, x)], axis=1
-            ).astype(BF16)
-
-        query_pair = split(query)
-        grad_pair = split(grad)
+        view = open_packet(packets[j], group, resp_bits)
+        boundary, first_at, second_at = view["boundary"], view["first_at"], view["second_at"]
         key_pair = jnp.concatenate([keys[first_at], keys[second_at]], axis=1)
         value_pair = jnp.concatenate([values[first_at], values[second_at]], axis=1)
-
         visible = (own_key <= row_in_lane) & ((own_key >= boundary) == (row_in_lane >= boundary))
         return dict(
-            boundary=boundary,
-            first_at=first_at,
-            second_at=second_at,
-            query=query,
-            grad=grad,
-            own_k=own_k,
-            query_pair=query_pair,
-            grad_pair=grad_pair,
-            key_pair=key_pair,
-            scores=dot(key_pair, query_pair, 1, 1),
-            own_scores=jnp.where(visible, dot(own_k, query, 1, 1), HIDDEN),
-            dprobs=dot(value_pair, grad_pair, 1, 1),
-            own_dprobs=dot(own_v, grad, 1, 1),
+            view,
+            scores=dot(key_pair, view["query_pair"], 1, 1),
+            own_scores=jnp.where(visible, dot(view["own_k"], view["query"], 1, 1), HIDDEN),
+            dprobs=dot(value_pair, view["grad_pair"], 1, 1),
+            own_dprobs=dot(view["own_v"], view["grad"], 1, 1),
         )
 
     def soften(scores, own_scores, dprobs, own_dprobs, **_):
@@ -291,64 +293,135 @@
             own_dscores=(own_probs * (own_dprobs - delta)).astype(BF16),
         )
 
-    def gradients(
-        grads, boundary, first_at, second_at, query, grad, own_k, query_pair, grad_pair, key_pair,
-        probs_low, own_probs_low, dscores, own_dscores, **_
-    ):
-        key_part = dot(dscores, query_pair, 1, 0)
-        value_part = dot(probs_low, grad_pair, 1, 0)
-        key_acc[first_at] += key_part[:, :E]
-        key_acc[second_at] += key_part[:, E:]
-        value_acc[first_at] += value_part[:, :E]
-        value_acc[second_at] += value_part[:, E:]
-
-        query_both = dot(key_pair, dscores, 0, 0)
-        query_part = jnp.where(lane_row < boundary, query_both[:E], query_both[E:])
-        query_part = (query_part + dot(own_k, own_dscores, 0, 0)) * SCALE
-        for h in range(group):
-            grads[:, h * E : (h + 1) * E] = query_part[:, h * rows : (h + 1) * rows].T.astype(BF16)
-        grads[:, group * E : (group + 1) * E] = (dot(own_dscores, query, 1, 0) * SCALE).astype(BF16)
-        grads[:, (group + 1) * E :] = dot(own_probs_low, grad, 1, 0).astype(BF16)
-
     ahead = products(0)
     for j in range(n):
         now = ahead
         if j + 1 < n:
             ahead = products(j + 1)
-        gradients(grads_out[j], **now, **soften(**now))
-
-    for index in range(pieces):
-        for j in range(blocks):
-            prompt, slot = slots[index][j]
-            span = slice(slot * part, (slot + 1) * part)
-            target = prefix_out[index]
-            target[j, :, :E] = (key_acc[prompt, span, :] * SCALE).astype(target.dtype)
-            target[j, :, E:] = value_acc[prompt, span, :].astype(target.dtype)
-
-
-def attend(packets, line, stacks, slots, prompts, resp_bits):
+        soft = soften(**now)
+        probs_out[j, :PLEN, :] = soft["probs_low"]
+        probs_out[j, PLEN:, :] = soft["own_probs_low"]
+        dscores_out[j, :PLEN, :] = soft["dscores"]
+        dscores_out[j, PLEN:, :] = soft["own_dscores"]
+        key_part = dot(soft["dscores"][PLEN - E :, :], now["query_pair"], 1, 0)
+        value_part = dot(soft["probs_low"][PLEN - E :, :], now["grad_pair"], 1, 0)
+        for total, part_sum in ((far_key, key_part), (far_value, value_part)):
+            total[now["first_at"]] += part_sum[:, :E]
+            total[now["second_at"]] += part_sum[:, E:]
+
+    for j in range(blocks):
+        prompt, slot = slots[-1][j]
+        span = slice(slot * part - (PLEN - E), (slot + 1) * part - (PLEN - E))
+        far_out[0, j, :, :E] = (far_key[prompt, span, :] * SCALE).astype(BF16)
+        far_out[0, j, :, E:] = far_value[prompt, span, :].astype(BF16)
+
+
+def attend_scores(packets, line, stacks, slots, prompts, resp_bits):
     rows, packet_width = packets[0].shape
     group = (packet_width // E - 3) // 2
-    sums_shape = (prompts, PLEN, E)
-    out_shape = [jax.ShapeDtypeStruct((rows, (group + 2) * E), BF16)] * len(packets)
-    out_shape += [jax.ShapeDtypeStruct(x.shape, F32) for x in line]
-    out_shape += [
-        jax.ShapeDtypeStruct((count, *line[0].shape), BF16) for count in (1, len(line) - 2, 1)
+    operands = [*packets, *line, *stacks]
+    low_shape = (len(packets), PLEN + rows, group * rows)
+    out_shape = [
+        jax.ShapeDtypeStruct(low_shape, BF16),
+        jax.ShapeDtypeStruct(low_shape, BF16),
+        jax.ShapeDtypeStruct((prompts, PLEN, E), BF16),
+        jax.ShapeDtypeStruct((1, *line[0].shape), BF16),
+        jax.ShapeDtypeStruct((prompts, E, E), F32),
+        jax.ShapeDtypeStruct((prompts, E, E), F32),
     ]
-    operands = [*packets, *line, *stacks]
-    outs = pl.pallas_call(
-        functools.partial(attend_kernel, slots, group, rows, resp_bits),
+    return pl.pallas_call(
+        functools.partial(scores_kernel, slots, group, rows, resp_bits),
         out_shape=out_shape,
         in_specs=[VMEM] * len(operands),
         out_specs=[VMEM] * len(out_shape),
-        scratch_shapes=[pltpu.VMEM(sums_shape, BF16)] * 2 + [pltpu.VMEM(sums_shape, F32)] * 2,
+        scratch_shapes=[pltpu.VMEM((prompts, PLEN, E), BF16)],
         compiler_params=params(32),
-        cost_estimate=cost(
-            20 * len(packets) * group * rows * (PLEN + rows) * E, 1 << 24
-        ),
-        name="attend_head",
+        cost_estimate=cost(10 * len(packets) * group * rows * (PLEN + rows) * E, 1 << 23),
+        name="attend_scores",
     )(*operands)
-    return outs[: len(packets)], outs[len(packets) : -3], outs[-3:]
+
+
+def prefix_kernel(slots, group, resp_bits, *rest):
+    rest = list(rest)
+    n = len(MEMBERS)
+    packets, rest = rest[:n], rest[n:]
+    probs, dscores, far_key, far_value, *outs = rest
+    *outs, key_acc, value_acc = outs
+    targets = unstack(outs[:-2], outs[-2:])
+    blocks, part, _ = targets[0].shape
+    start = PLEN - E
+    key_acc[...] = jnp.zeros_like(key_acc)
+    value_acc[...] = jnp.zeros_like(value_acc)
+    for j in range(n):
+        view = open_packet(packets[j], group, resp_bits)
+        key_part = dot(dscores[j, :start, :], view["query_pair"], 1, 0)
+        value_part = dot(probs[j, :start, :], view["grad_pair"], 1, 0)
+        for total, part_sum in ((key_acc, key_part), (value_acc, value_part)):
+            total[view["first_at"]] += part_sum[:, :E]
+            total[view["second_at"]] += part_sum[:, E:]
+    for index, target in enumerate(targets):
+        for j in range(blocks):
+            prompt, slot = slots[index][j]
+            at = slot * part
+            key_sum, value_sum = (key_acc, value_acc) if at < start else (far_key, far_value)
+            at = at if at < start else at - start
+            target[j, :, :E] = (key_sum[prompt, at : at + part, :] * SCALE).astype(target.dtype)
+            target[j, :, E:] = value_sum[prompt, at : at + part, :].astype(target.dtype)
+
+
+def attend_prefix(packets, probs, dscores, far_key, far_value, slots, shape, resp_bits):
+    rows, packet_width = packets[0].shape
+    group = (packet_width // E - 3) // 2
+    prompts = far_key.shape[0]
+    count = len(slots) // 2
+    out_shape = [jax.ShapeDtypeStruct(shape, F32)] * count
+    out_shape += [jax.ShapeDtypeStruct((k, *shape), BF16) for k in (1, count - 2)]
+    operands = [*packets, probs, dscores, far_key, far_value]
+    outs = pl.pallas_call(
+        functools.partial(prefix_kernel, slots, group, resp_bits),
+        out_shape=out_shape,
+        in_specs=[VMEM] * len(operands),
+        out_specs=[VMEM] * len(out_shape),
+        scratch_shapes=[pltpu.VMEM((prompts, PLEN - E, E), F32)] * 2,
+        compiler_params=params(32),
+        cost_estimate=cost(6 * len(packets) * group * rows * PLEN * E, 1 << 22),
+        name="attend_prefix",
+    )(*operands)
+    return outs[:-2], outs[-2], outs[-1]
+
+
+def rows_kernel(group, resp_bits, *rest):
+    n = len(MEMBERS)
+    packets, (probs, dscores, keys), outs = rest[:n], rest[n : n + 3], rest[n + 3 :]
+    rows = packets[0].shape[0]
+    lane_row = lax.broadcasted_iota(jnp.int32, (E, group * rows), 1) & (rows - 1)
+    for j, (packet, out) in enumerate(zip(packets, outs)):
+        view = open_packet(packet, group, resp_bits)
+        key_pair = jnp.concatenate([keys[view["first_at"]], keys[view["second_at"]]], axis=1)
+        own_dscores = dscores[j, PLEN:, :]
+        both = dot(key_pair, dscores[j, :PLEN, :], 0, 0)
+        whole = jnp.where(lane_row < view["boundary"], both[:E], both[E:])
+        whole = (whole + dot(view["own_k"], own_dscores, 0, 0)) * SCALE
+        for h in range(group):
+            out[:, h * E : (h + 1) * E] = whole[:, h * rows : (h + 1) * rows].T.astype(BF16)
+        key_grad = dot(own_dscores, view["query"], 1, 0) * SCALE
+        out[:, group * E : (group + 1) * E] = key_grad.astype(BF16)
+        out[:, (group + 1) * E :] = dot(probs[j, PLEN:, :], view["grad"], 1, 0).astype(BF16)
+
+
+def attend_rows(packets, probs, dscores, keys, resp_bits):
+    rows, packet_width = packets[0].shape
+    group = (packet_width // E - 3) // 2
+    operands = [*packets, probs, dscores, keys]
+    return pl.pallas_call(
+        functools.partial(rows_kernel, group, resp_bits),
+        out_shape=[jax.ShapeDtypeStruct((rows, (group + 2) * E), BF16)] * len(packets),
+        in_specs=[VMEM] * len(operands),
+        out_specs=[VMEM] * len(packets),
+        compiler_params=params(32),
+        cost_estimate=cost(6 * len(packets) * group * rows * PLEN * E, 1 << 22),
+        name="attend_rows",
+    )(*operands)
 
 
 def total_kernel(keep_ref, *rest):
@@ -485,15 +558,20 @@
             filled[at] += 1
         slots.append(tuple(places))
     resp_bits = n_resp.bit_length() - 1
-    grads, sums, back_stacks = attend(
-        packets, list(pieces.values()), stacks, tuple(slots), n_prompt, resp_bits
-    )
-
+    line = list(pieces.values())
+    slots = tuple(slots)
+    probs, dscores, keys, far, far_key, far_value = attend_scores(
+        packets, line, stacks, slots, n_prompt, resp_bits
+    )
+    far = give(far, 1 << Y)
+    sums, near, middle = attend_prefix(
+        packets, probs, dscores, far_key, far_value, slots, line[0].shape, resp_bits
+    )
     sums = dict(zip(offsets, sums))
-    far = give(back_stacks[2], 1 << Y)
-    middle = give(back_stacks[1], 1 << Y)
-    near = give(back_stacks[0], 1 << Y)
-    middle, grads = lax.optimization_barrier((middle, grads))
+    middle = give(middle, 1 << Y)
+    near = give(near, 1 << Y)
+    far, dscores = lax.optimization_barrier((far, dscores))
+    grads = attend_rows(packets, probs, dscores, keys, resp_bits)
     back = [grads[0]] + [give(grads[j], MEMBERS[j]) for j in range(1, len(MEMBERS))]
     arrived = {offset: [middle[index]] for index, offset in enumerate(offsets[1:-1])}
     arrived.update({offsets[0]: [near[0]], offsets[-1]: [far[0]]})

time: 70.5 us -> 71.5 us (1.014)
  starting transfers between devices: 28 us -> 32.4 us
  waiting for transfers between devices: 20.5 us -> 16.3 us
  Pallas kernels: 18.3 us -> 19.6 us
    ppermute x12, starting transfers between devices: 14.1 us -> 18.6 us  [give(): return lax.ppermute(x, ('prompt', 'resp'), pairs)]
    ppermute x12, waiting for transfers between devices: 8.33 us -> 4.1 us  [give(): return lax.ppermute(x, ('prompt', 'resp'), pairs)]
    pallas_call x1 -> x3, Pallas kernels: 7.88 us -> 9.19 us  [the longest x1 5.57 us: attend_scores(): pl.pallas_call(functools.partial(scores_kernel, slots, group, rows, resp_...]
  transfers between devices with their start and end apart: 22 -> 22, of which waited for: 11 -> 11; matrix products, arithmetic and copies ran while one was open for 0% -> 0% of each run, Pallas kernels for 10% -> 15%
where the time goes in v12:
time: 71.5 us; the launch traced here: 71.3 us
  starting transfers between devices  32.4 us (45%)
  Pallas kernels  19.6 us (27%)
  waiting for transfers between devices  16.3 us (23%)
  between operations  1.69 us (2%)
  local copies, waits for them, and re-layouts  1.13 us (2%)
    ppermute x12, starting transfers between devices, give(): return lax.ppermute(x, ('prompt', 'resp'), pairs)  18.6 us
    ppermute x10, starting transfers between devices, fetch(): return lax.ppermute(x, ('prompt', 'resp'), pairs)  13.8 us
    ppermute x10, waiting for transfers between devices, fetch(): return lax.ppermute(x, ('prompt', 'resp'), pairs)  12.2 us
    pallas_call x1, Pallas kernels, attend_scores(): pl.pallas_call(functools.partial(scores_kernel, slots, group, rows, resp_...  5.57 us
    ppermute x12, waiting for transfers between devices, give(): return lax.ppermute(x, ('prompt', 'resp'), pairs)  4.1 us
    pallas_call x1, Pallas kernels, project(): pl.pallas_call(functools.partial(project_kernel, steps), out_shape=[jax.S...  3.83 us
    pallas_call x2, Pallas kernels, prompt_gradient(): pl.pallas_call(functools.partial(prompt_kernel, chunk, members, first), o...  3.81 us
    pallas_call x1, Pallas kernels, attend_prefix(): pl.pallas_call(functools.partial(prefix_kernel, slots, group, resp_bits),...  1.88 us
  transfers between devices with their start and end apart: 22, of which 11 were waited for; matrix products, arithmetic and copies ran while one was open for 0% of the time, Pallas kernels for 15%

profile of v12, /device:TPU:0, one launch (start us, length us, event | category | flops | bytes accessed | tf_op | source)
XLA Modules:
  0.0 71.3 jit_solution(7456916039077436589)
XLA Ops:
  1.1 1.1 %copy-done.2 = bf16[64,5120]{1,0:T(8,128)(2,1)S(1)} copy-done((bf16[64,5120]{1,0:T(8,128)(2,1)S(1)}, bf16[64,5120]{1,0:T(8,128)(2,1)}, u32[]{:S(2)}) %copy-start.2) | copy-done | bytes 655384
  2.2 3.8 %project_own.1 = (bf16[64,512]{1,0:T(8,128)(2,1)S(1)}, bf16[5120,512]{1,0:T(8,128)(2,1)S(1)}) custom-call(bf16[64,5120]{1,0:T(8,128)(2,1)S(1)} %copy-done.2, bf16[5120,512]{1,0:T(8,128)(2,1)} %rest_2_.3, bf16[5120,512]{1,0:T(8,128)(2,1)} %rest_3_.3), custom_call_target="tpu_custom_call" | custom-call | flops 335544320 | bytes 5898240 | tf_op jit(solution)/shard_map/project_own/pallas_call | solution.py:91
  7.2 2.6 %collective-permute-start.1 = (bf16[128,256]{1,0:T(8,128)(2,1)S(1)}, bf16[128,256]{1,0:T(8,128)(2,1)S(1)}, u32[]{:S(2)}, u32[]{:S(2)}) collective-permute-start(bf16[128,256]{1,0:T(8,128)(2,1)S(1)} %get-tuple-element.63), channel_id=1, source_target_pairs={{8,0},{17,1},{10,2},{19,3},{12,4},{21,5},{14,6},{23,7},{0,8},{25,9... | collective-permute-start | bytes 196616 | tf_op jit(solution)/shard_map/ppermute | solution.py:520
  12.0 2.1 %collective-permute-start.3 = (bf16[128,1664]{1,0:T(8,128)(2,1)S(1)}, bf16[128,1664]{1,0:T(8,128)(2,1)S(1)}, u32[]{:S(2)}, u32[]{:S(2)}) collective-permute-start(bf16[128,1664]{1,0:T(8,128)(2,1)S(1)} %get-tuple-element.70), channel_id=1, source_target_pairs={{8,0},{17,1},{10,2},{19,3},{12,4},{21,5},{14,6},{23,7},{0,8},{25,9... | collective-permute-start | bytes 1277960 | tf_op jit(solution)/shard_map/ppermute | solution.py:520
  14.1 2.6 %collective-permute-start.2 = (bf16[4,64,256]{2,1,0:T(8,128)(2,1)S(1)}, bf16[4,64,256]{2,1,0:T(8,128)(2,1)S(1)}, u32[]{:S(2)}, u32[]{:S(2)}) collective-permute-start(bf16[4,64,256]{2,1,0:T(8,128)(2,1)S(1)} %bitcast.23), channel_id=1, source_target_pairs={{4,0},{5,1},{6,2},{7,3},{0,4},{1,5},{2,6},{3,7},{12,8},{13,9},{14,... | collective-permute-start | bytes 393224 | tf_op jit(solution)/shard_map/ppermute | solution.py:520
  16.7 1.6 %collective-permute-start.7 = (bf16[4,64,256]{2,1,0:T(8,128)(2,1)S(1)}, bf16[4,64,256]{2,1,0:T(8,128)(2,1)S(1)}, u32[]{:S(2)}, u32[]{:S(2)}) collective-permute-start(bf16[4,64,256]{2,1,0:T(8,128)(2,1)S(1)} %bitcast.24), channel_id=1, source_target_pairs={{2,0},{3,1},{0,2},{1,3},{6,4},{7,5},{4,6},{5,7},{10,8},{11,9},{8,1... | collective-permute-start | bytes 393224 | tf_op jit(solution)/shard_map/ppermute | solution.py:520
  18.3 1.6 %collective-permute-start.6 = (bf16[128,1664]{1,0:T(8,128)(2,1)S(1)}, bf16[128,1664]{1,0:T(8,128)(2,1)S(1)}, u32[]{:S(2)}, u32[]{:S(2)}) collective-permute-start(bf16[128,1664]{1,0:T(8,128)(2,1)S(1)} %get-tuple-element.75), channel_id=1, source_target_pairs={{9,0},{16,1},{11,2},{18,3},{13,4},{20,5},{15,6},{22,7},{1,8},{24,9... | collective-permute-start | bytes 1277960 | tf_op jit(solution)/shard_map/ppermute | solution.py:520
  19.9 2.7 %collective-permute-done.2.rest_5_ = bf16[4,64,256]{2,1,0:T(8,128)(2,1)S(1)} collective-permute-done((bf16[4,64,256]{2,1,0:T(8,128)(2,1)S(1)}, bf16[4,64,256]{2,1,0:T(8,128)(2,1)S(1)}, u32[]{:S(2)}, u32[]{:S(2)}) %collective-permute-start.2) | collective-permute-done | bytes 131104 | tf_op jit(solution)/shard_map/ppermute | solution.py:520
  23.5 1.4 %collective-permute-start.4 = (bf16[4,64,256]{2,1,0:T(8,128)(2,1)S(1)}, bf16[4,64,256]{2,1,0:T(8,128)(2,1)S(1)}, u32[]{:S(2)}, u32[]{:S(2)}) collective-permute-start(bf16[4,64,256]{2,1,0:T(8,128)(2,1)S(1)} %collective-permute-done.2.rest_5_), channel_id=1, source_target_pairs={{2,0},{3,1},{0,2},{1,3},{6,4},{7,5},{4,6},{5,7},{10,8},{11,9},{8,1... | collective-permute-start | bytes 393224 | tf_op jit(solution)/shard_map/ppermute | solution.py:520
  25.8 3.3 %collective-permute-done.4.rest_7_ = bf16[4,64,256]{2,1,0:T(8,128)(2,1)S(1)} collective-permute-done((bf16[4,64,256]{2,1,0:T(8,128)(2,1)S(1)}, bf16[4,64,256]{2,1,0:T(8,128)(2,1)S(1)}, u32[]{:S(2)}, u32[]{:S(2)}) %collective-permute-start.4) | collective-permute-done | bytes 131104 | tf_op jit(solution)/shard_map/ppermute | solution.py:520
  30.0 4.1 %collective-permute-done.9.rest_9_ = bf16[1,4,64,256]{3,2,1,0:T(8,128)(2,1)S(1)} collective-permute-done((bf16[1,4,64,256]{3,2,1,0:T(8,128)(2,1)S(1)}, bf16[1,4,64,256]{3,2,1,0:T(8,128)(2,1)S(1)}, u32[]{:S(2)}, u32[]{:S(2)}) %collective-permute-start.9) | collective-permute-done | bytes 131104 | tf_op jit(solution)/shard_map/ppermute | solution.py:520
  34.1 5.6 %attend_scores.1 = (bf16[4,640,640]{2,1,0:T(8,128)(2,1)S(1)}, bf16[4,640,640]{2,1,0:T(8,128)(2,1)S(1)}, bf16[4,512,128]{2,1,0:T(8,128)(2,1)S(1)}, bf16[1,4,64,25...) custom-call(bf16[128,1664]{1,0:T(8,128)(2,1)S(1)} %get-tuple-element.76.rest_0_, ...), custom_call_target="tpu_custom_call" | custom-call | flops 2097152000 | bytes 8388608 | tf_op jit(solution)/shard_map/attend_scores/pallas_call | solution.py:332
  40.6 1.9 %attend_prefix.1 = (f32[4,64,256]{2,1,0:T(8,128)S(1)}, f32[4,64,256]{2,1,0:T(8,128)S(1)}, f32[4,64,256]{2,1,0:T(8,128)S(1)}, f32[4,64,256]{2,1,0:T(8,128)S(1)}, ...) custom-call(bf16[128,1664]{1,0:T(8,128)(2,1)S(1)} %get-tuple-element.76.rest_0_, ...), custom_call_target="tpu_custom_call" | custom-call | flops 1006632960 | bytes 4194304 | tf_op jit(solution)/shard_map/attend_prefix/pallas_call | solution.py:380
  42.5 1.2 %collective-permute-start.10 = (bf16[1,4,64,256]{3,2,1,0:T(8,128)(2,1)S(1)}, bf16[1,4,64,256]{3,2,1,0:T(8,128)(2,1)S(1)}, u32[]{:S(2)}, u32[]{:S(2)}) collective-permute-start(bf16[1,4,64,256]{3,2,1,0:T(8,128)(2,1)S(1)} %get-tuple-element.85), channel_id=1, source_target_pairs={{0,16},{1,9},{2,18},{3,11},{4,20},{5,13},{6,22},{7,15},{8,24},{9,1... | collective-permute-start | bytes 393224 | tf_op jit(solution)/shard_map/ppermute | solution.py:524
  44.8 1.5 %collective-permute-start.13 = (bf16[4,64,256]{2,1,0:T(8,128)(2,1)S(1)}, bf16[4,64,256]{2,1,0:T(8,128)(2,1)S(1)}, u32[]{:S(2)}, u32[]{:S(2)}) collective-permute-start(bf16[4,64,256]{2,1,0:T(8,128)(2,1)S(1)} %fusion.2), channel_id=1, source_target_pairs={{0,2},{1,3},{2,0},{3,1},{4,6},{5,7},{6,4},{7,5},{8,10},{9,11},{10,... | collective-permute-start | bytes 393224 | tf_op jit(solution)/shard_map/ppermute | solution.py:524
  46.3 1.7 %attend_rows.1 = (bf16[128,896]{1,0:T(8,128)(2,1)S(1)}, bf16[128,896]{1,0:T(8,128)(2,1)S(1)}, bf16[128,896]{1,0:T(8,128)(2,1)S(1)}, bf16[128,896]{1,0:T(8,128)(2,1)S(1)}) custom-call(bf16[128,1664]{1,0:T(8,128)(2,1)S(1)} %get-tuple-element.76.rest_0_, bf16[128,1664]{1,0:T(8,128)(2,1)S(1)} %collective-permute-done.5.rest_1_, ...), custom_call_target="tpu_custom_call" | custom-call | flops 1006632960 | bytes 4194304 | tf_op jit(solution)/shard_map/attend_rows/pallas_call | solution.py:416
  48.1 1.4 %collective-permute-start.17 = (bf16[128,896]{1,0:T(8,128)(2,1)S(1)}, bf16[128,896]{1,0:T(8,128)(2,1)S(1)}, u32[]{:S(2)}, u32[]{:S(2)}) collective-permute-start(bf16[128,896]{1,0:T(8,128)(2,1)S(1)} %get-tuple-element.98), channel_id=1, source_target_pairs={{0,8},{1,17},{2,10},{3,19},{4,12},{5,21},{6,14},{7,23},{8,0},{9,25... | collective-permute-start | bytes 688136 | tf_op jit(solution)/shard_map/ppermute | solution.py:524
  50.4 1.4 %collective-permute-start.14 = (bf16[4,64,256]{2,1,0:T(8,128)(2,1)S(1)}, bf16[4,64,256]{2,1,0:T(8,128)(2,1)S(1)}, u32[]{:S(2)}, u32[]{:S(2)}) collective-permute-start(bf16[4,64,256]{2,1,0:T(8,128)(2,1)S(1)} %convert_add_fusion.2), channel_id=1, source_target_pairs={{0,2},{1,3},{2,0},{3,1},{4,6},{5,7},{6,4},{7,5},{8,10},{9,11},{10,... | collective-permute-start | bytes 393224 | tf_op jit(solution)/shard_map/ppermute | solution.py:524
  51.9 4.0 %collective-permute-start.15 = (bf16[4,64,256]{2,1,0:T(8,128)(2,1)S(1)}, bf16[4,64,256]{2,1,0:T(8,128)(2,1)S(1)}, u32[]{:S(2)}, u32[]{:S(2)}) collective-permute-start(bf16[4,64,256]{2,1,0:T(8,128)(2,1)S(1)} %fusion.1), channel_id=1, source_target_pairs={{0,4},{1,5},{2,6},{3,7},{4,0},{5,1},{6,2},{7,3},{8,12},{9,13},{10,... | collective-permute-start | bytes 393224 | tf_op jit(solution)/shard_map/ppermute | solution.py:524
  57.1 2.3 %collective-permute-done.15.rest_2_ = bf16[4,64,256]{2,1,0:T(8,128)(2,1)S(1)} collective-permute-done((bf16[4,64,256]{2,1,0:T(8,128)(2,1)S(1)}, bf16[4,64,256]{2,1,0:T(8,128)(2,1)S(1)}, u32[]{:S(2)}, u32[]{:S(2)}) %collective-permute-start.15) | collective-permute-done | bytes 131104 | tf_op jit(solution)/shard_map/ppermute | solution.py:524
  60.2 5.3 %collective-permute-start.19 = (bf16[64,256]{1,0:T(8,128)(2,1)S(1)}, bf16[64,256]{1,0:T(8,128)(2,1)S(1)}, u32[]{:S(2)}, u32[]{:S(2)}) collective-permute-start(bf16[64,256]{1,0:T(8,128)(2,1)S(1)} %get-tuple-element.110), channel_id=1, source_target_pairs={{0,8},{1,17},{2,10},{3,19},{4,12},{5,21},{6,14},{7,23},{8,0},{9,25... | collective-permute-start | bytes 98312 | tf_op jit(solution)/shard_map/ppermute | solution.py:524
  65.5 1.2 %collective-permute-start.20 = (bf16[64,256]{1,0:T(8,128)(2,1)S(1)}, bf16[64,256]{1,0:T(8,128)(2,1)S(1)}, u32[]{:S(2)}, u32[]{:S(2)}) collective-permute-start(bf16[64,256]{1,0:T(8,128)(2,1)S(1)} %get-tuple-element.111), channel_id=1, source_target_pairs={{0,9},{1,16},{2,11},{3,18},{4,13},{5,20},{6,15},{7,22},{8,1},{9,24... | collective-permute-start | bytes 98312 | tf_op jit(solution)/shard_map/ppermute | solution.py:524
  66.7 1.5 %prompt_gradient.2.rest_4_ = f32[5120,64]{1,0:T(8,128)S(1)} custom-call(bf16[64,256]{1,0:T(8,128)(2,1)S(1)} %get-tuple-element.112.rest_0_, bf16[64,256]{1,0:T(8,128)(2,1)S(1)} %collective-permute-done.21.rest_1_, bf16[5120,512]{1,0:T(8,128)(2,1)S(1)} %bitcast.20, bf16[5120,512]{1,0:T(8,128)(2,1)S(1)} %bitcast.22), custom_call_target="tpu_custom_call" | custom-call | flops 335544320 | bytes 5898240 | tf_op jit(solution)/shard_map/prompt_gradient/pallas_call | solution.py:485
  68.8 2.3 %prompt_gradient.3 = bf16[64,5120]{1,0:T(8,128)(2,1)} custom-call(bf16[64,256]{1,0:T(8,128)(2,1)S(1)} %collective-permute-done.19.rest_0_, bf16[64,256]{1,0:T(8,128)(2,1)S(1)} %collective-permute-done.20.rest_1_, bf16[5120,512]{1,0:T(8,128)(2,1)S(1)} %bitcast.20, bf16[5120,512]{1,0:T(8,128)(2,1)S(1)} %bitcast.22, f32[5120,64]{1,0:T(8,128)S(1)} %prompt_gradient.2.rest_4_), custom_call_target="tpu_custom_call" | custom-call | flops 335544320 | bytes 5898240 | tf_op jit(solution)/shard_map/prompt_gradient/pallas_call | solution.py:485
  (57 shorter events, 11.2 us)
Async XLA Ops:
  0.6 5.5 %collective-permute-start = (bf16[64,5120]{1,0:T(8,128)(2,1)}, bf16[64,5120]{1,0:T(8,128)(2,1)S(1)}, u32[]{:S(2)}, u32[]{:S(2)}) collective-permute-start(bf16[64,5120]{1,0:T(8,128)(2,1)} %x_ref.1), channel_id=1, source_target_pairs={{1,0},{0,1},{3,2},{2,3},{5,4},{4,5},{7,6},{6,7},{9,8},{8,9},{11,10... | collective-permute-start | bytes 1966088 | tf_op jit(solution)/shard_map/ppermute | solution.py:520
  7.2 4.8 %collective-permute-start.1 = (bf16[128,256]{1,0:T(8,128)(2,1)S(1)}, bf16[128,256]{1,0:T(8,128)(2,1)S(1)}, u32[]{:S(2)}, u32[]{:S(2)}) collective-permute-start(bf16[128,256]{1,0:T(8,128)(2,1)S(1)} %get-tuple-element.63), channel_id=1, source_target_pairs={{8,0},{17,1},{10,2},{19,3},{12,4},{21,5},{14,6},{23,7},{0,8},{25,9... | collective-permute-start | bytes 196616 | tf_op jit(solution)/shard_map/ppermute | solution.py:520
  12.0 10.6 %collective-permute-start.3 = (bf16[128,1664]{1,0:T(8,128)(2,1)S(1)}, bf16[128,1664]{1,0:T(8,128)(2,1)S(1)}, u32[]{:S(2)}, u32[]{:S(2)}) collective-permute-start(bf16[128,1664]{1,0:T(8,128)(2,1)S(1)} %get-tuple-element.70), channel_id=1, source_target_pairs={{8,0},{17,1},{10,2},{19,3},{12,4},{21,5},{14,6},{23,7},{0,8},{25,9... | collective-permute-start | bytes 1277960 | tf_op jit(solution)/shard_map/ppermute | solution.py:520
  14.1 8.5 %collective-permute-start.2 = (bf16[4,64,256]{2,1,0:T(8,128)(2,1)S(1)}, bf16[4,64,256]{2,1,0:T(8,128)(2,1)S(1)}, u32[]{:S(2)}, u32[]{:S(2)}) collective-permute-start(bf16[4,64,256]{2,1,0:T(8,128)(2,1)S(1)} %bitcast.23), channel_id=1, source_target_pairs={{4,0},{5,1},{6,2},{7,3},{0,4},{1,5},{2,6},{3,7},{12,8},{13,9},{14,... | collective-permute-start | bytes 393224 | tf_op jit(solution)/shard_map/ppermute | solution.py:520
  16.7 6.2 %collective-permute-start.7 = (bf16[4,64,256]{2,1,0:T(8,128)(2,1)S(1)}, bf16[4,64,256]{2,1,0:T(8,128)(2,1)S(1)}, u32[]{:S(2)}, u32[]{:S(2)}) collective-permute-start(bf16[4,64,256]{2,1,0:T(8,128)(2,1)S(1)} %bitcast.24), channel_id=1, source_target_pairs={{2,0},{3,1},{0,2},{1,3},{6,4},{7,5},{4,6},{5,7},{10,8},{11,9},{8,1... | collective-permute-start | bytes 393224 | tf_op jit(solution)/shard_map/ppermute | solution.py:520
  18.3 6.7 %collective-permute-start.5 = (bf16[128,1664]{1,0:T(8,128)(2,1)S(1)}, bf16[128,1664]{1,0:T(8,128)(2,1)S(1)}, u32[]{:S(2)}, u32[]{:S(2)}) collective-permute-start(bf16[128,1664]{1,0:T(8,128)(2,1)S(1)} %get-tuple-element.73), channel_id=1, source_target_pairs={{1,0},{0,1},{3,2},{2,3},{5,4},{4,5},{7,6},{6,7},{9,8},{8,9},{11,10... | collective-permute-start | bytes 1277960 | tf_op jit(solution)/shard_map/ppermute | solution.py:520
  18.3 7.6 %collective-permute-start.6 = (bf16[128,1664]{1,0:T(8,128)(2,1)S(1)}, bf16[128,1664]{1,0:T(8,128)(2,1)S(1)}, u32[]{:S(2)}, u32[]{:S(2)}) collective-permute-start(bf16[128,1664]{1,0:T(8,128)(2,1)S(1)} %get-tuple-element.75), channel_id=1, source_target_pairs={{9,0},{16,1},{11,2},{18,3},{13,4},{20,5},{15,6},{22,7},{1,8},{24,9... | collective-permute-start | bytes 1277960 | tf_op jit(solution)/shard_map/ppermute | solution.py:520
  22.9 11.2 %collective-permute-start.8 = (bf16[3,4,64,256]{3,2,1,0:T(8,128)(2,1)S(1)}, bf16[3,4,64,256]{3,2,1,0:T(8,128)(2,1)S(1)}, u32[]{:S(2)}, u32[]{:S(2)}) collective-permute-start(bf16[3,4,64,256]{3,2,1,0:T(8,128)(2,1)S(1)} %pad_maximum_fusion), channel_id=1, source_target_pairs={{16,0},{9,1},{18,2},{11,3},{20,4},{13,5},{22,6},{15,7},{24,8},{1,9... | collective-permute-start | bytes 1179656 | tf_op jit(solution)/shard_map/ppermute | solution.py:520
  23.5 5.6 %collective-permute-start.4 = (bf16[4,64,256]{2,1,0:T(8,128)(2,1)S(1)}, bf16[4,64,256]{2,1,0:T(8,128)(2,1)S(1)}, u32[]{:S(2)}, u32[]{:S(2)}) collective-permute-start(bf16[4,64,256]{2,1,0:T(8,128)(2,1)S(1)} %collective-permute-done.2.rest_5_), channel_id=1, source_target_pairs={{2,0},{3,1},{0,2},{1,3},{6,4},{7,5},{4,6},{5,7},{10,8},{11,9},{8,1... | collective-permute-start | bytes 393224 | tf_op jit(solution)/shard_map/ppermute | solution.py:520
  29.1 5.0 %collective-permute-start.9 = (bf16[1,4,64,256]{3,2,1,0:T(8,128)(2,1)S(1)}, bf16[1,4,64,256]{3,2,1,0:T(8,128)(2,1)S(1)}, u32[]{:S(2)}, u32[]{:S(2)}) collective-permute-start(bf16[1,4,64,256]{3,2,1,0:T(8,128)(2,1)S(1)} %bitcast.30), channel_id=1, source_target_pairs={{16,0},{9,1},{18,2},{11,3},{20,4},{13,5},{22,6},{15,7},{24,8},{1,9... | collective-permute-start | bytes 393224 | tf_op jit(solution)/shard_map/ppermute | solution.py:520
  34.1 32.6 %slice-start.2 = ((s8[5242880]{0:T(1024)(128)(4,1)}), s8[4194304]{0:T(1024)(128)(4,1)S(1)}, s32[]{:S(2)}) async-start(s8[5242880]{0:T(1024)(128)(4,1)} %bitcast.21), calls=%async_computation.2 | async-start | bytes 8388608
  39.7 5.0 %collective-permute-start.12 = (bf16[1,4,64,256]{3,2,1,0:T(8,128)(2,1)S(1)}, bf16[1,4,64,256]{3,2,1,0:T(8,128)(2,1)S(1)}, u32[]{:S(2)}, u32[]{:S(2)}) collective-permute-start(bf16[1,4,64,256]{3,2,1,0:T(8,128)(2,1)S(1)} %get-tuple-element.89), channel_id=1, source_target_pairs={{0,16},{1,9},{2,18},{3,11},{4,20},{5,13},{6,22},{7,15},{8,24},{9,1... | collective-permute-start | bytes 393224 | tf_op jit(solution)/shard_map/ppermute | solution.py:524
  40.6 26.1 %slice-start.3 = ((s8[5242880]{0:T(1024)(128)(4,1)}), s8[1048576]{0:T(1024)(128)(4,1)S(1)}, s32[]{:S(2)}) async-start(s8[5242880]{0:T(1024)(128)(4,1)} %bitcast.21), calls=%async_computation.3 | async-start | bytes 2097152
  42.5 14.6 %collective-permute-start.10 = (bf16[1,4,64,256]{3,2,1,0:T(8,128)(2,1)S(1)}, bf16[1,4,64,256]{3,2,1,0:T(8,128)(2,1)S(1)}, u32[]{:S(2)}, u32[]{:S(2)}) collective-permute-start(bf16[1,4,64,256]{3,2,1,0:T(8,128)(2,1)S(1)} %get-tuple-element.85), channel_id=1, source_target_pairs={{0,16},{1,9},{2,18},{3,11},{4,20},{5,13},{6,22},{7,15},{8,24},{9,1... | collective-permute-start | bytes 393224 | tf_op jit(solution)/shard_map/ppermute | solution.py:524
  43.8 6.6 %collective-permute-start.11 = (bf16[2,4,64,256]{3,2,1,0:T(8,128)(2,1)S(1)}, bf16[2,4,64,256]{3,2,1,0:T(8,128)(2,1)S(1)}, u32[]{:S(2)}, u32[]{:S(2)}) collective-permute-start(bf16[2,4,64,256]{3,2,1,0:T(8,128)(2,1)S(1)} %get-tuple-element.87), channel_id=1, source_target_pairs={{0,16},{1,9},{2,18},{3,11},{4,20},{5,13},{6,22},{7,15},{8,24},{9,1... | collective-permute-start | bytes 786440 | tf_op jit(solution)/shard_map/ppermute | solution.py:524
  44.8 5.6 %collective-permute-start.13 = (bf16[4,64,256]{2,1,0:T(8,128)(2,1)S(1)}, bf16[4,64,256]{2,1,0:T(8,128)(2,1)S(1)}, u32[]{:S(2)}, u32[]{:S(2)}) collective-permute-start(bf16[4,64,256]{2,1,0:T(8,128)(2,1)S(1)} %fusion.2), channel_id=1, source_target_pairs={{0,2},{1,3},{2,0},{3,1},{4,6},{5,7},{6,4},{7,5},{8,10},{9,11},{10,... | collective-permute-start | bytes 393224 | tf_op jit(solution)/shard_map/ppermute | solution.py:524
  48.0 3.9 %collective-permute-start.16 = (bf16[128,896]{1,0:T(8,128)(2,1)S(1)}, bf16[128,896]{1,0:T(8,128)(2,1)S(1)}, u32[]{:S(2)}, u32[]{:S(2)}) collective-permute-start(bf16[128,896]{1,0:T(8,128)(2,1)S(1)} %get-tuple-element.97), channel_id=1, source_target_pairs={{0,1},{1,0},{2,3},{3,2},{4,5},{5,4},{6,7},{7,6},{8,9},{9,8},{10,11... | collective-permute-start | bytes 688136 | tf_op jit(solution)/shard_map/ppermute | solution.py:524
  48.1 7.8 %collective-permute-start.17 = (bf16[128,896]{1,0:T(8,128)(2,1)S(1)}, bf16[128,896]{1,0:T(8,128)(2,1)S(1)}, u32[]{:S(2)}, u32[]{:S(2)}) collective-permute-start(bf16[128,896]{1,0:T(8,128)(2,1)S(1)} %get-tuple-element.98), channel_id=1, source_target_pairs={{0,8},{1,17},{2,10},{3,19},{4,12},{5,21},{6,14},{7,23},{8,0},{9,25... | collective-permute-start | bytes 688136 | tf_op jit(solution)/shard_map/ppermute | solution.py:524
  50.4 5.8 %collective-permute-start.18 = (bf16[128,896]{1,0:T(8,128)(2,1)S(1)}, bf16[128,896]{1,0:T(8,128)(2,1)S(1)}, u32[]{:S(2)}, u32[]{:S(2)}) collective-permute-start(bf16[128,896]{1,0:T(8,128)(2,1)S(1)} %get-tuple-element.99), channel_id=1, source_target_pairs={{0,9},{1,16},{2,11},{3,18},{4,13},{5,20},{6,15},{7,22},{8,1},{9,24... | collective-permute-start | bytes 688136 | tf_op jit(solution)/shard_map/ppermute | solution.py:524
  50.4 6.7 %collective-permute-start.14 = (bf16[4,64,256]{2,1,0:T(8,128)(2,1)S(1)}, bf16[4,64,256]{2,1,0:T(8,128)(2,1)S(1)}, u32[]{:S(2)}, u32[]{:S(2)}) collective-permute-start(bf16[4,64,256]{2,1,0:T(8,128)(2,1)S(1)} %convert_add_fusion.2), channel_id=1, source_target_pairs={{0,2},{1,3},{2,0},{3,1},{4,6},{5,7},{6,4},{7,5},{8,10},{9,11},{10,... | collective-permute-start | bytes 393224 | tf_op jit(solution)/shard_map/ppermute | solution.py:524
  51.9 7.6 %collective-permute-start.15 = (bf16[4,64,256]{2,1,0:T(8,128)(2,1)S(1)}, bf16[4,64,256]{2,1,0:T(8,128)(2,1)S(1)}, u32[]{:S(2)}, u32[]{:S(2)}) collective-permute-start(bf16[4,64,256]{2,1,0:T(8,128)(2,1)S(1)} %fusion.1), channel_id=1, source_target_pairs={{0,4},{1,5},{2,6},{3,7},{4,0},{5,1},{6,2},{7,3},{8,12},{9,13},{10,... | collective-permute-start | bytes 393224 | tf_op jit(solution)/shard_map/ppermute | solution.py:524
  59.5 7.1 %collective-permute-start.21 = (bf16[64,256]{1,0:T(8,128)(2,1)S(1)}, bf16[64,256]{1,0:T(8,128)(2,1)S(1)}, u32[]{:S(2)}, u32[]{:S(2)}) collective-permute-start(bf16[64,256]{1,0:T(8,128)(2,1)S(1)} %get-tuple-element.113), channel_id=1, source_target_pairs={{0,1},{1,0},{2,3},{3,2},{4,5},{5,4},{6,7},{7,6},{8,9},{9,8},{10,11... | collective-permute-start | bytes 98312 | tf_op jit(solution)/shard_map/ppermute | solution.py:524
  60.2 8.0 %collective-permute-start.19 = (bf16[64,256]{1,0:T(8,128)(2,1)S(1)}, bf16[64,256]{1,0:T(8,128)(2,1)S(1)}, u32[]{:S(2)}, u32[]{:S(2)}) collective-permute-start(bf16[64,256]{1,0:T(8,128)(2,1)S(1)} %get-tuple-element.110), channel_id=1, source_target_pairs={{0,8},{1,17},{2,10},{3,19},{4,12},{5,21},{6,14},{7,23},{8,0},{9,25... | collective-permute-start | bytes 98312 | tf_op jit(solution)/shard_map/ppermute | solution.py:524
  65.5 3.3 %collective-permute-start.20 = (bf16[64,256]{1,0:T(8,128)(2,1)S(1)}, bf16[64,256]{1,0:T(8,128)(2,1)S(1)}, u32[]{:S(2)}, u32[]{:S(2)}) collective-permute-start(bf16[64,256]{1,0:T(8,128)(2,1)S(1)} %get-tuple-element.111), channel_id=1, source_target_pairs={{0,9},{1,16},{2,11},{3,18},{4,13},{5,20},{6,15},{7,22},{8,1},{9,24... | collective-permute-start | bytes 98312 | tf_op jit(solution)/shard_map/ppermute | solution.py:524
  (8 other events, 63.5 us)

commit v13 on v12

--- a/solution.py
+++ b/solution.py
@@ -424,6 +424,25 @@
     )(*operands)
 
 
+def add_kernel(keep_ref, *rest):
+    result = keep_ref[...]
+    for part in rest[:-1]:
+        result = result + part[...].astype(F32)
+    rest[-1][...] = result
+
+
+def add(keep, parts):
+    return pl.pallas_call(
+        add_kernel,
+        out_shape=jax.ShapeDtypeStruct(keep.shape, F32),
+        in_specs=[VMEM] * (1 + len(parts)),
+        out_specs=VMEM,
+        compiler_params=params(16),
+        cost_estimate=cost(keep.size, 8 * keep.size),
+        name="add_far_grads",
+    )(keep, *parts)
+
+
 def total_kernel(keep_ref, *rest):
     parts, outs = rest[: -len(MEMBERS)], rest[-len(MEMBERS) :]
     for j, out in enumerate(outs):
@@ -569,12 +588,13 @@
     )
     sums = dict(zip(offsets, sums))
     middle = give(middle, 1 << Y)
-    near = give(near, 1 << Y)
     far, dscores = lax.optimization_barrier((far, dscores))
     grads = attend_rows(packets, probs, dscores, keys, resp_bits)
-    back = [grads[0]] + [give(grads[j], MEMBERS[j]) for j in range(1, len(MEMBERS))]
+    own, near = lax.optimization_barrier((grads[0], near))
+    near = give(near, 1 << Y)[0]
+    back = [own, None, give(grads[2], MEMBERS[2]), None]
     arrived = {offset: [middle[index]] for index, offset in enumerate(offsets[1:-1])}
-    arrived.update({offsets[0]: [near[0]], offsets[-1]: [far[0]]})
+    arrived.update({offsets[0]: [], offsets[-1]: [far[0]]})
     line_ahead = offsets[-1] ^ 1 << line_bits[-1]
     for bit in reversed(line_bits):
         for offset in sorted(sums, reverse=True):
@@ -584,12 +604,15 @@
                     piece = piece + x.astype(F32)
                 if offset == 1 << bit and bit == line_bits[-1]:
                     ahead = arrived[line_ahead]
-                    piece, ahead[-1] = lax.optimization_barrier((piece, ahead[-1]))
+                    piece, ahead[-1], later = lax.optimization_barrier(
+                        (piece, ahead[-1], [grads[1], grads[3]])
+                    )
+                    back[1], back[3] = give(later[0], MEMBERS[1]), give(later[1], MEMBERS[3])
                 arrived[offset ^ 1 << bit].append(give(piece.astype(BF16), 1 << bit))
     unpacked = unpack(back, queries.shape[1], own_keys.shape[1])
-    arrived[0], unpacked = lax.optimization_barrier((arrived[0], unpacked))
+    sums[0], unpacked = lax.optimization_barrier((sums[0], unpacked))
     query_grad, key_grad, value_grad = unpacked
-    blocks = total(sums[0], arrived[0])
+    blocks = total(add(sums[0], arrived[0]), [near])
     shares = [blocks[0]] + [give(blocks[j], MEMBERS[j]) for j in range(1, len(MEMBERS))]
     start = prompt_gradient((0, 1), shares[:2], key_weight, value_weight)
     prompt_grad = prompt_gradient((2, 3), shares[2:], key_weight, value_weight, start)

time: 71.5 us -> 72.1 us (level); the launches traced: 71.3 us -> 70.9 us
  starting transfers between devices: 32.4 us -> 30 us
  waiting for transfers between devices: 16.3 us -> 18.2 us
    ppermute x12, starting transfers between devices: 18.6 us -> 16.2 us  [give(): return lax.ppermute(x, ('prompt', 'resp'), pairs)]
    ppermute x12, waiting for transfers between devices: 4.1 us -> 6.08 us  [give(): return lax.ppermute(x, ('prompt', 'resp'), pairs)]
where the time goes in v13:
time: 72.1 us; the launch traced here: 70.9 us
  starting transfers between devices  30 us (42%)
  Pallas kernels  19.6 us (27%)
  waiting for transfers between devices  18.2 us (25%)
  between operations  1.7 us (2%)
  local copies, waits for them, and re-layouts  1.13 us (2%)
    ppermute x12, starting transfers between devices, give(): return lax.ppermute(x, ('prompt', 'resp'), pairs)  16.2 us
    ppermute x10, starting transfers between devices, fetch(): return lax.ppermute(x, ('prompt', 'resp'), pairs)  13.8 us
    ppermute x10, waiting for transfers between devices, fetch(): return lax.ppermute(x, ('prompt', 'resp'), pairs)  12.2 us
    ppermute x12, waiting for transfers between devices, give(): return lax.ppermute(x, ('prompt', 'resp'), pairs)  6.08 us
    pallas_call x1, Pallas kernels, attend_scores(): pl.pallas_call(functools.partial(scores_kernel, slots, group, rows, resp_...  5.57 us
    pallas_call x1, Pallas kernels, project(): pl.pallas_call(functools.partial(project_kernel, steps), out_shape=[jax.S...  3.83 us
    pallas_call x2, Pallas kernels, prompt_gradient(): pl.pallas_call(functools.partial(prompt_kernel, chunk, members, first), o...  3.81 us
    pallas_call x1, Pallas kernels, attend_prefix(): pl.pallas_call(functools.partial(prefix_kernel, slots, group, resp_bits),...  1.88 us
  transfers between devices with their start and end apart: 22, of which 11 were waited for; matrix products, arithmetic and copies ran while one was open for 0% of the time, Pallas kernels for 15%

profile of v13, /device:TPU:0, one launch (start us, length us, event | category | flops | bytes accessed | tf_op | source)
XLA Modules:
  0.0 70.9 jit_solution(2993952635298248272)
XLA Ops:
  2.2 3.8 %project_own.1 = (bf16[64,512]{1,0:T(8,128)(2,1)S(1)}, bf16[5120,512]{1,0:T(8,128)(2,1)S(1)}) custom-call(bf16[64,5120]{1,0:T(8,128)(2,1)S(1)} %copy-done.2, bf16[5120,512]{1,0:T(8,128)(2,1)} %rest_2_.3, bf16[5120,512]{1,0:T(8,128)(2,1)} %rest_3_.3), custom_call_target="tpu_custom_call" | custom-call | flops 335544320 | bytes 5898240 | tf_op jit(solution)/shard_map/project_own/pallas_call | solution.py:91
  7.2 2.6 %collective-permute-start.1 = (bf16[128,256]{1,0:T(8,128)(2,1)S(1)}, bf16[128,256]{1,0:T(8,128)(2,1)S(1)}, u32[]{:S(2)}, u32[]{:S(2)}) collective-permute-start(bf16[128,256]{1,0:T(8,128)(2,1)S(1)} %get-tuple-element.65), channel_id=1, source_target_pairs={{8,0},{17,1},{10,2},{19,3},{12,4},{21,5},{14,6},{23,7},{0,8},{25,9... | collective-permute-start | bytes 196616 | tf_op jit(solution)/shard_map/ppermute | solution.py:539
  12.0 2.1 %collective-permute-start.3 = (bf16[128,1664]{1,0:T(8,128)(2,1)S(1)}, bf16[128,1664]{1,0:T(8,128)(2,1)S(1)}, u32[]{:S(2)}, u32[]{:S(2)}) collective-permute-start(bf16[128,1664]{1,0:T(8,128)(2,1)S(1)} %get-tuple-element.72), channel_id=1, source_target_pairs={{8,0},{17,1},{10,2},{19,3},{12,4},{21,5},{14,6},{23,7},{0,8},{25,9... | collective-permute-start | bytes 1277960 | tf_op jit(solution)/shard_map/ppermute | solution.py:539
  14.1 2.6 %collective-permute-start.2 = (bf16[4,64,256]{2,1,0:T(8,128)(2,1)S(1)}, bf16[4,64,256]{2,1,0:T(8,128)(2,1)S(1)}, u32[]{:S(2)}, u32[]{:S(2)}) collective-permute-start(bf16[4,64,256]{2,1,0:T(8,128)(2,1)S(1)} %bitcast.23), channel_id=1, source_target_pairs={{4,0},{5,1},{6,2},{7,3},{0,4},{1,5},{2,6},{3,7},{12,8},{13,9},{14,... | collective-permute-start | bytes 393224 | tf_op jit(solution)/shard_map/ppermute | solution.py:539
  16.7 1.6 %collective-permute-start.7 = (bf16[4,64,256]{2,1,0:T(8,128)(2,1)S(1)}, bf16[4,64,256]{2,1,0:T(8,128)(2,1)S(1)}, u32[]{:S(2)}, u32[]{:S(2)}) collective-permute-start(bf16[4,64,256]{2,1,0:T(8,128)(2,1)S(1)} %bitcast.24), channel_id=1, source_target_pairs={{2,0},{3,1},{0,2},{1,3},{6,4},{7,5},{4,6},{5,7},{10,8},{11,9},{8,1... | collective-permute-start | bytes 393224 | tf_op jit(solution)/shard_map/ppermute | solution.py:539
  18.3 1.6 %collective-permute-start.6 = (bf16[128,1664]{1,0:T(8,128)(2,1)S(1)}, bf16[128,1664]{1,0:T(8,128)(2,1)S(1)}, u32[]{:S(2)}, u32[]{:S(2)}) collective-permute-start(bf16[128,1664]{1,0:T(8,128)(2,1)S(1)} %get-tuple-element.77), channel_id=1, source_target_pairs={{9,0},{16,1},{11,2},{18,3},{13,4},{20,5},{15,6},{22,7},{1,8},{24,9... | collective-permute-start | bytes 1277960 | tf_op jit(solution)/shard_map/ppermute | solution.py:539
  19.9 2.7 %collective-permute-done.2.rest_5_ = bf16[4,64,256]{2,1,0:T(8,128)(2,1)S(1)} collective-permute-done((bf16[4,64,256]{2,1,0:T(8,128)(2,1)S(1)}, bf16[4,64,256]{2,1,0:T(8,128)(2,1)S(1)}, u32[]{:S(2)}, u32[]{:S(2)}) %collective-permute-start.2) | collective-permute-done | bytes 131104 | tf_op jit(solution)/shard_map/ppermute | solution.py:539
  23.5 1.4 %collective-permute-start.4 = (bf16[4,64,256]{2,1,0:T(8,128)(2,1)S(1)}, bf16[4,64,256]{2,1,0:T(8,128)(2,1)S(1)}, u32[]{:S(2)}, u32[]{:S(2)}) collective-permute-start(bf16[4,64,256]{2,1,0:T(8,128)(2,1)S(1)} %collective-permute-done.2.rest_5_), channel_id=1, source_target_pairs={{2,0},{3,1},{0,2},{1,3},{6,4},{7,5},{4,6},{5,7},{10,8},{11,9},{8,1... | collective-permute-start | bytes 393224 | tf_op jit(solution)/shard_map/ppermute | solution.py:539
  25.8 3.3 %collective-permute-done.4.rest_7_ = bf16[4,64,256]{2,1,0:T(8,128)(2,1)S(1)} collective-permute-done((bf16[4,64,256]{2,1,0:T(8,128)(2,1)S(1)}, bf16[4,64,256]{2,1,0:T(8,128)(2,1)S(1)}, u32[]{:S(2)}, u32[]{:S(2)}) %collective-permute-start.4) | collective-permute-done | bytes 131104 | tf_op jit(solution)/shard_map/ppermute | solution.py:539
  30.0 4.1 %collective-permute-done.9.rest_9_ = bf16[1,4,64,256]{3,2,1,0:T(8,128)(2,1)S(1)} collective-permute-done((bf16[1,4,64,256]{3,2,1,0:T(8,128)(2,1)S(1)}, bf16[1,4,64,256]{3,2,1,0:T(8,128)(2,1)S(1)}, u32[]{:S(2)}, u32[]{:S(2)}) %collective-permute-start.9) | collective-permute-done | bytes 131104 | tf_op jit(solution)/shard_map/ppermute | solution.py:539
  34.1 5.6 %attend_scores.1 = (bf16[4,640,640]{2,1,0:T(8,128)(2,1)S(1)}, bf16[4,640,640]{2,1,0:T(8,128)(2,1)S(1)}, bf16[4,512,128]{2,1,0:T(8,128)(2,1)S(1)}, bf16[1,4,64,25...) custom-call(bf16[128,1664]{1,0:T(8,128)(2,1)S(1)} %get-tuple-element.78.rest_0_, ...), custom_call_target="tpu_custom_call" | custom-call | flops 2097152000 | bytes 8388608 | tf_op jit(solution)/shard_map/attend_scores/pallas_call | solution.py:332
  40.6 1.9 %attend_prefix.1 = (f32[4,64,256]{2,1,0:T(8,128)S(1)}, f32[4,64,256]{2,1,0:T(8,128)S(1)}, f32[4,64,256]{2,1,0:T(8,128)S(1)}, f32[4,64,256]{2,1,0:T(8,128)S(1)}, ...) custom-call(bf16[128,1664]{1,0:T(8,128)(2,1)S(1)} %get-tuple-element.78.rest_0_, ...), custom_call_target="tpu_custom_call" | custom-call | flops 1006632960 | bytes 4194304 | tf_op jit(solution)/shard_map/attend_prefix/pallas_call | solution.py:380
  42.5 1.2 %collective-permute-start.11 = (bf16[2,4,64,256]{3,2,1,0:T(8,128)(2,1)S(1)}, bf16[2,4,64,256]{3,2,1,0:T(8,128)(2,1)S(1)}, u32[]{:S(2)}, u32[]{:S(2)}) collective-permute-start(bf16[2,4,64,256]{3,2,1,0:T(8,128)(2,1)S(1)} %get-tuple-element.95), channel_id=1, source_target_pairs={{0,16},{1,9},{2,18},{3,11},{4,20},{5,13},{6,22},{7,15},{8,24},{9,1... | collective-permute-start | bytes 786440 | tf_op jit(solution)/shard_map/ppermute | solution.py:543
  44.8 1.5 %collective-permute-start.12 = (bf16[4,64,256]{2,1,0:T(8,128)(2,1)S(1)}, bf16[4,64,256]{2,1,0:T(8,128)(2,1)S(1)}, u32[]{:S(2)}, u32[]{:S(2)}) collective-permute-start(bf16[4,64,256]{2,1,0:T(8,128)(2,1)S(1)} %fusion.2), channel_id=1, source_target_pairs={{0,2},{1,3},{2,0},{3,1},{4,6},{5,7},{6,4},{7,5},{8,10},{9,11},{10,... | collective-permute-start | bytes 393224 | tf_op jit(solution)/shard_map/ppermute | solution.py:543
  46.3 1.7 %attend_rows.1 = (bf16[128,896]{1,0:T(8,128)(2,1)S(1)}, bf16[128,896]{1,0:T(8,128)(2,1)S(1)}, bf16[128,896]{1,0:T(8,128)(2,1)S(1)}, bf16[128,896]{1,0:T(8,128)(2,1)S(1)}) custom-call(bf16[128,1664]{1,0:T(8,128)(2,1)S(1)} %get-tuple-element.78.rest_0_, bf16[128,1664]{1,0:T(8,128)(2,1)S(1)} %collective-permute-done.5.rest_1_, ...), custom_call_target="tpu_custom_call" | custom-call | flops 1006632960 | bytes 4194304 | tf_op jit(solution)/shard_map/attend_rows/pallas_call | solution.py:416
  48.0 1.4 %collective-permute-start.14 = (bf16[128,896]{1,0:T(8,128)(2,1)S(1)}, bf16[128,896]{1,0:T(8,128)(2,1)S(1)}, u32[]{:S(2)}, u32[]{:S(2)}) collective-permute-start(bf16[128,896]{1,0:T(8,128)(2,1)S(1)} %get-tuple-element.101), channel_id=1, source_target_pairs={{0,8},{1,17},{2,10},{3,19},{4,12},{5,21},{6,14},{7,23},{8,0},{9,25... | collective-permute-start | bytes 688136 | tf_op jit(solution)/shard_map/ppermute | solution.py:543
  50.4 2.7 %collective-permute-start.15 = (bf16[128,896]{1,0:T(8,128)(2,1)S(1)}, bf16[128,896]{1,0:T(8,128)(2,1)S(1)}, u32[]{:S(2)}, u32[]{:S(2)}) collective-permute-start(bf16[128,896]{1,0:T(8,128)(2,1)S(1)} %get-tuple-element.102), channel_id=1, source_target_pairs={{0,9},{1,16},{2,11},{3,18},{4,13},{5,20},{6,15},{7,22},{8,1},{9,24... | collective-permute-start | bytes 688136 | tf_op jit(solution)/shard_map/ppermute | solution.py:543
  53.2 3.9 %collective-permute-start.17 = (bf16[4,64,256]{2,1,0:T(8,128)(2,1)S(1)}, bf16[4,64,256]{2,1,0:T(8,128)(2,1)S(1)}, u32[]{:S(2)}, u32[]{:S(2)}) collective-permute-start(bf16[4,64,256]{2,1,0:T(8,128)(2,1)S(1)} %fusion.1), channel_id=1, source_target_pairs={{0,4},{1,5},{2,6},{3,7},{4,0},{5,1},{6,2},{7,3},{8,12},{9,13},{10,... | collective-permute-start | bytes 393224 | tf_op jit(solution)/shard_map/ppermute | solution.py:543
  57.1 2.0 %collective-permute-start.16 = (bf16[4,64,256]{2,1,0:T(8,128)(2,1)S(1)}, bf16[4,64,256]{2,1,0:T(8,128)(2,1)S(1)}, u32[]{:S(2)}, u32[]{:S(2)}) collective-permute-start(bf16[4,64,256]{2,1,0:T(8,128)(2,1)S(1)} %convert_add_fusion.2), channel_id=1, source_target_pairs={{0,2},{1,3},{2,0},{3,1},{4,6},{5,7},{6,4},{7,5},{8,10},{9,11},{10,... | collective-permute-start | bytes 393224 | tf_op jit(solution)/shard_map/ppermute | solution.py:543
  60.2 2.8 %collective-permute-done.17.rest_1_ = bf16[4,64,256]{2,1,0:T(8,128)(2,1)S(1)} collective-permute-done((bf16[4,64,256]{2,1,0:T(8,128)(2,1)S(1)}, bf16[4,64,256]{2,1,0:T(8,128)(2,1)S(1)}, u32[]{:S(2)}, u32[]{:S(2)}) %collective-permute-start.17) | collective-permute-done | bytes 131104 | tf_op jit(solution)/shard_map/ppermute | solution.py:543
  63.0 1.3 %collective-permute-done.16.rest_0_ = bf16[4,64,256]{2,1,0:T(8,128)(2,1)S(1)} collective-permute-done((bf16[4,64,256]{2,1,0:T(8,128)(2,1)S(1)}, bf16[4,64,256]{2,1,0:T(8,128)(2,1)S(1)}, u32[]{:S(2)}, u32[]{:S(2)}) %collective-permute-start.16) | collective-permute-done | bytes 131104 | tf_op jit(solution)/shard_map/ppermute | solution.py:543
  64.8 2.0 %collective-permute-start.20 = (bf16[64,256]{1,0:T(8,128)(2,1)S(1)}, bf16[64,256]{1,0:T(8,128)(2,1)S(1)}, u32[]{:S(2)}, u32[]{:S(2)}) collective-permute-start(bf16[64,256]{1,0:T(8,128)(2,1)S(1)} %get-tuple-element.115), channel_id=1, source_target_pairs={{0,9},{1,16},{2,11},{3,18},{4,13},{5,20},{6,15},{7,22},{8,1},{9,24... | collective-permute-start | bytes 98312 | tf_op jit(solution)/shard_map/ppermute | solution.py:543
  66.9 1.5 %prompt_gradient.2.rest_4_ = f32[5120,64]{1,0:T(8,128)S(1)} custom-call(bf16[64,256]{1,0:T(8,128)(2,1)S(1)} %get-tuple-element.116.rest_0_, bf16[64,256]{1,0:T(8,128)(2,1)S(1)} %collective-permute-done.21.rest_1_, bf16[5120,512]{1,0:T(8,128)(2,1)S(1)} %bitcast.20, bf16[5120,512]{1,0:T(8,128)(2,1)S(1)} %bitcast.22), custom_call_target="tpu_custom_call" | custom-call | flops 335544320 | bytes 5898240 | tf_op jit(solution)/shard_map/prompt_gradient/pallas_call | solution.py:504
  68.4 2.3 %prompt_gradient.3 = bf16[64,5120]{1,0:T(8,128)(2,1)} custom-call(bf16[64,256]{1,0:T(8,128)(2,1)S(1)} %collective-permute-done.19.rest_0_, bf16[64,256]{1,0:T(8,128)(2,1)S(1)} %collective-permute-done.20.rest_1_, bf16[5120,512]{1,0:T(8,128)(2,1)S(1)} %bitcast.20, bf16[5120,512]{1,0:T(8,128)(2,1)S(1)} %bitcast.22, f32[5120,64]{1,0:T(8,128)S(1)} %prompt_gradient.2.rest_4_), custom_call_target="tpu_custom_call" | custom-call | flops 335544320 | bytes 5898240 | tf_op jit(solution)/shard_map/prompt_gradient/pallas_call | solution.py:504
  (58 shorter events, 11.5 us)
Async XLA Ops:
  0.6 5.5 %collective-permute-start = (bf16[64,5120]{1,0:T(8,128)(2,1)}, bf16[64,5120]{1,0:T(8,128)(2,1)S(1)}, u32[]{:S(2)}, u32[]{:S(2)}) collective-permute-start(bf16[64,5120]{1,0:T(8,128)(2,1)} %x_ref.1), channel_id=1, source_target_pairs={{1,0},{0,1},{3,2},{2,3},{5,4},{4,5},{7,6},{6,7},{9,8},{8,9},{11,10... | collective-permute-start | bytes 1966088 | tf_op jit(solution)/shard_map/ppermute | solution.py:539
  7.2 4.8 %collective-permute-start.1 = (bf16[128,256]{1,0:T(8,128)(2,1)S(1)}, bf16[128,256]{1,0:T(8,128)(2,1)S(1)}, u32[]{:S(2)}, u32[]{:S(2)}) collective-permute-start(bf16[128,256]{1,0:T(8,128)(2,1)S(1)} %get-tuple-element.65), channel_id=1, source_target_pairs={{8,0},{17,1},{10,2},{19,3},{12,4},{21,5},{14,6},{23,7},{0,8},{25,9... | collective-permute-start | bytes 196616 | tf_op jit(solution)/shard_map/ppermute | solution.py:539
  12.0 10.6 %collective-permute-start.3 = (bf16[128,1664]{1,0:T(8,128)(2,1)S(1)}, bf16[128,1664]{1,0:T(8,128)(2,1)S(1)}, u32[]{:S(2)}, u32[]{:S(2)}) collective-permute-start(bf16[128,1664]{1,0:T(8,128)(2,1)S(1)} %get-tuple-element.72), channel_id=1, source_target_pairs={{8,0},{17,1},{10,2},{19,3},{12,4},{21,5},{14,6},{23,7},{0,8},{25,9... | collective-permute-start | bytes 1277960 | tf_op jit(solution)/shard_map/ppermute | solution.py:539
  14.1 8.5 %collective-permute-start.2 = (bf16[4,64,256]{2,1,0:T(8,128)(2,1)S(1)}, bf16[4,64,256]{2,1,0:T(8,128)(2,1)S(1)}, u32[]{:S(2)}, u32[]{:S(2)}) collective-permute-start(bf16[4,64,256]{2,1,0:T(8,128)(2,1)S(1)} %bitcast.23), channel_id=1, source_target_pairs={{4,0},{5,1},{6,2},{7,3},{0,4},{1,5},{2,6},{3,7},{12,8},{13,9},{14,... | collective-permute-start | bytes 393224 | tf_op jit(solution)/shard_map/ppermute | solution.py:539
  16.7 6.2 %collective-permute-start.7 = (bf16[4,64,256]{2,1,0:T(8,128)(2,1)S(1)}, bf16[4,64,256]{2,1,0:T(8,128)(2,1)S(1)}, u32[]{:S(2)}, u32[]{:S(2)}) collective-permute-start(bf16[4,64,256]{2,1,0:T(8,128)(2,1)S(1)} %bitcast.24), channel_id=1, source_target_pairs={{2,0},{3,1},{0,2},{1,3},{6,4},{7,5},{4,6},{5,7},{10,8},{11,9},{8,1... | collective-permute-start | bytes 393224 | tf_op jit(solution)/shard_map/ppermute | solution.py:539
  18.3 6.7 %collective-permute-start.5 = (bf16[128,1664]{1,0:T(8,128)(2,1)S(1)}, bf16[128,1664]{1,0:T(8,128)(2,1)S(1)}, u32[]{:S(2)}, u32[]{:S(2)}) collective-permute-start(bf16[128,1664]{1,0:T(8,128)(2,1)S(1)} %get-tuple-element.75), channel_id=1, source_target_pairs={{1,0},{0,1},{3,2},{2,3},{5,4},{4,5},{7,6},{6,7},{9,8},{8,9},{11,10... | collective-permute-start | bytes 1277960 | tf_op jit(solution)/shard_map/ppermute | solution.py:539
  18.3 7.6 %collective-permute-start.6 = (bf16[128,1664]{1,0:T(8,128)(2,1)S(1)}, bf16[128,1664]{1,0:T(8,128)(2,1)S(1)}, u32[]{:S(2)}, u32[]{:S(2)}) collective-permute-start(bf16[128,1664]{1,0:T(8,128)(2,1)S(1)} %get-tuple-element.77), channel_id=1, source_target_pairs={{9,0},{16,1},{11,2},{18,3},{13,4},{20,5},{15,6},{22,7},{1,8},{24,9... | collective-permute-start | bytes 1277960 | tf_op jit(solution)/shard_map/ppermute | solution.py:539
  22.9 11.2 %collective-permute-start.8 = (bf16[3,4,64,256]{3,2,1,0:T(8,128)(2,1)S(1)}, bf16[3,4,64,256]{3,2,1,0:T(8,128)(2,1)S(1)}, u32[]{:S(2)}, u32[]{:S(2)}) collective-permute-start(bf16[3,4,64,256]{3,2,1,0:T(8,128)(2,1)S(1)} %pad_maximum_fusion), channel_id=1, source_target_pairs={{16,0},{9,1},{18,2},{11,3},{20,4},{13,5},{22,6},{15,7},{24,8},{1,9... | collective-permute-start | bytes 1179656 | tf_op jit(solution)/shard_map/ppermute | solution.py:539
  23.5 5.6 %collective-permute-start.4 = (bf16[4,64,256]{2,1,0:T(8,128)(2,1)S(1)}, bf16[4,64,256]{2,1,0:T(8,128)(2,1)S(1)}, u32[]{:S(2)}, u32[]{:S(2)}) collective-permute-start(bf16[4,64,256]{2,1,0:T(8,128)(2,1)S(1)} %collective-permute-done.2.rest_5_), channel_id=1, source_target_pairs={{2,0},{3,1},{0,2},{1,3},{6,4},{7,5},{4,6},{5,7},{10,8},{11,9},{8,1... | collective-permute-start | bytes 393224 | tf_op jit(solution)/shard_map/ppermute | solution.py:539
  29.1 5.0 %collective-permute-start.9 = (bf16[1,4,64,256]{3,2,1,0:T(8,128)(2,1)S(1)}, bf16[1,4,64,256]{3,2,1,0:T(8,128)(2,1)S(1)}, u32[]{:S(2)}, u32[]{:S(2)}) collective-permute-start(bf16[1,4,64,256]{3,2,1,0:T(8,128)(2,1)S(1)} %bitcast.30), channel_id=1, source_target_pairs={{16,0},{9,1},{18,2},{11,3},{20,4},{13,5},{22,6},{15,7},{24,8},{1,9... | collective-permute-start | bytes 393224 | tf_op jit(solution)/shard_map/ppermute | solution.py:539
  34.1 32.7 %slice-start.2 = ((s8[5242880]{0:T(1024)(128)(4,1)}), s8[4194304]{0:T(1024)(128)(4,1)S(1)}, s32[]{:S(2)}) async-start(s8[5242880]{0:T(1024)(128)(4,1)} %bitcast.21), calls=%async_computation.2 | async-start | bytes 8388608
  39.7 5.0 %collective-permute-start.10 = (bf16[1,4,64,256]{3,2,1,0:T(8,128)(2,1)S(1)}, bf16[1,4,64,256]{3,2,1,0:T(8,128)(2,1)S(1)}, u32[]{:S(2)}, u32[]{:S(2)}) collective-permute-start(bf16[1,4,64,256]{3,2,1,0:T(8,128)(2,1)S(1)} %get-tuple-element.88), channel_id=1, source_target_pairs={{0,16},{1,9},{2,18},{3,11},{4,20},{5,13},{6,22},{7,15},{8,24},{9,1... | collective-permute-start | bytes 393224 | tf_op jit(solution)/shard_map/ppermute | solution.py:543
  40.6 26.2 %slice-start.3 = ((s8[5242880]{0:T(1024)(128)(4,1)}), s8[1048576]{0:T(1024)(128)(4,1)S(1)}, s32[]{:S(2)}) async-start(s8[5242880]{0:T(1024)(128)(4,1)} %bitcast.21), calls=%async_computation.3 | async-start | bytes 2097152
  42.5 7.8 %collective-permute-start.11 = (bf16[2,4,64,256]{3,2,1,0:T(8,128)(2,1)S(1)}, bf16[2,4,64,256]{3,2,1,0:T(8,128)(2,1)S(1)}, u32[]{:S(2)}, u32[]{:S(2)}) collective-permute-start(bf16[2,4,64,256]{3,2,1,0:T(8,128)(2,1)S(1)} %get-tuple-element.95), channel_id=1, source_target_pairs={{0,16},{1,9},{2,18},{3,11},{4,20},{5,13},{6,22},{7,15},{8,24},{9,1... | collective-permute-start | bytes 786440 | tf_op jit(solution)/shard_map/ppermute | solution.py:543
  44.8 5.6 %collective-permute-start.12 = (bf16[4,64,256]{2,1,0:T(8,128)(2,1)S(1)}, bf16[4,64,256]{2,1,0:T(8,128)(2,1)S(1)}, u32[]{:S(2)}, u32[]{:S(2)}) collective-permute-start(bf16[4,64,256]{2,1,0:T(8,128)(2,1)S(1)} %fusion.2), channel_id=1, source_target_pairs={{0,2},{1,3},{2,0},{3,1},{4,6},{5,7},{6,4},{7,5},{8,10},{9,11},{10,... | collective-permute-start | bytes 393224 | tf_op jit(solution)/shard_map/ppermute | solution.py:543
  48.0 11.1 %collective-permute-start.14 = (bf16[128,896]{1,0:T(8,128)(2,1)S(1)}, bf16[128,896]{1,0:T(8,128)(2,1)S(1)}, u32[]{:S(2)}, u32[]{:S(2)}) collective-permute-start(bf16[128,896]{1,0:T(8,128)(2,1)S(1)} %get-tuple-element.101), channel_id=1, source_target_pairs={{0,8},{1,17},{2,10},{3,19},{4,12},{5,21},{6,14},{7,23},{8,0},{9,25... | collective-permute-start | bytes 688136 | tf_op jit(solution)/shard_map/ppermute | solution.py:543
  50.4 8.8 %collective-permute-start.13 = (bf16[128,896]{1,0:T(8,128)(2,1)S(1)}, bf16[128,896]{1,0:T(8,128)(2,1)S(1)}, u32[]{:S(2)}, u32[]{:S(2)}) collective-permute-start(bf16[128,896]{1,0:T(8,128)(2,1)S(1)} %get-tuple-element.100), channel_id=1, source_target_pairs={{0,1},{1,0},{2,3},{3,2},{4,5},{5,4},{6,7},{7,6},{8,9},{9,8},{10,11... | collective-permute-start | bytes 688136 | tf_op jit(solution)/shard_map/ppermute | solution.py:543
  50.4 8.8 %collective-permute-start.15 = (bf16[128,896]{1,0:T(8,128)(2,1)S(1)}, bf16[128,896]{1,0:T(8,128)(2,1)S(1)}, u32[]{:S(2)}, u32[]{:S(2)}) collective-permute-start(bf16[128,896]{1,0:T(8,128)(2,1)S(1)} %get-tuple-element.102), channel_id=1, source_target_pairs={{0,9},{1,16},{2,11},{3,18},{4,13},{5,20},{6,15},{7,22},{8,1},{9,24... | collective-permute-start | bytes 688136 | tf_op jit(solution)/shard_map/ppermute | solution.py:543
  53.2 9.8 %collective-permute-start.17 = (bf16[4,64,256]{2,1,0:T(8,128)(2,1)S(1)}, bf16[4,64,256]{2,1,0:T(8,128)(2,1)S(1)}, u32[]{:S(2)}, u32[]{:S(2)}) collective-permute-start(bf16[4,64,256]{2,1,0:T(8,128)(2,1)S(1)} %fusion.1), channel_id=1, source_target_pairs={{0,4},{1,5},{2,6},{3,7},{4,0},{5,1},{6,2},{7,3},{8,12},{9,13},{10,... | collective-permute-start | bytes 393224 | tf_op jit(solution)/shard_map/ppermute | solution.py:543
  57.1 7.2 %collective-permute-start.16 = (bf16[4,64,256]{2,1,0:T(8,128)(2,1)S(1)}, bf16[4,64,256]{2,1,0:T(8,128)(2,1)S(1)}, u32[]{:S(2)}, u32[]{:S(2)}) collective-permute-start(bf16[4,64,256]{2,1,0:T(8,128)(2,1)S(1)} %convert_add_fusion.2), channel_id=1, source_target_pairs={{0,2},{1,3},{2,0},{3,1},{4,6},{5,7},{6,4},{7,5},{8,10},{9,11},{10,... | collective-permute-start | bytes 393224 | tf_op jit(solution)/shard_map/ppermute | solution.py:543
  59.1 5.2 %collective-permute-start.18 = (bf16[1,4,64,256]{3,2,1,0:T(8,128)(2,1)S(1)}, bf16[1,4,64,256]{3,2,1,0:T(8,128)(2,1)S(1)}, u32[]{:S(2)}, u32[]{:S(2)}) collective-permute-start(bf16[1,4,64,256]{3,2,1,0:T(8,128)(2,1)S(1)} %get-tuple-element.113), channel_id=1, source_target_pairs={{0,16},{1,9},{2,18},{3,11},{4,20},{5,13},{6,22},{7,15},{8,24},{9,1... | collective-permute-start | bytes 393224 | tf_op jit(solution)/shard_map/ppermute | solution.py:543
  64.4 2.4 %collective-permute-start.21 = (bf16[64,256]{1,0:T(8,128)(2,1)S(1)}, bf16[64,256]{1,0:T(8,128)(2,1)S(1)}, u32[]{:S(2)}, u32[]{:S(2)}) collective-permute-start(bf16[64,256]{1,0:T(8,128)(2,1)S(1)} %get-tuple-element.117), channel_id=1, source_target_pairs={{0,1},{1,0},{2,3},{3,2},{4,5},{5,4},{6,7},{7,6},{8,9},{9,8},{10,11... | collective-permute-start | bytes 98312 | tf_op jit(solution)/shard_map/ppermute | solution.py:543
  64.5 4.0 %collective-permute-start.19 = (bf16[64,256]{1,0:T(8,128)(2,1)S(1)}, bf16[64,256]{1,0:T(8,128)(2,1)S(1)}, u32[]{:S(2)}, u32[]{:S(2)}) collective-permute-start(bf16[64,256]{1,0:T(8,128)(2,1)S(1)} %get-tuple-element.114), channel_id=1, source_target_pairs={{0,8},{1,17},{2,10},{3,19},{4,12},{5,21},{6,14},{7,23},{8,0},{9,25... | collective-permute-start | bytes 98312 | tf_op jit(solution)/shard_map/ppermute | solution.py:543
  64.8 3.6 %collective-permute-start.20 = (bf16[64,256]{1,0:T(8,128)(2,1)S(1)}, bf16[64,256]{1,0:T(8,128)(2,1)S(1)}, u32[]{:S(2)}, u32[]{:S(2)}) collective-permute-start(bf16[64,256]{1,0:T(8,128)(2,1)S(1)} %get-tuple-element.115), channel_id=1, source_target_pairs={{0,9},{1,16},{2,11},{3,18},{4,13},{5,20},{6,15},{7,22},{8,1},{9,24... | collective-permute-start | bytes 98312 | tf_op jit(solution)/shard_map/ppermute | solution.py:543
  (8 other events, 63.8 us)

commit v14 on v11

--- a/solution.py
+++ b/solution.py
@@ -15,7 +15,7 @@
 HIDDEN = -1e30
 BF16 = jnp.bfloat16
 F32 = jnp.float32
-NOTE_ROWS = 16
+NOTE_ROWS, NOTE_LANES = 16, 32
 CORE, X, Y = 0, 3, 4
 GATHER_BITS = (2, 1)
 MEMBERS = (0, 1 << CORE, 1 << X, 1 << X | 1 << CORE)
@@ -130,29 +130,33 @@
 
 def pack_kernel(length_ref, prompts_ref, q_ref, g_ref, k_ref, v_ref, *outs):
     heads, _, _ = place()
-    row = lax.broadcasted_iota(jnp.int32, (q_ref.shape[0], E), 0)
+    lane = lax.broadcasted_iota(jnp.int32, (NOTE_ROWS, E), 1)
     note = jnp.where(
-        row < NOTE_ROWS,
+        lane < NOTE_LANES,
         length_ref[0],
-        jnp.where(row < 2 * NOTE_ROWS, prompts_ref[0, 0], prompts_ref[0, 1]),
+        jnp.where(lane < 2 * NOTE_LANES, prompts_ref[0, 0], prompts_ref[0, 1]),
     )
     note = note.astype(F32).astype(BF16)
+    rows = q_ref.shape[0]
     for head, out in zip(heads, outs):
         start = 0
         for source in (q_ref, g_ref, k_ref, v_ref):
             width = source.shape[1] // len(outs)
-            out[:, start : start + width] = source[:, lanes(head, width)]
-            start += width
-        out[:, start:] = note
+            part = source[:, lanes(head, width)]
+            for at in range(0, width, E):
+                out[start : start + rows, :] = part[:, at : at + E]
+                start += rows
+        out[start:, :] = note
 
 
 def pack(first_length, resp_prompt, queries, out_grad, own_keys, own_values):
     rows = queries.shape[0]
     n = len(MEMBERS)
-    width = (2 * queries.shape[1] + 2 * own_keys.shape[1]) // n + E
+    width = (2 * queries.shape[1] + 2 * own_keys.shape[1]) // n
+    packet = (rows * width // E + NOTE_ROWS, E)
     return pl.pallas_call(
         pack_kernel,
-        out_shape=[jax.ShapeDtypeStruct((rows, width), BF16)] * n,
+        out_shape=[jax.ShapeDtypeStruct(packet, BF16)] * n,
         in_specs=[SMEM] * 2 + [VMEM] * 4,
         out_specs=[VMEM] * n,
         compiler_params=params(16),
@@ -226,18 +230,24 @@
 
     def products(j):
         packet = packets[j]
+        note = packet[(2 * group + 2) * rows :, :].astype(F32)
+        slot = lax.broadcasted_iota(jnp.int32, note.shape, 1) // NOTE_LANES
         boundary, first_at, second_at = (
-            jnp.max(packet[at : at + NOTE_ROWS, -E:].astype(F32)).astype(jnp.int32)
-            for at in (0, NOTE_ROWS, 2 * NOTE_ROWS)
+            jnp.max(jnp.where(slot == index, note, 0.0)).astype(jnp.int32) for index in range(3)
         )
         first_at, second_at = (
             crossed((prompt ^ prompt_place) << resp_bits, core) >> resp_bits
             for prompt in (first_at, second_at)
         )
-        heads = [packet[:, h * E : (h + 1) * E] for h in range(2 * group + 2)]
-        query = jnp.concatenate(heads[:group], axis=0)
-        grad = jnp.concatenate(heads[group : 2 * group], axis=0)
-        own_k, own_v = heads[2 * group], heads[2 * group + 1]
+        query, grad, own_k, own_v = (
+            packet[at * rows : end * rows, :]
+            for at, end in (
+                (0, group),
+                (group, 2 * group),
+                (2 * group, 2 * group + 1),
+                (2 * group + 1, 2 * group + 2),
+            )
+        )
         in_first = row_in_column < boundary
 
         def split(x):
@@ -326,9 +336,8 @@
             target[j, :, E:] = value_acc[prompt, span, :].astype(target.dtype)
 
 
-def attend(packets, line, stacks, slots, prompts, resp_bits):
-    rows, packet_width = packets[0].shape
-    group = (packet_width // E - 3) // 2
+def attend(packets, rows, line, stacks, slots, prompts, resp_bits):
+    group = (packets[0].shape[0] - NOTE_ROWS) // (2 * rows) - 1
     sums_shape = (prompts, PLEN, E)
     out_shape = [jax.ShapeDtypeStruct((rows, (group + 2) * E), BF16)] * len(packets)
     out_shape += [jax.ShapeDtypeStruct(x.shape, F32) for x in line]
@@ -486,7 +495,7 @@
         slots.append(tuple(places))
     resp_bits = n_resp.bit_length() - 1
     grads, sums, back_stacks = attend(
-        packets, list(pieces.values()), stacks, tuple(slots), n_prompt, resp_bits
+        packets, queries.shape[0], list(pieces.values()), stacks, tuple(slots), n_prompt, resp_bits
     )
 
     sums = dict(zip(offsets, sums))

time: 70.5 us -> 70 us (level)
  transfers between devices with their start and end apart: 22 -> 22, of which waited for: 11 -> 13; matrix products, arithmetic and copies ran while one was open for 0% -> 0% of each run, Pallas kernels for 10% -> 10%
where the time goes in v14:
time: 70 us; the launch traced here: 69.3 us
  starting transfers between devices  27.4 us (39%)
  waiting for transfers between devices  20.4 us (29%)
  Pallas kernels  18.5 us (26%)
  between operations  1.66 us (2%)
  local copies, waits for them, and re-layouts  1.13 us (2%)
    ppermute x10, starting transfers between devices, fetch(): return lax.ppermute(x, ('prompt', 'resp'), pairs)  13.9 us
    ppermute x12, starting transfers between devices, give(): return lax.ppermute(x, ('prompt', 'resp'), pairs)  13.5 us
    ppermute x10, waiting for transfers between devices, fetch(): return lax.ppermute(x, ('prompt', 'resp'), pairs)  12.1 us
    ppermute x12, waiting for transfers between devices, give(): return lax.ppermute(x, ('prompt', 'resp'), pairs)  8.37 us
    pallas_call x1, Pallas kernels, attend(): pl.pallas_call(functools.partial(attend_kernel, slots, group, rows, resp_...  7.98 us
    pallas_call x1, Pallas kernels, project(): pl.pallas_call(functools.partial(project_kernel, steps), out_shape=[jax.S...  3.83 us
    pallas_call x2, Pallas kernels, prompt_gradient(): pl.pallas_call(functools.partial(prompt_kernel, chunk, members, first), o...  3.81 us
  transfers between devices with their start and end apart: 22, of which 13 were waited for; matrix products, arithmetic and copies ran while one was open for 0% of the time, Pallas kernels for 10%

profile of v14, /device:TPU:0, one launch (start us, length us, event | category | flops | bytes accessed | tf_op | source)
XLA Modules:
  0.0 69.3 jit_solution(8567724941380137442)
XLA Ops:
  1.1 1.1 %copy-done.2 = bf16[64,5120]{1,0:T(8,128)(2,1)S(1)} copy-done((bf16[64,5120]{1,0:T(8,128)(2,1)S(1)}, bf16[64,5120]{1,0:T(8,128)(2,1)}, u32[]{:S(2)}) %copy-start.2) | copy-done | bytes 655384
  2.2 3.8 %project_own.1 = (bf16[64,512]{1,0:T(8,128)(2,1)S(1)}, bf16[5120,512]{1,0:T(8,128)(2,1)S(1)}) custom-call(bf16[64,5120]{1,0:T(8,128)(2,1)S(1)} %copy-done.2, bf16[5120,512]{1,0:T(8,128)(2,1)} %rest_2_.3, bf16[5120,512]{1,0:T(8,128)(2,1)} %rest_3_.3), custom_call_target="tpu_custom_call" | custom-call | flops 335544320 | bytes 5898240 | tf_op jit(solution)/shard_map/project_own/pallas_call | solution.py:91
  7.2 2.6 %collective-permute-start.1 = (bf16[128,256]{1,0:T(8,128)(2,1)S(1)}, bf16[128,256]{1,0:T(8,128)(2,1)S(1)}, u32[]{:S(2)}, u32[]{:S(2)}) collective-permute-start(bf16[128,256]{1,0:T(8,128)(2,1)S(1)} %get-tuple-element.61), channel_id=1, source_target_pairs={{8,0},{17,1},{10,2},{19,3},{12,4},{21,5},{14,6},{23,7},{0,8},{25,9... | collective-permute-start | bytes 196616 | tf_op jit(solution)/shard_map/ppermute | solution.py:456
  12.0 2.1 %collective-permute-start.3 = (bf16[1552,128]{1,0:T(8,128)(2,1)S(1)}, bf16[1552,128]{1,0:T(8,128)(2,1)S(1)}, u32[]{:S(2)}, u32[]{:S(2)}) collective-permute-start(bf16[1552,128]{1,0:T(8,128)(2,1)S(1)} %get-tuple-element.68), channel_id=1, source_target_pairs={{8,0},{17,1},{10,2},{19,3},{12,4},{21,5},{14,6},{23,7},{0,8},{25,9... | collective-permute-start | bytes 1191944 | tf_op jit(solution)/shard_map/ppermute | solution.py:456
  14.1 2.6 %collective-permute-start.2 = (bf16[4,64,256]{2,1,0:T(8,128)(2,1)S(1)}, bf16[4,64,256]{2,1,0:T(8,128)(2,1)S(1)}, u32[]{:S(2)}, u32[]{:S(2)}) collective-permute-start(bf16[4,64,256]{2,1,0:T(8,128)(2,1)S(1)} %bitcast.19), channel_id=1, source_target_pairs={{4,0},{5,1},{6,2},{7,3},{0,4},{1,5},{2,6},{3,7},{12,8},{13,9},{14,... | collective-permute-start | bytes 393224 | tf_op jit(solution)/shard_map/ppermute | solution.py:456
  16.7 1.6 %collective-permute-start.7 = (bf16[4,64,256]{2,1,0:T(8,128)(2,1)S(1)}, bf16[4,64,256]{2,1,0:T(8,128)(2,1)S(1)}, u32[]{:S(2)}, u32[]{:S(2)}) collective-permute-start(bf16[4,64,256]{2,1,0:T(8,128)(2,1)S(1)} %bitcast.20), channel_id=1, source_target_pairs={{2,0},{3,1},{0,2},{1,3},{6,4},{7,5},{4,6},{5,7},{10,8},{11,9},{8,1... | collective-permute-start | bytes 393224 | tf_op jit(solution)/shard_map/ppermute | solution.py:456
  18.3 1.6 %collective-permute-start.6 = (bf16[1552,128]{1,0:T(8,128)(2,1)S(1)}, bf16[1552,128]{1,0:T(8,128)(2,1)S(1)}, u32[]{:S(2)}, u32[]{:S(2)}) collective-permute-start(bf16[1552,128]{1,0:T(8,128)(2,1)S(1)} %get-tuple-element.73), channel_id=1, source_target_pairs={{9,0},{16,1},{11,2},{18,3},{13,4},{20,5},{15,6},{22,7},{1,8},{24,9... | collective-permute-start | bytes 1191944 | tf_op jit(solution)/shard_map/ppermute | solution.py:456
  19.9 2.7 %collective-permute-done.2.rest_5_ = bf16[4,64,256]{2,1,0:T(8,128)(2,1)S(1)} collective-permute-done((bf16[4,64,256]{2,1,0:T(8,128)(2,1)S(1)}, bf16[4,64,256]{2,1,0:T(8,128)(2,1)S(1)}, u32[]{:S(2)}, u32[]{:S(2)}) %collective-permute-start.2) | collective-permute-done | bytes 131104 | tf_op jit(solution)/shard_map/ppermute | solution.py:456
  23.5 1.4 %collective-permute-start.4 = (bf16[4,64,256]{2,1,0:T(8,128)(2,1)S(1)}, bf16[4,64,256]{2,1,0:T(8,128)(2,1)S(1)}, u32[]{:S(2)}, u32[]{:S(2)}) collective-permute-start(bf16[4,64,256]{2,1,0:T(8,128)(2,1)S(1)} %collective-permute-done.2.rest_5_), channel_id=1, source_target_pairs={{2,0},{3,1},{0,2},{1,3},{6,4},{7,5},{4,6},{5,7},{10,8},{11,9},{8,1... | collective-permute-start | bytes 393224 | tf_op jit(solution)/shard_map/ppermute | solution.py:456
  25.5 3.6 %collective-permute-done.4.rest_7_ = bf16[4,64,256]{2,1,0:T(8,128)(2,1)S(1)} collective-permute-done((bf16[4,64,256]{2,1,0:T(8,128)(2,1)S(1)}, bf16[4,64,256]{2,1,0:T(8,128)(2,1)S(1)}, u32[]{:S(2)}, u32[]{:S(2)}) %collective-permute-start.4) | collective-permute-done | bytes 131104 | tf_op jit(solution)/shard_map/ppermute | solution.py:456
  30.1 4.1 %collective-permute-done.9.rest_9_ = bf16[1,4,64,256]{3,2,1,0:T(8,128)(2,1)S(1)} collective-permute-done((bf16[1,4,64,256]{3,2,1,0:T(8,128)(2,1)S(1)}, bf16[1,4,64,256]{3,2,1,0:T(8,128)(2,1)S(1)}, u32[]{:S(2)}, u32[]{:S(2)}) %collective-permute-start.9) | collective-permute-done | bytes 131104 | tf_op jit(solution)/shard_map/ppermute | solution.py:456
  34.2 8.0 %attend_head.1 = (bf16[128,896]{1,0:T(8,128)(2,1)S(1)}, bf16[128,896]{1,0:T(8,128)(2,1)S(1)}, bf16[128,896]{1,0:T(8,128)(2,1)S(1)}, bf16[128,896]{1,0:T(8,128)(2...) custom-call(bf16[1552,128]{1,0:T(8,128)(2,1)S(1)} %get-tuple-element, ...), custom_call_target="tpu_custom_call" | custom-call | flops 4194304000 | bytes 16777216 | tf_op jit(solution)/shard_map/attend_head/pallas_call | solution.py:348
  43.1 1.2 %collective-permute-start.11 = (bf16[2,4,64,256]{3,2,1,0:T(8,128)(2,1)S(1)}, bf16[2,4,64,256]{3,2,1,0:T(8,128)(2,1)S(1)}, u32[]{:S(2)}, u32[]{:S(2)}) collective-permute-start(bf16[2,4,64,256]{3,2,1,0:T(8,128)(2,1)S(1)} %get-tuple-element.81), channel_id=1, source_target_pairs={{0,16},{1,9},{2,18},{3,11},{4,20},{5,13},{6,22},{7,15},{8,24},{9,1... | collective-permute-start | bytes 786440 | tf_op jit(solution)/shard_map/ppermute | solution.py:460
  45.1 2.1 %collective-permute-done.12 = bf16[1,4,64,256]{3,2,1,0:T(8,128)(2,1)S(1)} collective-permute-done((bf16[1,4,64,256]{3,2,1,0:T(8,128)(2,1)S(1)}, bf16[1,4,64,256]{3,2,1,0:T(8,128)(2,1)S(1)}, u32[]{:S(2)}, u32[]{:S(2)}) %collective-permute-start.12) | collective-permute-done | bytes 131104 | tf_op jit(solution)/shard_map/ppermute | solution.py:460
  47.2 1.5 %collective-permute-start.13 = (bf16[4,64,256]{2,1,0:T(8,128)(2,1)S(1)}, bf16[4,64,256]{2,1,0:T(8,128)(2,1)S(1)}, u32[]{:S(2)}, u32[]{:S(2)}) collective-permute-start(bf16[4,64,256]{2,1,0:T(8,128)(2,1)S(1)} %fusion.2), channel_id=1, source_target_pairs={{0,2},{1,3},{2,0},{3,1},{4,6},{5,7},{6,4},{7,5},{8,10},{9,11},{10,... | collective-permute-start | bytes 393224 | tf_op jit(solution)/shard_map/ppermute | solution.py:460
  48.7 1.3 %collective-permute-done.11 = bf16[2,4,64,256]{3,2,1,0:T(8,128)(2,1)S(1)} collective-permute-done((bf16[2,4,64,256]{3,2,1,0:T(8,128)(2,1)S(1)}, bf16[2,4,64,256]{3,2,1,0:T(8,128)(2,1)S(1)}, u32[]{:S(2)}, u32[]{:S(2)}) %collective-permute-start.11) | collective-permute-done | bytes 262176 | tf_op jit(solution)/shard_map/ppermute | solution.py:460
  51.0 1.2 %collective-permute-start.18 = (bf16[128,896]{1,0:T(8,128)(2,1)S(1)}, bf16[128,896]{1,0:T(8,128)(2,1)S(1)}, u32[]{:S(2)}, u32[]{:S(2)}) collective-permute-start(bf16[128,896]{1,0:T(8,128)(2,1)S(1)} %get-tuple-element.95), channel_id=1, source_target_pairs={{0,9},{1,16},{2,11},{3,18},{4,13},{5,20},{6,15},{7,22},{8,1},{9,24... | collective-permute-start | bytes 688136 | tf_op jit(solution)/shard_map/ppermute | solution.py:460
  52.3 3.4 %collective-permute-start.15 = (bf16[4,64,256]{2,1,0:T(8,128)(2,1)S(1)}, bf16[4,64,256]{2,1,0:T(8,128)(2,1)S(1)}, u32[]{:S(2)}, u32[]{:S(2)}) collective-permute-start(bf16[4,64,256]{2,1,0:T(8,128)(2,1)S(1)} %fusion.1), channel_id=1, source_target_pairs={{0,4},{1,5},{2,6},{3,7},{4,0},{5,1},{6,2},{7,3},{8,12},{9,13},{10,... | collective-permute-start | bytes 393224 | tf_op jit(solution)/shard_map/ppermute | solution.py:460
  55.7 2.0 %collective-permute-start.14 = (bf16[4,64,256]{2,1,0:T(8,128)(2,1)S(1)}, bf16[4,64,256]{2,1,0:T(8,128)(2,1)S(1)}, u32[]{:S(2)}, u32[]{:S(2)}) collective-permute-start(bf16[4,64,256]{2,1,0:T(8,128)(2,1)S(1)} %convert_add_fusion.2), channel_id=1, source_target_pairs={{0,2},{1,3},{2,0},{3,1},{4,6},{5,7},{6,4},{7,5},{8,10},{9,11},{10,... | collective-permute-start | bytes 393224 | tf_op jit(solution)/shard_map/ppermute | solution.py:460
  59.1 3.5 %collective-permute-done.15.rest_2_ = bf16[4,64,256]{2,1,0:T(8,128)(2,1)S(1)} collective-permute-done((bf16[4,64,256]{2,1,0:T(8,128)(2,1)S(1)}, bf16[4,64,256]{2,1,0:T(8,128)(2,1)S(1)}, u32[]{:S(2)}, u32[]{:S(2)}) %collective-permute-start.15) | collective-permute-done | bytes 131104 | tf_op jit(solution)/shard_map/ppermute | solution.py:460
  63.1 1.0 %collective-permute-start.20 = (bf16[64,256]{1,0:T(8,128)(2,1)S(1)}, bf16[64,256]{1,0:T(8,128)(2,1)S(1)}, u32[]{:S(2)}, u32[]{:S(2)}) collective-permute-start(bf16[64,256]{1,0:T(8,128)(2,1)S(1)} %get-tuple-element.107), channel_id=1, source_target_pairs={{0,9},{1,16},{2,11},{3,18},{4,13},{5,20},{6,15},{7,22},{8,1},{9,24... | collective-permute-start | bytes 98312 | tf_op jit(solution)/shard_map/ppermute | solution.py:460
  64.2 1.5 %prompt_gradient.2.rest_4_ = f32[5120,64]{1,0:T(8,128)S(1)} custom-call(bf16[64,256]{1,0:T(8,128)(2,1)S(1)} %get-tuple-element.108.rest_0_, bf16[64,256]{1,0:T(8,128)(2,1)S(1)} %collective-permute-done.21.rest_1_, bf16[5120,512]{1,0:T(8,128)(2,1)S(1)} %bitcast.16, bf16[5120,512]{1,0:T(8,128)(2,1)S(1)} %bitcast.18), custom_call_target="tpu_custom_call" | custom-call | flops 335544320 | bytes 5898240 | tf_op jit(solution)/shard_map/prompt_gradient/pallas_call | solution.py:421
  65.8 1.0 %collective-permute-done.19.rest_0_ = bf16[64,256]{1,0:T(8,128)(2,1)S(1)} collective-permute-done((bf16[64,256]{1,0:T(8,128)(2,1)S(1)}, bf16[64,256]{1,0:T(8,128)(2,1)S(1)}, u32[]{:S(2)}, u32[]{:S(2)}) %collective-permute-start.19) | collective-permute-done | bytes 32800 | tf_op jit(solution)/shard_map/ppermute | solution.py:460
  66.8 2.3 %prompt_gradient.3 = bf16[64,5120]{1,0:T(8,128)(2,1)} custom-call(bf16[64,256]{1,0:T(8,128)(2,1)S(1)} %collective-permute-done.19.rest_0_, bf16[64,256]{1,0:T(8,128)(2,1)S(1)} %collective-permute-done.20.rest_1_, bf16[5120,512]{1,0:T(8,128)(2,1)S(1)} %bitcast.16, bf16[5120,512]{1,0:T(8,128)(2,1)S(1)} %bitcast.18, f32[5120,64]{1,0:T(8,128)S(1)} %prompt_gradient.2.rest_4_), custom_call_target="tpu_custom_call" | custom-call | flops 335544320 | bytes 5898240 | tf_op jit(solution)/shard_map/prompt_gradient/pallas_call | solution.py:421
  (55 shorter events, 10.2 us)
Async XLA Ops:
  0.6 5.5 %collective-permute-start = (bf16[64,5120]{1,0:T(8,128)(2,1)}, bf16[64,5120]{1,0:T(8,128)(2,1)S(1)}, u32[]{:S(2)}, u32[]{:S(2)}) collective-permute-start(bf16[64,5120]{1,0:T(8,128)(2,1)} %x_ref.1), channel_id=1, source_target_pairs={{1,0},{0,1},{3,2},{2,3},{5,4},{4,5},{7,6},{6,7},{9,8},{8,9},{11,10... | collective-permute-start | bytes 1966088 | tf_op jit(solution)/shard_map/ppermute | solution.py:456
  7.2 4.8 %collective-permute-start.1 = (bf16[128,256]{1,0:T(8,128)(2,1)S(1)}, bf16[128,256]{1,0:T(8,128)(2,1)S(1)}, u32[]{:S(2)}, u32[]{:S(2)}) collective-permute-start(bf16[128,256]{1,0:T(8,128)(2,1)S(1)} %get-tuple-element.61), channel_id=1, source_target_pairs={{8,0},{17,1},{10,2},{19,3},{12,4},{21,5},{14,6},{23,7},{0,8},{25,9... | collective-permute-start | bytes 196616 | tf_op jit(solution)/shard_map/ppermute | solution.py:456
  12.0 10.6 %collective-permute-start.3 = (bf16[1552,128]{1,0:T(8,128)(2,1)S(1)}, bf16[1552,128]{1,0:T(8,128)(2,1)S(1)}, u32[]{:S(2)}, u32[]{:S(2)}) collective-permute-start(bf16[1552,128]{1,0:T(8,128)(2,1)S(1)} %get-tuple-element.68), channel_id=1, source_target_pairs={{8,0},{17,1},{10,2},{19,3},{12,4},{21,5},{14,6},{23,7},{0,8},{25,9... | collective-permute-start | bytes 1191944 | tf_op jit(solution)/shard_map/ppermute | solution.py:456
  14.1 8.5 %collective-permute-start.2 = (bf16[4,64,256]{2,1,0:T(8,128)(2,1)S(1)}, bf16[4,64,256]{2,1,0:T(8,128)(2,1)S(1)}, u32[]{:S(2)}, u32[]{:S(2)}) collective-permute-start(bf16[4,64,256]{2,1,0:T(8,128)(2,1)S(1)} %bitcast.19), channel_id=1, source_target_pairs={{4,0},{5,1},{6,2},{7,3},{0,4},{1,5},{2,6},{3,7},{12,8},{13,9},{14,... | collective-permute-start | bytes 393224 | tf_op jit(solution)/shard_map/ppermute | solution.py:456
  16.7 6.2 %collective-permute-start.7 = (bf16[4,64,256]{2,1,0:T(8,128)(2,1)S(1)}, bf16[4,64,256]{2,1,0:T(8,128)(2,1)S(1)}, u32[]{:S(2)}, u32[]{:S(2)}) collective-permute-start(bf16[4,64,256]{2,1,0:T(8,128)(2,1)S(1)} %bitcast.20), channel_id=1, source_target_pairs={{2,0},{3,1},{0,2},{1,3},{6,4},{7,5},{4,6},{5,7},{10,8},{11,9},{8,1... | collective-permute-start | bytes 393224 | tf_op jit(solution)/shard_map/ppermute | solution.py:456
  18.3 6.7 %collective-permute-start.5 = (bf16[1552,128]{1,0:T(8,128)(2,1)S(1)}, bf16[1552,128]{1,0:T(8,128)(2,1)S(1)}, u32[]{:S(2)}, u32[]{:S(2)}) collective-permute-start(bf16[1552,128]{1,0:T(8,128)(2,1)S(1)} %get-tuple-element.71), channel_id=1, source_target_pairs={{1,0},{0,1},{3,2},{2,3},{5,4},{4,5},{7,6},{6,7},{9,8},{8,9},{11,10... | collective-permute-start | bytes 1191944 | tf_op jit(solution)/shard_map/ppermute | solution.py:456
  18.3 7.2 %collective-permute-start.6 = (bf16[1552,128]{1,0:T(8,128)(2,1)S(1)}, bf16[1552,128]{1,0:T(8,128)(2,1)S(1)}, u32[]{:S(2)}, u32[]{:S(2)}) collective-permute-start(bf16[1552,128]{1,0:T(8,128)(2,1)S(1)} %get-tuple-element.73), channel_id=1, source_target_pairs={{9,0},{16,1},{11,2},{18,3},{13,4},{20,5},{15,6},{22,7},{1,8},{24,9... | collective-permute-start | bytes 1191944 | tf_op jit(solution)/shard_map/ppermute | solution.py:456
  22.9 11.3 %collective-permute-start.8 = (bf16[3,4,64,256]{3,2,1,0:T(8,128)(2,1)S(1)}, bf16[3,4,64,256]{3,2,1,0:T(8,128)(2,1)S(1)}, u32[]{:S(2)}, u32[]{:S(2)}) collective-permute-start(bf16[3,4,64,256]{3,2,1,0:T(8,128)(2,1)S(1)} %pad_maximum_fusion), channel_id=1, source_target_pairs={{16,0},{9,1},{18,2},{11,3},{20,4},{13,5},{22,6},{15,7},{24,8},{1,9... | collective-permute-start | bytes 1179656 | tf_op jit(solution)/shard_map/ppermute | solution.py:456
  23.5 5.6 %collective-permute-start.4 = (bf16[4,64,256]{2,1,0:T(8,128)(2,1)S(1)}, bf16[4,64,256]{2,1,0:T(8,128)(2,1)S(1)}, u32[]{:S(2)}, u32[]{:S(2)}) collective-permute-start(bf16[4,64,256]{2,1,0:T(8,128)(2,1)S(1)} %collective-permute-done.2.rest_5_), channel_id=1, source_target_pairs={{2,0},{3,1},{0,2},{1,3},{6,4},{7,5},{4,6},{5,7},{10,8},{11,9},{8,1... | collective-permute-start | bytes 393224 | tf_op jit(solution)/shard_map/ppermute | solution.py:456
  29.2 35.1 %slice-start.1 = ((s8[5242880]{0:T(1024)(128)(4,1)}), s8[1048576]{0:T(1024)(128)(4,1)S(1)}, s32[]{:S(2)}) async-start(s8[5242880]{0:T(1024)(128)(4,1)} %bitcast.15), calls=%async_computation.1 | async-start | bytes 2097152
  29.2 35.1 %slice-start.3 = ((s8[5242880]{0:T(1024)(128)(4,1)}), s8[1048576]{0:T(1024)(128)(4,1)S(1)}, s32[]{:S(2)}) async-start(s8[5242880]{0:T(1024)(128)(4,1)} %bitcast.17), calls=%async_computation.3 | async-start | bytes 2097152
  29.2 5.0 %collective-permute-start.9 = (bf16[1,4,64,256]{3,2,1,0:T(8,128)(2,1)S(1)}, bf16[1,4,64,256]{3,2,1,0:T(8,128)(2,1)S(1)}, u32[]{:S(2)}, u32[]{:S(2)}) collective-permute-start(bf16[1,4,64,256]{3,2,1,0:T(8,128)(2,1)S(1)} %bitcast.26), channel_id=1, source_target_pairs={{16,0},{9,1},{18,2},{11,3},{20,4},{13,5},{22,6},{15,7},{24,8},{1,9... | collective-permute-start | bytes 393224 | tf_op jit(solution)/shard_map/ppermute | solution.py:456
  42.2 5.0 %collective-permute-start.12 = (bf16[1,4,64,256]{3,2,1,0:T(8,128)(2,1)S(1)}, bf16[1,4,64,256]{3,2,1,0:T(8,128)(2,1)S(1)}, u32[]{:S(2)}, u32[]{:S(2)}) collective-permute-start(bf16[1,4,64,256]{3,2,1,0:T(8,128)(2,1)S(1)} %get-tuple-element.88), channel_id=1, source_target_pairs={{0,16},{1,9},{2,18},{3,11},{4,20},{5,13},{6,22},{7,15},{8,24},{9,1... | collective-permute-start | bytes 393224 | tf_op jit(solution)/shard_map/ppermute | solution.py:460
  43.1 6.9 %collective-permute-start.11 = (bf16[2,4,64,256]{3,2,1,0:T(8,128)(2,1)S(1)}, bf16[2,4,64,256]{3,2,1,0:T(8,128)(2,1)S(1)}, u32[]{:S(2)}, u32[]{:S(2)}) collective-permute-start(bf16[2,4,64,256]{3,2,1,0:T(8,128)(2,1)S(1)} %get-tuple-element.81), channel_id=1, source_target_pairs={{0,16},{1,9},{2,18},{3,11},{4,20},{5,13},{6,22},{7,15},{8,24},{9,1... | collective-permute-start | bytes 786440 | tf_op jit(solution)/shard_map/ppermute | solution.py:460
  44.3 14.8 %collective-permute-start.10 = (bf16[1,4,64,256]{3,2,1,0:T(8,128)(2,1)S(1)}, bf16[1,4,64,256]{3,2,1,0:T(8,128)(2,1)S(1)}, u32[]{:S(2)}, u32[]{:S(2)}) collective-permute-start(bf16[1,4,64,256]{3,2,1,0:T(8,128)(2,1)S(1)} %get-tuple-element.79), channel_id=1, source_target_pairs={{0,16},{1,9},{2,18},{3,11},{4,20},{5,13},{6,22},{7,15},{8,24},{9,1... | collective-permute-start | bytes 393224 | tf_op jit(solution)/shard_map/ppermute | solution.py:460
  47.2 5.0 %collective-permute-start.13 = (bf16[4,64,256]{2,1,0:T(8,128)(2,1)S(1)}, bf16[4,64,256]{2,1,0:T(8,128)(2,1)S(1)}, u32[]{:S(2)}, u32[]{:S(2)}) collective-permute-start(bf16[4,64,256]{2,1,0:T(8,128)(2,1)S(1)} %fusion.2), channel_id=1, source_target_pairs={{0,2},{1,3},{2,0},{3,1},{4,6},{5,7},{6,4},{7,5},{8,10},{9,11},{10,... | collective-permute-start | bytes 393224 | tf_op jit(solution)/shard_map/ppermute | solution.py:460
  50.0 5.7 %collective-permute-start.16 = (bf16[128,896]{1,0:T(8,128)(2,1)S(1)}, bf16[128,896]{1,0:T(8,128)(2,1)S(1)}, u32[]{:S(2)}, u32[]{:S(2)}) collective-permute-start(bf16[128,896]{1,0:T(8,128)(2,1)S(1)} %get-tuple-element.93), channel_id=1, source_target_pairs={{0,1},{1,0},{2,3},{3,2},{4,5},{5,4},{6,7},{7,6},{8,9},{9,8},{10,11... | collective-permute-start | bytes 688136 | tf_op jit(solution)/shard_map/ppermute | solution.py:460
  50.0 7.7 %collective-permute-start.17 = (bf16[128,896]{1,0:T(8,128)(2,1)S(1)}, bf16[128,896]{1,0:T(8,128)(2,1)S(1)}, u32[]{:S(2)}, u32[]{:S(2)}) collective-permute-start(bf16[128,896]{1,0:T(8,128)(2,1)S(1)} %get-tuple-element.94), channel_id=1, source_target_pairs={{0,8},{1,17},{2,10},{3,19},{4,12},{5,21},{6,14},{7,23},{8,0},{9,25... | collective-permute-start | bytes 688136 | tf_op jit(solution)/shard_map/ppermute | solution.py:460
  51.0 7.1 %collective-permute-start.18 = (bf16[128,896]{1,0:T(8,128)(2,1)S(1)}, bf16[128,896]{1,0:T(8,128)(2,1)S(1)}, u32[]{:S(2)}, u32[]{:S(2)}) collective-permute-start(bf16[128,896]{1,0:T(8,128)(2,1)S(1)} %get-tuple-element.95), channel_id=1, source_target_pairs={{0,9},{1,16},{2,11},{3,18},{4,13},{5,20},{6,15},{7,22},{8,1},{9,24... | collective-permute-start | bytes 688136 | tf_op jit(solution)/shard_map/ppermute | solution.py:460
  52.3 10.3 %collective-permute-start.15 = (bf16[4,64,256]{2,1,0:T(8,128)(2,1)S(1)}, bf16[4,64,256]{2,1,0:T(8,128)(2,1)S(1)}, u32[]{:S(2)}, u32[]{:S(2)}) collective-permute-start(bf16[4,64,256]{2,1,0:T(8,128)(2,1)S(1)} %fusion.1), channel_id=1, source_target_pairs={{0,4},{1,5},{2,6},{3,7},{4,0},{5,1},{6,2},{7,3},{8,12},{9,13},{10,... | collective-permute-start | bytes 393224 | tf_op jit(solution)/shard_map/ppermute | solution.py:460
  55.7 6.9 %collective-permute-start.14 = (bf16[4,64,256]{2,1,0:T(8,128)(2,1)S(1)}, bf16[4,64,256]{2,1,0:T(8,128)(2,1)S(1)}, u32[]{:S(2)}, u32[]{:S(2)}) collective-permute-start(bf16[4,64,256]{2,1,0:T(8,128)(2,1)S(1)} %convert_add_fusion.2), channel_id=1, source_target_pairs={{0,2},{1,3},{2,0},{3,1},{4,6},{5,7},{6,4},{7,5},{8,10},{9,11},{10,... | collective-permute-start | bytes 393224 | tf_op jit(solution)/shard_map/ppermute | solution.py:460
  62.7 1.5 %collective-permute-start.21 = (bf16[64,256]{1,0:T(8,128)(2,1)S(1)}, bf16[64,256]{1,0:T(8,128)(2,1)S(1)}, u32[]{:S(2)}, u32[]{:S(2)}) collective-permute-start(bf16[64,256]{1,0:T(8,128)(2,1)S(1)} %get-tuple-element.109), channel_id=1, source_target_pairs={{0,1},{1,0},{2,3},{3,2},{4,5},{5,4},{6,7},{7,6},{8,9},{9,8},{10,11... | collective-permute-start | bytes 98312 | tf_op jit(solution)/shard_map/ppermute | solution.py:460
  62.8 4.0 %collective-permute-start.19 = (bf16[64,256]{1,0:T(8,128)(2,1)S(1)}, bf16[64,256]{1,0:T(8,128)(2,1)S(1)}, u32[]{:S(2)}, u32[]{:S(2)}) collective-permute-start(bf16[64,256]{1,0:T(8,128)(2,1)S(1)} %get-tuple-element.106), channel_id=1, source_target_pairs={{0,8},{1,17},{2,10},{3,19},{4,12},{5,21},{6,14},{7,23},{8,0},{9,25... | collective-permute-start | bytes 98312 | tf_op jit(solution)/shard_map/ppermute | solution.py:460
  63.1 3.6 %collective-permute-start.20 = (bf16[64,256]{1,0:T(8,128)(2,1)S(1)}, bf16[64,256]{1,0:T(8,128)(2,1)S(1)}, u32[]{:S(2)}, u32[]{:S(2)}) collective-permute-start(bf16[64,256]{1,0:T(8,128)(2,1)S(1)} %get-tuple-element.107), channel_id=1, source_target_pairs={{0,9},{1,16},{2,11},{3,18},{4,13},{5,20},{6,15},{7,22},{8,1},{9,24... | collective-permute-start | bytes 98312 | tf_op jit(solution)/shard_map/ppermute | solution.py:460
  (8 other events, 92.8 us)

commit v15 on v14

--- a/solution.py
+++ b/solution.py
@@ -71,14 +71,14 @@
                     sems.at[len(copies)],
                 )
             )
-    for copy in copies[:8]:
+    for copy in copies[:12]:
         copy.start()
     total = None
     for step in range(steps):
         span = slice(step * chunk, (step + 1) * chunk)
         copies[2 * step].wait()
         copies[2 * step + 1].wait()
-        for copy in copies[2 * step + 8 : 2 * step + 10]:
+        for copy in copies[2 * step + 12 : 2 * step + 14]:
             copy.start()
         product = dot(x_ref[:, span], weights[span, :], 1, 0)
         total = product if step == 0 else total + product
@@ -499,10 +499,12 @@
     )
 
     sums = dict(zip(offsets, sums))
+    grads = list(grads)
     far = give(back_stacks[2], 1 << Y)
     middle = give(back_stacks[1], 1 << Y)
     near = give(back_stacks[0], 1 << Y)
-    middle, grads = lax.optimization_barrier((middle, grads))
+    far, grads[1] = lax.optimization_barrier((far, grads[1]))
+    middle, grads[2:] = lax.optimization_barrier((middle, grads[2:]))
     back = [grads[0]] + [give(grads[j], MEMBERS[j]) for j in range(1, len(MEMBERS))]
     arrived = {offset: [middle[index]] for index, offset in enumerate(offsets[1:-1])}
     arrived.update({offsets[0]: [near[0]], offsets[-1]: [far[0]]})

time: 70 us -> 71 us (1.014)
  waiting for transfers between devices: 20.4 us -> 22.9 us
    ppermute x12, waiting for transfers between devices: 8.37 us -> 10.8 us  [give(): return lax.ppermute(x, ('prompt', 'resp'), pairs)]
    pallas_call x1, Pallas kernels: 3.83 us -> 3.11 us  [project(): pl.pallas_call(functools.partial(project_kernel, steps), out_shape=[jax.S...]
  transfers between devices with their start and end apart: 22 -> 22, of which waited for: 13 -> 12; matrix products, arithmetic and copies ran while one was open for 0% -> 0% of each run, Pallas kernels for 10% -> 9%
where the time goes in v15:
time: 71 us; the launch traced here: 70.8 us
  starting transfers between devices  27.2 us (38%)
  waiting for transfers between devices  22.9 us (32%)
  Pallas kernels  17.8 us (25%)
  between operations  1.67 us (2%)
  local copies, waits for them, and re-layouts  1.13 us (2%)
    ppermute x10, starting transfers between devices, fetch(): return lax.ppermute(x, ('prompt', 'resp'), pairs)  13.9 us
    ppermute x12, starting transfers between devices, give(): return lax.ppermute(x, ('prompt', 'resp'), pairs)  13.3 us
    ppermute x10, waiting for transfers between devices, fetch(): return lax.ppermute(x, ('prompt', 'resp'), pairs)  12.1 us
    ppermute x12, waiting for transfers between devices, give(): return lax.ppermute(x, ('prompt', 'resp'), pairs)  10.8 us
    pallas_call x1, Pallas kernels, attend(): pl.pallas_call(functools.partial(attend_kernel, slots, group, rows, resp_...  7.97 us
    pallas_call x2, Pallas kernels, prompt_gradient(): pl.pallas_call(functools.partial(prompt_kernel, chunk, members, first), o...  3.81 us
    pallas_call x1, Pallas kernels, project(): pl.pallas_call(functools.partial(project_kernel, steps), out_shape=[jax.S...  3.11 us
  transfers between devices with their start and end apart: 22, of which 12 were waited for; matrix products, arithmetic and copies ran while one was open for 0% of the time, Pallas kernels for 9%

profile of v15, /device:TPU:0, one launch (start us, length us, event | category | flops | bytes accessed | tf_op | source)
XLA Modules:
  0.0 70.8 jit_solution(14678859678904516289)
XLA Ops:
  1.1 1.1 %copy-done.2 = bf16[64,5120]{1,0:T(8,128)(2,1)S(1)} copy-done((bf16[64,5120]{1,0:T(8,128)(2,1)S(1)}, bf16[64,5120]{1,0:T(8,128)(2,1)}, u32[]{:S(2)}) %copy-start.2) | copy-done | bytes 655384
  2.2 3.1 %project_own.1 = (bf16[64,512]{1,0:T(8,128)(2,1)S(1)}, bf16[5120,512]{1,0:T(8,128)(2,1)S(1)}) custom-call(bf16[64,5120]{1,0:T(8,128)(2,1)S(1)} %copy-done.2, bf16[5120,512]{1,0:T(8,128)(2,1)} %rest_2_.3, bf16[5120,512]{1,0:T(8,128)(2,1)} %rest_3_.3), custom_call_target="tpu_custom_call" | custom-call | flops 335544320 | bytes 5898240 | tf_op jit(solution)/shard_map/project_own/pallas_call | solution.py:91
  6.5 2.6 %collective-permute-start.1 = (bf16[128,256]{1,0:T(8,128)(2,1)S(1)}, bf16[128,256]{1,0:T(8,128)(2,1)S(1)}, u32[]{:S(2)}, u32[]{:S(2)}) collective-permute-start(bf16[128,256]{1,0:T(8,128)(2,1)S(1)} %get-tuple-element.61), channel_id=1, source_target_pairs={{8,0},{17,1},{10,2},{19,3},{12,4},{21,5},{14,6},{23,7},{0,8},{25,9... | collective-permute-start | bytes 196616 | tf_op jit(solution)/shard_map/ppermute | solution.py:456
  11.3 2.1 %collective-permute-start.3 = (bf16[1552,128]{1,0:T(8,128)(2,1)S(1)}, bf16[1552,128]{1,0:T(8,128)(2,1)S(1)}, u32[]{:S(2)}, u32[]{:S(2)}) collective-permute-start(bf16[1552,128]{1,0:T(8,128)(2,1)S(1)} %get-tuple-element.68), channel_id=1, source_target_pairs={{8,0},{17,1},{10,2},{19,3},{12,4},{21,5},{14,6},{23,7},{0,8},{25,9... | collective-permute-start | bytes 1191944 | tf_op jit(solution)/shard_map/ppermute | solution.py:456
  13.4 2.6 %collective-permute-start.2 = (bf16[4,64,256]{2,1,0:T(8,128)(2,1)S(1)}, bf16[4,64,256]{2,1,0:T(8,128)(2,1)S(1)}, u32[]{:S(2)}, u32[]{:S(2)}) collective-permute-start(bf16[4,64,256]{2,1,0:T(8,128)(2,1)S(1)} %bitcast.19), channel_id=1, source_target_pairs={{4,0},{5,1},{6,2},{7,3},{0,4},{1,5},{2,6},{3,7},{12,8},{13,9},{14,... | collective-permute-start | bytes 393224 | tf_op jit(solution)/shard_map/ppermute | solution.py:456
  16.0 1.6 %collective-permute-start.7 = (bf16[4,64,256]{2,1,0:T(8,128)(2,1)S(1)}, bf16[4,64,256]{2,1,0:T(8,128)(2,1)S(1)}, u32[]{:S(2)}, u32[]{:S(2)}) collective-permute-start(bf16[4,64,256]{2,1,0:T(8,128)(2,1)S(1)} %bitcast.20), channel_id=1, source_target_pairs={{2,0},{3,1},{0,2},{1,3},{6,4},{7,5},{4,6},{5,7},{10,8},{11,9},{8,1... | collective-permute-start | bytes 393224 | tf_op jit(solution)/shard_map/ppermute | solution.py:456
  17.5 1.6 %collective-permute-start.6 = (bf16[1552,128]{1,0:T(8,128)(2,1)S(1)}, bf16[1552,128]{1,0:T(8,128)(2,1)S(1)}, u32[]{:S(2)}, u32[]{:S(2)}) collective-permute-start(bf16[1552,128]{1,0:T(8,128)(2,1)S(1)} %get-tuple-element.73), channel_id=1, source_target_pairs={{9,0},{16,1},{11,2},{18,3},{13,4},{20,5},{15,6},{22,7},{1,8},{24,9... | collective-permute-start | bytes 1191944 | tf_op jit(solution)/shard_map/ppermute | solution.py:456
  19.2 2.7 %collective-permute-done.2.rest_5_ = bf16[4,64,256]{2,1,0:T(8,128)(2,1)S(1)} collective-permute-done((bf16[4,64,256]{2,1,0:T(8,128)(2,1)S(1)}, bf16[4,64,256]{2,1,0:T(8,128)(2,1)S(1)}, u32[]{:S(2)}, u32[]{:S(2)}) %collective-permute-start.2) | collective-permute-done | bytes 131104 | tf_op jit(solution)/shard_map/ppermute | solution.py:456
  22.8 1.4 %collective-permute-start.4 = (bf16[4,64,256]{2,1,0:T(8,128)(2,1)S(1)}, bf16[4,64,256]{2,1,0:T(8,128)(2,1)S(1)}, u32[]{:S(2)}, u32[]{:S(2)}) collective-permute-start(bf16[4,64,256]{2,1,0:T(8,128)(2,1)S(1)} %collective-permute-done.2.rest_5_), channel_id=1, source_target_pairs={{2,0},{3,1},{0,2},{1,3},{6,4},{7,5},{4,6},{5,7},{10,8},{11,9},{8,1... | collective-permute-start | bytes 393224 | tf_op jit(solution)/shard_map/ppermute | solution.py:456
  24.8 3.6 %collective-permute-done.4.rest_7_ = bf16[4,64,256]{2,1,0:T(8,128)(2,1)S(1)} collective-permute-done((bf16[4,64,256]{2,1,0:T(8,128)(2,1)S(1)}, bf16[4,64,256]{2,1,0:T(8,128)(2,1)S(1)}, u32[]{:S(2)}, u32[]{:S(2)}) %collective-permute-start.4) | collective-permute-done | bytes 131104 | tf_op jit(solution)/shard_map/ppermute | solution.py:456
  29.4 4.1 %collective-permute-done.9.rest_9_ = bf16[1,4,64,256]{3,2,1,0:T(8,128)(2,1)S(1)} collective-permute-done((bf16[1,4,64,256]{3,2,1,0:T(8,128)(2,1)S(1)}, bf16[1,4,64,256]{3,2,1,0:T(8,128)(2,1)S(1)}, u32[]{:S(2)}, u32[]{:S(2)}) %collective-permute-start.9) | collective-permute-done | bytes 131104 | tf_op jit(solution)/shard_map/ppermute | solution.py:456
  33.5 8.0 %attend_head.1 = (bf16[128,896]{1,0:T(8,128)(2,1)S(1)}, bf16[128,896]{1,0:T(8,128)(2,1)S(1)}, bf16[128,896]{1,0:T(8,128)(2,1)S(1)}, bf16[128,896]{1,0:T(8,128)(2...) custom-call(bf16[1552,128]{1,0:T(8,128)(2,1)S(1)} %get-tuple-element, ...), custom_call_target="tpu_custom_call" | custom-call | flops 4194304000 | bytes 16777216 | tf_op jit(solution)/shard_map/attend_head/pallas_call | solution.py:348
  42.4 1.2 %collective-permute-start.11 = (bf16[2,4,64,256]{3,2,1,0:T(8,128)(2,1)S(1)}, bf16[2,4,64,256]{3,2,1,0:T(8,128)(2,1)S(1)}, u32[]{:S(2)}, u32[]{:S(2)}) collective-permute-start(bf16[2,4,64,256]{3,2,1,0:T(8,128)(2,1)S(1)} %get-tuple-element.81), channel_id=1, source_target_pairs={{0,16},{1,9},{2,18},{3,11},{4,20},{5,13},{6,22},{7,15},{8,24},{9,1... | collective-permute-start | bytes 786440 | tf_op jit(solution)/shard_map/ppermute | solution.py:460
  44.4 2.1 %collective-permute-done.12 = bf16[1,4,64,256]{3,2,1,0:T(8,128)(2,1)S(1)} collective-permute-done((bf16[1,4,64,256]{3,2,1,0:T(8,128)(2,1)S(1)}, bf16[1,4,64,256]{3,2,1,0:T(8,128)(2,1)S(1)}, u32[]{:S(2)}, u32[]{:S(2)}) %collective-permute-start.12) | collective-permute-done | bytes 131104 | tf_op jit(solution)/shard_map/ppermute | solution.py:460
  46.5 1.5 %collective-permute-start.13 = (bf16[4,64,256]{2,1,0:T(8,128)(2,1)S(1)}, bf16[4,64,256]{2,1,0:T(8,128)(2,1)S(1)}, u32[]{:S(2)}, u32[]{:S(2)}) collective-permute-start(bf16[4,64,256]{2,1,0:T(8,128)(2,1)S(1)} %fusion.2), channel_id=1, source_target_pairs={{0,2},{1,3},{2,0},{3,1},{4,6},{5,7},{6,4},{7,5},{8,10},{9,11},{10,... | collective-permute-start | bytes 393224 | tf_op jit(solution)/shard_map/ppermute | solution.py:460
  48.0 1.3 %collective-permute-done.11 = bf16[2,4,64,256]{3,2,1,0:T(8,128)(2,1)S(1)} collective-permute-done((bf16[2,4,64,256]{3,2,1,0:T(8,128)(2,1)S(1)}, bf16[2,4,64,256]{3,2,1,0:T(8,128)(2,1)S(1)}, u32[]{:S(2)}, u32[]{:S(2)}) %collective-permute-start.11) | collective-permute-done | bytes 262176 | tf_op jit(solution)/shard_map/ppermute | solution.py:460
  50.3 2.2 %collective-permute-done.13 = bf16[4,64,256]{2,1,0:T(8,128)(2,1)S(1)} collective-permute-done((bf16[4,64,256]{2,1,0:T(8,128)(2,1)S(1)}, bf16[4,64,256]{2,1,0:T(8,128)(2,1)S(1)}, u32[]{:S(2)}, u32[]{:S(2)}) %collective-permute-start.13) | collective-permute-done | bytes 131104 | tf_op jit(solution)/shard_map/ppermute | solution.py:460
  52.6 2.9 %collective-permute-start.15 = (bf16[4,64,256]{2,1,0:T(8,128)(2,1)S(1)}, bf16[4,64,256]{2,1,0:T(8,128)(2,1)S(1)}, u32[]{:S(2)}, u32[]{:S(2)}) collective-permute-start(bf16[4,64,256]{2,1,0:T(8,128)(2,1)S(1)} %fusion.1), channel_id=1, source_target_pairs={{0,4},{1,5},{2,6},{3,7},{4,0},{5,1},{6,2},{7,3},{8,12},{9,13},{10,... | collective-permute-start | bytes 393224 | tf_op jit(solution)/shard_map/ppermute | solution.py:460
  55.5 1.7 %collective-permute-start.14 = (bf16[4,64,256]{2,1,0:T(8,128)(2,1)S(1)}, bf16[4,64,256]{2,1,0:T(8,128)(2,1)S(1)}, u32[]{:S(2)}, u32[]{:S(2)}) collective-permute-start(bf16[4,64,256]{2,1,0:T(8,128)(2,1)S(1)} %convert_add_fusion.2), channel_id=1, source_target_pairs={{0,2},{1,3},{2,0},{3,1},{4,6},{5,7},{6,4},{7,5},{8,10},{9,11},{10,... | collective-permute-start | bytes 393224 | tf_op jit(solution)/shard_map/ppermute | solution.py:460
  58.2 3.7 %collective-permute-done.15.rest_2_ = bf16[4,64,256]{2,1,0:T(8,128)(2,1)S(1)} collective-permute-done((bf16[4,64,256]{2,1,0:T(8,128)(2,1)S(1)}, bf16[4,64,256]{2,1,0:T(8,128)(2,1)S(1)}, u32[]{:S(2)}, u32[]{:S(2)}) %collective-permute-start.15) | collective-permute-done | bytes 131104 | tf_op jit(solution)/shard_map/ppermute | solution.py:460
  62.2 2.7 %collective-permute-start.19 = (bf16[64,256]{1,0:T(8,128)(2,1)S(1)}, bf16[64,256]{1,0:T(8,128)(2,1)S(1)}, u32[]{:S(2)}, u32[]{:S(2)}) collective-permute-start(bf16[64,256]{1,0:T(8,128)(2,1)S(1)} %get-tuple-element.106), channel_id=1, source_target_pairs={{0,8},{1,17},{2,10},{3,19},{4,12},{5,21},{6,14},{7,23},{8,0},{9,25... | collective-permute-start | bytes 98312 | tf_op jit(solution)/shard_map/ppermute | solution.py:460
  65.4 1.5 %prompt_gradient.2.rest_4_ = f32[5120,64]{1,0:T(8,128)S(1)} custom-call(bf16[64,256]{1,0:T(8,128)(2,1)S(1)} %get-tuple-element.108.rest_0_, bf16[64,256]{1,0:T(8,128)(2,1)S(1)} %collective-permute-done.21.rest_1_, bf16[5120,512]{1,0:T(8,128)(2,1)S(1)} %bitcast.16, bf16[5120,512]{1,0:T(8,128)(2,1)S(1)} %bitcast.18), custom_call_target="tpu_custom_call" | custom-call | flops 335544320 | bytes 5898240 | tf_op jit(solution)/shard_map/prompt_gradient/pallas_call | solution.py:421
  66.9 1.4 %collective-permute-done.20.rest_1_ = bf16[64,256]{1,0:T(8,128)(2,1)S(1)} collective-permute-done((bf16[64,256]{1,0:T(8,128)(2,1)S(1)}, bf16[64,256]{1,0:T(8,128)(2,1)S(1)}, u32[]{:S(2)}, u32[]{:S(2)}) %collective-permute-start.20) | collective-permute-done | bytes 32800 | tf_op jit(solution)/shard_map/ppermute | solution.py:460
  68.3 2.3 %prompt_gradient.3 = bf16[64,5120]{1,0:T(8,128)(2,1)} custom-call(bf16[64,256]{1,0:T(8,128)(2,1)S(1)} %collective-permute-done.19.rest_0_, bf16[64,256]{1,0:T(8,128)(2,1)S(1)} %collective-permute-done.20.rest_1_, bf16[5120,512]{1,0:T(8,128)(2,1)S(1)} %bitcast.16, bf16[5120,512]{1,0:T(8,128)(2,1)S(1)} %bitcast.18, f32[5120,64]{1,0:T(8,128)S(1)} %prompt_gradient.2.rest_4_), custom_call_target="tpu_custom_call" | custom-call | flops 335544320 | bytes 5898240 | tf_op jit(solution)/shard_map/prompt_gradient/pallas_call | solution.py:421
  (55 shorter events, 10.0 us)
Async XLA Ops:
  0.6 4.8 %collective-permute-start = (bf16[64,5120]{1,0:T(8,128)(2,1)}, bf16[64,5120]{1,0:T(8,128)(2,1)S(1)}, u32[]{:S(2)}, u32[]{:S(2)}) collective-permute-start(bf16[64,5120]{1,0:T(8,128)(2,1)} %x_ref.1), channel_id=1, source_target_pairs={{1,0},{0,1},{3,2},{2,3},{5,4},{4,5},{7,6},{6,7},{9,8},{8,9},{11,10... | collective-permute-start | bytes 1966088 | tf_op jit(solution)/shard_map/ppermute | solution.py:456
  6.5 4.8 %collective-permute-start.1 = (bf16[128,256]{1,0:T(8,128)(2,1)S(1)}, bf16[128,256]{1,0:T(8,128)(2,1)S(1)}, u32[]{:S(2)}, u32[]{:S(2)}) collective-permute-start(bf16[128,256]{1,0:T(8,128)(2,1)S(1)} %get-tuple-element.61), channel_id=1, source_target_pairs={{8,0},{17,1},{10,2},{19,3},{12,4},{21,5},{14,6},{23,7},{0,8},{25,9... | collective-permute-start | bytes 196616 | tf_op jit(solution)/shard_map/ppermute | solution.py:456
  11.3 10.6 %collective-permute-start.3 = (bf16[1552,128]{1,0:T(8,128)(2,1)S(1)}, bf16[1552,128]{1,0:T(8,128)(2,1)S(1)}, u32[]{:S(2)}, u32[]{:S(2)}) collective-permute-start(bf16[1552,128]{1,0:T(8,128)(2,1)S(1)} %get-tuple-element.68), channel_id=1, source_target_pairs={{8,0},{17,1},{10,2},{19,3},{12,4},{21,5},{14,6},{23,7},{0,8},{25,9... | collective-permute-start | bytes 1191944 | tf_op jit(solution)/shard_map/ppermute | solution.py:456
  13.4 8.5 %collective-permute-start.2 = (bf16[4,64,256]{2,1,0:T(8,128)(2,1)S(1)}, bf16[4,64,256]{2,1,0:T(8,128)(2,1)S(1)}, u32[]{:S(2)}, u32[]{:S(2)}) collective-permute-start(bf16[4,64,256]{2,1,0:T(8,128)(2,1)S(1)} %bitcast.19), channel_id=1, source_target_pairs={{4,0},{5,1},{6,2},{7,3},{0,4},{1,5},{2,6},{3,7},{12,8},{13,9},{14,... | collective-permute-start | bytes 393224 | tf_op jit(solution)/shard_map/ppermute | solution.py:456
  16.0 6.2 %collective-permute-start.7 = (bf16[4,64,256]{2,1,0:T(8,128)(2,1)S(1)}, bf16[4,64,256]{2,1,0:T(8,128)(2,1)S(1)}, u32[]{:S(2)}, u32[]{:S(2)}) collective-permute-start(bf16[4,64,256]{2,1,0:T(8,128)(2,1)S(1)} %bitcast.20), channel_id=1, source_target_pairs={{2,0},{3,1},{0,2},{1,3},{6,4},{7,5},{4,6},{5,7},{10,8},{11,9},{8,1... | collective-permute-start | bytes 393224 | tf_op jit(solution)/shard_map/ppermute | solution.py:456
  17.5 6.7 %collective-permute-start.5 = (bf16[1552,128]{1,0:T(8,128)(2,1)S(1)}, bf16[1552,128]{1,0:T(8,128)(2,1)S(1)}, u32[]{:S(2)}, u32[]{:S(2)}) collective-permute-start(bf16[1552,128]{1,0:T(8,128)(2,1)S(1)} %get-tuple-element.71), channel_id=1, source_target_pairs={{1,0},{0,1},{3,2},{2,3},{5,4},{4,5},{7,6},{6,7},{9,8},{8,9},{11,10... | collective-permute-start | bytes 1191944 | tf_op jit(solution)/shard_map/ppermute | solution.py:456
  17.5 7.2 %collective-permute-start.6 = (bf16[1552,128]{1,0:T(8,128)(2,1)S(1)}, bf16[1552,128]{1,0:T(8,128)(2,1)S(1)}, u32[]{:S(2)}, u32[]{:S(2)}) collective-permute-start(bf16[1552,128]{1,0:T(8,128)(2,1)S(1)} %get-tuple-element.73), channel_id=1, source_target_pairs={{9,0},{16,1},{11,2},{18,3},{13,4},{20,5},{15,6},{22,7},{1,8},{24,9... | collective-permute-start | bytes 1191944 | tf_op jit(solution)/shard_map/ppermute | solution.py:456
  22.2 11.3 %collective-permute-start.8 = (bf16[3,4,64,256]{3,2,1,0:T(8,128)(2,1)S(1)}, bf16[3,4,64,256]{3,2,1,0:T(8,128)(2,1)S(1)}, u32[]{:S(2)}, u32[]{:S(2)}) collective-permute-start(bf16[3,4,64,256]{3,2,1,0:T(8,128)(2,1)S(1)} %pad_maximum_fusion), channel_id=1, source_target_pairs={{16,0},{9,1},{18,2},{11,3},{20,4},{13,5},{22,6},{15,7},{24,8},{1,9... | collective-permute-start | bytes 1179656 | tf_op jit(solution)/shard_map/ppermute | solution.py:456
  22.8 5.6 %collective-permute-start.4 = (bf16[4,64,256]{2,1,0:T(8,128)(2,1)S(1)}, bf16[4,64,256]{2,1,0:T(8,128)(2,1)S(1)}, u32[]{:S(2)}, u32[]{:S(2)}) collective-permute-start(bf16[4,64,256]{2,1,0:T(8,128)(2,1)S(1)} %collective-permute-done.2.rest_5_), channel_id=1, source_target_pairs={{2,0},{3,1},{0,2},{1,3},{6,4},{7,5},{4,6},{5,7},{10,8},{11,9},{8,1... | collective-permute-start | bytes 393224 | tf_op jit(solution)/shard_map/ppermute | solution.py:456
  28.4 36.9 %slice-start.1 = ((s8[5242880]{0:T(1024)(128)(4,1)}), s8[1048576]{0:T(1024)(128)(4,1)S(1)}, s32[]{:S(2)}) async-start(s8[5242880]{0:T(1024)(128)(4,1)} %bitcast.15), calls=%async_computation.1 | async-start | bytes 2097152
  28.4 36.9 %slice-start.3 = ((s8[5242880]{0:T(1024)(128)(4,1)}), s8[1048576]{0:T(1024)(128)(4,1)S(1)}, s32[]{:S(2)}) async-start(s8[5242880]{0:T(1024)(128)(4,1)} %bitcast.17), calls=%async_computation.3 | async-start | bytes 2097152
  28.4 5.0 %collective-permute-start.9 = (bf16[1,4,64,256]{3,2,1,0:T(8,128)(2,1)S(1)}, bf16[1,4,64,256]{3,2,1,0:T(8,128)(2,1)S(1)}, u32[]{:S(2)}, u32[]{:S(2)}) collective-permute-start(bf16[1,4,64,256]{3,2,1,0:T(8,128)(2,1)S(1)} %bitcast.26), channel_id=1, source_target_pairs={{16,0},{9,1},{18,2},{11,3},{20,4},{13,5},{22,6},{15,7},{24,8},{1,9... | collective-permute-start | bytes 393224 | tf_op jit(solution)/shard_map/ppermute | solution.py:456
  41.5 5.0 %collective-permute-start.12 = (bf16[1,4,64,256]{3,2,1,0:T(8,128)(2,1)S(1)}, bf16[1,4,64,256]{3,2,1,0:T(8,128)(2,1)S(1)}, u32[]{:S(2)}, u32[]{:S(2)}) collective-permute-start(bf16[1,4,64,256]{3,2,1,0:T(8,128)(2,1)S(1)} %get-tuple-element.86), channel_id=1, source_target_pairs={{0,16},{1,9},{2,18},{3,11},{4,20},{5,13},{6,22},{7,15},{8,24},{9,1... | collective-permute-start | bytes 393224 | tf_op jit(solution)/shard_map/ppermute | solution.py:460
  42.4 6.9 %collective-permute-start.11 = (bf16[2,4,64,256]{3,2,1,0:T(8,128)(2,1)S(1)}, bf16[2,4,64,256]{3,2,1,0:T(8,128)(2,1)S(1)}, u32[]{:S(2)}, u32[]{:S(2)}) collective-permute-start(bf16[2,4,64,256]{3,2,1,0:T(8,128)(2,1)S(1)} %get-tuple-element.81), channel_id=1, source_target_pairs={{0,16},{1,9},{2,18},{3,11},{4,20},{5,13},{6,22},{7,15},{8,24},{9,1... | collective-permute-start | bytes 786440 | tf_op jit(solution)/shard_map/ppermute | solution.py:460
  43.6 14.7 %collective-permute-start.10 = (bf16[1,4,64,256]{3,2,1,0:T(8,128)(2,1)S(1)}, bf16[1,4,64,256]{3,2,1,0:T(8,128)(2,1)S(1)}, u32[]{:S(2)}, u32[]{:S(2)}) collective-permute-start(bf16[1,4,64,256]{3,2,1,0:T(8,128)(2,1)S(1)} %get-tuple-element.79), channel_id=1, source_target_pairs={{0,16},{1,9},{2,18},{3,11},{4,20},{5,13},{6,22},{7,15},{8,24},{9,1... | collective-permute-start | bytes 393224 | tf_op jit(solution)/shard_map/ppermute | solution.py:460
  46.5 9.0 %collective-permute-start.16 = (bf16[128,896]{1,0:T(8,128)(2,1)S(1)}, bf16[128,896]{1,0:T(8,128)(2,1)S(1)}, u32[]{:S(2)}, u32[]{:S(2)}) collective-permute-start(bf16[128,896]{1,0:T(8,128)(2,1)S(1)} %get-tuple-element.93), channel_id=1, source_target_pairs={{0,1},{1,0},{2,3},{3,2},{4,5},{5,4},{6,7},{7,6},{8,9},{9,8},{10,11... | collective-permute-start | bytes 688136 | tf_op jit(solution)/shard_map/ppermute | solution.py:460
  46.5 6.0 %collective-permute-start.13 = (bf16[4,64,256]{2,1,0:T(8,128)(2,1)S(1)}, bf16[4,64,256]{2,1,0:T(8,128)(2,1)S(1)}, u32[]{:S(2)}, u32[]{:S(2)}) collective-permute-start(bf16[4,64,256]{2,1,0:T(8,128)(2,1)S(1)} %fusion.2), channel_id=1, source_target_pairs={{0,2},{1,3},{2,0},{3,1},{4,6},{5,7},{6,4},{7,5},{8,10},{9,11},{10,... | collective-permute-start | bytes 393224 | tf_op jit(solution)/shard_map/ppermute | solution.py:460
  49.3 7.9 %collective-permute-start.17 = (bf16[128,896]{1,0:T(8,128)(2,1)S(1)}, bf16[128,896]{1,0:T(8,128)(2,1)S(1)}, u32[]{:S(2)}, u32[]{:S(2)}) collective-permute-start(bf16[128,896]{1,0:T(8,128)(2,1)S(1)} %get-tuple-element.94), channel_id=1, source_target_pairs={{0,8},{1,17},{2,10},{3,19},{4,12},{5,21},{6,14},{7,23},{8,0},{9,25... | collective-permute-start | bytes 688136 | tf_op jit(solution)/shard_map/ppermute | solution.py:460
  50.2 7.0 %collective-permute-start.18 = (bf16[128,896]{1,0:T(8,128)(2,1)S(1)}, bf16[128,896]{1,0:T(8,128)(2,1)S(1)}, u32[]{:S(2)}, u32[]{:S(2)}) collective-permute-start(bf16[128,896]{1,0:T(8,128)(2,1)S(1)} %get-tuple-element.95), channel_id=1, source_target_pairs={{0,9},{1,16},{2,11},{3,18},{4,13},{5,20},{6,15},{7,22},{8,1},{9,24... | collective-permute-start | bytes 688136 | tf_op jit(solution)/shard_map/ppermute | solution.py:460
  52.6 9.4 %collective-permute-start.15 = (bf16[4,64,256]{2,1,0:T(8,128)(2,1)S(1)}, bf16[4,64,256]{2,1,0:T(8,128)(2,1)S(1)}, u32[]{:S(2)}, u32[]{:S(2)}) collective-permute-start(bf16[4,64,256]{2,1,0:T(8,128)(2,1)S(1)} %fusion.1), channel_id=1, source_target_pairs={{0,4},{1,5},{2,6},{3,7},{4,0},{5,1},{6,2},{7,3},{8,12},{9,13},{10,... | collective-permute-start | bytes 393224 | tf_op jit(solution)/shard_map/ppermute | solution.py:460
  55.5 6.6 %collective-permute-start.14 = (bf16[4,64,256]{2,1,0:T(8,128)(2,1)S(1)}, bf16[4,64,256]{2,1,0:T(8,128)(2,1)S(1)}, u32[]{:S(2)}, u32[]{:S(2)}) collective-permute-start(bf16[4,64,256]{2,1,0:T(8,128)(2,1)S(1)} %convert_add_fusion.2), channel_id=1, source_target_pairs={{0,2},{1,3},{2,0},{3,1},{4,6},{5,7},{6,4},{7,5},{8,10},{9,11},{10,... | collective-permute-start | bytes 393224 | tf_op jit(solution)/shard_map/ppermute | solution.py:460
  62.1 3.2 %collective-permute-start.21 = (bf16[64,256]{1,0:T(8,128)(2,1)S(1)}, bf16[64,256]{1,0:T(8,128)(2,1)S(1)}, u32[]{:S(2)}, u32[]{:S(2)}) collective-permute-start(bf16[64,256]{1,0:T(8,128)(2,1)S(1)} %get-tuple-element.109), channel_id=1, source_target_pairs={{0,1},{1,0},{2,3},{3,2},{4,5},{5,4},{6,7},{7,6},{8,9},{9,8},{10,11... | collective-permute-start | bytes 98312 | tf_op jit(solution)/shard_map/ppermute | solution.py:460
  62.2 4.7 %collective-permute-start.19 = (bf16[64,256]{1,0:T(8,128)(2,1)S(1)}, bf16[64,256]{1,0:T(8,128)(2,1)S(1)}, u32[]{:S(2)}, u32[]{:S(2)}) collective-permute-start(bf16[64,256]{1,0:T(8,128)(2,1)S(1)} %get-tuple-element.106), channel_id=1, source_target_pairs={{0,8},{1,17},{2,10},{3,19},{4,12},{5,21},{6,14},{7,23},{8,0},{9,25... | collective-permute-start | bytes 98312 | tf_op jit(solution)/shard_map/ppermute | solution.py:460
  64.9 3.3 %collective-permute-start.20 = (bf16[64,256]{1,0:T(8,128)(2,1)S(1)}, bf16[64,256]{1,0:T(8,128)(2,1)S(1)}, u32[]{:S(2)}, u32[]{:S(2)}) collective-permute-start(bf16[64,256]{1,0:T(8,128)(2,1)S(1)} %get-tuple-element.107), channel_id=1, source_target_pairs={{0,9},{1,16},{2,11},{3,18},{4,13},{5,20},{6,15},{7,22},{8,1},{9,24... | collective-permute-start | bytes 98312 | tf_op jit(solution)/shard_map/ppermute | solution.py:460
  (8 other events, 96.6 us)

commit v16 on v15

--- a/solution.py
+++ b/solution.py
@@ -499,12 +499,10 @@
     )
 
     sums = dict(zip(offsets, sums))
-    grads = list(grads)
     far = give(back_stacks[2], 1 << Y)
     middle = give(back_stacks[1], 1 << Y)
     near = give(back_stacks[0], 1 << Y)
-    far, grads[1] = lax.optimization_barrier((far, grads[1]))
-    middle, grads[2:] = lax.optimization_barrier((middle, grads[2:]))
+    middle, grads = lax.optimization_barrier((middle, grads))
     back = [grads[0]] + [give(grads[j], MEMBERS[j]) for j in range(1, len(MEMBERS))]
     arrived = {offset: [middle[index]] for index, offset in enumerate(offsets[1:-1])}
     arrived.update({offsets[0]: [near[0]], offsets[-1]: [far[0]]})

time: 71 us -> 69.2 us (0.975)
  waiting for transfers between devices: 22.9 us -> 20.4 us
    ppermute x12, waiting for transfers between devices: 10.8 us -> 8.37 us  [give(): return lax.ppermute(x, ('prompt', 'resp'), pairs)]
  transfers between devices with their start and end apart: 22 -> 22, of which waited for: 12 -> 13; matrix products, arithmetic and copies ran while one was open for 0% -> 0% of each run, Pallas kernels for 9% -> 9%
where the time goes in v16:
time: 69.2 us; the launch traced here: 68.6 us
  starting transfers between devices  27.4 us (40%)
  waiting for transfers between devices  20.4 us (29%)
  Pallas kernels  17.8 us (26%)
  between operations  1.66 us (2%)
  local copies, waits for them, and re-layouts  1.13 us (2%)
    ppermute x10, starting transfers between devices, fetch(): return lax.ppermute(x, ('prompt', 'resp'), pairs)  13.9 us
    ppermute x12, starting transfers between devices, give(): return lax.ppermute(x, ('prompt', 'resp'), pairs)  13.5 us
    ppermute x10, waiting for transfers between devices, fetch(): return lax.ppermute(x, ('prompt', 'resp'), pairs)  12.1 us
    ppermute x12, waiting for transfers between devices, give(): return lax.ppermute(x, ('prompt', 'resp'), pairs)  8.37 us
    pallas_call x1, Pallas kernels, attend(): pl.pallas_call(functools.partial(attend_kernel, slots, group, rows, resp_...  7.97 us
    pallas_call x2, Pallas kernels, prompt_gradient(): pl.pallas_call(functools.partial(prompt_kernel, chunk, members, first), o...  3.81 us
    pallas_call x1, Pallas kernels, project(): pl.pallas_call(functools.partial(project_kernel, steps), out_shape=[jax.S...  3.11 us
  transfers between devices with their start and end apart: 22, of which 13 were waited for; matrix products, arithmetic and copies ran while one was open for 0% of the time, Pallas kernels for 9%

profile of v16, /device:TPU:0, one launch (start us, length us, event | category | flops | bytes accessed | tf_op | source)
XLA Modules:
  0.0 68.6 jit_solution(2120953033785983149)
XLA Ops:
  1.1 1.1 %copy-done.2 = bf16[64,5120]{1,0:T(8,128)(2,1)S(1)} copy-done((bf16[64,5120]{1,0:T(8,128)(2,1)S(1)}, bf16[64,5120]{1,0:T(8,128)(2,1)}, u32[]{:S(2)}) %copy-start.2) | copy-done | bytes 655384
  2.2 3.1 %project_own.1 = (bf16[64,512]{1,0:T(8,128)(2,1)S(1)}, bf16[5120,512]{1,0:T(8,128)(2,1)S(1)}) custom-call(bf16[64,5120]{1,0:T(8,128)(2,1)S(1)} %copy-done.2, bf16[5120,512]{1,0:T(8,128)(2,1)} %rest_2_.3, bf16[5120,512]{1,0:T(8,128)(2,1)} %rest_3_.3), custom_call_target="tpu_custom_call" | custom-call | flops 335544320 | bytes 5898240 | tf_op jit(solution)/shard_map/project_own/pallas_call | solution.py:91
  6.5 2.6 %collective-permute-start.1 = (bf16[128,256]{1,0:T(8,128)(2,1)S(1)}, bf16[128,256]{1,0:T(8,128)(2,1)S(1)}, u32[]{:S(2)}, u32[]{:S(2)}) collective-permute-start(bf16[128,256]{1,0:T(8,128)(2,1)S(1)} %get-tuple-element.61), channel_id=1, source_target_pairs={{8,0},{17,1},{10,2},{19,3},{12,4},{21,5},{14,6},{23,7},{0,8},{25,9... | collective-permute-start | bytes 196616 | tf_op jit(solution)/shard_map/ppermute | solution.py:456
  11.3 2.1 %collective-permute-start.3 = (bf16[1552,128]{1,0:T(8,128)(2,1)S(1)}, bf16[1552,128]{1,0:T(8,128)(2,1)S(1)}, u32[]{:S(2)}, u32[]{:S(2)}) collective-permute-start(bf16[1552,128]{1,0:T(8,128)(2,1)S(1)} %get-tuple-element.68), channel_id=1, source_target_pairs={{8,0},{17,1},{10,2},{19,3},{12,4},{21,5},{14,6},{23,7},{0,8},{25,9... | collective-permute-start | bytes 1191944 | tf_op jit(solution)/shard_map/ppermute | solution.py:456
  13.4 2.6 %collective-permute-start.2 = (bf16[4,64,256]{2,1,0:T(8,128)(2,1)S(1)}, bf16[4,64,256]{2,1,0:T(8,128)(2,1)S(1)}, u32[]{:S(2)}, u32[]{:S(2)}) collective-permute-start(bf16[4,64,256]{2,1,0:T(8,128)(2,1)S(1)} %bitcast.19), channel_id=1, source_target_pairs={{4,0},{5,1},{6,2},{7,3},{0,4},{1,5},{2,6},{3,7},{12,8},{13,9},{14,... | collective-permute-start | bytes 393224 | tf_op jit(solution)/shard_map/ppermute | solution.py:456
  16.0 1.6 %collective-permute-start.7 = (bf16[4,64,256]{2,1,0:T(8,128)(2,1)S(1)}, bf16[4,64,256]{2,1,0:T(8,128)(2,1)S(1)}, u32[]{:S(2)}, u32[]{:S(2)}) collective-permute-start(bf16[4,64,256]{2,1,0:T(8,128)(2,1)S(1)} %bitcast.20), channel_id=1, source_target_pairs={{2,0},{3,1},{0,2},{1,3},{6,4},{7,5},{4,6},{5,7},{10,8},{11,9},{8,1... | collective-permute-start | bytes 393224 | tf_op jit(solution)/shard_map/ppermute | solution.py:456
  17.5 1.6 %collective-permute-start.6 = (bf16[1552,128]{1,0:T(8,128)(2,1)S(1)}, bf16[1552,128]{1,0:T(8,128)(2,1)S(1)}, u32[]{:S(2)}, u32[]{:S(2)}) collective-permute-start(bf16[1552,128]{1,0:T(8,128)(2,1)S(1)} %get-tuple-element.73), channel_id=1, source_target_pairs={{9,0},{16,1},{11,2},{18,3},{13,4},{20,5},{15,6},{22,7},{1,8},{24,9... | collective-permute-start | bytes 1191944 | tf_op jit(solution)/shard_map/ppermute | solution.py:456
  19.2 2.7 %collective-permute-done.2.rest_5_ = bf16[4,64,256]{2,1,0:T(8,128)(2,1)S(1)} collective-permute-done((bf16[4,64,256]{2,1,0:T(8,128)(2,1)S(1)}, bf16[4,64,256]{2,1,0:T(8,128)(2,1)S(1)}, u32[]{:S(2)}, u32[]{:S(2)}) %collective-permute-start.2) | collective-permute-done | bytes 131104 | tf_op jit(solution)/shard_map/ppermute | solution.py:456
  22.8 1.4 %collective-permute-start.4 = (bf16[4,64,256]{2,1,0:T(8,128)(2,1)S(1)}, bf16[4,64,256]{2,1,0:T(8,128)(2,1)S(1)}, u32[]{:S(2)}, u32[]{:S(2)}) collective-permute-start(bf16[4,64,256]{2,1,0:T(8,128)(2,1)S(1)} %collective-permute-done.2.rest_5_), channel_id=1, source_target_pairs={{2,0},{3,1},{0,2},{1,3},{6,4},{7,5},{4,6},{5,7},{10,8},{11,9},{8,1... | collective-permute-start | bytes 393224 | tf_op jit(solution)/shard_map/ppermute | solution.py:456
  24.8 3.6 %collective-permute-done.4.rest_7_ = bf16[4,64,256]{2,1,0:T(8,128)(2,1)S(1)} collective-permute-done((bf16[4,64,256]{2,1,0:T(8,128)(2,1)S(1)}, bf16[4,64,256]{2,1,0:T(8,128)(2,1)S(1)}, u32[]{:S(2)}, u32[]{:S(2)}) %collective-permute-start.4) | collective-permute-done | bytes 131104 | tf_op jit(solution)/shard_map/ppermute | solution.py:456
  29.4 4.1 %collective-permute-done.9.rest_9_ = bf16[1,4,64,256]{3,2,1,0:T(8,128)(2,1)S(1)} collective-permute-done((bf16[1,4,64,256]{3,2,1,0:T(8,128)(2,1)S(1)}, bf16[1,4,64,256]{3,2,1,0:T(8,128)(2,1)S(1)}, u32[]{:S(2)}, u32[]{:S(2)}) %collective-permute-start.9) | collective-permute-done | bytes 131104 | tf_op jit(solution)/shard_map/ppermute | solution.py:456
  33.5 8.0 %attend_head.1 = (bf16[128,896]{1,0:T(8,128)(2,1)S(1)}, bf16[128,896]{1,0:T(8,128)(2,1)S(1)}, bf16[128,896]{1,0:T(8,128)(2,1)S(1)}, bf16[128,896]{1,0:T(8,128)(2...) custom-call(bf16[1552,128]{1,0:T(8,128)(2,1)S(1)} %get-tuple-element, ...), custom_call_target="tpu_custom_call" | custom-call | flops 4194304000 | bytes 16777216 | tf_op jit(solution)/shard_map/attend_head/pallas_call | solution.py:348
  42.4 1.2 %collective-permute-start.11 = (bf16[2,4,64,256]{3,2,1,0:T(8,128)(2,1)S(1)}, bf16[2,4,64,256]{3,2,1,0:T(8,128)(2,1)S(1)}, u32[]{:S(2)}, u32[]{:S(2)}) collective-permute-start(bf16[2,4,64,256]{3,2,1,0:T(8,128)(2,1)S(1)} %get-tuple-element.81), channel_id=1, source_target_pairs={{0,16},{1,9},{2,18},{3,11},{4,20},{5,13},{6,22},{7,15},{8,24},{9,1... | collective-permute-start | bytes 786440 | tf_op jit(solution)/shard_map/ppermute | solution.py:460
  44.4 2.1 %collective-permute-done.12 = bf16[1,4,64,256]{3,2,1,0:T(8,128)(2,1)S(1)} collective-permute-done((bf16[1,4,64,256]{3,2,1,0:T(8,128)(2,1)S(1)}, bf16[1,4,64,256]{3,2,1,0:T(8,128)(2,1)S(1)}, u32[]{:S(2)}, u32[]{:S(2)}) %collective-permute-start.12) | collective-permute-done | bytes 131104 | tf_op jit(solution)/shard_map/ppermute | solution.py:460
  46.5 1.5 %collective-permute-start.13 = (bf16[4,64,256]{2,1,0:T(8,128)(2,1)S(1)}, bf16[4,64,256]{2,1,0:T(8,128)(2,1)S(1)}, u32[]{:S(2)}, u32[]{:S(2)}) collective-permute-start(bf16[4,64,256]{2,1,0:T(8,128)(2,1)S(1)} %fusion.2), channel_id=1, source_target_pairs={{0,2},{1,3},{2,0},{3,1},{4,6},{5,7},{6,4},{7,5},{8,10},{9,11},{10,... | collective-permute-start | bytes 393224 | tf_op jit(solution)/shard_map/ppermute | solution.py:460
  48.0 1.3 %collective-permute-done.11 = bf16[2,4,64,256]{3,2,1,0:T(8,128)(2,1)S(1)} collective-permute-done((bf16[2,4,64,256]{3,2,1,0:T(8,128)(2,1)S(1)}, bf16[2,4,64,256]{3,2,1,0:T(8,128)(2,1)S(1)}, u32[]{:S(2)}, u32[]{:S(2)}) %collective-permute-start.11) | collective-permute-done | bytes 262176 | tf_op jit(solution)/shard_map/ppermute | solution.py:460
  50.2 1.2 %collective-permute-start.18 = (bf16[128,896]{1,0:T(8,128)(2,1)S(1)}, bf16[128,896]{1,0:T(8,128)(2,1)S(1)}, u32[]{:S(2)}, u32[]{:S(2)}) collective-permute-start(bf16[128,896]{1,0:T(8,128)(2,1)S(1)} %get-tuple-element.95), channel_id=1, source_target_pairs={{0,9},{1,16},{2,11},{3,18},{4,13},{5,20},{6,15},{7,22},{8,1},{9,24... | collective-permute-start | bytes 688136 | tf_op jit(solution)/shard_map/ppermute | solution.py:460
  51.6 3.4 %collective-permute-start.15 = (bf16[4,64,256]{2,1,0:T(8,128)(2,1)S(1)}, bf16[4,64,256]{2,1,0:T(8,128)(2,1)S(1)}, u32[]{:S(2)}, u32[]{:S(2)}) collective-permute-start(bf16[4,64,256]{2,1,0:T(8,128)(2,1)S(1)} %fusion.1), channel_id=1, source_target_pairs={{0,4},{1,5},{2,6},{3,7},{4,0},{5,1},{6,2},{7,3},{8,12},{9,13},{10,... | collective-permute-start | bytes 393224 | tf_op jit(solution)/shard_map/ppermute | solution.py:460
  55.0 2.0 %collective-permute-start.14 = (bf16[4,64,256]{2,1,0:T(8,128)(2,1)S(1)}, bf16[4,64,256]{2,1,0:T(8,128)(2,1)S(1)}, u32[]{:S(2)}, u32[]{:S(2)}) collective-permute-start(bf16[4,64,256]{2,1,0:T(8,128)(2,1)S(1)} %convert_add_fusion.2), channel_id=1, source_target_pairs={{0,2},{1,3},{2,0},{3,1},{4,6},{5,7},{6,4},{7,5},{8,10},{9,11},{10,... | collective-permute-start | bytes 393224 | tf_op jit(solution)/shard_map/ppermute | solution.py:460
  58.3 3.5 %collective-permute-done.15.rest_2_ = bf16[4,64,256]{2,1,0:T(8,128)(2,1)S(1)} collective-permute-done((bf16[4,64,256]{2,1,0:T(8,128)(2,1)S(1)}, bf16[4,64,256]{2,1,0:T(8,128)(2,1)S(1)}, u32[]{:S(2)}, u32[]{:S(2)}) %collective-permute-start.15) | collective-permute-done | bytes 131104 | tf_op jit(solution)/shard_map/ppermute | solution.py:460
  62.4 1.1 %collective-permute-start.20 = (bf16[64,256]{1,0:T(8,128)(2,1)S(1)}, bf16[64,256]{1,0:T(8,128)(2,1)S(1)}, u32[]{:S(2)}, u32[]{:S(2)}) collective-permute-start(bf16[64,256]{1,0:T(8,128)(2,1)S(1)} %get-tuple-element.107), channel_id=1, source_target_pairs={{0,9},{1,16},{2,11},{3,18},{4,13},{5,20},{6,15},{7,22},{8,1},{9,24... | collective-permute-start | bytes 98312 | tf_op jit(solution)/shard_map/ppermute | solution.py:460
  63.5 1.5 %prompt_gradient.2.rest_4_ = f32[5120,64]{1,0:T(8,128)S(1)} custom-call(bf16[64,256]{1,0:T(8,128)(2,1)S(1)} %get-tuple-element.108.rest_0_, bf16[64,256]{1,0:T(8,128)(2,1)S(1)} %collective-permute-done.21.rest_1_, bf16[5120,512]{1,0:T(8,128)(2,1)S(1)} %bitcast.16, bf16[5120,512]{1,0:T(8,128)(2,1)S(1)} %bitcast.18), custom_call_target="tpu_custom_call" | custom-call | flops 335544320 | bytes 5898240 | tf_op jit(solution)/shard_map/prompt_gradient/pallas_call | solution.py:421
  65.0 1.0 %collective-permute-done.19.rest_0_ = bf16[64,256]{1,0:T(8,128)(2,1)S(1)} collective-permute-done((bf16[64,256]{1,0:T(8,128)(2,1)S(1)}, bf16[64,256]{1,0:T(8,128)(2,1)S(1)}, u32[]{:S(2)}, u32[]{:S(2)}) %collective-permute-start.19) | collective-permute-done | bytes 32800 | tf_op jit(solution)/shard_map/ppermute | solution.py:460
  66.1 2.3 %prompt_gradient.3 = bf16[64,5120]{1,0:T(8,128)(2,1)} custom-call(bf16[64,256]{1,0:T(8,128)(2,1)S(1)} %collective-permute-done.19.rest_0_, bf16[64,256]{1,0:T(8,128)(2,1)S(1)} %collective-permute-done.20.rest_1_, bf16[5120,512]{1,0:T(8,128)(2,1)S(1)} %bitcast.16, bf16[5120,512]{1,0:T(8,128)(2,1)S(1)} %bitcast.18, f32[5120,64]{1,0:T(8,128)S(1)} %prompt_gradient.2.rest_4_), custom_call_target="tpu_custom_call" | custom-call | flops 335544320 | bytes 5898240 | tf_op jit(solution)/shard_map/prompt_gradient/pallas_call | solution.py:421
  (55 shorter events, 10.2 us)
Async XLA Ops:
  0.6 4.8 %collective-permute-start = (bf16[64,5120]{1,0:T(8,128)(2,1)}, bf16[64,5120]{1,0:T(8,128)(2,1)S(1)}, u32[]{:S(2)}, u32[]{:S(2)}) collective-permute-start(bf16[64,5120]{1,0:T(8,128)(2,1)} %x_ref.1), channel_id=1, source_target_pairs={{1,0},{0,1},{3,2},{2,3},{5,4},{4,5},{7,6},{6,7},{9,8},{8,9},{11,10... | collective-permute-start | bytes 1966088 | tf_op jit(solution)/shard_map/ppermute | solution.py:456
  6.5 4.8 %collective-permute-start.1 = (bf16[128,256]{1,0:T(8,128)(2,1)S(1)}, bf16[128,256]{1,0:T(8,128)(2,1)S(1)}, u32[]{:S(2)}, u32[]{:S(2)}) collective-permute-start(bf16[128,256]{1,0:T(8,128)(2,1)S(1)} %get-tuple-element.61), channel_id=1, source_target_pairs={{8,0},{17,1},{10,2},{19,3},{12,4},{21,5},{14,6},{23,7},{0,8},{25,9... | collective-permute-start | bytes 196616 | tf_op jit(solution)/shard_map/ppermute | solution.py:456
  11.3 10.6 %collective-permute-start.3 = (bf16[1552,128]{1,0:T(8,128)(2,1)S(1)}, bf16[1552,128]{1,0:T(8,128)(2,1)S(1)}, u32[]{:S(2)}, u32[]{:S(2)}) collective-permute-start(bf16[1552,128]{1,0:T(8,128)(2,1)S(1)} %get-tuple-element.68), channel_id=1, source_target_pairs={{8,0},{17,1},{10,2},{19,3},{12,4},{21,5},{14,6},{23,7},{0,8},{25,9... | collective-permute-start | bytes 1191944 | tf_op jit(solution)/shard_map/ppermute | solution.py:456
  13.4 8.5 %collective-permute-start.2 = (bf16[4,64,256]{2,1,0:T(8,128)(2,1)S(1)}, bf16[4,64,256]{2,1,0:T(8,128)(2,1)S(1)}, u32[]{:S(2)}, u32[]{:S(2)}) collective-permute-start(bf16[4,64,256]{2,1,0:T(8,128)(2,1)S(1)} %bitcast.19), channel_id=1, source_target_pairs={{4,0},{5,1},{6,2},{7,3},{0,4},{1,5},{2,6},{3,7},{12,8},{13,9},{14,... | collective-permute-start | bytes 393224 | tf_op jit(solution)/shard_map/ppermute | solution.py:456
  16.0 6.2 %collective-permute-start.7 = (bf16[4,64,256]{2,1,0:T(8,128)(2,1)S(1)}, bf16[4,64,256]{2,1,0:T(8,128)(2,1)S(1)}, u32[]{:S(2)}, u32[]{:S(2)}) collective-permute-start(bf16[4,64,256]{2,1,0:T(8,128)(2,1)S(1)} %bitcast.20), channel_id=1, source_target_pairs={{2,0},{3,1},{0,2},{1,3},{6,4},{7,5},{4,6},{5,7},{10,8},{11,9},{8,1... | collective-permute-start | bytes 393224 | tf_op jit(solution)/shard_map/ppermute | solution.py:456
  17.5 6.7 %collective-permute-start.5 = (bf16[1552,128]{1,0:T(8,128)(2,1)S(1)}, bf16[1552,128]{1,0:T(8,128)(2,1)S(1)}, u32[]{:S(2)}, u32[]{:S(2)}) collective-permute-start(bf16[1552,128]{1,0:T(8,128)(2,1)S(1)} %get-tuple-element.71), channel_id=1, source_target_pairs={{1,0},{0,1},{3,2},{2,3},{5,4},{4,5},{7,6},{6,7},{9,8},{8,9},{11,10... | collective-permute-start | bytes 1191944 | tf_op jit(solution)/shard_map/ppermute | solution.py:456
  17.5 7.2 %collective-permute-start.6 = (bf16[1552,128]{1,0:T(8,128)(2,1)S(1)}, bf16[1552,128]{1,0:T(8,128)(2,1)S(1)}, u32[]{:S(2)}, u32[]{:S(2)}) collective-permute-start(bf16[1552,128]{1,0:T(8,128)(2,1)S(1)} %get-tuple-element.73), channel_id=1, source_target_pairs={{9,0},{16,1},{11,2},{18,3},{13,4},{20,5},{15,6},{22,7},{1,8},{24,9... | collective-permute-start | bytes 1191944 | tf_op jit(solution)/shard_map/ppermute | solution.py:456
  22.2 11.3 %collective-permute-start.8 = (bf16[3,4,64,256]{3,2,1,0:T(8,128)(2,1)S(1)}, bf16[3,4,64,256]{3,2,1,0:T(8,128)(2,1)S(1)}, u32[]{:S(2)}, u32[]{:S(2)}) collective-permute-start(bf16[3,4,64,256]{3,2,1,0:T(8,128)(2,1)S(1)} %pad_maximum_fusion), channel_id=1, source_target_pairs={{16,0},{9,1},{18,2},{11,3},{20,4},{13,5},{22,6},{15,7},{24,8},{1,9... | collective-permute-start | bytes 1179656 | tf_op jit(solution)/shard_map/ppermute | solution.py:456
  22.8 5.6 %collective-permute-start.4 = (bf16[4,64,256]{2,1,0:T(8,128)(2,1)S(1)}, bf16[4,64,256]{2,1,0:T(8,128)(2,1)S(1)}, u32[]{:S(2)}, u32[]{:S(2)}) collective-permute-start(bf16[4,64,256]{2,1,0:T(8,128)(2,1)S(1)} %collective-permute-done.2.rest_5_), channel_id=1, source_target_pairs={{2,0},{3,1},{0,2},{1,3},{6,4},{7,5},{4,6},{5,7},{10,8},{11,9},{8,1... | collective-permute-start | bytes 393224 | tf_op jit(solution)/shard_map/ppermute | solution.py:456
  28.4 35.1 %slice-start.1 = ((s8[5242880]{0:T(1024)(128)(4,1)}), s8[1048576]{0:T(1024)(128)(4,1)S(1)}, s32[]{:S(2)}) async-start(s8[5242880]{0:T(1024)(128)(4,1)} %bitcast.15), calls=%async_computation.1 | async-start | bytes 2097152
  28.4 35.1 %slice-start.3 = ((s8[5242880]{0:T(1024)(128)(4,1)}), s8[1048576]{0:T(1024)(128)(4,1)S(1)}, s32[]{:S(2)}) async-start(s8[5242880]{0:T(1024)(128)(4,1)} %bitcast.17), calls=%async_computation.3 | async-start | bytes 2097152
  28.4 5.0 %collective-permute-start.9 = (bf16[1,4,64,256]{3,2,1,0:T(8,128)(2,1)S(1)}, bf16[1,4,64,256]{3,2,1,0:T(8,128)(2,1)S(1)}, u32[]{:S(2)}, u32[]{:S(2)}) collective-permute-start(bf16[1,4,64,256]{3,2,1,0:T(8,128)(2,1)S(1)} %bitcast.26), channel_id=1, source_target_pairs={{16,0},{9,1},{18,2},{11,3},{20,4},{13,5},{22,6},{15,7},{24,8},{1,9... | collective-permute-start | bytes 393224 | tf_op jit(solution)/shard_map/ppermute | solution.py:456
  41.5 5.0 %collective-permute-start.12 = (bf16[1,4,64,256]{3,2,1,0:T(8,128)(2,1)S(1)}, bf16[1,4,64,256]{3,2,1,0:T(8,128)(2,1)S(1)}, u32[]{:S(2)}, u32[]{:S(2)}) collective-permute-start(bf16[1,4,64,256]{3,2,1,0:T(8,128)(2,1)S(1)} %get-tuple-element.88), channel_id=1, source_target_pairs={{0,16},{1,9},{2,18},{3,11},{4,20},{5,13},{6,22},{7,15},{8,24},{9,1... | collective-permute-start | bytes 393224 | tf_op jit(solution)/shard_map/ppermute | solution.py:460
  42.4 6.9 %collective-permute-start.11 = (bf16[2,4,64,256]{3,2,1,0:T(8,128)(2,1)S(1)}, bf16[2,4,64,256]{3,2,1,0:T(8,128)(2,1)S(1)}, u32[]{:S(2)}, u32[]{:S(2)}) collective-permute-start(bf16[2,4,64,256]{3,2,1,0:T(8,128)(2,1)S(1)} %get-tuple-element.81), channel_id=1, source_target_pairs={{0,16},{1,9},{2,18},{3,11},{4,20},{5,13},{6,22},{7,15},{8,24},{9,1... | collective-permute-start | bytes 786440 | tf_op jit(solution)/shard_map/ppermute | solution.py:460
  43.6 14.8 %collective-permute-start.10 = (bf16[1,4,64,256]{3,2,1,0:T(8,128)(2,1)S(1)}, bf16[1,4,64,256]{3,2,1,0:T(8,128)(2,1)S(1)}, u32[]{:S(2)}, u32[]{:S(2)}) collective-permute-start(bf16[1,4,64,256]{3,2,1,0:T(8,128)(2,1)S(1)} %get-tuple-element.79), channel_id=1, source_target_pairs={{0,16},{1,9},{2,18},{3,11},{4,20},{5,13},{6,22},{7,15},{8,24},{9,1... | collective-permute-start | bytes 393224 | tf_op jit(solution)/shard_map/ppermute | solution.py:460
  46.5 5.0 %collective-permute-start.13 = (bf16[4,64,256]{2,1,0:T(8,128)(2,1)S(1)}, bf16[4,64,256]{2,1,0:T(8,128)(2,1)S(1)}, u32[]{:S(2)}, u32[]{:S(2)}) collective-permute-start(bf16[4,64,256]{2,1,0:T(8,128)(2,1)S(1)} %fusion.2), channel_id=1, source_target_pairs={{0,2},{1,3},{2,0},{3,1},{4,6},{5,7},{6,4},{7,5},{8,10},{9,11},{10,... | collective-permute-start | bytes 393224 | tf_op jit(solution)/shard_map/ppermute | solution.py:460
  49.3 5.7 %collective-permute-start.16 = (bf16[128,896]{1,0:T(8,128)(2,1)S(1)}, bf16[128,896]{1,0:T(8,128)(2,1)S(1)}, u32[]{:S(2)}, u32[]{:S(2)}) collective-permute-start(bf16[128,896]{1,0:T(8,128)(2,1)S(1)} %get-tuple-element.93), channel_id=1, source_target_pairs={{0,1},{1,0},{2,3},{3,2},{4,5},{5,4},{6,7},{7,6},{8,9},{9,8},{10,11... | collective-permute-start | bytes 688136 | tf_op jit(solution)/shard_map/ppermute | solution.py:460
  49.3 7.7 %collective-permute-start.17 = (bf16[128,896]{1,0:T(8,128)(2,1)S(1)}, bf16[128,896]{1,0:T(8,128)(2,1)S(1)}, u32[]{:S(2)}, u32[]{:S(2)}) collective-permute-start(bf16[128,896]{1,0:T(8,128)(2,1)S(1)} %get-tuple-element.94), channel_id=1, source_target_pairs={{0,8},{1,17},{2,10},{3,19},{4,12},{5,21},{6,14},{7,23},{8,0},{9,25... | collective-permute-start | bytes 688136 | tf_op jit(solution)/shard_map/ppermute | solution.py:460
  50.2 7.1 %collective-permute-start.18 = (bf16[128,896]{1,0:T(8,128)(2,1)S(1)}, bf16[128,896]{1,0:T(8,128)(2,1)S(1)}, u32[]{:S(2)}, u32[]{:S(2)}) collective-permute-start(bf16[128,896]{1,0:T(8,128)(2,1)S(1)} %get-tuple-element.95), channel_id=1, source_target_pairs={{0,9},{1,16},{2,11},{3,18},{4,13},{5,20},{6,15},{7,22},{8,1},{9,24... | collective-permute-start | bytes 688136 | tf_op jit(solution)/shard_map/ppermute | solution.py:460
  51.6 10.3 %collective-permute-start.15 = (bf16[4,64,256]{2,1,0:T(8,128)(2,1)S(1)}, bf16[4,64,256]{2,1,0:T(8,128)(2,1)S(1)}, u32[]{:S(2)}, u32[]{:S(2)}) collective-permute-start(bf16[4,64,256]{2,1,0:T(8,128)(2,1)S(1)} %fusion.1), channel_id=1, source_target_pairs={{0,4},{1,5},{2,6},{3,7},{4,0},{5,1},{6,2},{7,3},{8,12},{9,13},{10,... | collective-permute-start | bytes 393224 | tf_op jit(solution)/shard_map/ppermute | solution.py:460
  55.0 6.9 %collective-permute-start.14 = (bf16[4,64,256]{2,1,0:T(8,128)(2,1)S(1)}, bf16[4,64,256]{2,1,0:T(8,128)(2,1)S(1)}, u32[]{:S(2)}, u32[]{:S(2)}) collective-permute-start(bf16[4,64,256]{2,1,0:T(8,128)(2,1)S(1)} %convert_add_fusion.2), channel_id=1, source_target_pairs={{0,2},{1,3},{2,0},{3,1},{4,6},{5,7},{6,4},{7,5},{8,10},{9,11},{10,... | collective-permute-start | bytes 393224 | tf_op jit(solution)/shard_map/ppermute | solution.py:460
  62.0 1.5 %collective-permute-start.21 = (bf16[64,256]{1,0:T(8,128)(2,1)S(1)}, bf16[64,256]{1,0:T(8,128)(2,1)S(1)}, u32[]{:S(2)}, u32[]{:S(2)}) collective-permute-start(bf16[64,256]{1,0:T(8,128)(2,1)S(1)} %get-tuple-element.109), channel_id=1, source_target_pairs={{0,1},{1,0},{2,3},{3,2},{4,5},{5,4},{6,7},{7,6},{8,9},{9,8},{10,11... | collective-permute-start | bytes 98312 | tf_op jit(solution)/shard_map/ppermute | solution.py:460
  62.1 4.0 %collective-permute-start.19 = (bf16[64,256]{1,0:T(8,128)(2,1)S(1)}, bf16[64,256]{1,0:T(8,128)(2,1)S(1)}, u32[]{:S(2)}, u32[]{:S(2)}) collective-permute-start(bf16[64,256]{1,0:T(8,128)(2,1)S(1)} %get-tuple-element.106), channel_id=1, source_target_pairs={{0,8},{1,17},{2,10},{3,19},{4,12},{5,21},{6,14},{7,23},{8,0},{9,25... | collective-permute-start | bytes 98312 | tf_op jit(solution)/shard_map/ppermute | solution.py:460
  62.4 3.7 %collective-permute-start.20 = (bf16[64,256]{1,0:T(8,128)(2,1)S(1)}, bf16[64,256]{1,0:T(8,128)(2,1)S(1)}, u32[]{:S(2)}, u32[]{:S(2)}) collective-permute-start(bf16[64,256]{1,0:T(8,128)(2,1)S(1)} %get-tuple-element.107), channel_id=1, source_target_pairs={{0,9},{1,16},{2,11},{3,18},{4,13},{5,20},{6,15},{7,22},{8,1},{9,24... | collective-permute-start | bytes 98312 | tf_op jit(solution)/shard_map/ppermute | solution.py:460
  (8 other events, 92.8 us)
